TPU v7x, 32 devices: a whole 2x2x4 slice. The times are simulated.
32 devices in a mesh: batch: 8 (over z, y), ctx: 4 (over x, core).
Axes of the slice: x: 2, y: 2, z: 4, core: 2. Of those that a mesh axis runs over, the one named last changes fastest.
Arguments:
- block_input: bfloat16 [8, 1024, 2048], P('batch', 'ctx'), may hold values from -6 to 6
- output_grad: bfloat16 [8, 1024, 2048], P('batch', 'ctx'), may hold values from -6 to 6
- documents: int32 [8, 1024], P('batch'), may hold values from 0 to 3, as said below
- span_order: int32 [8, 4], P('batch'), may hold values from 0 to 3, as said below
- attention_norm_gain: bfloat16 [2048], P(('batch', 'ctx')), may hold values from 0.5 to 1.5
- attention_norm_bias: bfloat16 [2048], P(('batch', 'ctx')), may hold values from -1.75 to 1.75
- query_key_value_weight: bfloat16 [2048, 6144], P(('batch', 'ctx')), may hold values from -0.125 to 0.125
- query_key_value_bias: bfloat16 [6144], P(('batch', 'ctx')), may hold values from -1.75 to 1.75
- dense_weight: bfloat16 [2048, 2048], P(('batch', 'ctx')), may hold values from -2 to 2
- dense_bias: bfloat16 [2048], P(('batch', 'ctx')), may hold values from -1.75 to 1.75
- mlp_norm_gain: bfloat16 [2048], P(('batch', 'ctx')), may hold values from 0.5 to 1.5
- mlp_norm_bias: bfloat16 [2048], P(('batch', 'ctx')), may hold values from -1.75 to 1.75
- to_hidden_weight: bfloat16 [2048, 8192], P(('batch', 'ctx')), may hold values from -0.125 to 0.125
- to_hidden_bias: bfloat16 [8192], P(('batch', 'ctx')), may hold values from -3 to 3
- from_hidden_weight: bfloat16 [8192, 2048], P(('batch', 'ctx')), may hold values from -0.0625 to 0.0625
- from_hidden_bias: bfloat16 [2048], P(('batch', 'ctx')), may hold values from -1.75 to 1.75
Outputs:
- block_output: bfloat16 [8, 1024, 2048], P('batch', 'ctx')
- input_grad: bfloat16 [8, 1024, 2048], P('batch', 'ctx')
- attention_norm_gain_grad: float32 [2048], P(('batch', 'ctx'))
- attention_norm_bias_grad: float32 [2048], P(('batch', 'ctx'))
- query_key_value_weight_grad: float32 [2048, 6144], P(('batch', 'ctx'))
- query_key_value_bias_grad: float32 [6144], P(('batch', 'ctx'))
- dense_weight_grad: float32 [2048, 2048], P(('batch', 'ctx'))
- dense_bias_grad: float32 [2048], P(('batch', 'ctx'))
- mlp_norm_gain_grad: float32 [2048], P(('batch', 'ctx'))
- mlp_norm_bias_grad: float32 [2048], P(('batch', 'ctx'))
- to_hidden_weight_grad: float32 [2048, 8192], P(('batch', 'ctx'))
- to_hidden_bias_grad: float32 [8192], P(('batch', 'ctx'))
- from_hidden_weight_grad: float32 [8192, 2048], P(('batch', 'ctx'))
- from_hidden_bias_grad: float32 [2048], P(('batch', 'ctx'))
Inputs may be any that keep to these rules, and one draw needn't show every extreme that they name: `span_order`: each row is a permutation of 0 to 3. documents[s, c * 256 + i] is the document of the token at position span_order[s, c] * 256 + i of sequence s; documents are numbered from 0 upward in order of position.
All inputs are finite; a program needn't handle non-finite values.
Results may differ from a plain program's by a relative error of at most 0.0096.
Values may be sent and summed in bfloat16 or wider, within the bound.
No kernel may reach another device: no remote copies, remote signals or barrier semaphores. Data moves between devices by JAX's collectives and lax.ppermute only.
A program may use at most 448 MiB of HBM per device.

v0:
```python
import jax
import jax.numpy as jnp
from jax import lax
from jax.sharding import PartitionSpec as P

D = 2048
H = 16
HD = 128
ROT = 32


epsilon = 1e-05
neg_large = -1e30
theta_base = 10000.0


def layer_norm(values, scaling, offset_row):
    centre = values - jnp.mean(values, axis=-1, keepdims=True)
    spread = jnp.mean(centre * centre, axis=-1, keepdims=True)
    return centre * lax.rsqrt(spread + epsilon) * scaling + offset_row


def rotate(values, positions, direction):
    half_rot = ROT // 2
    powers = jnp.arange(half_rot, dtype=jnp.float32) * (2.0 / ROT)
    inverse = jnp.power(theta_base, -powers)
    angles = positions.astype(jnp.float32)[:, None] * inverse[None, :]
    cosine = jnp.cos(angles)[:, None, :]
    sine_part = direction * jnp.sin(angles)[:, None, :]
    first_half = values[..., :half_rot]
    second = values[..., half_rot:ROT]
    remainder = values[..., ROT:]
    return jnp.concatenate(
        [
            first_half * cosine - second * sine_part,
            second * cosine + first_half * sine_part,
            remainder,
        ],
        axis=-1,
    )


def exact_gelu(values):
    return jax.nn.gelu(values, approximate=False)


def contract_rows(left_side, right_side):
    return lax.dot_general(
        left_side, right_side, (((0,), (0,)), ((), ())), preferred_element_type=jnp.float32
    )


def contract_cols(left_side, right_side):
    return lax.dot_general(
        left_side, right_side, (((1,), (1,)), ((), ())), preferred_element_type=jnp.float32
    )


def attend(query_part, key_heads, value_heads, allowed, score_scale):
    raw_scores = (
        jnp.einsum("qhd,khd->hqk", query_part, key_heads, preferred_element_type=jnp.float32)
        * score_scale
    )
    masked = jnp.where(allowed[None], raw_scores, neg_large)
    highest_score = jnp.max(masked, axis=-1, keepdims=True)
    exponent = jnp.exp(masked - highest_score)
    row_total = jnp.sum(exponent, axis=-1, keepdims=True)
    weights_low = (exponent / row_total).astype(jnp.bfloat16)
    log_total = highest_score + jnp.log(row_total)
    mixed = jnp.einsum("hqk,khd->qhd", weights_low, value_heads, preferred_element_type=jnp.float32)
    return (mixed, log_total)


def attend_back(
    query_part, key_heads, value_heads, allowed, log_total, grad_mixed_low, score_scale
):
    again_scores = (
        jnp.einsum("qhd,khd->hqk", query_part, key_heads, preferred_element_type=jnp.float32)
        * score_scale
    )
    weights_again = jnp.where(allowed[None], jnp.exp(again_scores - log_total), 0.0)
    weights_again_low = weights_again.astype(jnp.bfloat16)
    grad_values = jnp.einsum(
        "hqk,qhd->khd", weights_again_low, grad_mixed_low, preferred_element_type=jnp.float32
    )
    grad_weights = jnp.einsum(
        "qhd,khd->hqk", grad_mixed_low, value_heads, preferred_element_type=jnp.float32
    )
    inner_sum = jnp.sum(weights_again * grad_weights, axis=-1, keepdims=True)
    grad_scores_low = (weights_again * (grad_weights - inner_sum)).astype(jnp.bfloat16)
    grad_queries = (
        jnp.einsum("hqk,khd->qhd", grad_scores_low, key_heads, preferred_element_type=jnp.float32)
        * score_scale
    )
    grad_keys = (
        jnp.einsum("hqk,qhd->khd", grad_scores_low, query_part, preferred_element_type=jnp.float32)
        * score_scale
    )
    return (grad_queries, grad_keys, grad_values)


def shards(
    block_input,
    output_grad,
    documents,
    span_order,
    attention_norm_gain,
    attention_norm_bias,
    query_key_value_weight,
    query_key_value_bias,
    dense_weight,
    dense_bias,
    mlp_norm_gain,
    mlp_norm_bias,
    to_hidden_weight,
    to_hidden_bias,
    from_hidden_weight,
    from_hidden_bias,
):
    span_len = block_input.shape[1]
    score_scale = HD ** (-0.5)
    offsets = jnp.arange(span_len, dtype=jnp.int32)
    all_positions = (span_order[0][:, None] * span_len + offsets[None, :]).reshape(-1)
    own_start = lax.axis_index("ctx") * span_len
    own_positions = lax.dynamic_slice_in_dim(all_positions, own_start, span_len)
    all_documents = documents[0]
    own_documents = lax.dynamic_slice_in_dim(all_documents, own_start, span_len)
    tokens_in = block_input[0].astype(jnp.float32)
    upstream = output_grad[0]
    upstream_wide = upstream.astype(jnp.float32)
    attention_set = (
        lax.all_gather(attention_norm_gain, ("batch", "ctx"), axis=0, tiled=True),
        lax.all_gather(attention_norm_bias, ("batch", "ctx"), axis=0, tiled=True),
        lax.all_gather(query_key_value_weight, ("batch", "ctx"), axis=0, tiled=True),
        lax.all_gather(query_key_value_bias, ("batch", "ctx"), axis=0, tiled=True),
        lax.all_gather(dense_weight, ("batch", "ctx"), axis=0, tiled=True),
        lax.all_gather(dense_bias, ("batch", "ctx"), axis=0, tiled=True),
    )
    mlp_set = (
        lax.all_gather(mlp_norm_gain, ("batch", "ctx"), axis=0, tiled=True),
        lax.all_gather(mlp_norm_bias, ("batch", "ctx"), axis=0, tiled=True),
        lax.all_gather(to_hidden_weight, ("batch", "ctx"), axis=0, tiled=True),
        lax.all_gather(to_hidden_bias, ("batch", "ctx"), axis=0, tiled=True),
        lax.all_gather(from_hidden_weight, ("batch", "ctx"), axis=0, tiled=True),
        lax.all_gather(from_hidden_bias, ("batch", "ctx"), axis=0, tiled=True),
    )
    allowed = (all_positions[None, :] <= own_positions[:, None]) & (
        all_documents[None, :] == own_documents[:, None]
    )
    gain_one, shift_one, joined_full, joined_shift, dense_full, dense_shift = attention_set
    normed, norm_pull = jax.vjp(
        layer_norm, tokens_in, gain_one.astype(jnp.float32), shift_one.astype(jnp.float32)
    )
    normed_low = normed.astype(jnp.bfloat16)
    joined_lin = jnp.dot(
        normed_low, joined_full, preferred_element_type=jnp.float32
    ) + joined_shift.astype(jnp.float32)
    query_part = rotate(joined_lin[:, :D].reshape(span_len, H, HD), own_positions, 1.0).astype(
        jnp.bfloat16
    )
    key_part = rotate(joined_lin[:, D : 2 * D].reshape(span_len, H, HD), own_positions, 1.0).astype(
        jnp.bfloat16
    )
    value_part = joined_lin[:, 2 * D :].astype(jnp.bfloat16)
    key_all, value_all = (
        lax.all_gather(key_part.reshape(span_len, D), "ctx", axis=0, tiled=True),
        lax.all_gather(value_part, "ctx", axis=0, tiled=True),
    )
    key_heads = key_all.reshape(-1, H, HD)
    value_heads = value_all.reshape(-1, H, HD)
    mixed, log_total = attend(query_part, key_heads, value_heads, allowed, score_scale)
    mixed_low = mixed.reshape(span_len, D).astype(jnp.bfloat16)
    attention = jnp.dot(
        mixed_low, dense_full, preferred_element_type=jnp.float32
    ) + dense_shift.astype(jnp.float32)
    gain_two, shift_two, hidden_full, hidden_shift, back_full, back_shift = mlp_set
    normed_two, norm_pull_two = jax.vjp(
        layer_norm, tokens_in, gain_two.astype(jnp.float32), shift_two.astype(jnp.float32)
    )
    normed_two_low = normed_two.astype(jnp.bfloat16)
    hidden = jnp.dot(
        normed_two_low, hidden_full, preferred_element_type=jnp.float32
    ) + hidden_shift.astype(jnp.float32)
    activated, gelu_pull = jax.vjp(exact_gelu, hidden)
    activated_low = activated.astype(jnp.bfloat16)
    feed_out = jnp.dot(
        activated_low, back_full, preferred_element_type=jnp.float32
    ) + back_shift.astype(jnp.float32)
    block_output = (tokens_in + attention + feed_out).astype(jnp.bfloat16)[None]
    back_mlp = (
        lax.all_gather(mlp_norm_gain, ("batch", "ctx"), axis=0, tiled=True),
        lax.all_gather(mlp_norm_bias, ("batch", "ctx"), axis=0, tiled=True),
        lax.all_gather(to_hidden_weight, ("batch", "ctx"), axis=0, tiled=True),
        lax.all_gather(to_hidden_bias, ("batch", "ctx"), axis=0, tiled=True),
        lax.all_gather(from_hidden_weight, ("batch", "ctx"), axis=0, tiled=True),
        lax.all_gather(from_hidden_bias, ("batch", "ctx"), axis=0, tiled=True),
    )
    back_attention = (
        lax.all_gather(attention_norm_gain, ("batch", "ctx"), axis=0, tiled=True),
        lax.all_gather(attention_norm_bias, ("batch", "ctx"), axis=0, tiled=True),
        lax.all_gather(query_key_value_weight, ("batch", "ctx"), axis=0, tiled=True),
        lax.all_gather(query_key_value_bias, ("batch", "ctx"), axis=0, tiled=True),
        lax.all_gather(dense_weight, ("batch", "ctx"), axis=0, tiled=True),
        lax.all_gather(dense_bias, ("batch", "ctx"), axis=0, tiled=True),
    )
    grad_back_weight = contract_rows(activated_low, upstream)
    grad_back_bias = jnp.sum(upstream_wide, axis=0)
    grad_activated = contract_cols(upstream, back_mlp[4])
    grad_hidden_low = gelu_pull(grad_activated)[0].astype(jnp.bfloat16)
    grad_hidden_bias = jnp.sum(grad_hidden_low.astype(jnp.float32), axis=0)
    grad_hidden_weight = contract_rows(normed_two_low, grad_hidden_low)
    grad_normed_two = contract_cols(grad_hidden_low, back_mlp[2])
    grad_from_two, grad_gain_two, grad_shift_two = norm_pull_two(grad_normed_two)
    mlp_grads = (
        lax.psum_scatter(grad_gain_two, ("batch", "ctx"), scatter_dimension=0, tiled=True),
        lax.psum_scatter(grad_shift_two, ("batch", "ctx"), scatter_dimension=0, tiled=True),
        lax.psum_scatter(grad_hidden_weight, ("batch", "ctx"), scatter_dimension=0, tiled=True),
        lax.psum_scatter(grad_hidden_bias, ("batch", "ctx"), scatter_dimension=0, tiled=True),
        lax.psum_scatter(grad_back_weight, ("batch", "ctx"), scatter_dimension=0, tiled=True),
        lax.psum_scatter(grad_back_bias, ("batch", "ctx"), scatter_dimension=0, tiled=True),
    )
    grad_dense_weight = contract_rows(mixed_low, upstream)
    grad_dense_bias = jnp.sum(upstream_wide, axis=0)
    grad_mixed_low = (
        contract_cols(upstream, back_attention[4]).astype(jnp.bfloat16).reshape(span_len, H, HD)
    )
    grad_queries, grad_keys, grad_values = attend_back(
        query_part, key_heads, value_heads, allowed, log_total, grad_mixed_low, score_scale
    )
    grad_keys_own, grad_values_own = (
        lax.psum_scatter(grad_keys.reshape(-1, D), "ctx", scatter_dimension=0, tiled=True),
        lax.psum_scatter(grad_values.reshape(-1, D), "ctx", scatter_dimension=0, tiled=True),
    )
    grad_query_lin = rotate(grad_queries, own_positions, -1.0).reshape(span_len, D)
    grad_key_lin = rotate(grad_keys_own.reshape(span_len, H, HD), own_positions, -1.0).reshape(
        span_len, D
    )
    grad_joined_low = jnp.concatenate(
        [grad_query_lin, grad_key_lin, grad_values_own], axis=1
    ).astype(jnp.bfloat16)
    grad_joined_bias = jnp.sum(grad_joined_low.astype(jnp.float32), axis=0)
    grad_joined_weight = contract_rows(normed_low, grad_joined_low)
    grad_normed = contract_cols(grad_joined_low, back_attention[2])
    grad_from_one, grad_gain_one, grad_shift_one = norm_pull(grad_normed)
    attention_grads = (
        lax.psum_scatter(grad_gain_one, ("batch", "ctx"), scatter_dimension=0, tiled=True),
        lax.psum_scatter(grad_shift_one, ("batch", "ctx"), scatter_dimension=0, tiled=True),
        lax.psum_scatter(grad_joined_weight, ("batch", "ctx"), scatter_dimension=0, tiled=True),
        lax.psum_scatter(grad_joined_bias, ("batch", "ctx"), scatter_dimension=0, tiled=True),
        lax.psum_scatter(grad_dense_weight, ("batch", "ctx"), scatter_dimension=0, tiled=True),
        lax.psum_scatter(grad_dense_bias, ("batch", "ctx"), scatter_dimension=0, tiled=True),
    )
    input_grad = (upstream_wide + grad_from_one + grad_from_two).astype(jnp.bfloat16)[None]
    return (
        block_output,
        input_grad,
        attention_grads[0],
        attention_grads[1],
        attention_grads[2],
        attention_grads[3],
        attention_grads[4],
        attention_grads[5],
        mlp_grads[0],
        mlp_grads[1],
        mlp_grads[2],
        mlp_grads[3],
        mlp_grads[4],
        mlp_grads[5],
    )


def solution(mesh):
    return jax.shard_map(
        shards,
        mesh=mesh,
        in_specs=(
            P("batch", "ctx", None),
            P("batch", "ctx", None),
            P("batch", None),
            P("batch", None),
            P(("batch", "ctx")),
            P(("batch", "ctx")),
            P(("batch", "ctx"), None),
            P(("batch", "ctx")),
            P(("batch", "ctx"), None),
            P(("batch", "ctx")),
            P(("batch", "ctx")),
            P(("batch", "ctx")),
            P(("batch", "ctx"), None),
            P(("batch", "ctx")),
            P(("batch", "ctx"), None),
            P(("batch", "ctx")),
        ),
        out_specs=(
            P("batch", "ctx", None),
            P("batch", "ctx", None),
            P(("batch", "ctx")),
            P(("batch", "ctx")),
            P(("batch", "ctx"), None),
            P(("batch", "ctx")),
            P(("batch", "ctx"), None),
            P(("batch", "ctx")),
            P(("batch", "ctx")),
            P(("batch", "ctx")),
            P(("batch", "ctx"), None),
            P(("batch", "ctx")),
            P(("batch", "ctx"), None),
            P(("batch", "ctx")),
        ),
        check_vma=False,
    )
```

profile of v0, /device:TPU:0, one launch (start us, length us, event | category | flops | bytes accessed | tf_op | source)
XLA Modules:
  0.0 3067.2 jit_solution(1352736010477356038)
XLA Ops:
  14.5 0.8 dynamic-update-slice.2
  15.4 44.4 %all-reduce.15 = (bf16[6144]{0:T(1024)(128)(2,1)S(1)}, bf16[2048]{0:T(1024)(128)(2,1)S(1)}, bf16[2048]{0:T(1024)(128)(2,1)S(1)}, bf16[2048]{0:T(1024)(128)(2,1)}...) all-reduce(bf16[6144]{0:T(1024)(128)(2,1)S(1)} %dynamic-update-slic, ...), channel_id=1, replica_groups=mesh['batch'=8,'ctx'=4] {'batch','ctx'}, use_global_device_ids=true, to_apply=%add.2 | all-reduce | flops 18432 | bytes 73728
  59.9 1.4 convert_reduce_fusion.3
  61.4 1.6 fusion.41
  64.3 105.3 %all-gather.8.cloned.1.call-done = bf16[2048,6144]{1,0:T(8,128)(2,1)} async-done(((bf16[64,6144]{1,0:T(8,128)(2,1)}), bf16[2048,6144]{1,0:T(8,128)(2,1)}) %all-gather.8.cloned.1.call-update) | async-done | bytes 25165840 | tf_op jit(solution)/shard_map/all_gather | solution.py:134
  169.7 12.1 convolution_add_fusion.1
  181.7 2.7 copy-done.5
  184.4 1.6 fusion.79
  186.0 2.9 copy.84
  188.9 1.8 copy.85
  190.7 1.5 slice.104
  192.2 1.4 subtract_convert_fusion.3
  193.5 1.1 pad_maximum_fusion.2
  194.7 2.7 slice.101
  199.1 49.0 %all-gather.14.cloned.1.call-done = bf16[2048,2048]{1,0:T(8,128)(2,1)} async-done(((bf16[64,2048]{1,0:T(8,128)(2,1)}), bf16[2048,2048]{1,0:T(8,128)(2,1)}) %all-gather.14.cloned.1.call-update) | async-done | bytes 8388624 | tf_op jit(solution)/shard_map/all_gather | solution.py:136
  248.2 6.7 convolution_convert_fusion
  254.9 1.5 copy.94
  256.4 1.7 slice.105
  258.1 25.8 all-gather.12.cloned.1.call-done
  284.0 5.2 select_reduce_fusion
  289.2 4.4 fusion
  293.6 2.6 copy-done
  296.2 24.3 all-gather.10.cloned.1.call-done
  320.5 14.2 multiply_reduce_fusion
  334.7 12.3 multiply_convert_fusion
  347.0 5.4 broadcast_multiply_fusion
  353.4 9.7 fusion.2
  363.8 41.6 %all-gather = bf16[32,1,256]{2,1,0:T(2,128)(2,1)S(1)} all-gather(bf16[1,1,256]{2,1,0:T(2,128)(2,1)S(1)} %reshape.314), channel_id=1, replica_groups=mesh['batch'=8,'ctx'=4] {'batch','ctx'}, dimensions={0}, use_global_device_ids=true | all-gather | bytes 16896 | tf_op jit(solution)/shard_map/all_gather | solution.py:143
  405.5 7.6 multiply_bitcast_fusion
  413.1 1.3 copy-done.4
  414.4 1.0 slice.103
  415.4 11.8 fusion.46
  427.2 91.2 %all-gather.16.cloned.1.call-done = bf16[2048,8192]{1,0:T(8,128)(2,1)} async-done(((bf16[64,8192]{1,0:T(8,128)(2,1)}), bf16[2048,8192]{1,0:T(8,128)(2,1)}) %all-gather.16.cloned.1.call-update) | async-done | bytes 33554448 | tf_op jit(solution)/shard_map/all_gather | solution.py:142
  518.4 18.0 convolution_add_fusion
  536.4 177.7 %all-gather.18.cloned.1.call-done = bf16[8192,2048]{1,0:T(8,128)(2,1)} async-done(((bf16[256,2048]{1,0:T(8,128)(2,1)}), bf16[8192,2048]{1,0:T(8,128)(2,1)}) %all-gather.18.cloned.1.call-update) | async-done | bytes 33554448 | tf_op jit(solution)/shard_map/all_gather | solution.py:144
  714.2 33.7 %convert_reduce_fusion = (f32[8192]{0:T(1024)}, bf16[256,8192]{1,0:T(8,128)(2,1)}) fusion(f32[256,8192]{1,0:T(8,128)} %convolution_add_fusion, bf16[8192,2048]{1,0:T(8,128)(2,1)} %all-gather.18.cloned.1.call-done, bf16[1,256,2048]{2,1,0:T(8,128)(2,1)S(1)} %copy-done.6), kind=kOutput, calls=%fused_computation.12 | convolution fusion | flops 8745115648 | bytes 47218688 | tf_op jit(solution)/shard_map/dot_general | solution.py:54
  747.9 17.3 fusion.80
  765.2 21.5 reduce-scatter.7.cloned.1.call-done
  786.7 1.5 slice.102
  788.2 1.4 subtract_convert_fusion.1
  789.6 1.2 pad_maximum_fusion.3
  790.7 70.4 %reduce-scatter.9.cloned.1.call-done = f32[256,2048]{0,1:T(8,128)} async-done(((f32[1024,2048]{0,1:T(8,128)}), f32[256,2048]{0,1:T(8,128)}) %reduce-scatter.9.cloned.1.call-update) | async-done | bytes 2097168 | tf_op jit(solution)/shard_map/reduce_scatter | solution.py:232
  861.2 1.7 convert.63
  862.9 2.6 convert_reduce_fusion.1
  865.5 14.6 fusion.77
  880.2 4.4 fusion.40
  884.6 5.4 convert_reduce_fusion.2
  890.1 9.7 fusion.52
  900.5 19.0 fusion.70
  919.6 1.1 copy-done.8
  920.8 34.0 %fusion.50 = f32[8192,2048]{1,0:T(8,128)} fusion(bf16[1,256,2048]{2,1,0:T(8,128)(2,1)S(1)} %copy-done.8, f32[256,8192]{1,0:T(8,128)} %convolution_add_fusion), kind=kOutput, calls=%fused_computation.89 | convolution fusion | flops 8726249472 | bytes 76546048 | tf_op jit(solution)/shard_map/dot_general | solution.py:48
  955.4 25.5 fusion.67
  982.1 5.7 fusion.20
  987.9 31.2 %fusion.34 = bf16[1,256,2048]{2,1,0:T(8,128)(2,1)} fusion(f32[256,2048]{1,0:T(8,128)S(1)} %fusion.20, bf16[8192,2048]{1,0:T(8,128)(2,1)} %all-gather.18.cloned.1.call-done, f32[2048]{0:T(1024)S(1)} %convert_element_type.112, f32[256,8192]{1,0:T(8,128)} %convolution_add_fusion), kind=kOutput, calls=%fused_computation.65 | convolution fusion | flops 8727822336 | bytes 45096960 | tf_op jit(solution)/shard_map/dot_general | solution.py:186
  1019.1 1.3 dynamic-slice.1
  1021.1 1.3 dynamic-slice.2
  1022.3 1.3 dynamic-slice.5
  1023.6 1.3 dynamic-slice.6
  1024.9 1.3 dynamic-slice.3
  1026.2 1.3 dynamic-slice.7
  1027.5 173.3 %reduce-scatter.13.cloned.1.call-done = f32[64,2048]{1,0:T(8,128)} async-done(((f32[2048,2048]{1,0:T(8,128)}), f32[64,2048]{1,0:T(8,128)}) %reduce-scatter.13.cloned.1.call-update) | async-done | bytes 524304 | tf_op jit(solution)/shard_map/reduce_scatter | solution.py:250
  1200.8 441.4 %reduce-scatter.11.cloned.1.call-done = f32[64,6144]{1,0:T(8,128)} async-done(((f32[2048,6144]{1,0:T(8,128)}), f32[64,6144]{1,0:T(8,128)}) %reduce-scatter.11.cloned.1.call-update) | async-done | bytes 1572880 | tf_op jit(solution)/shard_map/reduce_scatter | solution.py:248
  1642.2 704.5 %reduce-scatter.17.cloned.1.call-done = f32[256,2048]{1,0:T(8,128)} async-done(((f32[8192,2048]{1,0:T(8,128)}), f32[256,2048]{1,0:T(8,128)}) %reduce-scatter.17.cloned.1.call-update) | async-done | bytes 2097168 | tf_op jit(solution)/shard_map/reduce_scatter | solution.py:219
  2346.7 713.3 %reduce-scatter.15.cloned.1.call-done = f32[64,8192]{1,0:T(8,128)} async-done(((f32[2048,8192]{1,0:T(8,128)}), f32[64,8192]{1,0:T(8,128)}) %reduce-scatter.15.cloned.1.call-update) | async-done | bytes 2097168 | tf_op jit(solution)/shard_map/reduce_scatter | solution.py:217
  (116 shorter events, 16.1 us)
Async XLA Ops:
  7.2 162.5 %all-gather.8.cloned.1.call-start = ((), (), s32[]{:S(2)}) async-start(), calls=%async_computation.6 | async-start | bytes 25952256 | tf_op jit(solution)/shard_map/all_gather | solution.py:134
  7.9 240.3 %all-gather.14.cloned.1.call-start = ((), (), s32[]{:S(2)}) async-start(), calls=%async_computation.9 | async-start | bytes 8650752 | tf_op jit(solution)/shard_map/all_gather | solution.py:136
  8.7 275.3 %all-gather.12.cloned.1.call-start = ((), (), s32[]{:S(2)}) async-start(), calls=%async_computation.8 | async-start | bytes 5242880 | tf_op jit(solution)/shard_map/all_gather | solution.py:166
  59.8 109.8 %copy-start.11 = (f32[2048]{0:T(1024)}, f32[2048]{0:T(1024)S(1)}, u32[]{:S(2)}) copy-start(f32[2048]{0:T(1024)S(1)} %convert_element_type.96) | copy-start | bytes 24580
  59.8 109.8 %copy-start.13 = (f32[2048]{0:T(1024)}, f32[2048]{0:T(1024)S(1)}, u32[]{:S(2)}) copy-start(f32[2048]{0:T(1024)S(1)} %convert_element_type.97) | copy-start | bytes 24580
  63.0 0.6 copy-start.20
  64.3 127.8 %copy-start.17 = (f32[256,16]{0,1:T(8,128)}, f32[256,16]{0,1:T(8,128)S(1)}, u32[]{:S(2)}) copy-start(f32[256,16]{0,1:T(8,128)S(1)} %get-tuple-element.62) | copy-start | bytes 49156
  181.7 2.7 copy-start.5
  188.8 10.0 copy-start.22
  188.8 59.3 %copy-start.6 = (bf16[1,256,2048]{2,1,0:T(8,128)(2,1)S(1)}, bf16[1,256,2048]{2,1,0:T(8,128)(2,1)}, u32[]{:S(2)}) copy-start(bf16[1,256,2048]{2,1,0:T(8,128)(2,1)} %param.17) | copy-start | bytes 3145732
  194.6 125.9 %all-gather.10.cloned.1.call-start = ((), (), s32[]{:S(2)}) async-start(), calls=%async_computation.7 | async-start | bytes 5242880 | tf_op jit(solution)/shard_map/all_gather | solution.py:167
  197.4 321.0 %all-gather.16.cloned.1.call-start = ((), (), s32[]{:S(2)}) async-start(), calls=%async_computation.10 | async-start | bytes 34603008 | tf_op jit(solution)/shard_map/all_gather | solution.py:142
  198.0 516.2 %all-gather.18.cloned.1.call-start = ((), (), s32[]{:S(2)}) async-start(), calls=%async_computation.11 | async-start | bytes 34603008 | tf_op jit(solution)/shard_map/all_gather | solution.py:144
  198.6 588.1 %reduce-scatter.7.cloned.1.call-start = ((), (), s32[]{:S(2)}) async-start(), calls=%async_computation.12 | async-start | bytes 10485760 | tf_op jit(solution)/shard_map/reduce_scatter | solution.py:231
  289.2 7.0 copy-start
  347.0 5.8 copy-start.1
  352.9 508.3 %reduce-scatter.9.cloned.1.call-start = ((), (), s32[]{:S(2)}) async-start(), calls=%async_computation.13 | async-start | bytes 10485760 | tf_op jit(solution)/shard_map/reduce_scatter | solution.py:232
  363.1 0.7 copy-start.25
  363.1 656.0 %all-reduce.18.cloned.1.call-start = ((), (), s32[]{:S(2)}) async-start(), calls=%async_computation.18 | async-start | bytes 196608
  363.7 51.6 %copy-start.9 = (bf16[1024,2048]{1,0:T(8,128)(2,1)S(1)}, bf16[1024,2048]{1,0:T(8,128)(2,1)}, u32[]{:S(2)}) copy-start(bf16[1024,2048]{1,0:T(8,128)(2,1)} %all-gather.10.cloned.1.call-done) | copy-start | bytes 12582916
  363.8 154.7 %copy-start.15 = (f32[2048]{0:T(1024)}, f32[2048]{0:T(1024)S(1)}, u32[]{:S(2)}) copy-start(f32[2048]{0:T(1024)S(1)} %convert_element_type.108) | copy-start | bytes 24580
  413.1 1.3 copy-start.4
  415.4 103.1 %copy-start.2 = (bf16[1,256,2048]{2,1,0:T(8,128)(2,1)S(1)}, bf16[1,256,2048]{2,1,0:T(8,128)(2,1)}, u32[]{:S(2)}) copy-start(bf16[1,256,2048]{2,1,0:T(8,128)(2,1)} %param.16) | copy-start | bytes 3145732
  747.9 40.3 %copy-start.18 = (f32[256,16]{0,1:T(8,128)S(1)}, f32[256,16]{0,1:T(8,128)}, u32[]{:S(2)}) copy-start(f32[256,16]{0,1:T(8,128)} %copy-done.17) | copy-start | bytes 49156
  747.9 40.3 %copy-start.19 = (f32[256,16]{0,1:T(8,128)S(1)}, f32[256,16]{0,1:T(8,128)}, u32[]{:S(2)}) copy-start(f32[256,16]{0,1:T(8,128)} %get-tuple-element.60) | copy-start | bytes 49156
  747.9 41.7 %copy-start.10 = (bf16[256,16,96]{0,2,1:T(8,128)(2,1)S(1)}, bf16[256,16,96]{0,2,1:T(8,128)(2,1)}, u32[]{:S(2)}) copy-start(bf16[256,16,96]{0,2,1:T(8,128)(2,1)} %slice.103) | copy-start | bytes 2359300
  765.2 100.3 %copy-start.12 = (f32[2048]{0:T(1024)S(1)}, f32[2048]{0:T(1024)}, u32[]{:S(2)}) copy-start(f32[2048]{0:T(1024)} %copy-done.11) | copy-start | bytes 24580
  865.5 14.6 copy-start.21
  865.5 19.1 copy-start.7
  890.0 310.8 %reduce-scatter.13.cloned.1.call-start = ((), (), s32[]{:S(2)}) async-start(), calls=%async_computation.15 | async-start | bytes 17301504 | tf_op jit(solution)/shard_map/reduce_scatter | solution.py:250
  899.8 0.7 copy-start.14
  899.8 742.4 %reduce-scatter.11.cloned.1.call-start = ((), (), s32[]{:S(2)}) async-start(), calls=%async_computation.14 | async-start | bytes 51904512 | tf_op jit(solution)/shard_map/reduce_scatter | solution.py:248
  919.5 1.2 copy-start.8
  919.6 1427.1 %reduce-scatter.17.cloned.1.call-start = ((), (), s32[]{:S(2)}) async-start(), calls=%async_computation.17 | async-start | bytes 69206016 | tf_op jit(solution)/shard_map/reduce_scatter | solution.py:219
  954.7 0.7 copy-start.16
  954.7 2105.2 %reduce-scatter.15.cloned.1.call-start = ((), (), s32[]{:S(2)}) async-start(), calls=%async_computation.16 | async-start | bytes 69206016 | tf_op jit(solution)/shard_map/reduce_scatter | solution.py:217
  980.9 0.7 copy-start.24
  980.9 0.7 copy-start.23
  980.9 1.2 copy-start.3
  1021.1 2039.4 %copy-start.26 = (f32[64]{0:T(128)}, f32[64]{0:T(128)S(1)}, u32[]{:S(2)}) copy-start(f32[64]{0:T(128)S(1)} %dynamic-slice.4) | copy-start | bytes 772
Sparse Core Ops, SparseCore 0:
  10.9 158.7 all-gather.7
  172.5 75.6 all-gather.13
  250.3 33.5 all-gather.11
  285.9 34.4 all-gather.9
  323.2 195.1 all-gather.15
  521.1 192.9 all-gather.17
  716.8 69.8 reduce-scatter.6
  789.4 71.6 reduce-scatter.8
  890.2 124.0 all-reduce.17
  1017.1 183.6 reduce-scatter.12
  1208.9 433.1 reduce-scatter.10
  1645.1 701.5 reduce-scatter.16
  2349.7 710.2 reduce-scatter.14
where the time goes:
time: 3080 us; the launch traced here: 3070 us
  waiting for transfers between devices  2600 us (84%)
  matrix products  282 us (9%)
  blocking collectives  86.1 us (3%)
  local copies, waits for them, and re-layouts  42.8 us (1%)
  other arithmetic  40.8 us (1%)
    reduce_scatter x1, waiting for transfers between devices, shards(): lax.psum_scatter(grad_hidden_weight, ('batch', 'ctx'), scatter_dimension=...  713 us
    reduce_scatter x1, waiting for transfers between devices, shards(): lax.psum_scatter(grad_back_weight, ('batch', 'ctx'), scatter_dimension=0,...  704 us
    reduce_scatter x1, waiting for transfers between devices, shards(): lax.psum_scatter(grad_joined_weight, ('batch', 'ctx'), scatter_dimension=...  441 us
    all_gather x1, waiting for transfers between devices, shards(): lax.all_gather(from_hidden_weight, ('batch', 'ctx'), axis=0, tiled=True)  178 us
    reduce_scatter x1, waiting for transfers between devices, shards(): lax.psum_scatter(grad_dense_weight, ('batch', 'ctx'), scatter_dimension=0...  173 us
    all_gather x1, waiting for transfers between devices, shards(): lax.all_gather(query_key_value_weight, ('batch', 'ctx'), axis=0, tiled=True)  105 us
    all_gather x1, waiting for transfers between devices, shards(): lax.all_gather(to_hidden_weight, ('batch', 'ctx'), axis=0, tiled=True)  91.2 us
    dot_general x4, matrix products, contract_rows(): lax.dot_general(left_side, right_side, (((0,), (0,)), ((), ())), preferre...  88.2 us
  transfers between devices with their start and end apart: 13, of which 12 were waited for; matrix products, arithmetic and copies ran while one was open for 11% of the time, Pallas kernels for 0%

commit v1 on v0

v1 whole, which is shorter than its diff:
```python
import functools

import jax
import jax.numpy as jnp
from jax import lax
from jax.experimental import pallas as pl
from jax.experimental.pallas import tpu as pltpu
from jax.sharding import Mesh, PartitionSpec as P

D = 2048
H = 16
HD = 128
ROT = 32
FF = 8192
EPS = 1e-05
NEG = -1e30
THETA = 10000.0
BF = jnp.bfloat16
F32 = jnp.float32
AXES = ("zh", "zl", "y", "x", "core")
QB = 256


def flip(v, axis):
    return lax.ppermute(v, axis, [(0, 1), (1, 0)])


def dot(a, b, ca, cb):
    return lax.dot_general(a, b, (((ca,), (cb,)), ((), ())), preferred_element_type=F32)


def turn(v, cos, sin):
    lane = lax.broadcasted_iota(jnp.int32, v.shape, 1)
    half = ROT // 2
    swapped = jnp.where(lane < half, pltpu.roll(v, HD - half, 1), pltpu.roll(v, half, 1))
    return v * cos + swapped * sin


def attention_kernel(
    q, k, v, do, cq, sq, ck, sk, pq, eq, pk, ek, o, dq, dk, dv, ks, vs, dka, dva
):
    i = pl.program_id(2)
    scale = HD ** (-0.5)

    @pl.when(i == 0)
    def _():
        ks[...] = turn(k[...], ck[...], sk[...]).astype(BF)
        vs[...] = v[...].astype(BF)
        dka[...] = jnp.zeros_like(dka)
        dva[...] = jnp.zeros_like(dva)

    qr = turn(q[...], cq[...], sq[...]).astype(BF)
    s = dot(qr, ks[...], 1, 1) * scale
    allowed = (pk[...] <= pq[...]) & (ek[...] == eq[...])
    s = jnp.where(allowed, s, NEG)
    e = jnp.exp(s - jnp.max(s, axis=-1, keepdims=True))
    p = e / jnp.sum(e, axis=-1, keepdims=True)
    low = p.astype(BF)
    o[...] = dot(low, vs[...], 1, 0).astype(BF)
    dp = dot(do[...], vs[...], 1, 1)
    ds = (p * (dp - jnp.sum(p * dp, axis=-1, keepdims=True))).astype(BF)
    dq[...] = turn(dot(ds, ks[...], 1, 0) * scale, cq[...], -sq[...]).astype(BF)
    dva[...] += dot(low, do[...], 0, 0)
    dka[...] += dot(ds, qr, 0, 0)

    @pl.when(i == pl.num_programs(2) - 1)
    def _():
        dk[...] = turn(dka[...] * scale, ck[...], -sk[...]).astype(BF)
        dv[...] = dva[...].astype(BF)


def attention(joined, grad, cos, sin, pos, doc):
    seqs, length, _ = joined.shape
    heads = grad.shape[2] // HD
    part = lambda off: pl.BlockSpec((None, QB, HD), lambda s, h, i: (s, i, off + h))
    whole = lambda off: pl.BlockSpec((None, length, HD), lambda s, h, i: (s, 0, off + h))
    tq = pl.BlockSpec((None, QB, HD), lambda s, h, i: (s, i, 0))
    tk = pl.BlockSpec((None, length, HD), lambda s, h, i: (s, 0, 0))
    col = pl.BlockSpec((None, QB, 1), lambda s, h, i: (s, i, 0))
    row = pl.BlockSpec((None, 1, length), lambda s, h, i: (s, 0, 0))
    out = jax.ShapeDtypeStruct((seqs, length, heads * HD), BF)
    return pl.pallas_call(
        attention_kernel,
        grid=(seqs, heads, length // QB),
        in_specs=[part(0), whole(heads), whole(2 * heads), part(0), tq, tq, tk, tk, col, col, row, row],
        out_specs=[part(0), part(0), whole(0), whole(0)],
        out_shape=[out] * 4,
        scratch_shapes=[
            pltpu.VMEM((length, HD), BF),
            pltpu.VMEM((length, HD), BF),
            pltpu.VMEM((length, HD), F32),
            pltpu.VMEM((length, HD), F32),
        ],
        compiler_params=pltpu.CompilerParams(vmem_limit_bytes=40 * 2**20),
        cost_estimate=pl.CostEstimate(
            flops=seqs * heads * length * length * HD * 14,
            bytes_accessed=seqs * length * heads * HD * 24,
            transcendentals=seqs * heads * length * length,
        ),
    )(
        joined, joined, joined, grad, cos, sin, cos, sin,
        pos[:, :, None], doc[:, :, None], pos[:, None, :], doc[:, None, :],
    )


def gather_tokens(v):
    far = flip(v, "zl")
    near_x = flip(v, "x")
    far_x = flip(far, "x")
    blocks = []
    for b in (v, near_x, far, far_x):
        blocks += [b, flip(b, "core")]
    return jnp.concatenate(blocks, axis=0)


def reduce_tokens(p, span):
    p = p.reshape(2, 2, 2, span, -1)

    def near(half):
        return [half[b, 0].astype(F32) + flip(half[b, 1], "core").astype(F32) for b in (1, 0)]

    away, mine = near(p[1])
    total = mine + flip(away.astype(BF), "x").astype(F32)
    from_far = flip(total.astype(BF), "zl")
    away, mine = near(p[0])
    total = mine + flip(away.astype(BF), "x").astype(F32)
    return total + from_far.astype(F32)


def gather_replicas(v, copies):
    p, r, c = v.shape
    if copies != 2:
        w = lax.all_gather(v, ("zh", "y"), axis=0, tiled=False)
        return w.reshape(2, copies, p, r, c).transpose(0, 2, 1, 3, 4)
    zh, y = lax.axis_index("zh"), lax.axis_index("y")
    far = flip(v, "zh")
    pieces = {(0, 0): v, (0, 1): flip(v, "y"), (1, 0): far, (1, 1): flip(far, "y")}
    w = jnp.zeros((2, p, 2, r, c), v.dtype)
    for (a, b), piece in pieces.items():
        w = lax.dynamic_update_slice(w, piece[None, :, None], (zh ^ a, 0, y ^ b, 0, 0))
    return w


def reduce_replicas(v, copies):
    h, p, _, r, c = v.shape
    if copies != 2:
        w = v.transpose(0, 2, 1, 3, 4).reshape(h * copies, p, r, c)
        return lax.psum_scatter(w, ("zh", "y"), scatter_dimension=0, tiled=False)
    zh, y = lax.axis_index("zh"), lax.axis_index("y")
    part = lambda a, b: lax.dynamic_slice(v, (zh ^ a, 0, y ^ b, 0, 0), (1, p, 1, r, c)).reshape(p, r, c)
    far = part(1, 0) + flip(part(1, 1).astype(BF), "y").astype(F32)
    from_far = flip(far.astype(BF), "zh")
    near = part(0, 0) + flip(part(0, 1).astype(BF), "y").astype(F32)
    return near + from_far.astype(F32)


def gather_small(v, copies):
    if copies != 2:
        return lax.all_gather(v, AXES, axis=0, tiled=False)
    v = v[None]
    for axis in reversed(AXES):
        other, first = flip(v, axis), lax.axis_index(axis) == 0
        v = jnp.concatenate([jnp.where(first, v, other), jnp.where(first, other, v)], axis=0)
    return v


def reduce_small(v, copies):
    if copies != 2:
        return lax.psum_scatter(v, AXES, scatter_dimension=0, tiled=False)
    for axis in AXES:
        n, first = v.shape[0] // 2, lax.axis_index(axis) == 0
        v = jnp.where(first, v[:n], v[n:]) + flip(jnp.where(first, v[n:], v[:n]), axis)
    return v[0]


def gather_dense(w, copies):
    core, x = lax.axis_index("core"), lax.axis_index("x")
    if copies != 2:
        w = lax.all_gather(w, ("zh", "y", "x", "core"), axis=0, tiled=True)
        w = w.reshape(2, 2, 2, HD, D)
        w = lax.dynamic_slice(w, (core, 0, x, 0, 0), (1, 2, 1, HD, D))
        return w.reshape(2 * HD, D)
    w = gather_replicas(w[None], copies)[:, 0]
    first = core == 0
    keep = jnp.where(first, w[0], w[1])
    other = flip(jnp.where(first, w[1], w[0]), "core")
    low, high = jnp.where(first, keep, other), jnp.where(first, other, keep)
    return jnp.stack([low, high], axis=1).reshape(2 * HD, D)


def reduce_dense(g, copies):
    core, x = lax.axis_index("core"), lax.axis_index("x")
    if copies != 2:
        w = jnp.zeros((2, 2, 2, HD, D), F32)
        w = lax.dynamic_update_slice(w, g.reshape(1, 2, 1, HD, D), (core, 0, x, 0, 0))
        w = w.reshape(-1, D)
        return lax.psum_scatter(w, ("zh", "y", "x", "core"), scatter_dimension=0, tiled=True)
    g = g.reshape(2, 2, HD // 2, D)
    first = core == 0
    keep = jnp.where(first, g[:, 0], g[:, 1])
    other = flip(jnp.where(first, g[:, 1], g[:, 0]).astype(BF), "core").astype(F32)
    w = jnp.stack([jnp.where(first, keep, other), jnp.where(first, other, keep)])
    return reduce_replicas(w[:, None], copies)[0]


def swap_shards(v):
    return lax.all_to_all(v, ("zl", "x", "core"), 0, 0, tiled=True)


def shards(
    copies,
    block_input,
    output_grad,
    documents,
    span_order,
    attention_norm_gain,
    attention_norm_bias,
    query_key_value_weight,
    query_key_value_bias,
    dense_weight,
    dense_bias,
    mlp_norm_gain,
    mlp_norm_bias,
    to_hidden_weight,
    to_hidden_bias,
    from_hidden_weight,
    from_hidden_bias,
):
    span = block_input.shape[1]
    count = 16 * copies
    rows = D // count
    units = FF // count
    length = 4 * span
    zl, x, core = (lax.axis_index(a) for a in ("zl", "x", "core"))
    own_in, own_grad = block_input[0], output_grad[0]

    wide = query_key_value_weight.reshape(rows, 3, 2, 2, 2, 2, HD)
    wide = wide.transpose(3, 5, 2, 0, 1, 4, 6).reshape(8, rows, 6 * HD)
    tall = to_hidden_weight.reshape(rows, 2, 2, copies, 2, 2, units)
    tall = tall.transpose(2, 4, 5, 0, 1, 3, 6).reshape(8, rows, FF // 8)
    both = swap_shards(jnp.concatenate([wide, tall], axis=2).reshape(8 * rows, -1))
    both = both.reshape(2, 4 * rows, -1)
    joined_w = gather_replicas(both[:, :, : 6 * HD], copies).reshape(D, 6 * HD)
    hidden_w = gather_replicas(both[:, :, 6 * HD :], copies).reshape(D, FF // 8)
    dense_w = gather_dense(dense_weight, copies)
    back_w = gather_replicas(from_hidden_weight[None], copies).reshape(FF // 8, D)

    small = gather_small(
        jnp.concatenate(
            [
                attention_norm_gain,
                attention_norm_bias,
                dense_bias,
                mlp_norm_gain,
                mlp_norm_bias,
                from_hidden_bias,
                query_key_value_bias,
                to_hidden_bias,
            ]
        ),
        copies,
    ).astype(F32)
    take = lambda a, n: small[:, a : a + n].reshape(-1)
    gain_one, shift_one, dense_shift, gain_two, shift_two, back_shift = (
        take(j * rows, rows) for j in range(6)
    )
    joined_shift = take(6 * rows, 3 * rows).reshape(3, 2, 2, 2, 2, HD)
    joined_shift = lax.dynamic_slice(joined_shift, (0, core, zl, 0, x, 0), (3, 1, 1, 2, 1, HD))
    joined_shift = joined_shift.reshape(6 * HD)
    hidden_shift = take(9 * rows, units).reshape(2, 2, copies, 2, 2, units)
    hidden_shift = lax.dynamic_slice(
        hidden_shift, (0, zl, 0, x, core, 0), (2, 1, copies, 1, 1, units)
    ).reshape(FF // 8)

    tokens = gather_tokens(own_in)
    upstream = gather_tokens(own_grad)
    facts = jnp.concatenate([documents[0], span_order[0]])
    offsets = jnp.arange(span, dtype=jnp.int32)
    pos, doc = [], []
    for known in (facts, flip(facts, "zl")):
        for b in (0, 1):
            for c in (0, 1):
                block = (x ^ b) * 2 + (core ^ c)
                doc.append(lax.dynamic_slice(known, (block * span,), (span,)))
                pos.append(lax.dynamic_slice(known, (length + block,), (1,)) * span + offsets)
    pos = jnp.concatenate(pos).reshape(2, length)
    doc = jnp.concatenate(doc).reshape(2, length)
    inverse = jnp.power(THETA, -jnp.arange(ROT // 2, dtype=F32) * (2.0 / ROT))
    angles = pos.astype(F32)[:, :, None] * inverse
    cosine, sine = jnp.cos(angles), jnp.sin(angles)
    rest = jnp.zeros((2, length, HD - ROT), F32)
    cos_table = jnp.concatenate([cosine, cosine, rest + 1.0], axis=-1)
    sin_table = jnp.concatenate([-sine, sine, rest], axis=-1)

    tokens_wide = tokens.astype(F32)
    centre = tokens_wide - jnp.mean(tokens_wide, axis=-1, keepdims=True)
    spread = lax.rsqrt(jnp.mean(centre * centre, axis=-1, keepdims=True) + EPS)
    normal = centre * spread
    normed_one = (normal * gain_one + shift_one).astype(BF)
    normed_two = (normal * gain_two + shift_two).astype(BF)

    joined = dot(normed_one, joined_w, 1, 0) + joined_shift
    grad_mixed = dot(upstream, dense_w, 1, 1).astype(BF)
    mixed, *grad_joined = attention(
        joined.reshape(2, length, 6 * HD),
        grad_mixed.reshape(2, length, 2 * HD),
        cos_table,
        sin_table,
        pos,
        doc,
    )
    mixed = mixed.reshape(2 * length, 2 * HD)
    grad_joined = jnp.concatenate(grad_joined, axis=-1).reshape(2 * length, 6 * HD)

    hidden = dot(normed_two, hidden_w, 1, 0) + hidden_shift
    below = 0.5 * (1.0 + lax.erf(hidden * (0.5**0.5)))
    active = (hidden * below).astype(BF)
    slope = below + hidden * jnp.exp(-0.5 * hidden * hidden) * ((2.0 * jnp.pi) ** (-0.5))
    grad_hidden = (dot(upstream, back_w, 1, 1) * slope).astype(BF)

    inner = jnp.concatenate([mixed, active], axis=1)
    out = dot(inner, jnp.concatenate([dense_w, back_w], axis=0), 1, 0).astype(BF)
    out = reduce_tokens(out, span)
    block_output = (own_in.astype(F32) + (out + (dense_shift + back_shift))).astype(BF)[None]

    grad_dense = reduce_dense(dot(mixed, upstream, 0, 0), copies)
    grad_back = dot(active, upstream, 0, 0).reshape(2, 1, copies, units, D)
    grad_back = reduce_replicas(grad_back, copies)[0]
    grad_tall = dot(normed_two, grad_hidden, 0, 0).reshape(2, 2, copies, 4 * rows, FF // 8)
    grad_tall = reduce_replicas(grad_tall, copies)
    grad_wide = dot(normed_one, grad_joined, 0, 0).reshape(2, 2, copies, 4 * rows, 6 * HD)
    grad_wide = reduce_replicas(grad_wide, copies)
    grads = jnp.concatenate([grad_wide, grad_tall], axis=2).astype(BF)
    grads = swap_shards(grads.reshape(8 * rows, -1)).astype(F32)
    grad_wide = grads[:, : 6 * HD].reshape(2, 2, 2, rows, 3, 2, HD)
    grad_wide = grad_wide.transpose(3, 4, 2, 0, 5, 1, 6).reshape(rows, 3 * D)
    grad_tall = grads[:, 6 * HD :].reshape(2, 2, 2, rows, 2, copies, units)
    grad_tall = grad_tall.transpose(3, 4, 0, 5, 1, 2, 6).reshape(rows, FF)

    grad_one = dot(grad_joined, joined_w, 1, 1)
    grad_two = dot(grad_hidden, hidden_w, 1, 1)
    pull = reduce_tokens((grad_one * gain_one + grad_two * gain_two).astype(BF), span)
    own_wide = own_in.astype(F32)
    own_centre = own_wide - jnp.mean(own_wide, axis=-1, keepdims=True)
    own_spread = lax.rsqrt(jnp.mean(own_centre * own_centre, axis=-1, keepdims=True) + EPS)
    own_normal = own_centre * own_spread
    pull = own_spread * (
        pull
        - jnp.mean(pull, axis=-1, keepdims=True)
        - own_normal * jnp.mean(pull * own_normal, axis=-1, keepdims=True)
    )
    grad_wide_own = own_grad.astype(F32)
    input_grad = (grad_wide_own + pull).astype(BF)[None]

    vectors = [
        jnp.sum(grad_one * normal, axis=0),
        jnp.sum(grad_one, axis=0),
        jnp.sum(grad_two * normal, axis=0),
        jnp.sum(grad_two, axis=0),
        jnp.sum(grad_wide_own, axis=0),
    ]
    joined_sum = jnp.sum(grad_joined.astype(F32), axis=0).reshape(3, 1, 1, 2, 1, HD)
    joined_sum = lax.dynamic_update_slice(
        jnp.zeros((3, 2, 2, 2, 2, HD), F32), joined_sum, (0, core, zl, 0, x, 0)
    )
    hidden_sum = jnp.sum(grad_hidden.astype(F32), axis=0).reshape(2, 1, copies, 1, 1, units)
    hidden_sum = lax.dynamic_update_slice(
        jnp.zeros((2, 2, copies, 2, 2, units), F32), hidden_sum, (0, zl, 0, x, core, 0)
    )
    sums = [v.reshape(count, -1) for v in (*vectors, joined_sum, hidden_sum)]
    sums = reduce_small(jnp.concatenate(sums, axis=1), copies)
    cut = lambda a, n: sums[a : a + n]
    bias_sum = cut(4 * rows, rows)

    return (
        block_output,
        input_grad,
        cut(0, rows),
        cut(rows, rows),
        grad_wide,
        cut(5 * rows, 3 * rows),
        grad_dense,
        bias_sum,
        cut(2 * rows, rows),
        cut(3 * rows, rows),
        grad_tall,
        cut(8 * rows, units),
        grad_back,
        bias_sum,
    )


def solution(mesh):
    copies = mesh.shape["batch"] // 4
    inner = Mesh(mesh.devices.reshape(2, 2, copies, 2, 2), AXES)
    batch, ctx = AXES[:3], AXES[3:]
    tokens = P(batch, ctx, None)
    vector, matrix = P(AXES), P(AXES, None)
    params = (vector, vector, matrix, vector, matrix, vector) * 1
    params = params + (vector, vector, matrix, vector, matrix, vector)
    return jax.shard_map(
        functools.partial(shards, copies),
        mesh=inner,
        in_specs=(tokens, tokens, P(batch, None), P(batch, None)) + params,
        out_specs=(tokens, tokens) + params,
        check_vma=False,
    )
```

time: 3080 us -> 753 us (0.24)
  waiting for transfers between devices: 2600 us -> 329 us
  matrix products: 282 us -> 135 us
  blocking collectives: 86.1 us -> 0 us
  local copies, waits for them, and re-layouts: 42.8 us -> 123 us
  starting transfers between devices: 1.14 us -> 63.7 us
  Pallas kernels: 0 us -> 32.8 us
    reduce_scatter x6 -> x0, waiting for transfers between devices: 2120 us -> none  [the longest x1 713 us: shards(): lax.psum_scatter(grad_hidden_weight, ('batch', 'ctx'), scatter_dimension=...]
    all_gather x6 -> x0, waiting for transfers between devices: 473 us -> none  [the longest x1 178 us: shards(): lax.all_gather(from_hidden_weight, ('batch', 'ctx'), axis=0, tiled=True)]
    ppermute x0 -> x65, waiting for transfers between devices: none -> 329 us  [flip(): return lax.ppermute(v, axis, [(0, 1), (1, 0)])]
    dot_general x18 -> x11, matrix products: 282 us -> 135 us  [dot(): lax.dot_general(a, b, (((ca,), (cb,)), ((), ())), preferred_element_type=...]
    ppermute x0 -> x65, starting transfers between devices: none -> 54.8 us  [flip(): return lax.ppermute(v, axis, [(0, 1), (1, 0)])]
    unnamed x1 -> x0, blocking collectives: 44.4 us -> none
    all_gather x1 -> x0, blocking collectives: 41.6 us -> none  [shards(): lax.all_gather(to_hidden_bias, ('batch', 'ctx'), axis=0, tiled=True)]
    pallas_call x0 -> x1, Pallas kernels: none -> 32.8 us  [attention(): pl.pallas_call(attention_kernel, grid=(seqs, heads, length // QB), in_spe...]
  transfers between devices with their start and end apart: 13 -> 67, of which waited for: 12 -> 24; matrix products, arithmetic and copies ran while one was open for 11% -> 37% of each run, Pallas kernels for 0% -> 4%
where the time goes in v1:
time: 753 us; the launch traced here: 747 us
  waiting for transfers between devices  329 us (44%)
  matrix products  135 us (18%)
  local copies, waits for them, and re-layouts  123 us (16%)
  starting transfers between devices  63.7 us (8%)
  other arithmetic  53.6 us (7%)
  Pallas kernels  32.8 us (4%)
  between operations  10.1 us (1%)
    ppermute x65, waiting for transfers between devices, flip(): return lax.ppermute(v, axis, [(0, 1), (1, 0)])  329 us
    dot_general x11, matrix products, dot(): lax.dot_general(a, b, (((ca,), (cb,)), ((), ())), preferred_element_type=...  135 us
    ppermute x65, starting transfers between devices, flip(): return lax.ppermute(v, axis, [(0, 1), (1, 0)])  54.8 us
    pallas_call x1, Pallas kernels, attention(): pl.pallas_call(attention_kernel, grid=(seqs, heads, length // QB), in_spe...  32.8 us
    unnamed x150, local copies, waits for them, and re-layouts  29.3 us
    dynamic_update_slice x16, local copies, waits for them, and re-layouts, gather_replicas(): lax.dynamic_update_slice(w, piece[None, :, None], (zh ^ a, 0, y ^ b, 0, 0))  17.2 us
  transfers between devices with their start and end apart: 67, of which 24 were waited for; matrix products, arithmetic and copies ran while one was open for 37% of the time, Pallas kernels for 4%

profile of v1, /device:TPU:0, one launch (start us, length us, event | category | flops | bytes accessed | tf_op | source)
XLA Modules:
  0.0 747.1 jit_solution(5035192085059485117)
XLA Ops:
  0.6 4.1 collective-permute-start.23
  6.9 5.4 concatenate.71
  12.4 2.6 reshape.352
  20.5 4.6 all-to-all-start
  35.3 2.5 broadcast_in_dim.93
  42.5 32.6 %collective-permute-done.26 = s32[1028]{0:T(1024)S(1)} collective-permute-done((s32[1028]{0:T(1024)S(1)}, s32[1028]{0:T(1024)S(1)}, u32[]{:S(2)}, u32[]{:S(2)}) %collective-permute-start.26) | collective-permute-done | bytes 4144 | tf_op jit(solution)/shard_map/ppermute | solution.py:25
  79.9 3.7 fusion.86
  100.3 3.0 collective-permute-start.11
  104.0 2.0 select_bitcast_fusion
  106.1 8.6 %collective-permute-done.11 = bf16[16,832]{1,0:T(8,128)(2,1)S(1)} collective-permute-done((bf16[16,832]{1,0:T(8,128)(2,1)S(1)}, bf16[16,832]{1,0:T(8,128)(2,1)S(1)}, u32[]{:S(2)}, u32[]{:S(2)}) %collective-permute-start.11) | collective-permute-done | bytes 26656 | tf_op jit(solution)/shard_map/ppermute | solution.py:25
  119.2 4.7 collective-permute-start.3
  123.8 2.3 bitcast_dynamic-update-slice_fusion.6
  126.2 2.3 bitcast_dynamic-update-slice_fusion.5
  131.6 13.2 %collective-permute-done.1 = bf16[256,2048]{1,0:T(8,128)(2,1)S(1)} collective-permute-done((bf16[256,2048]{1,0:T(8,128)(2,1)}, bf16[256,2048]{1,0:T(8,128)(2,1)S(1)}, u32[]{:S(2)}, u32[]{:S(2)}) %collective-permute-start.1) | collective-permute-done | bytes 1048608 | tf_op jit(solution)/shard_map/ppermute | solution.py:25
  144.9 2.6 collective-permute-done.3
  148.9 2.3 constant_dynamic-update-slice_fusion.13
  155.1 3.1 constant_dynamic-update-slice_fusion.11
  158.1 9.2 %collective-permute-done.20 = bf16[256,2048]{1,0:T(8,128)(2,1)S(1)} collective-permute-done((bf16[256,2048]{1,0:T(8,128)(2,1)}, bf16[256,2048]{1,0:T(8,128)(2,1)S(1)}, u32[]{:S(2)}, u32[]{:S(2)}) %collective-permute-start.20) | collective-permute-done | bytes 1048608 | tf_op jit(solution)/shard_map/ppermute | solution.py:25
  168.8 20.5 %collective-permute-done.5 = bf16[256,2048]{1,0:T(8,128)(2,1)S(1)} collective-permute-done((bf16[256,2048]{1,0:T(8,128)(2,1)S(1)}, bf16[256,2048]{1,0:T(8,128)(2,1)S(1)}, u32[]{:S(2)}, u32[]{:S(2)}) %collective-permute-start.5) | collective-permute-done | bytes 1048608 | tf_op jit(solution)/shard_map/ppermute | solution.py:25
  197.4 6.8 convolution_convert_fusion.1
  206.9 3.4 collective-permute-start.13
  210.3 5.7 fusion.12
  221.6 46.4 %collective-permute-done.13 = bf16[2,256,768]{2,1,0:T(8,128)(2,1)S(1)} collective-permute-done((bf16[2,256,768]{2,1,0:T(8,128)(2,1)S(1)}, bf16[2,256,768]{2,1,0:T(8,128)(2,1)S(1)}, u32[]{:S(2)}, u32[]{:S(2)}) %collective-permute-start.13) | collective-permute-done | bytes 786464 | tf_op jit(solution)/shard_map/ppermute | solution.py:25
  268.7 21.5 %collective-permute-done.28 = bf16[2,256,1024]{2,1,0:T(8,128)(2,1)} collective-permute-done((bf16[2,256,1024]{2,1,0:T(8,128)(2,1)S(1)}, bf16[2,256,1024]{2,1,0:T(8,128)(2,1)}, u32[]{:S(2)}, u32[]{:S(2)}) %collective-permute-start.28) | collective-permute-done | bytes 1048608 | tf_op jit(solution)/shard_map/ppermute | solution.py:25
  292.3 2.0 copy-done.31
  294.3 9.7 %broadcast_add_fusion = f32[2048,768]{1,0:T(8,128)} fusion(f32[768]{0:T(1024)S(1)} %add.448, bf16[2048,768]{1,0:T(8,128)(2,1)S(1)} %bitcast.379, bf16[2048,2048]{1,0:T(8,128)(2,1)S(1)} %bitcast.338, f32[2048]{0:T(1024)S(1)} %add.438, f32[2048]{0:T(1024)S(1)} %mul.188, f32[2048]{0:T(1024)S(1)} %add_rsqrt_fusion, f32[2048]{0:T(1024)S(1)} %broadcast_multiply_fusion), kind=kOutput, calls=%fused_computation.44 | convolution fusion | flops 6469189632 | bytes 17861632 | tf_op jit(solution)/shard_map/dot_general | solution.py:29
  304.0 32.8 %shard_map.263 = (bf16[2,1024,256]{2,1,0:T(8,128)(2,1)S(1)}, bf16[2,1024,256]{2,1,0:T(8,128)(2,1)S(1)}, bf16[2,1024,256]{2,1,0:T(8,128)(2,1)S(1)}, bf16[2,1024,256]{2,1,0:T(8,128)(2,1)S(1)}) custom-call(f32[2,1024,768]{2,1,0:T(8,128)} %bitcast.407, f32[2,1024,768]{2,1,0:T(8,128)} %bitcast.408, f32[2,1024,768]{2,1,0:T(8,128)} %bitcast.409, ...), custom_call_target="tpu_custom_call" | custom-call | flops 7516192768 | bytes 12582912 | tf_op jit(solution)/shard_map/pallas_call | solution.py:82
  342.2 5.8 fusion.19
  350.6 9.6 %fusion.108 = f32[2048,2048]{1,0:T(8,128)} fusion(bf16[2048,768]{1,0:T(8,128)(2,1)S(1)} %bitcast.362, bf16[2048,768]{1,0:T(8,128)(2,1)S(1)} %bitcast.380), kind=kOutput, calls=%fused_computation.291 | convolution fusion | flops 6442450944 | bytes 23068672 | tf_op jit(solution)/shard_map/dot_general | solution.py:29
  366.4 15.5 %multiply_convert_fusion = (bf16[2048,1024]{1,0:T(8,128)(2,1)S(1)}, f32[2048,1024]{1,0:T(8,128)}) fusion(f32[1024]{0:T(1024)S(1)} %bitcast.402, bf16[2048,1024]{1,0:T(8,128)(2,1)S(1)} %bitcast.373, bf16[2048,2048]{1,0:T(8,128)(2,1)} %copy-done.11, f32[2048]{0:T(1024)S(1)} %add.492, f32[2048]{0:T(1024)S(1)} %mul.209, f32[2048]{0:T(1024)S(1)} %add_rsqrt_fusion, ...), kind=kOutput, calls=%fused_computation.26 | convolution fusion | flops 8627683328 | bytes 25202688 | tf_op jit(solution)/shard_map/dot_general | solution.py:29
  381.9 11.6 %fusion.110 = f32[1024,2048]{1,0:T(8,128)} fusion(bf16[2048,1024]{1,0:T(8,128)(2,1)S(1)} %get-tuple-element.94, bf16[2048,2048]{1,0:T(8,128)(2,1)S(1)} %bitcast.395), kind=kOutput, calls=%fused_computation.293 | convolution fusion | flops 8589934592 | bytes 20971520 | tf_op jit(solution)/shard_map/dot_general | solution.py:29
  393.5 17.2 %convert_reduce_fusion.1 = (f32[1024]{0:T(1024)S(1)}, bf16[2048,1024]{1,0:T(8,128)(2,1)}) fusion(f32[2048,1024]{1,0:T(8,128)} %get-tuple-element.95, f32[1024]{0:T(1024)S(1)} %bitcast.403, bf16[2048,2048]{1,0:T(8,128)(2,1)S(1)} %bitcast.395, bf16[1024,2048]{1,0:T(8,128)(2,1)} %bitcast.53), kind=kOutput, calls=%fused_computation.25 | convolution fusion | flops 8617196544 | bytes 25174016 | tf_op jit(solution)/shard_map/dot_general | solution.py:29
  410.7 14.3 %convolution_convert_fusion = bf16[2048,2048]{1,0:T(8,128)(2,1)S(1)} fusion(bf16[2048,1024]{1,0:T(8,128)(2,1)} %copy-done.55, bf16[2048,256]{1,0:T(8,128)(2,1)S(1)} %bitcast.333, bf16[1024,2048]{1,0:T(8,128)(2,1)} %bitcast.53, bf16[256,2048]{1,0:T(8,128)(2,1)S(1)} %bitcast.382), kind=kOutput, calls=%fused_computation.28 | convolution fusion | flops 10762584064 | bytes 18874368 | tf_op jit(solution)/shard_map/dot_general | solution.py:29
  431.2 12.9 %fusion.99 = f32[2048,1024]{1,0:T(8,128)} fusion(bf16[2048,1024]{1,0:T(8,128)(2,1)S(1)} %copy-done.56, bf16[2048,2048]{1,0:T(8,128)(2,1)S(1)} %bitcast.340, f32[2048]{0:T(1024)S(1)} %add.492, f32[2048]{0:T(1024)S(1)} %mul.209, f32[2048]{0:T(1024)S(1)} %add_rsqrt_fusion, f32[2048]{0:T(1024)S(1)} %broadcast_multiply_fusion), kind=kOutput, calls=%fused_computation.284 | convolution fusion | flops 8615100416 | bytes 21004288 | tf_op jit(solution)/shard_map/dot_general | solution.py:29
  444.1 22.6 %fusion.103 = (f32[2048]{0:T(1024)S(1)}, f32[2048]{0:T(1024)S(1)}, bf16[2048,2048]{1,0:T(8,128)(2,1)}, f32[2048]{0:T(1024)S(1)}, f32[2048]{0:T(1024)S(1)}, /*index=5*/bf16[2048,2048]{0,1:T(8,128)(2,1)}) fusion(f32[2048]{0:T(1024)S(1)} %add_rsqrt_fusion, f32[2048]{0:T(1024)S(1)} %broadcast_multiply_fusion, bf16[2048,2048]{1,0:T(8,128)(2,1)} %copy-done.11, ...), kind=kOutput, calls=%fused_computation.286 | convolution fusion | flops 8657035264 | bytes 50405376 | tf_op jit(solution)/shard_map/dot_general | solution.py:29
  466.7 12.5 %copy.112 = bf16[2048,2048]{1,0:T(8,128)(2,1)} copy(bf16[2048,2048]{0,1:T(8,128)(2,1)} %get-tuple-element.31) | data formatting | bytes 16777216 | tf_op jit(solution)/shard_map/dot_general | solution.py:29
  479.2 9.4 %fusion.109 = f32[2,2,2,256,768]{4,3,2,1,0:T(8,128)S(1)} fusion(bf16[2,2,2,256,2048]{4,3,2,1,0:T(8,128)(2,1)} %bitcast.359, bf16[2048,768,1,1,1]{1,0,4,3,2:T(8,128)(2,1)S(1)} %bitcast.363), kind=kOutput, calls=%fused_computation.292 | convolution fusion | flops 6442450944 | bytes 17825792 | tf_op jit(solution)/shard_map/dot_general | solution.py:29
  494.6 2.1 slice_bitcast_fusion.6
  497.5 3.7 fusion.64
  501.6 4.1 fusion.62
  507.5 2.7 collective-permute-done.53
  521.6 21.0 %collective-permute-done.45 = bf16[256,2048]{1,0:T(8,128)(2,1)S(1)} collective-permute-done((bf16[256,2048]{1,0:T(8,128)(2,1)S(1)}, bf16[256,2048]{1,0:T(8,128)(2,1)S(1)}, u32[]{:S(2)}, u32[]{:S(2)}) %collective-permute-start.45) | collective-permute-done | bytes 1048608 | tf_op jit(solution)/shard_map/ppermute | solution.py:25
  543.9 21.1 %collective-permute-done.38 = bf16[256,2048]{1,0:T(8,128)(2,1)S(1)} collective-permute-done((bf16[256,2048]{1,0:T(8,128)(2,1)S(1)}, bf16[256,2048]{1,0:T(8,128)(2,1)S(1)}, u32[]{:S(2)}, u32[]{:S(2)}) %collective-permute-start.38) | collective-permute-done | bytes 1048608 | tf_op jit(solution)/shard_map/ppermute | solution.py:25
  565.7 2.9 fusion.53
  571.3 9.8 %collective-permute-done.54 = bf16[2,256,768]{2,1,0:T(8,128)(2,1)S(1)} collective-permute-done((bf16[2,256,768]{2,1,0:T(8,128)(2,1)S(1)}, bf16[2,256,768]{2,1,0:T(8,128)(2,1)S(1)}, u32[]{:S(2)}, u32[]{:S(2)}) %collective-permute-start.54) | collective-permute-done | bytes 786464 | tf_op jit(solution)/shard_map/ppermute | solution.py:25
  582.8 4.7 collective-permute-done.42
  588.3 15.2 %collective-permute-done.46 = bf16[256,2048]{1,0:T(8,128)(2,1)S(1)} collective-permute-done((bf16[256,2048]{1,0:T(8,128)(2,1)S(1)}, bf16[256,2048]{1,0:T(8,128)(2,1)S(1)}, u32[]{:S(2)}, u32[]{:S(2)}) %collective-permute-start.46) | collective-permute-done | bytes 1048608 | tf_op jit(solution)/shard_map/ppermute | solution.py:25
  605.4 3.7 collective-permute-done.35
  610.0 21.3 %collective-permute-done.39 = bf16[256,2048]{1,0:T(8,128)(2,1)S(1)} collective-permute-done((bf16[256,2048]{1,0:T(8,128)(2,1)S(1)}, bf16[256,2048]{1,0:T(8,128)(2,1)S(1)}, u32[]{:S(2)}, u32[]{:S(2)}) %collective-permute-start.39) | collective-permute-done | bytes 1048608 | tf_op jit(solution)/shard_map/ppermute | solution.py:25
  632.4 4.1 convert_reduce_fusion.4
  636.8 22.1 %collective-permute-done.57 = bf16[2,256,1024]{2,1,0:T(8,128)(2,1)} collective-permute-done((bf16[2,256,1024]{2,1,0:T(8,128)(2,1)}, bf16[2,256,1024]{2,1,0:T(8,128)(2,1)}, u32[]{:S(2)}, u32[]{:S(2)}) %collective-permute-start.57) | collective-permute-done | bytes 1048608 | tf_op jit(solution)/shard_map/ppermute | solution.py:25
  658.9 2.7 fusion.55
  661.7 3.9 collective-permute-done.47
  667.1 4.3 all-to-all-start.1
  672.3 2.2 fusion.50
  678.3 2.0 fusion.77
  680.2 6.0 collective-permute-done.50
  686.3 36.8 %collective-permute-done.64 = bf16[1,256,2048]{2,1,0:T(8,128)(2,1)S(1)} collective-permute-done((bf16[1,256,2048]{2,1,0:T(8,128)(2,1)S(1)}, bf16[1,256,2048]{2,1,0:T(8,128)(2,1)S(1)}, u32[]{:S(2)}, u32[]{:S(2)}) %collective-permute-start.64) | collective-permute-done | bytes 1048608 | tf_op jit(solution)/shard_map/ppermute | solution.py:25
  723.1 3.7 fusion.52
  732.0 2.8 reshape.382
  734.8 3.2 copy.107
  738.0 2.7 reshape.383
  740.6 2.1 reshape.378
  744.0 2.4 reshape.379
  (404 shorter events, 134.6 us)
Async XLA Ops:
  0.6 92.5 %collective-permute-start.23 = (bf16[1,64,2048]{2,1,0:T(8,128)(2,1)}, bf16[1,64,2048]{2,1,0:T(8,128)(2,1)}, u32[]{:S(2)}, u32[]{:S(2)}) collective-permute-start(bf16[1,64,2048]{2,1,0:T(8,128)(2,1)} %bitcast.386), channel_id=1, source_target_pairs={{0,16},{16,0},{1,17},{17,1},{2,18},{18,2},{3,19},{19,3},{4,20},{20... | collective-permute-start | bytes 786440 | tf_op jit(solution)/shard_map/ppermute | solution.py:25
  4.7 89.0 %collective-permute-start.22 = (bf16[1,64,2048]{2,1,0:T(8,128)(2,1)}, bf16[1,64,2048]{2,1,0:T(8,128)(2,1)}, u32[]{:S(2)}, u32[]{:S(2)}) collective-permute-start(bf16[1,64,2048]{2,1,0:T(8,128)(2,1)} %bitcast.387), channel_id=1, source_target_pairs={{0,4},{4,0},{1,5},{5,1},{2,6},{6,2},{3,7},{7,3},{8,12},{12,8},{9,1... | collective-permute-start | bytes 786440 | tf_op jit(solution)/shard_map/ppermute | solution.py:25
  6.3 112.3 %collective-permute-start.31 = (bf16[1,256,2048]{2,1,0:T(8,128)(2,1)}, bf16[1,256,2048]{2,1,0:T(8,128)(2,1)}, u32[]{:S(2)}, u32[]{:S(2)}) collective-permute-start(bf16[1,256,2048]{2,1,0:T(8,128)(2,1)} %bitcast.384), channel_id=1, source_target_pairs={{0,16},{16,0},{1,17},{17,1},{2,18},{18,2},{3,19},{19,3},{4,20},{20... | collective-permute-start | bytes 3145736 | tf_op jit(solution)/shard_map/ppermute | solution.py:25
  6.6 112.5 %collective-permute-start.30 = (bf16[1,256,2048]{2,1,0:T(8,128)(2,1)}, bf16[1,256,2048]{2,1,0:T(8,128)(2,1)}, u32[]{:S(2)}, u32[]{:S(2)}) collective-permute-start(bf16[1,256,2048]{2,1,0:T(8,128)(2,1)} %bitcast.385), channel_id=1, source_target_pairs={{0,4},{4,0},{1,5},{5,1},{2,6},{6,2},{3,7},{7,3},{8,12},{12,8},{9,1... | collective-permute-start | bytes 3145736 | tf_op jit(solution)/shard_map/ppermute | solution.py:25
  12.3 28.2 %collective-permute-start.7 = (bf16[1,832]{1,0:T(2,128)(2,1)S(1)}, bf16[1,832]{1,0:T(2,128)(2,1)S(1)}, u32[]{:S(2)}, u32[]{:S(2)}) collective-permute-start(bf16[1,832]{1,0:T(2,128)(2,1)S(1)} %broadcast_in_dim.80), channel_id=1, source_target_pairs={{0,1},{1,0},{2,3},{3,2},{4,5},{5,4},{6,7},{7,6},{8,9},{9,8},{10,11... | collective-permute-start | bytes 5000 | tf_op jit(solution)/shard_map/ppermute | solution.py:25
  20.5 183.7 %all-to-all-start = ((bf16[8,64,1792]{2,1,0:T(8,128)(2,1)}), bf16[8,64,1792]{2,1,0:T(8,128)(2,1)}, u32[]{:S(2)}, u32[]{:S(2)}) async-start(bf16[8,64,1792]{2,1,0:T(8,128)(2,1)} %pad_maximum_fusion), calls=%async_computation | async-start | bytes 3670016 | tf_op jit(solution)/shard_map/all_to_all | solution.py:207
  40.5 34.6 %collective-permute-start.26 = (s32[1028]{0:T(1024)S(1)}, s32[1028]{0:T(1024)S(1)}, u32[]{:S(2)}, u32[]{:S(2)}) collective-permute-start(s32[1028]{0:T(1024)S(1)} %pad_add_fusion), channel_id=1, source_target_pairs={{0,8},{8,0},{1,9},{9,1},{2,10},{10,2},{3,11},{11,3},{4,12},{12,4},... | collective-permute-start | bytes 12344 | tf_op jit(solution)/shard_map/ppermute | solution.py:25
  75.1 9.4 %collective-permute-start.8 = (bf16[2,832]{1,0:T(2,128)(2,1)S(1)}, bf16[2,832]{1,0:T(2,128)(2,1)S(1)}, u32[]{:S(2)}, u32[]{:S(2)}) collective-permute-start(bf16[2,832]{1,0:T(2,128)(2,1)S(1)} %pad_maximum_fusion.6), channel_id=1, source_target_pairs={{0,2},{2,0},{1,3},{3,1},{4,6},{6,4},{5,7},{7,5},{8,10},{10,8},{9,1... | collective-permute-start | bytes 9992 | tf_op jit(solution)/shard_map/ppermute | solution.py:25
  84.5 3.7 collective-permute-start.9
  88.3 3.8 collective-permute-start.10
  92.0 34.1 %collective-permute-start.18 = (bf16[256,2048]{1,0:T(8,128)(2,1)}, bf16[256,2048]{1,0:T(8,128)(2,1)}, u32[]{:S(2)}, u32[]{:S(2)}) collective-permute-start(bf16[256,2048]{1,0:T(8,128)(2,1)} %bitcast.370), channel_id=1, source_target_pairs={{0,8},{8,0},{1,9},{9,1},{2,10},{10,2},{3,11},{11,3},{4,12},{12,4},... | collective-permute-start | bytes 3145736 | tf_op jit(solution)/shard_map/ppermute | solution.py:25
  93.2 35.3 %collective-permute-start.16 = (bf16[256,2048]{1,0:T(8,128)(2,1)}, bf16[256,2048]{1,0:T(8,128)(2,1)}, u32[]{:S(2)}, u32[]{:S(2)}) collective-permute-start(bf16[256,2048]{1,0:T(8,128)(2,1)} %bitcast.371), channel_id=1, source_target_pairs={{0,2},{2,0},{1,3},{3,1},{4,6},{6,4},{5,7},{7,5},{8,10},{10,8},{9,1... | collective-permute-start | bytes 3145736 | tf_op jit(solution)/shard_map/ppermute | solution.py:25
  93.7 6.6 collective-permute-start.24
  100.3 14.4 %collective-permute-start.11 = (bf16[16,832]{1,0:T(8,128)(2,1)S(1)}, bf16[16,832]{1,0:T(8,128)(2,1)S(1)}, u32[]{:S(2)}, u32[]{:S(2)}) collective-permute-start(bf16[16,832]{1,0:T(8,128)(2,1)S(1)} %pad_maximum_fusion.3), channel_id=1, source_target_pairs={{0,16},{16,0},{1,17},{17,1},{2,18},{18,2},{3,19},{19,3},{4,20},{20... | collective-permute-start | bytes 79880 | tf_op jit(solution)/shard_map/ppermute | solution.py:25
  117.0 12.1 %collective-permute-start.15 = (bf16[256,2048]{1,0:T(8,128)(2,1)}, bf16[256,2048]{1,0:T(8,128)(2,1)S(1)}, u32[]{:S(2)}, u32[]{:S(2)}) collective-permute-start(bf16[256,2048]{1,0:T(8,128)(2,1)} %bitcast.372), channel_id=1, source_target_pairs={{0,1},{1,0},{2,3},{3,2},{4,5},{5,4},{6,7},{7,6},{8,9},{9,8},{10,11... | collective-permute-start | bytes 3145736 | tf_op jit(solution)/shard_map/ppermute | solution.py:25
  118.6 26.3 %collective-permute-start.1 = (bf16[256,2048]{1,0:T(8,128)(2,1)}, bf16[256,2048]{1,0:T(8,128)(2,1)S(1)}, u32[]{:S(2)}, u32[]{:S(2)}) collective-permute-start(bf16[256,2048]{1,0:T(8,128)(2,1)} %bitcast.341), channel_id=1, source_target_pairs={{0,2},{2,0},{1,3},{3,1},{4,6},{6,4},{5,7},{7,5},{8,10},{10,8},{9,1... | collective-permute-start | bytes 3145736 | tf_op jit(solution)/shard_map/ppermute | solution.py:25
  119.2 28.3 %collective-permute-start.3 = (bf16[256,2048]{1,0:T(8,128)(2,1)}, bf16[256,2048]{1,0:T(8,128)(2,1)S(1)}, u32[]{:S(2)}, u32[]{:S(2)}) collective-permute-start(bf16[256,2048]{1,0:T(8,128)(2,1)} %bitcast.342), channel_id=1, source_target_pairs={{0,8},{8,0},{1,9},{9,1},{2,10},{10,2},{3,11},{11,3},{4,12},{12,4},... | collective-permute-start | bytes 3145736 | tf_op jit(solution)/shard_map/ppermute | solution.py:25
  126.2 25.0 %collective-permute-start = (bf16[256,2048]{1,0:T(8,128)(2,1)S(1)}, bf16[256,2048]{1,0:T(8,128)(2,1)S(1)}, u32[]{:S(2)}, u32[]{:S(2)}) collective-permute-start(bf16[256,2048]{1,0:T(8,128)(2,1)S(1)} %bitcast.343), channel_id=1, source_target_pairs={{0,1},{1,0},{2,3},{3,2},{4,5},{5,4},{6,7},{7,6},{8,9},{9,8},{10,11... | collective-permute-start | bytes 3145736 | tf_op jit(solution)/shard_map/ppermute | solution.py:25
  128.5 24.9 %collective-permute-start.17 = (bf16[256,2048]{1,0:T(8,128)(2,1)}, bf16[256,2048]{1,0:T(8,128)(2,1)S(1)}, u32[]{:S(2)}, u32[]{:S(2)}) collective-permute-start(bf16[256,2048]{1,0:T(8,128)(2,1)} %collective-permute-done.16), channel_id=1, source_target_pairs={{0,1},{1,0},{2,3},{3,2},{4,5},{5,4},{6,7},{7,6},{8,9},{9,8},{10,11... | collective-permute-start | bytes 3145736 | tf_op jit(solution)/shard_map/ppermute | solution.py:25
  129.1 38.3 %collective-permute-start.20 = (bf16[256,2048]{1,0:T(8,128)(2,1)}, bf16[256,2048]{1,0:T(8,128)(2,1)S(1)}, u32[]{:S(2)}, u32[]{:S(2)}) collective-permute-start(bf16[256,2048]{1,0:T(8,128)(2,1)} %collective-permute-done.18), channel_id=1, source_target_pairs={{0,2},{2,0},{1,3},{3,1},{4,6},{6,4},{5,7},{7,5},{8,10},{10,8},{9,1... | collective-permute-start | bytes 3145736 | tf_op jit(solution)/shard_map/ppermute | solution.py:25
  144.9 23.9 %collective-permute-start.19 = (bf16[256,2048]{1,0:T(8,128)(2,1)}, bf16[256,2048]{1,0:T(8,128)(2,1)S(1)}, u32[]{:S(2)}, u32[]{:S(2)}) collective-permute-start(bf16[256,2048]{1,0:T(8,128)(2,1)} %collective-permute-done.18), channel_id=1, source_target_pairs={{0,1},{1,0},{2,3},{3,2},{4,5},{5,4},{6,7},{7,6},{8,9},{9,8},{10,11... | collective-permute-start | bytes 3145736 | tf_op jit(solution)/shard_map/ppermute | solution.py:25
  147.4 41.8 %collective-permute-start.5 = (bf16[256,2048]{1,0:T(8,128)(2,1)S(1)}, bf16[256,2048]{1,0:T(8,128)(2,1)S(1)}, u32[]{:S(2)}, u32[]{:S(2)}) collective-permute-start(bf16[256,2048]{1,0:T(8,128)(2,1)S(1)} %collective-permute-done.3), channel_id=1, source_target_pairs={{0,2},{2,0},{1,3},{3,1},{4,6},{6,4},{5,7},{7,5},{8,10},{10,8},{9,1... | collective-permute-start | bytes 3145736 | tf_op jit(solution)/shard_map/ppermute | solution.py:25
  151.2 40.3 %collective-permute-start.2 = (bf16[256,2048]{1,0:T(8,128)(2,1)S(1)}, bf16[256,2048]{1,0:T(8,128)(2,1)S(1)}, u32[]{:S(2)}, u32[]{:S(2)}) collective-permute-start(bf16[256,2048]{1,0:T(8,128)(2,1)S(1)} %collective-permute-done.1), channel_id=1, source_target_pairs={{0,1},{1,0},{2,3},{3,2},{4,5},{5,4},{6,7},{7,6},{8,9},{9,8},{10,11... | collective-permute-start | bytes 3145736 | tf_op jit(solution)/shard_map/ppermute | solution.py:25
  153.4 38.3 %collective-permute-start.4 = (bf16[256,2048]{1,0:T(8,128)(2,1)S(1)}, bf16[256,2048]{1,0:T(8,128)(2,1)S(1)}, u32[]{:S(2)}, u32[]{:S(2)}) collective-permute-start(bf16[256,2048]{1,0:T(8,128)(2,1)S(1)} %collective-permute-done.3), channel_id=1, source_target_pairs={{0,1},{1,0},{2,3},{3,2},{4,5},{5,4},{6,7},{7,6},{8,9},{9,8},{10,11... | collective-permute-start | bytes 3145736 | tf_op jit(solution)/shard_map/ppermute | solution.py:25
  167.3 24.5 %collective-permute-start.32 = (bf16[1,256,2048]{2,1,0:T(8,128)(2,1)}, bf16[1,256,2048]{2,1,0:T(8,128)(2,1)S(1)}, u32[]{:S(2)}, u32[]{:S(2)}) collective-permute-start(bf16[1,256,2048]{2,1,0:T(8,128)(2,1)} %collective-permute-done.31), channel_id=1, source_target_pairs={{0,4},{4,0},{1,5},{5,1},{2,6},{6,2},{3,7},{7,3},{8,12},{12,8},{9,1... | collective-permute-start | bytes 3145736 | tf_op jit(solution)/shard_map/ppermute | solution.py:25
  168.8 27.6 %collective-permute-start.21 = (bf16[256,2048]{1,0:T(8,128)(2,1)S(1)}, bf16[256,2048]{1,0:T(8,128)(2,1)S(1)}, u32[]{:S(2)}, u32[]{:S(2)}) collective-permute-start(bf16[256,2048]{1,0:T(8,128)(2,1)S(1)} %collective-permute-done.20), channel_id=1, source_target_pairs={{0,1},{1,0},{2,3},{3,2},{4,5},{5,4},{6,7},{7,6},{8,9},{9,8},{10,11... | collective-permute-start | bytes 3145736 | tf_op jit(solution)/shard_map/ppermute | solution.py:25
  205.4 63.2 %collective-permute-start.12 = (bf16[2,256,768]{2,1,0:T(8,128)(2,1)S(1)}, bf16[2,256,768]{2,1,0:T(8,128)(2,1)S(1)}, u32[]{:S(2)}, u32[]{:S(2)}) collective-permute-start(bf16[2,256,768]{2,1,0:T(8,128)(2,1)S(1)} %slice.260), channel_id=1, source_target_pairs={{0,4},{4,0},{1,5},{5,1},{2,6},{6,2},{3,7},{7,3},{8,12},{12,8},{9,1... | collective-permute-start | bytes 2359304 | tf_op jit(solution)/shard_map/ppermute | solution.py:25
  206.9 61.0 %collective-permute-start.13 = (bf16[2,256,768]{2,1,0:T(8,128)(2,1)S(1)}, bf16[2,256,768]{2,1,0:T(8,128)(2,1)S(1)}, u32[]{:S(2)}, u32[]{:S(2)}) collective-permute-start(bf16[2,256,768]{2,1,0:T(8,128)(2,1)S(1)} %slice.260), channel_id=1, source_target_pairs={{0,16},{16,0},{1,17},{17,1},{2,18},{18,2},{3,19},{19,3},{4,20},{20... | collective-permute-start | bytes 2359304 | tf_op jit(solution)/shard_map/ppermute | solution.py:25
  217.3 73.4 %collective-permute-start.27 = (bf16[2,256,1024]{2,1,0:T(8,128)(2,1)S(1)}, bf16[2,256,1024]{2,1,0:T(8,128)(2,1)S(1)}, u32[]{:S(2)}, u32[]{:S(2)}) collective-permute-start(bf16[2,256,1024]{2,1,0:T(8,128)(2,1)S(1)} %slice.266), channel_id=1, source_target_pairs={{0,4},{4,0},{1,5},{5,1},{2,6},{6,2},{3,7},{7,3},{8,12},{12,8},{9,1... | collective-permute-start | bytes 3145736 | tf_op jit(solution)/shard_map/ppermute | solution.py:25
  218.0 72.2 %collective-permute-start.28 = (bf16[2,256,1024]{2,1,0:T(8,128)(2,1)S(1)}, bf16[2,256,1024]{2,1,0:T(8,128)(2,1)}, u32[]{:S(2)}, u32[]{:S(2)}) collective-permute-start(bf16[2,256,1024]{2,1,0:T(8,128)(2,1)S(1)} %slice.266), channel_id=1, source_target_pairs={{0,16},{16,0},{1,17},{17,1},{2,18},{18,2},{3,19},{19,3},{4,20},{20... | collective-permute-start | bytes 3145736 | tf_op jit(solution)/shard_map/ppermute | solution.py:25
  268.0 24.2 %collective-permute-start.14 = (bf16[2,256,768]{2,1,0:T(8,128)(2,1)S(1)}, bf16[2,256,768]{2,1,0:T(8,128)(2,1)S(1)}, u32[]{:S(2)}, u32[]{:S(2)}) collective-permute-start(bf16[2,256,768]{2,1,0:T(8,128)(2,1)S(1)} %collective-permute-done.13), channel_id=1, source_target_pairs={{0,4},{4,0},{1,5},{5,1},{2,6},{6,2},{3,7},{7,3},{8,12},{12,8},{9,1... | collective-permute-start | bytes 2359304 | tf_op jit(solution)/shard_map/ppermute | solution.py:25
  290.2 74.9 %collective-permute-start.29 = (bf16[2,256,1024]{2,1,0:T(8,128)(2,1)}, bf16[2,256,1024]{2,1,0:T(8,128)(2,1)}, u32[]{:S(2)}, u32[]{:S(2)}) collective-permute-start(bf16[2,256,1024]{2,1,0:T(8,128)(2,1)} %collective-permute-done.28), channel_id=1, source_target_pairs={{0,4},{4,0},{1,5},{5,1},{2,6},{6,2},{3,7},{7,3},{8,12},{12,8},{9,1... | collective-permute-start | bytes 3145736 | tf_op jit(solution)/shard_map/ppermute | solution.py:25
  348.2 13.3 %collective-permute-start.58 = (bf16[2,64,2048]{2,1,0:T(8,128)(2,1)S(1)}, bf16[2,64,2048]{2,1,0:T(8,128)(2,1)S(1)}, u32[]{:S(2)}, u32[]{:S(2)}) collective-permute-start(bf16[2,64,2048]{2,1,0:T(8,128)(2,1)S(1)} %fusion.70), channel_id=1, source_target_pairs={{0,1},{1,0},{2,3},{3,2},{4,5},{5,4},{6,7},{7,6},{8,9},{9,8},{10,11... | collective-permute-start | bytes 1572872 | tf_op jit(solution)/shard_map/ppermute | solution.py:25
  363.6 142.0 %collective-permute-start.60 = (bf16[1,64,2048]{2,1,0:T(8,128)(2,1)}, bf16[1,64,2048]{2,1,0:T(8,128)(2,1)}, u32[]{:S(2)}, u32[]{:S(2)}) collective-permute-start(bf16[1,64,2048]{2,1,0:T(8,128)(2,1)} %get-tuple-element.53), channel_id=1, source_target_pairs={{0,4},{4,0},{1,5},{5,1},{2,6},{6,2},{3,7},{7,3},{8,12},{12,8},{9,1... | collective-permute-start | bytes 786440 | tf_op jit(solution)/shard_map/ppermute | solution.py:25
  427.2 115.9 %collective-permute-start.36 = (bf16[256,2048]{1,0:T(8,128)(2,1)}, bf16[256,2048]{1,0:T(8,128)(2,1)}, u32[]{:S(2)}, u32[]{:S(2)}) collective-permute-start(bf16[256,2048]{1,0:T(8,128)(2,1)} %get-tuple-element.48), channel_id=1, source_target_pairs={{0,1},{1,0},{2,3},{3,2},{4,5},{5,4},{6,7},{7,6},{8,9},{9,8},{10,11... | collective-permute-start | bytes 3145736 | tf_op jit(solution)/shard_map/ppermute | solution.py:25
  427.2 86.1 %collective-permute-start.37 = (bf16[256,2048]{1,0:T(8,128)(2,1)}, bf16[256,2048]{1,0:T(8,128)(2,1)}, u32[]{:S(2)}, u32[]{:S(2)}) collective-permute-start(bf16[256,2048]{1,0:T(8,128)(2,1)} %get-tuple-element.49), channel_id=1, source_target_pairs={{0,1},{1,0},{2,3},{3,2},{4,5},{5,4},{6,7},{7,6},{8,9},{9,8},{10,11... | collective-permute-start | bytes 3145736 | tf_op jit(solution)/shard_map/ppermute | solution.py:25
  431.2 85.3 %collective-permute-start.34 = (bf16[256,2048]{1,0:T(8,128)(2,1)}, bf16[256,2048]{1,0:T(8,128)(2,1)}, u32[]{:S(2)}, u32[]{:S(2)}) collective-permute-start(bf16[256,2048]{1,0:T(8,128)(2,1)} %get-tuple-element.47), channel_id=1, source_target_pairs={{0,1},{1,0},{2,3},{3,2},{4,5},{5,4},{6,7},{7,6},{8,9},{9,8},{10,11... | collective-permute-start | bytes 3145736 | tf_op jit(solution)/shard_map/ppermute | solution.py:25
  490.0 20.3 %collective-permute-start.53 = (bf16[2,256,768]{2,1,0:T(8,128)(2,1)}, bf16[2,256,768]{2,1,0:T(8,128)(2,1)}, u32[]{:S(2)}, u32[]{:S(2)}) collective-permute-start(bf16[2,256,768]{2,1,0:T(8,128)(2,1)} %get-tuple-element.41), channel_id=1, source_target_pairs={{0,4},{4,0},{1,5},{5,1},{2,6},{6,2},{3,7},{7,3},{8,12},{12,8},{9,1... | collective-permute-start | bytes 2359304 | tf_op jit(solution)/shard_map/ppermute | solution.py:25
  505.6 9.6 %collective-permute-start.44 = (bf16[256,2048]{1,0:T(8,128)(2,1)}, bf16[256,2048]{1,0:T(8,128)(2,1)S(1)}, u32[]{:S(2)}, u32[]{:S(2)}) collective-permute-start(bf16[256,2048]{1,0:T(8,128)(2,1)} %get-tuple-element.45), channel_id=1, source_target_pairs={{0,1},{1,0},{2,3},{3,2},{4,5},{5,4},{6,7},{7,6},{8,9},{9,8},{10,11... | collective-permute-start | bytes 3145736 | tf_op jit(solution)/shard_map/ppermute | solution.py:25
  510.3 33.0 %collective-permute-start.56 = (bf16[2,256,1024]{2,1,0:T(8,128)(2,1)S(1)}, bf16[2,256,1024]{2,1,0:T(8,128)(2,1)S(1)}, u32[]{:S(2)}, u32[]{:S(2)}) collective-permute-start(bf16[2,256,1024]{2,1,0:T(8,128)(2,1)S(1)} %get-tuple-element.35), channel_id=1, source_target_pairs={{0,4},{4,0},{1,5},{5,1},{2,6},{6,2},{3,7},{7,3},{8,12},{12,8},{9,1... | collective-permute-start | bytes 3145736 | tf_op jit(solution)/shard_map/ppermute | solution.py:25
  513.4 7.3 collective-permute-start.43
  516.5 26.1 %collective-permute-start.45 = (bf16[256,2048]{1,0:T(8,128)(2,1)S(1)}, bf16[256,2048]{1,0:T(8,128)(2,1)S(1)}, u32[]{:S(2)}, u32[]{:S(2)}) collective-permute-start(bf16[256,2048]{1,0:T(8,128)(2,1)S(1)} %fusion.37), channel_id=1, source_target_pairs={{0,2},{2,0},{1,3},{3,1},{4,6},{6,4},{5,7},{7,5},{8,10},{10,8},{9,1... | collective-permute-start | bytes 3145736 | tf_op jit(solution)/shard_map/ppermute | solution.py:25
  518.8 46.3 %collective-permute-start.38 = (bf16[256,2048]{1,0:T(8,128)(2,1)S(1)}, bf16[256,2048]{1,0:T(8,128)(2,1)S(1)}, u32[]{:S(2)}, u32[]{:S(2)}) collective-permute-start(bf16[256,2048]{1,0:T(8,128)(2,1)S(1)} %fusion.43), channel_id=1, source_target_pairs={{0,2},{2,0},{1,3},{3,1},{4,6},{6,4},{5,7},{7,5},{8,10},{10,8},{9,1... | collective-permute-start | bytes 3145736 | tf_op jit(solution)/shard_map/ppermute | solution.py:25
  520.7 49.8 %collective-permute-start.52 = (bf16[2,256,768]{2,1,0:T(8,128)(2,1)S(1)}, bf16[2,256,768]{2,1,0:T(8,128)(2,1)S(1)}, u32[]{:S(2)}, u32[]{:S(2)}) collective-permute-start(bf16[2,256,768]{2,1,0:T(8,128)(2,1)S(1)} %copy-done.45), channel_id=1, source_target_pairs={{0,4},{4,0},{1,5},{5,1},{2,6},{6,2},{3,7},{7,3},{8,12},{12,8},{9,1... | collective-permute-start | bytes 2359304 | tf_op jit(solution)/shard_map/ppermute | solution.py:25
  542.6 28.0 %collective-permute-start.40 = (bf16[256,2048]{1,0:T(8,128)(2,1)S(1)}, bf16[256,2048]{1,0:T(8,128)(2,1)S(1)}, u32[]{:S(2)}, u32[]{:S(2)}) collective-permute-start(bf16[256,2048]{1,0:T(8,128)(2,1)S(1)} %copy-done.42), channel_id=1, source_target_pairs={{0,1},{1,0},{2,3},{3,2},{4,5},{5,4},{6,7},{7,6},{8,9},{9,8},{10,11... | collective-permute-start | bytes 3145736 | tf_op jit(solution)/shard_map/ppermute | solution.py:25
  543.2 37.9 %collective-permute-start.54 = (bf16[2,256,768]{2,1,0:T(8,128)(2,1)S(1)}, bf16[2,256,768]{2,1,0:T(8,128)(2,1)S(1)}, u32[]{:S(2)}, u32[]{:S(2)}) collective-permute-start(bf16[2,256,768]{2,1,0:T(8,128)(2,1)S(1)} %fusion.56), channel_id=1, source_target_pairs={{0,16},{16,0},{1,17},{17,1},{2,18},{18,2},{3,19},{19,3},{4,20},{20... | collective-permute-start | bytes 2359304 | tf_op jit(solution)/shard_map/ppermute | solution.py:25
  543.3 44.2 %collective-permute-start.42 = (bf16[256,2048]{1,0:T(8,128)(2,1)S(1)}, bf16[256,2048]{1,0:T(8,128)(2,1)S(1)}, u32[]{:S(2)}, u32[]{:S(2)}) collective-permute-start(bf16[256,2048]{1,0:T(8,128)(2,1)S(1)} %fusion.40), channel_id=1, source_target_pairs={{0,2},{2,0},{1,3},{3,1},{4,6},{6,4},{5,7},{7,5},{8,10},{10,8},{9,1... | collective-permute-start | bytes 3145736 | tf_op jit(solution)/shard_map/ppermute | solution.py:25
  565.1 38.5 %collective-permute-start.46 = (bf16[256,2048]{1,0:T(8,128)(2,1)S(1)}, bf16[256,2048]{1,0:T(8,128)(2,1)S(1)}, u32[]{:S(2)}, u32[]{:S(2)}) collective-permute-start(bf16[256,2048]{1,0:T(8,128)(2,1)S(1)} %fusion.39), channel_id=1, source_target_pairs={{0,8},{8,0},{1,9},{9,1},{2,10},{10,2},{3,11},{11,3},{4,12},{12,4},... | collective-permute-start | bytes 3145736 | tf_op jit(solution)/shard_map/ppermute | solution.py:25
  570.6 34.0 %collective-permute-start.33 = (bf16[256,2048]{1,0:T(8,128)(2,1)S(1)}, bf16[256,2048]{1,0:T(8,128)(2,1)S(1)}, u32[]{:S(2)}, u32[]{:S(2)}) collective-permute-start(bf16[256,2048]{1,0:T(8,128)(2,1)S(1)} %copy-done.41), channel_id=1, source_target_pairs={{0,1},{1,0},{2,3},{3,2},{4,5},{5,4},{6,7},{7,6},{8,9},{9,8},{10,11... | collective-permute-start | bytes 3145736 | tf_op jit(solution)/shard_map/ppermute | solution.py:25
  570.6 38.4 %collective-permute-start.35 = (bf16[256,2048]{1,0:T(8,128)(2,1)S(1)}, bf16[256,2048]{1,0:T(8,128)(2,1)S(1)}, u32[]{:S(2)}, u32[]{:S(2)}) collective-permute-start(bf16[256,2048]{1,0:T(8,128)(2,1)S(1)} %fusion.46), channel_id=1, source_target_pairs={{0,2},{2,0},{1,3},{3,1},{4,6},{6,4},{5,7},{7,5},{8,10},{10,8},{9,1... | collective-permute-start | bytes 3145736 | tf_op jit(solution)/shard_map/ppermute | solution.py:25
  581.1 50.3 %collective-permute-start.39 = (bf16[256,2048]{1,0:T(8,128)(2,1)S(1)}, bf16[256,2048]{1,0:T(8,128)(2,1)S(1)}, u32[]{:S(2)}, u32[]{:S(2)}) collective-permute-start(bf16[256,2048]{1,0:T(8,128)(2,1)S(1)} %fusion.45), channel_id=1, source_target_pairs={{0,8},{8,0},{1,9},{9,1},{2,10},{10,2},{3,11},{11,3},{4,12},{12,4},... | collective-permute-start | bytes 3145736 | tf_op jit(solution)/shard_map/ppermute | solution.py:25
  587.5 49.2 %collective-permute-start.55 = (bf16[2,256,1024]{2,1,0:T(8,128)(2,1)}, bf16[2,256,1024]{2,1,0:T(8,128)(2,1)}, u32[]{:S(2)}, u32[]{:S(2)}) collective-permute-start(bf16[2,256,1024]{2,1,0:T(8,128)(2,1)} %get-tuple-element.34), channel_id=1, source_target_pairs={{0,4},{4,0},{1,5},{5,1},{2,6},{6,2},{3,7},{7,3},{8,12},{12,8},{9,1... | collective-permute-start | bytes 3145736 | tf_op jit(solution)/shard_map/ppermute | solution.py:25
  603.5 55.4 %collective-permute-start.57 = (bf16[2,256,1024]{2,1,0:T(8,128)(2,1)}, bf16[2,256,1024]{2,1,0:T(8,128)(2,1)}, u32[]{:S(2)}, u32[]{:S(2)}) collective-permute-start(bf16[2,256,1024]{2,1,0:T(8,128)(2,1)} %fusion.53), channel_id=1, source_target_pairs={{0,16},{16,0},{1,17},{17,1},{2,18},{18,2},{3,19},{19,3},{4,20},{20... | collective-permute-start | bytes 3145736 | tf_op jit(solution)/shard_map/ppermute | solution.py:25
  604.6 73.7 %collective-permute-start.59 = (bf16[1,64,2048]{2,1,0:T(8,128)(2,1)}, bf16[1,64,2048]{2,1,0:T(8,128)(2,1)}, u32[]{:S(2)}, u32[]{:S(2)}) collective-permute-start(bf16[1,64,2048]{2,1,0:T(8,128)(2,1)} %get-tuple-element.52), channel_id=1, source_target_pairs={{0,4},{4,0},{1,5},{5,1},{2,6},{6,2},{3,7},{7,3},{8,12},{12,8},{9,1... | collective-permute-start | bytes 786440 | tf_op jit(solution)/shard_map/ppermute | solution.py:25
  609.1 77.3 %collective-permute-start.62 = (bf16[1,256,2048]{2,1,0:T(8,128)(2,1)}, bf16[1,256,2048]{2,1,0:T(8,128)(2,1)}, u32[]{:S(2)}, u32[]{:S(2)}) collective-permute-start(bf16[1,256,2048]{2,1,0:T(8,128)(2,1)} %get-tuple-element.32), channel_id=1, source_target_pairs={{0,4},{4,0},{1,5},{5,1},{2,6},{6,2},{3,7},{7,3},{8,12},{12,8},{9,1... | collective-permute-start | bytes 3145736 | tf_op jit(solution)/shard_map/ppermute | solution.py:25
  631.3 41.0 %collective-permute-start.63 = (bf16[1,256,2048]{2,1,0:T(8,128)(2,1)}, bf16[1,256,2048]{2,1,0:T(8,128)(2,1)}, u32[]{:S(2)}, u32[]{:S(2)}) collective-permute-start(bf16[1,256,2048]{2,1,0:T(8,128)(2,1)} %get-tuple-element.33), channel_id=1, source_target_pairs={{0,4},{4,0},{1,5},{5,1},{2,6},{6,2},{3,7},{7,3},{8,12},{12,8},{9,1... | collective-permute-start | bytes 3145736 | tf_op jit(solution)/shard_map/ppermute | solution.py:25
  636.7 41.6 %collective-permute-start.61 = (bf16[1,64,2048]{2,1,0:T(8,128)(2,1)S(1)}, bf16[1,64,2048]{2,1,0:T(8,128)(2,1)}, u32[]{:S(2)}, u32[]{:S(2)}) collective-permute-start(bf16[1,64,2048]{2,1,0:T(8,128)(2,1)S(1)} %fusion.83), channel_id=1, source_target_pairs={{0,16},{16,0},{1,17},{17,1},{2,18},{18,2},{3,19},{19,3},{4,20},{20... | collective-permute-start | bytes 786440 | tf_op jit(solution)/shard_map/ppermute | solution.py:25
  658.9 6.7 collective-permute-start.47
  665.6 5.8 collective-permute-start.48
  667.1 61.6 %all-to-all-start.1 = ((bf16[8,64,1792]{2,1,0:T(8,128)(2,1)}), bf16[8,64,1792]{2,1,0:T(8,128)(2,1)}, u32[]{:S(2)}, u32[]{:S(2)}) async-start(bf16[8,64,1792]{2,1,0:T(8,128)(2,1)} %pad_maximum_fusion.1), calls=%async_computation.1 | async-start | bytes 3670016 | tf_op jit(solution)/shard_map/all_to_all | solution.py:207
  671.4 4.9 collective-permute-start.49
  674.5 48.6 %collective-permute-start.64 = (bf16[1,256,2048]{2,1,0:T(8,128)(2,1)S(1)}, bf16[1,256,2048]{2,1,0:T(8,128)(2,1)S(1)}, u32[]{:S(2)}, u32[]{:S(2)}) collective-permute-start(bf16[1,256,2048]{2,1,0:T(8,128)(2,1)S(1)} %fusion.50), channel_id=1, source_target_pairs={{0,16},{16,0},{1,17},{17,1},{2,18},{18,2},{3,19},{19,3},{4,20},{20... | collective-permute-start | bytes 3145736 | tf_op jit(solution)/shard_map/ppermute | solution.py:25
  676.3 9.9 %collective-permute-start.50 = (f32[2,768]{1,0:T(2,128)S(1)}, f32[2,768]{1,0:T(2,128)S(1)}, u32[]{:S(2)}, u32[]{:S(2)}) collective-permute-start(f32[2,768]{1,0:T(2,128)S(1)} %broadcast_select_fusion.11), channel_id=1, source_target_pairs={{0,2},{2,0},{1,3},{3,1},{4,6},{6,4},{5,7},{7,5},{8,10},{10,8},{9,1... | collective-permute-start | bytes 18440 | tf_op jit(solution)/shard_map/ppermute | solution.py:25
  686.3 40.6 %collective-permute-start.51 = (f32[1,768]{1,0:T(1,128)S(1)}, f32[1,768]{1,0:T(1,128)S(1)}, u32[]{:S(2)}, u32[]{:S(2)}) collective-permute-start(f32[1,768]{1,0:T(1,128)S(1)} %broadcast_select_fusion.12), channel_id=1, source_target_pairs={{0,1},{1,0},{2,3},{3,2},{4,5},{5,4},{6,7},{7,6},{8,9},{9,8},{10,11... | collective-permute-start | bytes 9224 | tf_op jit(solution)/shard_map/ppermute | solution.py:25
  (68 other events, 987.2 us)

commit v2 on v1

v2 whole, which is shorter than its diff:
```python
import functools

import jax
import jax.numpy as jnp
from jax import lax
from jax.experimental import pallas as pl
from jax.experimental.pallas import tpu as pltpu
from jax.sharding import Mesh, PartitionSpec as P

D = 2048
H = 16
HD = 128
ROT = 32
FF = 8192
WIDE = 6 * HD
UNITS = FF // 8
BLK = 256
NBLK = D // BLK
EPS = 1e-05
NEG = -1e30
THETA = 10000.0
BF = jnp.bfloat16
F32 = jnp.float32
AXES = ("zh", "zl", "y", "x", "core")
VMEM = 50 * 2**20
COST = 1.0


LINE = {}
DEPTH = {"core": 4}


def after(v, *others):
    return lax.optimization_barrier((v, *others))[0]


def queue(channel, v, step):
    line = LINE.setdefault(channel, [])
    depth = DEPTH.get(channel, 1)
    if len(line) >= depth:
        v = after(v, line[-depth])
    out = step(v)
    line.append(out[0] if isinstance(out, (list, tuple)) else out)
    return out


def flip(v, axis, channel=None):
    return queue(channel or axis, v, lambda w: lax.ppermute(w, axis, [(0, 1), (1, 0)]))


def dot(a, b, ca, cb):
    return lax.dot_general(a, b, (((ca,), (cb,)), ((), ())), preferred_element_type=F32)


def call(kernel, grid, ins, outs, shapes, scratch=(), flops=0, traffic=0, special=0, scalars=1):
    return pl.pallas_call(
        kernel,
        grid_spec=pltpu.PrefetchScalarGridSpec(
            num_scalar_prefetch=scalars,
            grid=grid,
            in_specs=ins,
            out_specs=outs,
            scratch_shapes=scratch,
        ),
        out_shape=shapes,
        compiler_params=pltpu.CompilerParams(vmem_limit_bytes=VMEM),
        cost_estimate=pl.CostEstimate(
            flops=int(flops * COST), bytes_accessed=int(traffic * COST), transcendentals=int(special * COST)
        ),
    )


def shape(*dims, dtype=BF):
    return jax.ShapeDtypeStruct(dims, dtype)


def fixed(*dims):
    return pl.BlockSpec(dims, lambda *_: (0,) * len(dims))


def rows_of(width, rows=BLK):
    return pl.BlockSpec((rows, width), lambda i, *_: (i, 0))


def two_halves(width):
    return [
        pl.BlockSpec((BLK, width), lambda i, *_: (jnp.minimum(i, 3), 0)),
        pl.BlockSpec((BLK, width), lambda i, *_: (jnp.maximum(i - 4, 0), 0)),
    ]


def pick(near, far):
    return jnp.where(pl.program_id(0) < 4, near[...], far[...])


def place(base, r, p):
    s = r ^ base
    return (s // 2) * 4 + p * 2 + s % 2


def columns(index):
    return pl.ds(pl.multiple_of(index * BLK, BLK), BLK)


def norm_kernel(near, far, gains, one, two, mean, scale):
    v = pick(near, far).astype(F32)
    mu = jnp.mean(v, axis=-1, keepdims=True)
    v = v - mu
    r = lax.rsqrt(jnp.mean(v * v, axis=-1, keepdims=True) + EPS)
    v = v * r
    one[...] = (v * gains[0:1] + gains[1:2]).astype(BF)
    two[...] = (v * gains[2:3] + gains[3:4]).astype(BF)
    mean[...] = mu
    scale[...] = r


def norms(near, far, gains):
    n = 2 * near.shape[0]
    return call(
        norm_kernel,
        (n // BLK,),
        [*two_halves(D), fixed(4, D)],
        [rows_of(D), rows_of(D), rows_of(1), rows_of(1)],
        [shape(n, D), shape(n, D), shape(n, 1, dtype=F32), shape(n, 1, dtype=F32)],
        traffic=n * D * 6,
        flops=n * D * 10,
        scalars=0,
    )(near, far, gains)


def joined_kernel(base, v, w0, w1, w2, w3, shift, out):
    total = jnp.zeros((BLK, WIDE), F32) + shift[...]
    for r, w in enumerate((w0, w1, w2, w3)):
        for p in range(2):
            total += dot(v[:, columns(place(base[0], r, p))], w[p], 1, 0)
    out[...] = total


def joined_product(base, v, pieces, shift):
    n = v.shape[0]
    return call(
        joined_kernel,
        (n // BLK,),
        [rows_of(D), *[fixed(2, BLK, WIDE)] * 4, fixed(1, WIDE)],
        rows_of(WIDE),
        shape(n, WIDE, dtype=F32),
        flops=2 * n * D * WIDE,
        traffic=n * D * 2 + n * WIDE * 4 + D * WIDE * 2,
    )(base, v, *pieces, shift)


def mixed_grad_kernel(near, far, w, out):
    out[...] = dot(pick(near, far), w[...], 1, 1).astype(BF)


def mixed_grad(near, far, w):
    n, wide = 2 * near.shape[0], w.shape[0]
    return call(
        mixed_grad_kernel,
        (n // BLK,),
        [*two_halves(D), fixed(wide, D)],
        rows_of(wide),
        shape(n, wide),
        flops=2 * n * D * wide,
        traffic=n * D * 2,
        scalars=0,
    )(near, far, w)


def hidden_kernel(
    skip, base, v, near, far, w0, w1, w2, w3, b0, b1, b2, b3, shift, active, grad, sums, back
):
    up = pick(near, far)
    for r, w in enumerate((b0, b1, b2, b3)):
        back[:, columns(r ^ base[0])] = dot(up, w[skip:], 1, 1)
    u = jnp.zeros((BLK, UNITS), F32) + shift[...]
    for r, w in enumerate((w0, w1, w2, w3)):
        for p in range(2):
            u += dot(v[:, columns(place(base[0], r, p))], w[p], 1, 0)
    below = 0.5 * (1.0 + lax.erf(u * (0.5**0.5)))
    active[...] = (u * below).astype(BF)
    slope = below + u * jnp.exp(-0.5 * u * u) * ((2.0 * jnp.pi) ** (-0.5))
    low = (back[...] * slope).astype(BF)
    grad[...] = low

    @pl.when(pl.program_id(0) == 0)
    def _():
        sums[...] = jnp.zeros_like(sums)

    sums[...] += jnp.sum(low.astype(F32), axis=0, keepdims=True)


def hidden_products(base, v, near, far, pieces, back_pieces, shift):
    n, tall = v.shape[0], back_pieces[0].shape[0]
    return call(
        functools.partial(hidden_kernel, tall - BLK),
        (n // BLK,),
        [rows_of(D), *two_halves(D), *[fixed(2, BLK, UNITS)] * 4, *[fixed(tall, D)] * 4, fixed(1, UNITS)],
        [rows_of(UNITS), rows_of(UNITS), fixed(1, UNITS)],
        [shape(n, UNITS), shape(n, UNITS), shape(1, UNITS, dtype=F32)],
        [pltpu.VMEM((BLK, UNITS), F32)],
        flops=4 * n * D * UNITS,
        traffic=n * D * 4 + n * UNITS * 4 + D * UNITS * 4,
        special=2 * n * UNITS,
    )(base, v, near, far, *pieces, *back_pieces, shift)


def out_kernel(skip, base, mixed, active, w, b0, b1, b2, b3, out):
    total = dot(mixed[...], w[...], 1, 0)
    for r, b in enumerate((b0, b1, b2, b3)):
        total += dot(active[:, columns(r ^ base[0])], b[skip:], 1, 0)
    out[...] = total.astype(BF)


def out_product(base, half, mixed, active, dense_w, back_pieces):
    n, tall = mixed.shape[0] // 2, back_pieces[0].shape[0]
    steps = n // BLK
    half_rows = lambda width: pl.BlockSpec((BLK, width), lambda i, *_: (i + half * steps, 0))
    return call(
        functools.partial(out_kernel, tall - BLK),
        (steps,),
        [half_rows(2 * HD), half_rows(UNITS), fixed(2 * HD, D), *[fixed(tall, D)] * 4],
        rows_of(D),
        shape(n, D),
        flops=2 * n * D * (UNITS + 2 * HD),
        traffic=n * D * 2 + n * UNITS * 2 + D * UNITS * 2,
    )(base, mixed, active, dense_w, *back_pieces)


def pull_kernel(
    base, dq, dk, dv, du, tokens, mean, scale, gains, q0, q1, q2, q3, w0, w1, w2, w3, out, sums, wide
):
    @pl.when(pl.program_id(0) == 0)
    def _():
        sums[...] = jnp.zeros_like(sums)
        wide[...] = jnp.zeros_like(wide)

    add = lambda v: jnp.sum(v, axis=0, keepdims=True)
    for t, v in enumerate((dq, dk, dv)):
        wide[:, 2 * HD * t : 2 * HD * (t + 1)] += add(v[...].astype(F32))
    for r, (q, w) in enumerate(((q0, w0), (q1, w1), (q2, w2), (q3, w3))):
        for p in range(2):
            at = columns(place(base[0], r, p))
            one = (
                dot(dq[...], q[p, :, 0 : 2 * HD], 1, 1)
                + dot(dk[...], q[p, :, 2 * HD : 4 * HD], 1, 1)
                + dot(dv[...], q[p, :, 4 * HD :], 1, 1)
            )
            two = dot(du[...], w[p], 1, 1)
            normal = (tokens[:, at].astype(F32) - mean[...]) * scale[...]
            sums[0:1, at] += add(one * normal)
            sums[1:2, at] += add(one)
            sums[2:3, at] += add(two * normal)
            sums[3:4, at] += add(two)
            out[:, at] = (one * gains[0:1, at] + two * gains[2:3, at]).astype(BF)


def pull_product(base, half, grads, du, tokens, mean, scale, gains, joined_pieces, pieces):
    n = du.shape[0] // 2
    steps = n // BLK
    half_rows = lambda width: pl.BlockSpec((BLK, width), lambda i, *_: (i + half * steps, 0))
    return call(
        pull_kernel,
        (steps,),
        [
            *[half_rows(2 * HD)] * 3,
            half_rows(UNITS),
            rows_of(D),
            half_rows(1),
            half_rows(1),
            fixed(4, D),
            *[fixed(2, BLK, WIDE)] * 4,
            *[fixed(2, BLK, UNITS)] * 4,
        ],
        [rows_of(D), fixed(4, D), fixed(1, WIDE)],
        [shape(n, D), shape(4, D, dtype=F32), shape(1, WIDE, dtype=F32)],
        flops=2 * n * D * (UNITS + WIDE),
        traffic=n * D * 4 + n * UNITS * 4 + D * (UNITS + WIDE) * 2,
    )(base, *grads, du, tokens, mean, scale, gains, *joined_pieces, *pieces)


def rows_grad_kernel(count, base, v, *refs):
    rights, outs = refs[:count], refs[count:]
    step = pl.program_id(0)
    v = v[...]
    parts, width = [], 0
    for right in rights:
        parts.append(dot(v, right[...], 0, 0).astype(BF))
    for j, out in enumerate(outs):

        @pl.when(step // 2 == j)
        def _(out=out):
            at = 0
            for part in parts:
                out[:, at : at + part.shape[1]] = part
                at += part.shape[1]


def rows_grad(base, v, rights, order):
    n, width = v.shape[0], sum(r.shape[1] for r in rights)

    def chosen(i, b):
        r = sum(jnp.where(i // 2 == j, r, 0) for j, r in enumerate(order))
        return (0, place(b[0], r, i % 2))

    def slot(j):
        return pl.BlockSpec((BLK, width), lambda i, b: (jnp.clip(i - 2 * j, 0, 1), 0))

    return call(
        functools.partial(rows_grad_kernel, len(rights)),
        (2 * len(order),),
        [pl.BlockSpec((n, BLK), chosen), *[fixed(*r.shape) for r in rights]],
        [slot(j) for j in range(len(order))],
        [shape(2 * BLK, width)] * len(order),
        flops=2 * n * BLK * 2 * len(order) * width,
        traffic=n * width * 2 + n * BLK * 4 * len(order),
    )(base, v, *rights)


def units_grad_kernel(base, v, near, far, *outs):
    step, n = pl.program_id(0), near.shape[0]
    part = dot(v[:n], near[...], 0, 0) + dot(v[n:], far[...], 0, 0)
    part = part.astype(BF)
    for j, out in enumerate(outs):

        @pl.when(step == j)
        def _(out=out):
            out[...] = part


def units_grad(base, v, near, far, order):
    n = v.shape[0]

    def chosen(i, b):
        return (0, sum(jnp.where(i == j, r, 0) for j, r in enumerate(order)) ^ b[0])

    return call(
        units_grad_kernel,
        (len(order),),
        [pl.BlockSpec((n, BLK), chosen), fixed(n // 2, D), fixed(n // 2, D)],
        [fixed(BLK, D)] * len(order),
        [shape(BLK, D)] * len(order),
        flops=2 * n * BLK * D * len(order),
        traffic=n * D * 2 + (n + D) * BLK * 2 * len(order),
    )(base, v, near, far)


def turn(v, cos, sin):
    lane = lax.broadcasted_iota(jnp.int32, v.shape, 1)
    half = ROT // 2
    swapped = jnp.where(lane < half, pltpu.roll(v, HD - half, 1), pltpu.roll(v, half, 1))
    return v * cos + swapped * sin


def attention_kernel(
    q, k, v, do, cq, sq, ck, sk, pq, eq, pk, ek, o, dq, dk, dv, ks, vs, dka, dva
):
    i = pl.program_id(2)
    scale = HD ** (-0.5)
    flat = lambda a: a.reshape(-1, HD)

    @pl.when(i == 0)
    def _():
        ks[...] = turn(flat(k[...]), ck[...], sk[...]).astype(BF)
        vs[...] = flat(v[...]).astype(BF)
        dka[...] = jnp.zeros_like(dka)
        dva[...] = jnp.zeros_like(dva)

    qr = turn(q[...], cq[...], sq[...]).astype(BF)
    s = dot(qr, ks[...], 1, 1) * scale
    allowed = (pk[...] <= pq[...]) & (ek[...] == eq[...])
    s = jnp.where(allowed, s, NEG)
    e = jnp.exp(s - jnp.max(s, axis=-1, keepdims=True))
    p = e / jnp.sum(e, axis=-1, keepdims=True)
    low = p.astype(BF)
    o[...] = dot(low, vs[...], 1, 0).astype(BF)
    dp = dot(do[...], vs[...], 1, 1)
    ds = (p * (dp - jnp.sum(p * dp, axis=-1, keepdims=True))).astype(BF)
    dq[...] = turn(dot(ds, ks[...], 1, 0) * scale, cq[...], -sq[...]).astype(BF)
    dva[...] += dot(low, do[...], 0, 0)
    dka[...] += dot(ds, qr, 0, 0)

    @pl.when(i == pl.num_programs(2) - 1)
    def _():
        dk[...] = turn(dka[...] * scale, ck[...], -sk[...]).astype(BF).reshape(dk.shape)
        dv[...] = dva[...].astype(BF).reshape(dv.shape)


def attention(joined, grad, cos, sin, pos, doc):
    half = 2 * BLK
    length = 2 * half
    joined = joined.reshape(2, 2, half, WIDE)
    grad = grad.reshape(2, 2, half, 2 * HD)
    part = lambda off: pl.BlockSpec(
        (None, None, BLK, HD), lambda s, h, i: (i // 2, s, i % 2, off + h)
    )
    whole = lambda off: pl.BlockSpec((2, None, half, HD), lambda s, h, i: (0, s, 0, off + h))
    tq = pl.BlockSpec((None, BLK, HD), lambda s, h, i: (s, i, 0))
    tk = pl.BlockSpec((None, length, HD), lambda s, h, i: (s, 0, 0))
    col = pl.BlockSpec((None, BLK, 1), lambda s, h, i: (s, i, 0))
    row = pl.BlockSpec((None, 1, length), lambda s, h, i: (s, 0, 0))
    results = call(
        attention_kernel,
        (2, 2, length // BLK),
        [part(0), whole(2), whole(4), part(0), tq, tq, tk, tk, col, col, row, row],
        [part(0), part(0), whole(0), whole(0)],
        [shape(2, 2, half, 2 * HD)] * 4,
        [
            pltpu.VMEM((length, HD), BF),
            pltpu.VMEM((length, HD), BF),
            pltpu.VMEM((length, HD), F32),
            pltpu.VMEM((length, HD), F32),
        ],
        flops=4 * length * length * HD * 14,
        traffic=4 * length * HD * 24,
        special=4 * length * length,
        scalars=0,
    )(
        joined, joined, joined, grad, cos, sin, cos, sin,
        pos[:, :, None], doc[:, :, None], pos[:, None, :], doc[:, None, :],
    )
    return [r.reshape(2 * length, 2 * HD) for r in results]


def column_plan(copies):
    units = FF // (16 * copies)
    for d in range(8):
        zl, x, core = d // 4, d // 2 % 2, d % 2
        for t in range(3):
            for m in range(2):
                head = core * 8 + zl * 4 + m * 2 + x
                yield 0, t * D + head * HD, HD, d, (t * 2 + m) * HD
        for zh in range(2):
            for y in range(copies):
                owner = (((zh * 2 + zl) * copies + y) * 2 + x) * 2 + core
                yield 1, owner * units, units, d, (zh * copies + y) * units


def deal_kernel(copies, wide, tall, wide_out, tall_out):
    pairs = ((wide, wide_out), (tall, tall_out))
    for which, start, width, d, at in column_plan(copies):
        source, target = pairs[which]
        target[d, :, at : at + width] = source[:, start : start + width]


def deal_columns(wide, tall, copies):
    rows = wide.shape[0]
    return call(
        functools.partial(deal_kernel, copies),
        (1,),
        [fixed(*wide.shape), fixed(*tall.shape)],
        [fixed(8, rows, WIDE), fixed(8, rows, UNITS)],
        [shape(8, rows, WIDE), shape(8, rows, UNITS)],
        traffic=rows * (3 * D + FF) * 4,
        scalars=0,
    )(wide, tall)


def collect_kernel(copies, which_one, source, target):
    for which, start, width, d, at in column_plan(copies):
        if which == which_one:
            target[:, start : start + width] = source[d, :, at : at + width].astype(F32)


def collect_columns(v, which, copies):
    rows, width = v.shape[1], (3 * D, FF)[which]
    return call(
        functools.partial(collect_kernel, copies, which),
        (1,),
        [fixed(*v.shape)],
        fixed(rows, width),
        shape(rows, width, dtype=F32),
        traffic=rows * width * 6,
        scalars=0,
    )(v)


def pack_kernel(*refs):
    for j, v in enumerate(refs[:-1]):
        refs[-1][j : j + 1, 0 : v.shape[1]] = v[...]


def pack_rows(vectors):
    vectors = [v[None] for v in vectors]
    return call(
        pack_kernel,
        (1,),
        [fixed(*v.shape) for v in vectors],
        fixed(len(vectors), BLK),
        shape(len(vectors), BLK),
        scalars=0,
    )(*vectors)


def swap(v, axes=("zl", "x", "core")):
    return queue("swap", v, lambda w: lax.all_to_all(w, axes, 0, 0, tiled=True))


def gather_plain(v, split):
    return split(lax.all_gather(v, ("zh", "y"), axis=0, tiled=False))


def half_sum(v, other):
    return (v.astype(F32) + other.astype(F32)).astype(BF)


def split_rows(copies):
    def split(w):
        c = w.shape[-1]
        w = w.reshape(2, copies, 2, -1, c).transpose(0, 2, 1, 3, 4).reshape(2, 2, 2, BLK, c)
        return [w[a, :, b] for a in (0, 1) for b in (0, 1)]

    return split


def join_rows(copies):
    def join(w):
        c = w.shape[-1]
        w = w.reshape(2, 2, 2, BLK, c).transpose(0, 2, 1, 3, 4)
        w = w.reshape(2, 2, copies, -1, c).transpose(0, 2, 1, 3, 4)
        return w.reshape(2 * copies, -1, c)

    return join


def reduce_tokens(near, far, span):
    block = lambda v, f: v[f * span : (f + 1) * span]
    got = {f: flip(block(far, f), "core") for f in (3, 1, 2, 0)}
    total = lambda f: block(near, f).astype(F32) + got[f].astype(F32)
    away_x = flip(total(3).astype(BF), "x")
    mine_x = flip(total(1).astype(BF), "x")
    from_far = flip((total(2) + away_x.astype(F32)).astype(BF), "zl")
    return total(0) + mine_x.astype(F32) + from_far.astype(F32)


def flip_parts(v, axis, parts=2, cut=0):
    size = v.shape[cut] // parts
    pieces = [lax.slice_in_dim(v, j * size, (j + 1) * size, axis=cut) for j in range(parts)]
    return [flip(p, axis) for p in pieces]


def dense_rows(pieces):
    core = lax.axis_index("core")
    zh, y = lax.axis_index("zh"), lax.axis_index("y")
    first = core == 0
    w = jnp.stack(pieces).reshape(2, 2, HD // 2, D)
    w = jnp.where(y == 0, w, w[:, ::-1])
    same = zh == core
    keep, send = jnp.where(same, w[0], w[1]), jnp.where(same, w[1], w[0])
    other = flip(send, "core")
    low, high = jnp.where(first, keep, other), jnp.where(first, other, keep)
    return jnp.stack([low, high], axis=1).reshape(2 * HD, D)


def gather_dense_plain(w):
    core, x = lax.axis_index("core"), lax.axis_index("x")
    w = lax.all_gather(w, ("zh", "y", "x", "core"), axis=0, tiled=True).reshape(2, 2, 2, HD, D)
    w = lax.dynamic_slice(w, (core, 0, x, 0, 0), (1, 2, 1, HD, D))
    return w.reshape(2 * HD, D)


def reduce_dense(g, copies):
    core, x = lax.axis_index("core"), lax.axis_index("x")
    if copies != 2:
        w = jnp.zeros((2, 2, 2, HD, D), F32)
        g = g.astype(F32).reshape(1, 2, 1, HD, D)
        w = lax.dynamic_update_slice(w, g, (core, 0, x, 0, 0)).reshape(-1, D)
        return lax.psum_scatter(w, ("zh", "y", "x", "core"), scatter_dimension=0, tiled=True)
    zh, y = lax.axis_index("zh"), lax.axis_index("y")
    g = g.reshape(2, 2, HD // 2, D)
    first, same = core == 0, zh == core
    keep = jnp.where(first, g[:, 0], g[:, 1])
    other = flip(jnp.where(first, g[:, 1], g[:, 0]), "core")
    w = jnp.stack([jnp.where(same, keep, other), jnp.where(same, other, keep)])
    w = jnp.where(y == 0, w, w[:, ::-1])
    w = w[:, 0].astype(F32) + flip(w[:, 1], "y").astype(F32)
    return w[0] + flip(w[1].astype(BF), "zh").astype(F32)


def shards(
    copies,
    block_input,
    output_grad,
    documents,
    span_order,
    attention_norm_gain,
    attention_norm_bias,
    query_key_value_weight,
    query_key_value_bias,
    dense_weight,
    dense_bias,
    mlp_norm_gain,
    mlp_norm_bias,
    to_hidden_weight,
    to_hidden_bias,
    from_hidden_weight,
    from_hidden_bias,
):
    LINE.clear()
    span = block_input.shape[1]
    count = 16 * copies
    rows = D // count
    units = FF // count
    length = 4 * span
    zl, x, core = (lax.axis_index(a) for a in ("zl", "x", "core"))
    own_in, own_grad = block_input[0], output_grad[0]
    kernel = lambda v, step, *first: queue("kernel", after(v, *first) if first else v, step)
    base = jnp.zeros((1,), jnp.int32)
    if copies == 2:
        base = base + lax.axis_index("zh") * 2 + lax.axis_index("y")

    vectors = (
        attention_norm_gain,
        attention_norm_bias,
        mlp_norm_gain,
        mlp_norm_bias,
        dense_bias,
        from_hidden_bias,
        query_key_value_bias,
        to_hidden_bias,
    )
    if copies == 2:
        small = pack_rows(vectors)
    else:
        small = jnp.stack([jnp.pad(v, (0, BLK - v.shape[0])) for v in vectors])
    facts = jnp.concatenate([documents[0], jnp.pad(span_order[0], (0, length - 4))])
    small = jnp.concatenate([small, facts.astype(BF).reshape(8, BLK)], axis=0)
    small = jnp.broadcast_to(small[None], (count, 16, BLK)).reshape(count * 16, BLK)

    wide, tall = deal_columns(query_key_value_weight, to_hidden_weight, copies)
    wide = swap(wide).reshape(2, 4 * rows, WIDE)
    tall = swap(tall).reshape(2, 4 * rows, UNITS)
    small = swap(small, AXES).reshape(count, 16, BLK)
    in_zl, in_x = flip(own_in, "zl"), flip(own_in, "x")
    if copies == 2:
        chunk = jnp.concatenate([dense_weight, from_hidden_weight], axis=0)
        join = lambda v: jnp.concatenate(v, axis=0)
        back_near = flip(chunk, "y")
        back_far = flip_parts(chunk, "zh")
        wide_near = flip(wide, "y")
        wide_far = flip(wide, "zh")
        tall_near = flip(tall, "y")
        tall_far = flip_parts(tall, "zh")
        back_both = flip(join(back_far), "y")
        wide_pieces = [wide, wide_near, wide_far, flip(wide_far, "y")]
        tall_both = [flip(v, "y") for v in tall_far]
        tall_pieces = [tall, tall_near, join(tall_far), join(tall_both)]
        back_pieces = [chunk, back_near, join(back_far), back_both]
    in_both = flip(in_zl, "x")
    other_core = lambda blocks: jnp.concatenate([flip(v, "core") for v in blocks], axis=0)
    near = [own_in, in_x, in_zl, in_both]
    far = other_core(near)
    near = jnp.concatenate(near, axis=0)
    up_zl, up_x = flip(own_grad, "zl"), own_grad
    if copies == 2:
        up_x = after(up_x, back_far[1])
    up_x = flip(up_x, "x")
    if copies == 2:
        up_zl = after(up_zl, wide_far, tall_near)
    up_both = flip(up_zl, "x")
    near_up = [own_grad, up_x, up_zl, up_both]
    far_up = other_core(near_up)
    near_up = jnp.concatenate(near_up, axis=0)
    if copies == 2:
        dense_w = dense_rows([p[:rows] for p in back_pieces])
    else:
        wide_pieces = gather_plain(wide, split_rows(copies))
        tall_pieces = gather_plain(tall, split_rows(copies))
        back_pieces = gather_plain(from_hidden_weight, lambda w: list(w.reshape(4, BLK, D)))
        dense_w = gather_dense_plain(dense_weight)

    row = (lax.axis_index("zh") * 2 * copies + lax.axis_index("y")) * 4
    facts = [lax.dynamic_slice(small, (row + s * copies * 4, 8, 0), (1, 8, BLK)) for s in (zl, 1 - zl)]
    facts = [v.astype(jnp.int32).reshape(2 * length) for v in facts]
    small = small[:, :8].astype(F32)
    take = lambda j, n: small[:, j, :n].reshape(-1)
    gains = jnp.stack([take(j, rows) for j in range(4)])
    out_shift = take(4, rows) + take(5, rows)
    joined_shift = take(6, 3 * rows).reshape(3, 2, 2, 2, 2, HD)
    joined_shift = lax.dynamic_slice(joined_shift, (0, core, zl, 0, x, 0), (3, 1, 1, 2, 1, HD))
    joined_shift = joined_shift.reshape(1, WIDE)
    hidden_shift = take(7, units).reshape(2, 2, copies, 2, 2, units)
    hidden_shift = lax.dynamic_slice(
        hidden_shift, (0, zl, 0, x, core, 0), (2, 1, copies, 1, 1, units)
    ).reshape(1, UNITS)

    offsets = jnp.arange(span, dtype=jnp.int32)
    pos, doc = [], []
    for known in facts:
        for c in (0, 1):
            for b in (0, 1):
                block = (x ^ b) * 2 + (core ^ c)
                doc.append(lax.dynamic_slice(known, (block * span,), (span,)))
                pos.append(lax.dynamic_slice(known, (length + block,), (1,)) * span + offsets)
    pos = jnp.concatenate(pos).reshape(2, length)
    doc = jnp.concatenate(doc).reshape(2, length)
    inverse = jnp.power(THETA, -jnp.arange(ROT // 2, dtype=F32) * (2.0 / ROT))
    angles = pos.astype(F32)[:, :, None] * inverse
    cosine, sine = jnp.cos(angles), jnp.sin(angles)
    rest = jnp.zeros((2, length, HD - ROT), F32)
    cos_table = jnp.concatenate([cosine, cosine, rest + 1.0], axis=-1)
    sin_table = jnp.concatenate([-sine, sine, rest], axis=-1)

    order = (3, 1, 2, 0)
    ordered = lambda v: [v[order.index(r)] for r in range(4)]
    normed_one, normed_two, mean, scale = kernel(gains, lambda v: norms(near, far, v))
    grad_mixed = kernel(dense_w, lambda v: mixed_grad(near_up, far_up, v))
    joined = kernel(normed_one, lambda v: joined_product(base, v, wide_pieces, joined_shift))
    mixed, *grads = kernel(
        joined, lambda v: attention(v, grad_mixed, cos_table, sin_table, pos, doc)
    )
    pair = copies == 2
    ties = lambda *v: v if pair else ()
    far_half = lambda v: half_sum(v[2], flip(v[3], "y")) if pair else v[2]
    grad_wide = ordered(kernel(normed_one, lambda v: rows_grad(base, v, grads, order)))
    wide_far = far_half(grad_wide)
    half = mixed.shape[0] // 2
    grad_dense = dot(mixed[:half], near_up, 0, 0) + dot(mixed[half:], far_up, 0, 0)
    grad_dense = grad_dense.astype(BF)
    active, grad_hidden, hidden_sum = kernel(
        normed_two,
        lambda v: hidden_products(
            base, v, near_up, far_up, tall_pieces, back_pieces, hidden_shift
        ),
        grad_dense,
    )
    grad_tall = ordered(
        kernel(grad_hidden, lambda v: rows_grad(base, normed_two, [v], order), *ties(wide_far))
    )
    wide_sum = flip(wide_far, "zh") if pair else None
    tall_far = far_half(grad_tall)
    grad_back = ordered(kernel(active, lambda v: units_grad(base, v, near_up, far_up, order)))
    pull_half = lambda h, *first: kernel(
        grad_hidden,
        lambda v: pull_product(
            base, h, grads, v, far if h else near, mean, scale, gains, wide_pieces, tall_pieces
        ),
        *first,
    )
    out_half = lambda h, *first: kernel(
        mixed, lambda v: out_product(base, h, v, active, dense_w, back_pieces), *first
    )
    pull_far, pull_far_sums, pull_far_wide = pull_half(1, *ties(tall_far, wide_sum))
    back_far = far_half(grad_back)
    pull_near, pull_near_sums, pull_near_wide = pull_half(0)
    tall_sum = flip_parts(tall_far, "zh") if pair else ()
    out_far = out_half(1, *ties(back_far), *tall_sum[:1])
    out_near = out_half(0, *tall_sum[1:])
    tall_sum = jnp.concatenate(tall_sum) if pair else None
    pull = reduce_tokens(pull_near, pull_far, span)
    back_sum = jnp.concatenate(flip_parts(back_far, "zh")) if pair else None
    out = reduce_tokens(out_near, out_far, span)

    def near_half(v, far, join):
        if pair:
            return v[0].astype(F32) + flip(v[1], "y").astype(F32) + far.astype(F32)
        w = join(jnp.stack(v).astype(F32))
        return lax.psum_scatter(w, ("zh", "y"), scatter_dimension=0, tiled=False)

    own_wide = own_in.astype(F32)
    block_output = (own_wide + (out + out_shift)).astype(BF)[None]
    own_centre = own_wide - jnp.mean(own_wide, axis=-1, keepdims=True)
    own_spread = lax.rsqrt(jnp.mean(own_centre * own_centre, axis=-1, keepdims=True) + EPS)
    own_normal = own_centre * own_spread
    pull = own_spread * (
        pull
        - jnp.mean(pull, axis=-1, keepdims=True)
        - own_normal * jnp.mean(pull * own_normal, axis=-1, keepdims=True)
    )
    grad_own = own_grad.astype(F32)
    input_grad = (grad_own + pull).astype(BF)[None]

    vectors = pull_near_sums + pull_far_sums
    joined_sum = (pull_near_wide + pull_far_wide).reshape(3, 1, 1, 2, 1, HD)
    joined_sum = lax.dynamic_update_slice(
        jnp.zeros((3, 2, 2, 2, 2, HD), F32), joined_sum, (0, core, zl, 0, x, 0)
    )
    hidden_sum = lax.dynamic_update_slice(
        jnp.zeros((2, 2, copies, 2, 2, units), F32),
        hidden_sum.reshape(2, 1, copies, 1, 1, units),
        (0, zl, 0, x, core, 0),
    )
    sums = [*vectors, jnp.sum(grad_own, axis=0), joined_sum, hidden_sum]
    sums = jnp.concatenate([v.reshape(count, -1) for v in sums], axis=1)
    sums = jnp.sum(swap(sums, AXES), axis=0)
    cut = lambda a, n: sums[a : a + n]
    bias_sum = cut(4 * rows, rows)

    grad_wide = near_half(grad_wide, wide_sum, join_rows(copies)).astype(BF)
    grad_wide = collect_columns(swap(grad_wide.reshape(8, rows, WIDE)), 0, copies)
    grad_tall = near_half(grad_tall, tall_sum, join_rows(copies)).astype(BF)
    grad_tall = collect_columns(swap(grad_tall.reshape(8, rows, UNITS)), 1, copies)
    grad_dense = reduce_dense(grad_dense, copies)
    grad_back = near_half(grad_back, back_sum, lambda w: w.reshape(2 * copies, units, D))


    return (
        block_output,
        input_grad,
        cut(0, rows),
        cut(rows, rows),
        grad_wide,
        cut(5 * rows, 3 * rows),
        grad_dense,
        bias_sum,
        cut(2 * rows, rows),
        cut(3 * rows, rows),
        grad_tall,
        cut(8 * rows, units),
        grad_back,
        bias_sum,
    )


def solution(mesh):
    copies = mesh.shape["batch"] // 4
    inner = Mesh(mesh.devices.reshape(2, 2, copies, 2, 2), AXES)
    batch, ctx = AXES[:3], AXES[3:]
    tokens = P(batch, ctx, None)
    vector, matrix = P(AXES), P(AXES, None)
    params = (vector, vector, matrix, vector, matrix, vector)
    return jax.shard_map(
        functools.partial(shards, copies),
        mesh=inner,
        in_specs=(tokens, tokens, P(batch, None), P(batch, None)) + params + params,
        out_specs=(tokens, tokens) + params + params,
        check_vma=False,
    )
```

time: 753 us -> 601 us (0.80)
  Pallas kernels: 32.8 us -> 195 us
  matrix products: 135 us -> 4.72 us
  waiting for transfers between devices: 329 us -> 200 us
  local copies, waits for them, and re-layouts: 123 us -> 62.2 us
  starting transfers between devices: 63.7 us -> 71.3 us
    pallas_call x1 -> x16, Pallas kernels: 32.8 us -> 195 us  [the longest x1 35.1 us: attention(): call(attention_kernel, (2, 2, length // BLK), [part(0), whole(2), whole(4...]
    ppermute x65 -> x55, waiting for transfers between devices: 329 us -> 181 us  [flip(): lax.ppermute(w, axis, [(0, 1), (1, 0)])]
    dot_general x11 -> x2, matrix products: 135 us -> 4.72 us  [dot(): lax.dot_general(a, b, (((ca,), (cb,)), ((), ())), preferred_element_type=...]
    all_to_all x2 -> x6, waiting for transfers between devices: 0.01 us -> 19.1 us  [swap(): return queue('swap', v, lambda w: lax.all_to_all(w, axes, 0, 0, tiled=True))]
    dynamic_update_slice x16 -> x0, local copies, waits for them, and re-layouts: 17.2 us -> none  [gather_replicas(): lax.dynamic_update_slice(w, piece[None, :, None], (zh ^ a, 0, y ^ b, 0, 0))]
    reshape x16 -> x4, local copies, waits for them, and re-layouts: 16.7 us -> 0.29 us  [the longest x3 0.19 us: shards(): sums = jnp.concatenate([v.reshape(count, -1) for v in sums], axis=1)]
    dot_general x2 -> x0, local copies, waits for them, and re-layouts: 13.9 us -> none  [dot(): lax.dot_general(a, b, (((ca,), (cb,)), ((), ())), preferred_element_type=...]
    all_to_all x2 -> x6, starting transfers between devices: 8.98 us -> 22.1 us  [swap(): return queue('swap', v, lambda w: lax.all_to_all(w, axes, 0, 0, tiled=True))]
  transfers between devices with their start and end apart: 67 -> 61, of which waited for: 24 -> 20; matrix products, arithmetic and copies ran while one was open for 37% -> 18% of each run, Pallas kernels for 4% -> 22%
where the time goes in v2:
time: 601 us; the launch traced here: 595 us
  waiting for transfers between devices  200 us (33%)
  Pallas kernels  195 us (32%)
  starting transfers between devices  71.3 us (12%)
  local copies, waits for them, and re-layouts  62.2 us (10%)
  other arithmetic  54.3 us (9%)
  between operations  7.31 us (1%)
    ppermute x55, waiting for transfers between devices, flip(): lax.ppermute(w, axis, [(0, 1), (1, 0)])  181 us
    ppermute x55, starting transfers between devices, flip(): lax.ppermute(w, axis, [(0, 1), (1, 0)])  49.2 us
    pallas_call x1, Pallas kernels, attention(): call(attention_kernel, (2, 2, length // BLK), [part(0), whole(2), whole(4...  35.1 us
    pallas_call x2, Pallas kernels, pull_product(): call(pull_kernel, (steps,), [*[half_rows(2 * HD)] * 3, half_rows(UNITS),...  30.1 us
    pallas_call x1, Pallas kernels, hidden_products(): call(functools.partial(hidden_kernel, tall - BLK), (n // BLK,), [rows_of(...  28.3 us
    pallas_call x2, Pallas kernels, rows_grad(): call(functools.partial(rows_grad_kernel, len(rights)), (2 * len(order),),...  27.4 us
    unnamed x156, local copies, waits for them, and re-layouts  24.9 us
    all_to_all x6, starting transfers between devices, swap(): return queue('swap', v, lambda w: lax.all_to_all(w, axes, 0, 0, tiled=True))  22.1 us
  transfers between devices with their start and end apart: 61, of which 20 were waited for; matrix products, arithmetic and copies ran while one was open for 18% of the time, Pallas kernels for 22%

profile of v2, /device:TPU:0, one launch (start us, length us, event | category | flops | bytes accessed | tf_op | source)
XLA Modules:
  0.0 595.3 jit_solution(10048309555569360679)
XLA Ops:
  1.2 2.6 collective-permute-start
  9.1 3.5 all-to-all-start
  16.0 2.0 slice.238
  18.1 2.7 collective-permute-start.7
  24.2 26.7 %collective-permute-done.7 = bf16[160,2048]{1,0:T(8,128)(2,1)} collective-permute-done((bf16[160,2048]{1,0:T(8,128)(2,1)}, bf16[160,2048]{1,0:T(8,128)(2,1)}, u32[]{:S(2)}, u32[]{:S(2)}) %collective-permute-start.7) | collective-permute-done | bytes 655392 | tf_op jit(solution)/shard_map/ppermute | solution.py:48
  50.9 3.4 collective-permute-start.8
  59.0 3.6 all-to-all-start.1
  62.6 2.3 constant_dynamic-update-slice_fusion.3
  66.9 16.0 %collective-permute-done.8 = bf16[160,2048]{1,0:T(8,128)(2,1)} collective-permute-done((bf16[160,2048]{1,0:T(8,128)(2,1)}, bf16[160,2048]{1,0:T(8,128)(2,1)}, u32[]{:S(2)}, u32[]{:S(2)}) %collective-permute-start.8) | collective-permute-done | bytes 655392 | tf_op jit(solution)/shard_map/ppermute | solution.py:48
  83.0 2.0 constant_dynamic-update-slice_fusion.10.b2
  84.9 3.0 collective-permute-done.2
  88.5 3.6 pad_maximum_fusion.near.tokens
  93.6 2.3 constant_dynamic-update-slice_fusion.9
  95.9 2.3 constant_dynamic-update-slice_fusion.2
  98.3 3.0 collective-permute-start.10
  102.4 11.7 %collective-permute-done.9 = bf16[256,2048]{1,0:T(8,128)(2,1)} collective-permute-done((bf16[256,2048]{1,0:T(8,128)(2,1)}, bf16[256,2048]{1,0:T(8,128)(2,1)}, u32[]{:S(2)}, u32[]{:S(2)}) %collective-permute-start.9) | collective-permute-done | bytes 1048608 | tf_op jit(solution)/shard_map/ppermute | solution.py:48
  114.9 4.4 all-to-all-start.2
  119.3 2.3 constant_dynamic-update-slice_fusion.far.tokens
  125.4 8.0 %collective-permute-done.11.w2.q2 = bf16[2,256,768]{2,1,0:T(8,128)(2,1)} collective-permute-done((bf16[2,256,768]{2,1,0:T(8,128)(2,1)S(1)}, bf16[2,256,768]{2,1,0:T(8,128)(2,1)}, u32[]{:S(2)}, u32[]{:S(2)}) %collective-permute-start.11) | collective-permute-done | bytes 786464 | tf_op jit(solution)/shard_map/ppermute | solution.py:48
  133.4 16.3 %all-to-all-done.2 = bf16[32,16,256]{2,1,0:T(8,128)(2,1)S(1)} async-done(((bf16[32,16,256]{2,1,0:T(8,128)(2,1)}), bf16[32,16,256]{2,1,0:T(8,128)(2,1)S(1)}, u32[]{:S(2)}, u32[]{:S(2)}) %all-to-all-start.2) | async-done | bytes 262176 | tf_op jit(solution)/shard_map/all_to_all | solution.py:496
  157.9 4.4 fusion.18
  172.9 14.4 %shard_map.265 = (bf16[2048,2048]{1,0:T(8,128)(2,1)}, bf16[2048,2048]{1,0:T(8,128)(2,1)}, f32[2048,1]{1,0:T(8,128)S(1)}, f32[2048,1]{1,0:T(8,128)S(1)}) custom-call(bf16[1024,2048]{1,0:T(8,128)(2,1)} %pad_maximum_fusion.near.tokens, bf16[1024,2048]{1,0:T(8,128)(2,1)} %constant_dynamic-update-slice_fusion.far.tokens, f32[4,2048]{1,0:T(4,128)S(1)} %pad_maximum_fusion.5.gains), custom_call_target="tpu_custom_call" | custom-call | flops 41943040 | bytes 25165824 | tf_op jit(solution)/shard_map/pallas_call | solution.py:119
  190.3 3.4 collective-permute-done.24
  197.2 3.7 pad_maximum_fusion.1.near
  202.2 2.0 copy-done.32
  204.2 7.9 %shard_map.266 = bf16[2048,256]{1,0:T(8,128)(2,1)S(1)} custom-call(bf16[1024,2048]{1,0:T(8,128)(2,1)} %pad_maximum_fusion.1.near, bf16[1024,2048]{1,0:T(8,128)(2,1)} %copy-done.32, bf16[256,2048]{1,0:T(8,128)(2,1)S(1)} %bitcast.156), custom_call_target="tpu_custom_call" | custom-call | flops 2147483648 | bytes 8388608 | tf_op jit(solution)/shard_map/pallas_call | solution.py:158
  213.1 8.1 %collective-permute-done.22.w3.q3 = bf16[2,256,768]{2,1,0:T(8,128)(2,1)S(1)} collective-permute-done((bf16[2,256,768]{2,1,0:T(8,128)(2,1)}, bf16[2,256,768]{2,1,0:T(8,128)(2,1)S(1)}, u32[]{:S(2)}, u32[]{:S(2)}) %collective-permute-start.22) | collective-permute-done | bytes 786464 | tf_op jit(solution)/shard_map/ppermute | solution.py:48
  221.2 12.4 %shard_map.267 = f32[2048,768]{1,0:T(8,128)} custom-call(s32[1]{0:T(128)} %bitcast.1.base, bf16[2048,2048]{1,0:T(8,128)(2,1)} %get-tuple-element.139.v, bf16[2,256,768]{2,1,0:T(8,128)(2,1)S(1)} %bitcast.168, bf16[2,256,768]{2,1,0:T(8,128)(2,1)S(1)} %copy-done.22, bf16[2,256,768]{2,1,0:T(8,128)(2,1)} %collective-permute-done.11.w2.q2, ...), custom_call_target="tpu_custom_call" | custom-call | flops 6442450944 | bytes 17825792 | tf_op jit(solution)/shard_map/pallas_call | solution.py:141
  233.6 35.1 %shard_map.268 = (bf16[2,2,512,256]{3,2,1,0:T(8,128)(2,1)S(1)}, bf16[2,2,512,256]{3,2,1,0:T(8,128)(2,1)S(1)}, bf16[2,2,512,256]{3,2,1,0:T(8,128)(2,1)S(1)}, bf16[2,2,512,256]{3,2,1,0:T(8,128)(2,1)}) custom-call(f32[2,2,512,768]{3,2,1,0:T(8,128)} %bitcast.211, f32[2,2,512,768]{3,2,1,0:T(8,128)} %bitcast.212, f32[2,2,512,768]{3,2,1,0:T(8,128)} %bitcast.213, ...), custom_call_target="tpu_custom_call" | custom-call | flops 7516192768 | bytes 12582912 | tf_op jit(solution)/shard_map/pallas_call | solution.py:402
  271.0 3.5 fusion
  274.4 8.2 %collective-permute-done.25 = bf16[1,256,1024]{2,1,0:T(8,128)(2,1)S(1)} collective-permute-done((bf16[1,256,1024]{2,1,0:T(8,128)(2,1)}, bf16[1,256,1024]{2,1,0:T(8,128)(2,1)S(1)}, u32[]{:S(2)}, u32[]{:S(2)}) %collective-permute-start.25) | collective-permute-done | bytes 524320 | tf_op jit(solution)/shard_map/ppermute | solution.py:48
  283.4 12.3 %shard_map.269 = (bf16[512,768]{1,0:T(8,128)(2,1)S(1)}, bf16[512,768]{1,0:T(8,128)(2,1)}, bf16[512,768]{1,0:T(8,128)(2,1)S(1)}, bf16[512,768]{1,0:T(8,128)(2,1)S(1)}) custom-call(s32[1]{0:T(128)} %bitcast.1.base, bf16[2048,2048]{1,0:T(8,128)(2,1)} %get-tuple-element.139.v, bf16[2048,256]{1,0:T(8,128)(2,1)} %bitcast.182, bf16[2048,256]{1,0:T(8,128)(2,1)} %bitcast.185, ...), custom_call_target="tpu_custom_call" | custom-call | flops 6442450944 | bytes 11534336 | tf_op jit(solution)/shard_map/pallas_call | solution.py:309
  299.1 28.3 %shard_map.270 = (bf16[2048,1024]{1,0:T(8,128)(2,1)}, bf16[2048,1024]{1,0:T(8,128)(2,1)}, f32[1,1024]{1,0:T(1,128)S(1)}) custom-call(s32[1]{0:T(128)} %bitcast.1.base, bf16[2048,2048]{1,0:T(8,128)(2,1)} %get-tuple-element.144.v, bf16[1024,2048]{1,0:T(8,128)(2,1)} %pad_maximum_fusion.1.near, bf16[1024,2048]{1,0:T(8,128)(2,1)} %copy-done.32, ...), custom_call_target="tpu_custom_call" | custom-call | flops 17179869184 | bytes 33554432 | tf_op jit(solution)/shard_map/pallas_call | solution.py:195
  328.5 15.1 %shard_map.271 = (bf16[512,1024]{1,0:T(8,128)(2,1)}, bf16[512,1024]{1,0:T(8,128)(2,1)}, bf16[512,1024]{1,0:T(8,128)(2,1)S(1)}, bf16[512,1024]{1,0:T(8,128)(2,1)}) custom-call(s32[1]{0:T(128)} %bitcast.1.base, bf16[2048,2048]{1,0:T(8,128)(2,1)} %get-tuple-element.144.v, bf16[2048,1024]{1,0:T(8,128)(2,1)} %get-tuple-element.172.refs_0_.du), custom_call_target="tpu_custom_call" | custom-call | flops 8589934592 | bytes 12582912 | tf_op jit(solution)/shard_map/pallas_call | solution.py:309
  345.3 15.0 %shard_map.272 = (bf16[256,2048]{1,0:T(8,128)(2,1)S(1)}, bf16[256,2048]{1,0:T(8,128)(2,1)S(1)}, bf16[256,2048]{1,0:T(8,128)(2,1)S(1)}, bf16[256,2048]{1,0:T(8,128)(2,1)}) custom-call(s32[1]{0:T(128)} %bitcast.1.base, bf16[2048,1024]{1,0:T(8,128)(2,1)} %get-tuple-element.162.v.active, bf16[1024,2048]{1,0:T(8,128)(2,1)} %pad_maximum_fusion.1.near, ...), custom_call_target="tpu_custom_call" | custom-call | flops 8589934592 | bytes 16777216 | tf_op jit(solution)/shard_map/pallas_call | solution.py:337
  360.3 7.0 %collective-permute-done.28 = bf16[512,1024]{1,0:T(8,128)(2,1)} collective-permute-done((bf16[512,1024]{1,0:T(8,128)(2,1)}, bf16[512,1024]{1,0:T(8,128)(2,1)}, u32[]{:S(2)}, u32[]{:S(2)}) %collective-permute-start.28) | collective-permute-done | bytes 1048608 | tf_op jit(solution)/shard_map/ppermute | solution.py:48
  370.6 8.7 %collective-permute-done.29 = bf16[512,768]{1,0:T(8,128)(2,1)S(1)} collective-permute-done((bf16[512,768]{1,0:T(8,128)(2,1)}, bf16[512,768]{1,0:T(8,128)(2,1)S(1)}, u32[]{:S(2)}, u32[]{:S(2)}) %collective-permute-start.29) | collective-permute-done | bytes 786464 | tf_op jit(solution)/shard_map/ppermute | solution.py:48
  379.3 15.2 %shard_map.273 = (bf16[1024,2048]{1,0:T(8,128)(2,1)}, f32[4,2048]{1,0:T(4,128)S(1)}, f32[1,768]{1,0:T(1,128)S(1)}) custom-call(s32[1]{0:T(128)} %bitcast.1.base, bf16[2048,256]{1,0:T(8,128)(2,1)} %bitcast.183, bf16[2048,256]{1,0:T(8,128)(2,1)} %bitcast.186, bf16[2048,256]{1,0:T(8,128)(2,1)} %bitcast.215, bf16[2048,1024]{1,0:T(8,128)(2,1)} %get-tuple-element.172.refs_0_.du, ...), custom_call_target="tpu_custom_call" | custom-call | flops 7516192768 | bytes 19922944 | tf_op jit(solution)/shard_map/pallas_call | solution.py:262
  394.5 4.3 fusion.22
  399.3 15.0 %shard_map.274 = (bf16[1024,2048]{1,0:T(8,128)(2,1)}, f32[4,2048]{1,0:T(4,128)S(1)}, f32[1,768]{1,0:T(1,128)S(1)}) custom-call(s32[1]{0:T(128)} %bitcast.1.base, bf16[2048,256]{1,0:T(8,128)(2,1)} %bitcast.184, bf16[2048,256]{1,0:T(8,128)(2,1)} %bitcast.187, bf16[2048,256]{1,0:T(8,128)(2,1)} %bitcast.216, bf16[2048,1024]{1,0:T(8,128)(2,1)} %get-tuple-element.172.refs_0_.du, ...), custom_call_target="tpu_custom_call" | custom-call | flops 7516192768 | bytes 19922944 | tf_op jit(solution)/shard_map/pallas_call | solution.py:262
  414.9 2.6 collective-permute-start.31
  417.9 9.9 %shard_map.275 = bf16[1024,2048]{1,0:T(8,128)(2,1)} custom-call(s32[1]{0:T(128)} %bitcast.1.base, bf16[2048,256]{1,0:T(8,128)(2,1)S(1)} %bitcast.164, bf16[2048,1024]{1,0:T(8,128)(2,1)} %get-tuple-element.162.v.active, bf16[256,2048]{1,0:T(8,128)(2,1)S(1)} %bitcast.157, bf16[320,2048]{1,0:T(8,128)(2,1)} %constant_dynamic-update-slice_fusion.4.b0, ...), custom_call_target="tpu_custom_call" | custom-call | flops 5368709120 | bytes 10485760 | tf_op jit(solution)/shard_map/pallas_call | solution.py:219
  427.8 4.4 fusion.23
  433.5 2.9 add_convert_fusion.3
  436.4 4.7 collective-permute-done.31
  445.1 10.3 %shard_map.276 = bf16[1024,2048]{1,0:T(8,128)(2,1)} custom-call(s32[1]{0:T(128)} %bitcast.1.base, bf16[2048,256]{1,0:T(8,128)(2,1)S(1)} %bitcast.165, bf16[2048,1024]{1,0:T(8,128)(2,1)} %get-tuple-element.162.v.active, bf16[256,2048]{1,0:T(8,128)(2,1)S(1)} %bitcast.158, bf16[320,2048]{1,0:T(8,128)(2,1)} %constant_dynamic-update-slice_fusion.4.b0, ...), custom_call_target="tpu_custom_call" | custom-call | flops 5368709120 | bytes 10485760 | tf_op jit(solution)/shard_map/pallas_call | solution.py:219
  455.3 13.0 %collective-permute-done.51 = bf16[128,2048]{1,0:T(8,128)(2,1)} collective-permute-done((bf16[128,2048]{1,0:T(8,128)(2,1)}, bf16[128,2048]{1,0:T(8,128)(2,1)}, u32[]{:S(2)}, u32[]{:S(2)}) %collective-permute-start.51) | collective-permute-done | bytes 524320 | tf_op jit(solution)/shard_map/ppermute | solution.py:48
  469.7 2.5 add_convert_fusion.9
  472.2 3.5 all-to-all-start.4
  476.2 3.1 add_convert_fusion.1
  481.1 2.9 add_convert_fusion.5
  486.1 8.2 %collective-permute-done.49 = bf16[512,1024]{1,0:T(8,128)(2,1)} collective-permute-done((bf16[512,1024]{1,0:T(8,128)(2,1)}, bf16[512,1024]{1,0:T(8,128)(2,1)}, u32[]{:S(2)}, u32[]{:S(2)}) %collective-permute-start.49) | collective-permute-done | bytes 1048608 | tf_op jit(solution)/shard_map/ppermute | solution.py:48
  495.6 14.2 %collective-permute-done.40 = bf16[256,2048]{1,0:T(8,128)(2,1)S(1)} collective-permute-done((bf16[256,2048]{1,0:T(8,128)(2,1)S(1)}, bf16[256,2048]{1,0:T(8,128)(2,1)S(1)}, u32[]{:S(2)}, u32[]{:S(2)}) %collective-permute-start.40) | collective-permute-done | bytes 1048608 | tf_op jit(solution)/shard_map/ppermute | solution.py:48
  510.2 3.0 add_convert_fusion
  514.2 2.8 fusion.21
  517.0 3.9 all-to-all-start.5
  522.2 14.9 %collective-permute-done.41 = bf16[256,2048]{1,0:T(8,128)(2,1)} collective-permute-done((bf16[256,2048]{1,0:T(8,128)(2,1)}, bf16[256,2048]{1,0:T(8,128)(2,1)}, u32[]{:S(2)}, u32[]{:S(2)}) %collective-permute-start.41) | collective-permute-done | bytes 1048608 | tf_op jit(solution)/shard_map/ppermute | solution.py:48
  537.1 3.7 add_convert_fusion.6
  541.0 6.6 %collective-permute-start.46 = (bf16[256,2048]{1,0:T(8,128)(2,1)S(1)}, bf16[256,2048]{1,0:T(8,128)(2,1)S(1)}, u32[]{:S(2)}, u32[]{:S(2)}) collective-permute-start(bf16[256,2048]{1,0:T(8,128)(2,1)S(1)} %get-tuple-element.189), channel_id=1, source_target_pairs={{0,8},{8,0},{1,9},{9,1},{2,10},{10,2},{3,11},{11,3},{4,12},{12,4},... | collective-permute-start | bytes 3145736 | tf_op jit(solution)/shard_map/ppermute | solution.py:48
  549.9 23.4 %collective-permute-done.53 = bf16[64,2048]{1,0:T(8,128)(2,1)S(1)} collective-permute-done((bf16[64,2048]{1,0:T(8,128)(2,1)S(1)}, bf16[64,2048]{1,0:T(8,128)(2,1)S(1)}, u32[]{:S(2)}, u32[]{:S(2)}) %collective-permute-start.53) | collective-permute-done | bytes 262176 | tf_op jit(solution)/shard_map/ppermute | solution.py:48
  575.5 5.3 convert_reduce_fusion.1
  581.6 3.2 all-to-all-start.3
  584.8 3.5 convert_add_fusion.2
  589.8 2.8 all-to-all-done.3
  (352 shorter events, 87.0 us)
Async XLA Ops:
  0.6 57.8 %collective-permute-start.3 = (bf16[256,2048]{1,0:T(8,128)(2,1)}, bf16[256,2048]{1,0:T(8,128)(2,1)}, u32[]{:S(2)}, u32[]{:S(2)}) collective-permute-start(bf16[256,2048]{1,0:T(8,128)(2,1)} %bitcast.188), channel_id=1, source_target_pairs={{0,1},{1,0},{2,3},{3,2},{4,5},{5,4},{6,7},{7,6},{8,9},{9,8},{10,11... | collective-permute-start | bytes 3145736 | tf_op jit(solution)/shard_map/ppermute | solution.py:48
  1.2 54.8 %collective-permute-start = (bf16[256,2048]{1,0:T(8,128)(2,1)}, bf16[256,2048]{1,0:T(8,128)(2,1)}, u32[]{:S(2)}, u32[]{:S(2)}) collective-permute-start(bf16[256,2048]{1,0:T(8,128)(2,1)} %bitcast.189), channel_id=1, source_target_pairs={{0,2},{2,0},{1,3},{3,1},{4,6},{6,4},{5,7},{7,5},{8,10},{10,8},{9,1... | collective-permute-start | bytes 3145736 | tf_op jit(solution)/shard_map/ppermute | solution.py:48
  3.7 52.2 %collective-permute-start.1 = (bf16[256,2048]{1,0:T(8,128)(2,1)}, bf16[256,2048]{1,0:T(8,128)(2,1)}, u32[]{:S(2)}, u32[]{:S(2)}) collective-permute-start(bf16[256,2048]{1,0:T(8,128)(2,1)} %bitcast.190), channel_id=1, source_target_pairs={{0,8},{8,0},{1,9},{9,1},{2,10},{10,2},{3,11},{11,3},{4,12},{12,4},... | collective-permute-start | bytes 3145736 | tf_op jit(solution)/shard_map/ppermute | solution.py:48
  9.1 49.9 %all-to-all-start = ((bf16[8,64,768]{2,1,0:T(8,128)(2,1)}), bf16[8,64,768]{2,1,0:T(8,128)(2,1)S(1)}, u32[]{:S(2)}, u32[]{:S(2)}) async-start(bf16[8,64,768]{2,1,0:T(8,128)(2,1)} %get-tuple-element.114), calls=%async_computation | async-start | bytes 1572864 | tf_op jit(solution)/shard_map/all_to_all | solution.py:496
  14.5 50.4 %collective-permute-start.12 = (bf16[320,2048]{1,0:T(8,128)(2,1)}, bf16[320,2048]{1,0:T(8,128)(2,1)}, u32[]{:S(2)}, u32[]{:S(2)}) collective-permute-start(bf16[320,2048]{1,0:T(8,128)(2,1)} %constant_dynamic-update-slice_fusion.4.b0), channel_id=1, source_target_pairs={{0,4},{4,0},{1,5},{5,1},{2,6},{6,2},{3,7},{7,3},{8,12},{12,8},{9,1... | collective-permute-start | bytes 3932168 | tf_op jit(solution)/shard_map/ppermute | solution.py:48
  18.1 32.8 %collective-permute-start.7 = (bf16[160,2048]{1,0:T(8,128)(2,1)}, bf16[160,2048]{1,0:T(8,128)(2,1)}, u32[]{:S(2)}, u32[]{:S(2)}) collective-permute-start(bf16[160,2048]{1,0:T(8,128)(2,1)} %slice.238), channel_id=1, source_target_pairs={{0,16},{16,0},{1,17},{17,1},{2,18},{18,2},{3,19},{19,3},{4,20},{20... | collective-permute-start | bytes 1966088 | tf_op jit(solution)/shard_map/ppermute | solution.py:48
  50.9 32.1 %collective-permute-start.8 = (bf16[160,2048]{1,0:T(8,128)(2,1)}, bf16[160,2048]{1,0:T(8,128)(2,1)}, u32[]{:S(2)}, u32[]{:S(2)}) collective-permute-start(bf16[160,2048]{1,0:T(8,128)(2,1)} %slice.181), channel_id=1, source_target_pairs={{0,16},{16,0},{1,17},{17,1},{2,18},{18,2},{3,19},{19,3},{4,20},{20... | collective-permute-start | bytes 1966088 | tf_op jit(solution)/shard_map/ppermute | solution.py:48
  55.9 32.0 %collective-permute-start.2 = (bf16[256,2048]{1,0:T(8,128)(2,1)}, bf16[256,2048]{1,0:T(8,128)(2,1)}, u32[]{:S(2)}, u32[]{:S(2)}) collective-permute-start(bf16[256,2048]{1,0:T(8,128)(2,1)} %collective-permute-done.1), channel_id=1, source_target_pairs={{0,2},{2,0},{1,3},{3,1},{4,6},{6,4},{5,7},{7,5},{8,10},{10,8},{9,1... | collective-permute-start | bytes 3145736 | tf_op jit(solution)/shard_map/ppermute | solution.py:48
  58.5 33.6 %collective-permute-start.16 = (bf16[256,2048]{1,0:T(8,128)(2,1)}, bf16[256,2048]{1,0:T(8,128)(2,1)}, u32[]{:S(2)}, u32[]{:S(2)}) collective-permute-start(bf16[256,2048]{1,0:T(8,128)(2,1)} %bitcast.11), channel_id=1, source_target_pairs={{0,1},{1,0},{2,3},{3,2},{4,5},{5,4},{6,7},{7,6},{8,9},{9,8},{10,11... | collective-permute-start | bytes 3145736 | tf_op jit(solution)/shard_map/ppermute | solution.py:48
  58.5 37.5 %collective-permute-start.4 = (bf16[256,2048]{1,0:T(8,128)(2,1)}, bf16[256,2048]{1,0:T(8,128)(2,1)}, u32[]{:S(2)}, u32[]{:S(2)}) collective-permute-start(bf16[256,2048]{1,0:T(8,128)(2,1)} %collective-permute-done), channel_id=1, source_target_pairs={{0,1},{1,0},{2,3},{3,2},{4,5},{5,4},{6,7},{7,6},{8,9},{9,8},{10,11... | collective-permute-start | bytes 3145736 | tf_op jit(solution)/shard_map/ppermute | solution.py:48
  59.0 162.2 %copy-start.4 = (bf16[8,64,768]{2,1,0:T(8,128)(2,1)}, bf16[8,64,768]{2,1,0:T(8,128)(2,1)S(1)}, u32[]{:S(2)}) copy-start(bf16[8,64,768]{2,1,0:T(8,128)(2,1)S(1)} %all-to-all-done) | copy-start | bytes 2359300
  59.0 55.1 %all-to-all-start.1 = ((bf16[8,64,1024]{2,1,0:T(8,128)(2,1)}), bf16[8,64,1024]{2,1,0:T(8,128)(2,1)S(1)}, u32[]{:S(2)}, u32[]{:S(2)}) async-start(bf16[8,64,1024]{2,1,0:T(8,128)(2,1)} %get-tuple-element.115), calls=%async_computation.1 | async-start | bytes 2097152 | tf_op jit(solution)/shard_map/all_to_all | solution.py:496
  64.9 33.4 %collective-permute-start.5 = (bf16[256,2048]{1,0:T(8,128)(2,1)}, bf16[256,2048]{1,0:T(8,128)(2,1)S(1)}, u32[]{:S(2)}, u32[]{:S(2)}) collective-permute-start(bf16[256,2048]{1,0:T(8,128)(2,1)} %collective-permute-done.1), channel_id=1, source_target_pairs={{0,1},{1,0},{2,3},{3,2},{4,5},{5,4},{6,7},{7,6},{8,9},{9,8},{10,11... | collective-permute-start | bytes 3145736 | tf_op jit(solution)/shard_map/ppermute | solution.py:48
  88.0 26.1 %collective-permute-start.9 = (bf16[256,2048]{1,0:T(8,128)(2,1)}, bf16[256,2048]{1,0:T(8,128)(2,1)}, u32[]{:S(2)}, u32[]{:S(2)}) collective-permute-start(bf16[256,2048]{1,0:T(8,128)(2,1)} %bitcast.11), channel_id=1, source_target_pairs={{0,2},{2,0},{1,3},{3,1},{4,6},{6,4},{5,7},{7,5},{8,10},{10,8},{9,1... | collective-permute-start | bytes 3145736 | tf_op jit(solution)/shard_map/ppermute | solution.py:48
  88.5 30.7 %collective-permute-start.6 = (bf16[256,2048]{1,0:T(8,128)(2,1)}, bf16[256,2048]{1,0:T(8,128)(2,1)}, u32[]{:S(2)}, u32[]{:S(2)}) collective-permute-start(bf16[256,2048]{1,0:T(8,128)(2,1)} %collective-permute-done.2), channel_id=1, source_target_pairs={{0,1},{1,0},{2,3},{3,2},{4,5},{5,4},{6,7},{7,6},{8,9},{9,8},{10,11... | collective-permute-start | bytes 3145736 | tf_op jit(solution)/shard_map/ppermute | solution.py:48
  92.1 29.5 %collective-permute-start.13 = (bf16[2,256,768]{2,1,0:T(8,128)(2,1)S(1)}, bf16[2,256,768]{2,1,0:T(8,128)(2,1)S(1)}, u32[]{:S(2)}, u32[]{:S(2)}) collective-permute-start(bf16[2,256,768]{2,1,0:T(8,128)(2,1)S(1)} %bitcast.166), channel_id=1, source_target_pairs={{0,4},{4,0},{1,5},{5,1},{2,6},{6,2},{3,7},{7,3},{8,12},{12,8},{9,1... | collective-permute-start | bytes 2359304 | tf_op jit(solution)/shard_map/ppermute | solution.py:48
  95.9 37.5 %collective-permute-start.11 = (bf16[2,256,768]{2,1,0:T(8,128)(2,1)S(1)}, bf16[2,256,768]{2,1,0:T(8,128)(2,1)}, u32[]{:S(2)}, u32[]{:S(2)}) collective-permute-start(bf16[2,256,768]{2,1,0:T(8,128)(2,1)S(1)} %bitcast.167), channel_id=1, source_target_pairs={{0,16},{16,0},{1,17},{17,1},{2,18},{18,2},{3,19},{19,3},{4,20},{20... | collective-permute-start | bytes 2359304 | tf_op jit(solution)/shard_map/ppermute | solution.py:48
  98.3 68.8 %collective-permute-start.10 = (bf16[256,2048]{1,0:T(8,128)(2,1)}, bf16[256,2048]{1,0:T(8,128)(2,1)}, u32[]{:S(2)}, u32[]{:S(2)}) collective-permute-start(bf16[256,2048]{1,0:T(8,128)(2,1)} %bitcast.11), channel_id=1, source_target_pairs={{0,8},{8,0},{1,9},{9,1},{2,10},{10,2},{3,11},{11,3},{4,12},{12,4},... | collective-permute-start | bytes 3145736 | tf_op jit(solution)/shard_map/ppermute | solution.py:48
  114.1 74.8 %collective-permute-start.17 = (bf16[256,2048]{1,0:T(8,128)(2,1)}, bf16[256,2048]{1,0:T(8,128)(2,1)}, u32[]{:S(2)}, u32[]{:S(2)}) collective-permute-start(bf16[256,2048]{1,0:T(8,128)(2,1)} %collective-permute-done.9), channel_id=1, source_target_pairs={{0,1},{1,0},{2,3},{3,2},{4,5},{5,4},{6,7},{7,6},{8,9},{9,8},{10,11... | collective-permute-start | bytes 3145736 | tf_op jit(solution)/shard_map/ppermute | solution.py:48
  114.1 184.0 %copy-start = (bf16[8,64,1024]{2,1,0:T(8,128)(2,1)}, bf16[8,64,1024]{2,1,0:T(8,128)(2,1)S(1)}, u32[]{:S(2)}) copy-start(bf16[8,64,1024]{2,1,0:T(8,128)(2,1)S(1)} %all-to-all-done.1) | copy-start | bytes 3145732
  114.9 34.8 %all-to-all-start.2 = ((bf16[32,16,256]{2,1,0:T(8,128)(2,1)}), bf16[32,16,256]{2,1,0:T(8,128)(2,1)S(1)}, u32[]{:S(2)}, u32[]{:S(2)}) async-start(bf16[32,16,256]{2,1,0:T(8,128)(2,1)} %bitcast.10), calls=%async_computation.2 | async-start | bytes 524288 | tf_op jit(solution)/shard_map/all_to_all | solution.py:496
  122.4 41.8 %collective-permute-start.14 = (bf16[2,256,1024]{2,1,0:T(8,128)(2,1)S(1)}, bf16[2,256,1024]{2,1,0:T(8,128)(2,1)S(1)}, u32[]{:S(2)}, u32[]{:S(2)}) collective-permute-start(bf16[2,256,1024]{2,1,0:T(8,128)(2,1)S(1)} %bitcast.159), channel_id=1, source_target_pairs={{0,4},{4,0},{1,5},{5,1},{2,6},{6,2},{3,7},{7,3},{8,12},{12,8},{9,1... | collective-permute-start | bytes 3145736 | tf_op jit(solution)/shard_map/ppermute | solution.py:48
  133.4 35.5 %collective-permute-start.23 = (bf16[1,256,1024]{2,1,0:T(8,128)(2,1)}, bf16[1,256,1024]{2,1,0:T(8,128)(2,1)}, u32[]{:S(2)}, u32[]{:S(2)}) collective-permute-start(bf16[1,256,1024]{2,1,0:T(8,128)(2,1)} %bitcast.46), channel_id=1, source_target_pairs={{0,16},{16,0},{1,17},{17,1},{2,18},{18,2},{3,19},{19,3},{4,20},{20... | collective-permute-start | bytes 1572872 | tf_op jit(solution)/shard_map/ppermute | solution.py:48
  164.3 31.3 %collective-permute-start.20 = (bf16[320,2048]{1,0:T(8,128)(2,1)}, bf16[320,2048]{1,0:T(8,128)(2,1)}, u32[]{:S(2)}, u32[]{:S(2)}) collective-permute-start(bf16[320,2048]{1,0:T(8,128)(2,1)} %constant_dynamic-update-slice_fusion.10.b2), channel_id=1, source_target_pairs={{0,4},{4,0},{1,5},{5,1},{2,6},{6,2},{3,7},{7,3},{8,12},{12,8},{9,1... | collective-permute-start | bytes 3932168 | tf_op jit(solution)/shard_map/ppermute | solution.py:48
  167.0 27.8 %collective-permute-start.15 = (bf16[256,2048]{1,0:T(8,128)(2,1)}, bf16[256,2048]{1,0:T(8,128)(2,1)}, u32[]{:S(2)}, u32[]{:S(2)}) collective-permute-start(bf16[256,2048]{1,0:T(8,128)(2,1)} %collective-permute-done.10), channel_id=1, source_target_pairs={{0,2},{2,0},{1,3},{3,1},{4,6},{6,4},{5,7},{7,5},{8,10},{10,8},{9,1... | collective-permute-start | bytes 3145736 | tf_op jit(solution)/shard_map/ppermute | solution.py:48
  168.9 24.8 %collective-permute-start.24 = (bf16[1,256,1024]{2,1,0:T(8,128)(2,1)}, bf16[1,256,1024]{2,1,0:T(8,128)(2,1)}, u32[]{:S(2)}, u32[]{:S(2)}) collective-permute-start(bf16[1,256,1024]{2,1,0:T(8,128)(2,1)} %bitcast.47), channel_id=1, source_target_pairs={{0,16},{16,0},{1,17},{17,1},{2,18},{18,2},{3,19},{19,3},{4,20},{20... | collective-permute-start | bytes 1572872 | tf_op jit(solution)/shard_map/ppermute | solution.py:48
  190.2 10.7 %collective-permute-start.18 = (bf16[256,2048]{1,0:T(8,128)(2,1)}, bf16[256,2048]{1,0:T(8,128)(2,1)S(1)}, u32[]{:S(2)}, u32[]{:S(2)}) collective-permute-start(bf16[256,2048]{1,0:T(8,128)(2,1)} %collective-permute-done.10), channel_id=1, source_target_pairs={{0,1},{1,0},{2,3},{3,2},{4,5},{5,4},{6,7},{7,6},{8,9},{9,8},{10,11... | collective-permute-start | bytes 3145736 | tf_op jit(solution)/shard_map/ppermute | solution.py:48
  194.8 103.3 %copy-start.8 = (bf16[2,256,1024]{2,1,0:T(8,128)(2,1)}, bf16[2,256,1024]{2,1,0:T(8,128)(2,1)S(1)}, u32[]{:S(2)}) copy-start(bf16[2,256,1024]{2,1,0:T(8,128)(2,1)S(1)} %constant_dynamic-update-slice_fusion.14.w2) | copy-start | bytes 3145732
  194.8 7.2 %collective-permute-start.19 = (bf16[256,2048]{1,0:T(8,128)(2,1)}, bf16[256,2048]{1,0:T(8,128)(2,1)S(1)}, u32[]{:S(2)}, u32[]{:S(2)}) collective-permute-start(bf16[256,2048]{1,0:T(8,128)(2,1)} %collective-permute-done.15), channel_id=1, source_target_pairs={{0,1},{1,0},{2,3},{3,2},{4,5},{5,4},{6,7},{7,6},{8,9},{9,8},{10,11... | collective-permute-start | bytes 3145736 | tf_op jit(solution)/shard_map/ppermute | solution.py:48
  197.1 4.7 collective-permute-start.21
  201.0 20.2 %collective-permute-start.22 = (bf16[2,256,768]{2,1,0:T(8,128)(2,1)}, bf16[2,256,768]{2,1,0:T(8,128)(2,1)S(1)}, u32[]{:S(2)}, u32[]{:S(2)}) collective-permute-start(bf16[2,256,768]{2,1,0:T(8,128)(2,1)} %collective-permute-done.11.w2.q2), channel_id=1, source_target_pairs={{0,4},{4,0},{1,5},{5,1},{2,6},{6,2},{3,7},{7,3},{8,12},{12,8},{9,1... | collective-permute-start | bytes 2359304 | tf_op jit(solution)/shard_map/ppermute | solution.py:48
  268.9 13.8 %collective-permute-start.25 = (bf16[1,256,1024]{2,1,0:T(8,128)(2,1)}, bf16[1,256,1024]{2,1,0:T(8,128)(2,1)S(1)}, u32[]{:S(2)}, u32[]{:S(2)}) collective-permute-start(bf16[1,256,1024]{2,1,0:T(8,128)(2,1)} %collective-permute-done.23), channel_id=1, source_target_pairs={{0,4},{4,0},{1,5},{5,1},{2,6},{6,2},{3,7},{7,3},{8,12},{12,8},{9,1... | collective-permute-start | bytes 1572872 | tf_op jit(solution)/shard_map/ppermute | solution.py:48
  282.7 14.0 %collective-permute-start.26 = (bf16[1,256,1024]{2,1,0:T(8,128)(2,1)}, bf16[1,256,1024]{2,1,0:T(8,128)(2,1)S(1)}, u32[]{:S(2)}, u32[]{:S(2)}) collective-permute-start(bf16[1,256,1024]{2,1,0:T(8,128)(2,1)} %collective-permute-done.24), channel_id=1, source_target_pairs={{0,4},{4,0},{1,5},{5,1},{2,6},{6,2},{3,7},{7,3},{8,12},{12,8},{9,1... | collective-permute-start | bytes 1572872 | tf_op jit(solution)/shard_map/ppermute | solution.py:48
  296.7 30.7 %collective-permute-start.27 = (bf16[512,768]{1,0:T(8,128)(2,1)S(1)}, bf16[512,768]{1,0:T(8,128)(2,1)S(1)}, u32[]{:S(2)}, u32[]{:S(2)}) collective-permute-start(bf16[512,768]{1,0:T(8,128)(2,1)S(1)} %get-tuple-element.151), channel_id=1, source_target_pairs={{0,4},{4,0},{1,5},{5,1},{2,6},{6,2},{3,7},{7,3},{8,12},{12,8},{9,1... | collective-permute-start | bytes 2359304 | tf_op jit(solution)/shard_map/ppermute | solution.py:48
  343.6 23.6 %collective-permute-start.28 = (bf16[512,1024]{1,0:T(8,128)(2,1)}, bf16[512,1024]{1,0:T(8,128)(2,1)}, u32[]{:S(2)}, u32[]{:S(2)}) collective-permute-start(bf16[512,1024]{1,0:T(8,128)(2,1)} %get-tuple-element.157), channel_id=1, source_target_pairs={{0,4},{4,0},{1,5},{5,1},{2,6},{6,2},{3,7},{7,3},{8,12},{12,8},{9,1... | collective-permute-start | bytes 3145736 | tf_op jit(solution)/shard_map/ppermute | solution.py:48
  345.2 34.0 %collective-permute-start.29 = (bf16[512,768]{1,0:T(8,128)(2,1)}, bf16[512,768]{1,0:T(8,128)(2,1)S(1)}, u32[]{:S(2)}, u32[]{:S(2)}) collective-permute-start(bf16[512,768]{1,0:T(8,128)(2,1)} %add_convert_fusion.10), channel_id=1, source_target_pairs={{0,16},{16,0},{1,17},{17,1},{2,18},{18,2},{3,19},{19,3},{4,20},{20... | collective-permute-start | bytes 2359304 | tf_op jit(solution)/shard_map/ppermute | solution.py:48
  367.3 47.6 %collective-permute-start.32 = (bf16[256,2048]{1,0:T(8,128)(2,1)S(1)}, bf16[256,2048]{1,0:T(8,128)(2,1)S(1)}, u32[]{:S(2)}, u32[]{:S(2)}) collective-permute-start(bf16[256,2048]{1,0:T(8,128)(2,1)S(1)} %get-tuple-element.165), channel_id=1, source_target_pairs={{0,4},{4,0},{1,5},{5,1},{2,6},{6,2},{3,7},{7,3},{8,12},{12,8},{9,1... | collective-permute-start | bytes 3145736 | tf_op jit(solution)/shard_map/ppermute | solution.py:48
  379.2 35.1 %collective-permute-start.30 = (bf16[256,1024]{1,0:T(8,128)(2,1)S(1)}, bf16[256,1024]{1,0:T(8,128)(2,1)S(1)}, u32[]{:S(2)}, u32[]{:S(2)}) collective-permute-start(bf16[256,1024]{1,0:T(8,128)(2,1)S(1)} %get-tuple-element.159), channel_id=1, source_target_pairs={{0,16},{16,0},{1,17},{17,1},{2,18},{18,2},{3,19},{19,3},{4,20},{20... | collective-permute-start | bytes 1572872 | tf_op jit(solution)/shard_map/ppermute | solution.py:48
  398.8 33.4 %collective-permute-start.37 = (bf16[256,2048]{1,0:T(8,128)(2,1)}, bf16[256,2048]{1,0:T(8,128)(2,1)}, u32[]{:S(2)}, u32[]{:S(2)}) collective-permute-start(bf16[256,2048]{1,0:T(8,128)(2,1)} %get-tuple-element.180), channel_id=1, source_target_pairs={{0,1},{1,0},{2,3},{3,2},{4,5},{5,4},{6,7},{7,6},{8,9},{9,8},{10,11... | collective-permute-start | bytes 3145736 | tf_op jit(solution)/shard_map/ppermute | solution.py:48
  398.8 37.6 %collective-permute-start.33 = (bf16[256,2048]{1,0:T(8,128)(2,1)}, bf16[256,2048]{1,0:T(8,128)(2,1)S(1)}, u32[]{:S(2)}, u32[]{:S(2)}) collective-permute-start(bf16[256,2048]{1,0:T(8,128)(2,1)} %get-tuple-element.176), channel_id=1, source_target_pairs={{0,1},{1,0},{2,3},{3,2},{4,5},{5,4},{6,7},{7,6},{8,9},{9,8},{10,11... | collective-permute-start | bytes 3145736 | tf_op jit(solution)/shard_map/ppermute | solution.py:48
  399.3 44.3 %collective-permute-start.43 = (bf16[256,2048]{1,0:T(8,128)(2,1)}, bf16[256,2048]{1,0:T(8,128)(2,1)S(1)}, u32[]{:S(2)}, u32[]{:S(2)}) collective-permute-start(bf16[256,2048]{1,0:T(8,128)(2,1)} %get-tuple-element.186), channel_id=1, source_target_pairs={{0,1},{1,0},{2,3},{3,2},{4,5},{5,4},{6,7},{7,6},{8,9},{9,8},{10,11... | collective-permute-start | bytes 3145736 | tf_op jit(solution)/shard_map/ppermute | solution.py:48
  414.3 30.7 %collective-permute-start.35 = (bf16[256,2048]{1,0:T(8,128)(2,1)}, bf16[256,2048]{1,0:T(8,128)(2,1)}, u32[]{:S(2)}, u32[]{:S(2)}) collective-permute-start(bf16[256,2048]{1,0:T(8,128)(2,1)} %get-tuple-element.178), channel_id=1, source_target_pairs={{0,1},{1,0},{2,3},{3,2},{4,5},{5,4},{6,7},{7,6},{8,9},{9,8},{10,11... | collective-permute-start | bytes 3145736 | tf_op jit(solution)/shard_map/ppermute | solution.py:48
  414.9 26.3 %collective-permute-start.31 = (bf16[256,1024]{1,0:T(8,128)(2,1)}, bf16[256,1024]{1,0:T(8,128)(2,1)S(1)}, u32[]{:S(2)}, u32[]{:S(2)}) collective-permute-start(bf16[256,1024]{1,0:T(8,128)(2,1)} %get-tuple-element.160), channel_id=1, source_target_pairs={{0,16},{16,0},{1,17},{17,1},{2,18},{18,2},{3,19},{19,3},{4,20},{20... | collective-permute-start | bytes 1572872 | tf_op jit(solution)/shard_map/ppermute | solution.py:48
  432.2 36.2 %collective-permute-start.47 = (bf16[512,768]{1,0:T(8,128)(2,1)}, bf16[512,768]{1,0:T(8,128)(2,1)}, u32[]{:S(2)}, u32[]{:S(2)}) collective-permute-start(bf16[512,768]{1,0:T(8,128)(2,1)} %get-tuple-element.197), channel_id=1, source_target_pairs={{0,4},{4,0},{1,5},{5,1},{2,6},{6,2},{3,7},{7,3},{8,12},{12,8},{9,1... | collective-permute-start | bytes 2359304 | tf_op jit(solution)/shard_map/ppermute | solution.py:48
  436.4 39.4 %collective-permute-start.38 = (bf16[256,2048]{1,0:T(8,128)(2,1)}, bf16[256,2048]{1,0:T(8,128)(2,1)}, u32[]{:S(2)}, u32[]{:S(2)}) collective-permute-start(bf16[256,2048]{1,0:T(8,128)(2,1)} %get-tuple-element.181), channel_id=1, source_target_pairs={{0,1},{1,0},{2,3},{3,2},{4,5},{5,4},{6,7},{7,6},{8,9},{9,8},{10,11... | collective-permute-start | bytes 3145736 | tf_op jit(solution)/shard_map/ppermute | solution.py:48
  441.1 35.1 %collective-permute-start.39 = (bf16[256,2048]{1,0:T(8,128)(2,1)}, bf16[256,2048]{1,0:T(8,128)(2,1)}, u32[]{:S(2)}, u32[]{:S(2)}) collective-permute-start(bf16[256,2048]{1,0:T(8,128)(2,1)} %add_convert_fusion.3), channel_id=1, source_target_pairs={{0,2},{2,0},{1,3},{3,1},{4,6},{6,4},{5,7},{7,5},{8,10},{10,8},{9,1... | collective-permute-start | bytes 3145736 | tf_op jit(solution)/shard_map/ppermute | solution.py:48
  443.6 24.7 %collective-permute-start.51 = (bf16[128,2048]{1,0:T(8,128)(2,1)}, bf16[128,2048]{1,0:T(8,128)(2,1)}, u32[]{:S(2)}, u32[]{:S(2)}) collective-permute-start(bf16[128,2048]{1,0:T(8,128)(2,1)} %get-tuple-element.202), channel_id=1, source_target_pairs={{0,16},{16,0},{1,17},{17,1},{2,18},{18,2},{3,19},{19,3},{4,20},{20... | collective-permute-start | bytes 1572872 | tf_op jit(solution)/shard_map/ppermute | solution.py:48
  445.0 77.2 %collective-permute-start.44 = (bf16[256,2048]{1,0:T(8,128)(2,1)}, bf16[256,2048]{1,0:T(8,128)(2,1)}, u32[]{:S(2)}, u32[]{:S(2)}) collective-permute-start(bf16[256,2048]{1,0:T(8,128)(2,1)} %get-tuple-element.187), channel_id=1, source_target_pairs={{0,1},{1,0},{2,3},{3,2},{4,5},{5,4},{6,7},{7,6},{8,9},{9,8},{10,11... | collective-permute-start | bytes 3145736 | tf_op jit(solution)/shard_map/ppermute | solution.py:48
  468.4 53.9 %collective-permute-start.36 = (bf16[256,2048]{1,0:T(8,128)(2,1)}, bf16[256,2048]{1,0:T(8,128)(2,1)}, u32[]{:S(2)}, u32[]{:S(2)}) collective-permute-start(bf16[256,2048]{1,0:T(8,128)(2,1)} %get-tuple-element.179), channel_id=1, source_target_pairs={{0,1},{1,0},{2,3},{3,2},{4,5},{5,4},{6,7},{7,6},{8,9},{9,8},{10,11... | collective-permute-start | bytes 3145736 | tf_op jit(solution)/shard_map/ppermute | solution.py:48
  468.4 25.9 %collective-permute-start.49 = (bf16[512,1024]{1,0:T(8,128)(2,1)}, bf16[512,1024]{1,0:T(8,128)(2,1)}, u32[]{:S(2)}, u32[]{:S(2)}) collective-permute-start(bf16[512,1024]{1,0:T(8,128)(2,1)} %get-tuple-element.200), channel_id=1, source_target_pairs={{0,4},{4,0},{1,5},{5,1},{2,6},{6,2},{3,7},{7,3},{8,12},{12,8},{9,1... | collective-permute-start | bytes 3145736 | tf_op jit(solution)/shard_map/ppermute | solution.py:48
  472.2 44.7 %all-to-all-start.4 = ((bf16[8,64,768]{2,1,0:T(8,128)(2,1)}), bf16[8,64,768]{2,1,0:T(8,128)(2,1)S(1)}, u32[]{:S(2)}, u32[]{:S(2)}) async-start(bf16[8,64,768]{2,1,0:T(8,128)(2,1)} %bitcast.54), calls=%async_computation.4 | async-start | bytes 1572864 | tf_op jit(solution)/shard_map/all_to_all | solution.py:496
  475.8 8.3 %collective-permute-start.48 = (bf16[2,64,2048]{2,1,0:T(8,128)(2,1)S(1)}, bf16[2,64,2048]{2,1,0:T(8,128)(2,1)S(1)}, u32[]{:S(2)}, u32[]{:S(2)}) collective-permute-start(bf16[2,64,2048]{2,1,0:T(8,128)(2,1)S(1)} %copy-done.54), channel_id=1, source_target_pairs={{0,1},{1,0},{2,3},{3,2},{4,5},{5,4},{6,7},{7,6},{8,9},{9,8},{10,11... | collective-permute-start | bytes 1572872 | tf_op jit(solution)/shard_map/ppermute | solution.py:48
  479.4 30.4 %collective-permute-start.40 = (bf16[256,2048]{1,0:T(8,128)(2,1)S(1)}, bf16[256,2048]{1,0:T(8,128)(2,1)S(1)}, u32[]{:S(2)}, u32[]{:S(2)}) collective-permute-start(bf16[256,2048]{1,0:T(8,128)(2,1)S(1)} %get-tuple-element.183), channel_id=1, source_target_pairs={{0,2},{2,0},{1,3},{3,1},{4,6},{6,4},{5,7},{7,5},{8,10},{10,8},{9,1... | collective-permute-start | bytes 3145736 | tf_op jit(solution)/shard_map/ppermute | solution.py:48
  484.0 29.2 %collective-permute-start.45 = (bf16[256,2048]{1,0:T(8,128)(2,1)S(1)}, bf16[256,2048]{1,0:T(8,128)(2,1)S(1)}, u32[]{:S(2)}, u32[]{:S(2)}) collective-permute-start(bf16[256,2048]{1,0:T(8,128)(2,1)S(1)} %get-tuple-element.188), channel_id=1, source_target_pairs={{0,8},{8,0},{1,9},{9,1},{2,10},{10,2},{3,11},{11,3},{4,12},{12,4},... | collective-permute-start | bytes 3145736 | tf_op jit(solution)/shard_map/ppermute | solution.py:48
  494.3 26.6 %collective-permute-start.50 = (bf16[2,64,2048]{2,1,0:T(8,128)(2,1)S(1)}, bf16[2,64,2048]{2,1,0:T(8,128)(2,1)}, u32[]{:S(2)}, u32[]{:S(2)}) collective-permute-start(bf16[2,64,2048]{2,1,0:T(8,128)(2,1)S(1)} %slice_bitcast_fusion.1), channel_id=1, source_target_pairs={{0,4},{4,0},{1,5},{5,1},{2,6},{6,2},{3,7},{7,3},{8,12},{12,8},{9,1... | collective-permute-start | bytes 1572872 | tf_op jit(solution)/shard_map/ppermute | solution.py:48
  509.8 27.3 %collective-permute-start.41 = (bf16[256,2048]{1,0:T(8,128)(2,1)}, bf16[256,2048]{1,0:T(8,128)(2,1)}, u32[]{:S(2)}, u32[]{:S(2)}) collective-permute-start(bf16[256,2048]{1,0:T(8,128)(2,1)} %add_convert_fusion.5), channel_id=1, source_target_pairs={{0,2},{2,0},{1,3},{3,1},{4,6},{6,4},{5,7},{7,5},{8,10},{10,8},{9,1... | collective-permute-start | bytes 3145736 | tf_op jit(solution)/shard_map/ppermute | solution.py:48
  513.2 61.0 %collective-permute-start.34 = (bf16[256,2048]{1,0:T(8,128)(2,1)}, bf16[256,2048]{1,0:T(8,128)(2,1)}, u32[]{:S(2)}, u32[]{:S(2)}) collective-permute-start(bf16[256,2048]{1,0:T(8,128)(2,1)} %get-tuple-element.177), channel_id=1, source_target_pairs={{0,1},{1,0},{2,3},{3,2},{4,5},{5,4},{6,7},{7,6},{8,9},{9,8},{10,11... | collective-permute-start | bytes 3145736 | tf_op jit(solution)/shard_map/ppermute | solution.py:48
  517.0 64.7 %all-to-all-start.5 = ((bf16[8,64,1024]{2,1,0:T(8,128)(2,1)}), bf16[8,64,1024]{2,1,0:T(8,128)(2,1)S(1)}, u32[]{:S(2)}, u32[]{:S(2)}) async-start(bf16[8,64,1024]{2,1,0:T(8,128)(2,1)} %bitcast.195), calls=%async_computation.5 | async-start | bytes 2097152 | tf_op jit(solution)/shard_map/all_to_all | solution.py:496
  520.8 26.8 %collective-permute-start.52 = (bf16[128,2048]{1,0:T(8,128)(2,1)}, bf16[128,2048]{1,0:T(8,128)(2,1)S(1)}, u32[]{:S(2)}, u32[]{:S(2)}) collective-permute-start(bf16[128,2048]{1,0:T(8,128)(2,1)} %get-tuple-element.203), channel_id=1, source_target_pairs={{0,16},{16,0},{1,17},{17,1},{2,18},{18,2},{3,19},{19,3},{4,20},{20... | collective-permute-start | bytes 1572872 | tf_op jit(solution)/shard_map/ppermute | solution.py:48
  540.9 33.4 %collective-permute-start.42 = (bf16[256,2048]{1,0:T(8,128)(2,1)S(1)}, bf16[256,2048]{1,0:T(8,128)(2,1)S(1)}, u32[]{:S(2)}, u32[]{:S(2)}) collective-permute-start(bf16[256,2048]{1,0:T(8,128)(2,1)S(1)} %get-tuple-element.185), channel_id=1, source_target_pairs={{0,2},{2,0},{1,3},{3,1},{4,6},{6,4},{5,7},{7,5},{8,10},{10,8},{9,1... | collective-permute-start | bytes 3145736 | tf_op jit(solution)/shard_map/ppermute | solution.py:48
  541.0 34.5 %collective-permute-start.46 = (bf16[256,2048]{1,0:T(8,128)(2,1)S(1)}, bf16[256,2048]{1,0:T(8,128)(2,1)S(1)}, u32[]{:S(2)}, u32[]{:S(2)}) collective-permute-start(bf16[256,2048]{1,0:T(8,128)(2,1)S(1)} %get-tuple-element.189), channel_id=1, source_target_pairs={{0,8},{8,0},{1,9},{9,1},{2,10},{10,2},{3,11},{11,3},{4,12},{12,4},... | collective-permute-start | bytes 3145736 | tf_op jit(solution)/shard_map/ppermute | solution.py:48
  547.7 25.7 %collective-permute-start.53 = (bf16[64,2048]{1,0:T(8,128)(2,1)S(1)}, bf16[64,2048]{1,0:T(8,128)(2,1)S(1)}, u32[]{:S(2)}, u32[]{:S(2)}) collective-permute-start(bf16[64,2048]{1,0:T(8,128)(2,1)S(1)} %fusion.19), channel_id=1, source_target_pairs={{0,16},{16,0},{1,17},{17,1},{2,18},{18,2},{3,19},{19,3},{4,20},{20... | collective-permute-start | bytes 786440 | tf_op jit(solution)/shard_map/ppermute | solution.py:48
  549.2 35.6 %collective-permute-start.54 = (bf16[256,2048]{1,0:T(8,128)(2,1)S(1)}, bf16[256,2048]{1,0:T(8,128)(2,1)}, u32[]{:S(2)}, u32[]{:S(2)}) collective-permute-start(bf16[256,2048]{1,0:T(8,128)(2,1)S(1)} %copy-done.16), channel_id=1, source_target_pairs={{0,4},{4,0},{1,5},{5,1},{2,6},{6,2},{3,7},{7,3},{8,12},{12,8},{9,1... | collective-permute-start | bytes 3145736 | tf_op jit(solution)/shard_map/ppermute | solution.py:48
  581.6 11.0 %all-to-all-start.3 = ((f32[32,1,768]{2,1,0:T(1,128)}), f32[32,1,768]{2,1,0:T(1,128)S(1)}, u32[]{:S(2)}, u32[]{:S(2)}) async-start(f32[32,1,768]{2,1,0:T(1,128)} %copy.89), calls=%async_computation.3 | async-start | bytes 196608 | tf_op jit(solution)/shard_map/all_to_all | solution.py:496
  (65 other events, 729.7 us)

commit v3 on v2

--- a/solution.py
+++ b/solution.py
@@ -26,26 +26,62 @@
 COST = 1.0
 
 
-LINE = {}
-DEPTH = {"core": 4}
+CFG = {
+    "swap": ["sw", "st", "ss", "gw", "gt", "gs"],
+    "kernel": ["deal", "norms", "joined", "dO", "A", "W", "H", "T", "Pf", "Pn", "B", "Of", "On"],
+    "x": ["ix", "ib", "ux", "ub", "p3", "p1", "o3", "o1"],
+    "zl": ["iz", "uz", "pz", "oz"],
+    "core": ["i0", "i1", "i2", "i3", "u0", "u1", "u2", "u3", "dc", "gd", "pc3", "pc1", "pc2", "pc0", "oc3", "oc1", "oc2", "oc0"],
+    "y": ["An", "Wn", "Af0", "Wf", "Af1", "W3", "T3", "W1", "D1", "T1"],
+    "zh": ["A0z", "Wz", "A1z", "zW", "zT0", "zT1", "zD"],
+    "sc": ["Tg", "Br"],
+    "depth": {"core": 3},
+    "ties": {
+        "T": ["W3"],
+        "Pn": ["zW", "T3"],
+        "B": ["zT0"],
+        "o1": ["zT1", "T1"],
+        "oz": ["gt"],
+    },
+}
 
 
 def after(v, *others):
     return lax.optimization_barrier((v, *others))[0]
 
 
-def queue(channel, v, step):
-    line = LINE.setdefault(channel, [])
-    depth = DEPTH.get(channel, 1)
-    if len(line) >= depth:
-        v = after(v, line[-depth])
-    out = step(v)
-    line.append(out[0] if isinstance(out, (list, tuple)) else out)
-    return out
-
-
-def flip(v, axis, channel=None):
-    return queue(channel or axis, v, lambda w: lax.ppermute(w, axis, [(0, 1), (1, 0)]))
+def flip(v, axis):
+    return lax.ppermute(v, axis, [(0, 1), (1, 0)])
+
+
+def run(tasks, skip=()):
+    channels = ("swap", "kernel", "x", "zl", "core", "y", "zh", "sc")
+    lines = {c: [n for n in CFG[c] if n not in skip] for c in channels}
+    done, at = {}, dict.fromkeys(lines, 0)
+    first = lambda v: v[0] if isinstance(v, (list, tuple)) else v
+    while any(at[c] < len(lines[c]) for c in lines):
+        moved = False
+        for c, names in lines.items():
+            while at[c] < len(names):
+                name = names[at[c]]
+                source, step = tasks[name]
+                waits = [w for w in CFG["ties"].get(name, ()) if w not in skip]
+                place = at[c] - CFG["depth"].get(c, 1)
+                if place >= 0:
+                    waits.append(names[place])
+                if any(w not in done for w in waits):
+                    break
+                try:
+                    v = source(done)
+                    if waits:
+                        v = after(v, *[first(done[w]) for w in waits])
+                    done[name] = step(v, done)
+                except KeyError:
+                    break
+                at[c] += 1
+                moved = True
+        assert moved
+    return done
 
 
 def dot(a, b, ca, cb):
@@ -168,15 +204,15 @@
 
 
 def hidden_kernel(
-    skip, base, v, near, far, w0, w1, w2, w3, b0, b1, b2, b3, shift, active, grad, sums, back
+    skip, base, v, near, far, w, b0, b1, b2, b3, shift, active, grad, sums, back
 ):
     up = pick(near, far)
-    for r, w in enumerate((b0, b1, b2, b3)):
-        back[:, columns(r ^ base[0])] = dot(up, w[skip:], 1, 1)
+    for r, b in enumerate((b0, b1, b2, b3)):
+        back[:, columns(r ^ base[0])] = dot(up, b[skip:], 1, 1)
     u = jnp.zeros((BLK, UNITS), F32) + shift[...]
-    for r, w in enumerate((w0, w1, w2, w3)):
+    for r in range(4):
         for p in range(2):
-            u += dot(v[:, columns(place(base[0], r, p))], w[p], 1, 0)
+            u += dot(v[:, columns(place(base[1], r, p))], w[r, p], 1, 0)
     below = 0.5 * (1.0 + lax.erf(u * (0.5**0.5)))
     active[...] = (u * below).astype(BF)
     slope = below + u * jnp.exp(-0.5 * u * u) * ((2.0 * jnp.pi) ** (-0.5))
@@ -195,14 +231,14 @@
     return call(
         functools.partial(hidden_kernel, tall - BLK),
         (n // BLK,),
-        [rows_of(D), *two_halves(D), *[fixed(2, BLK, UNITS)] * 4, *[fixed(tall, D)] * 4, fixed(1, UNITS)],
+        [rows_of(D), *two_halves(D), fixed(4, 2, BLK, UNITS), *[fixed(tall, D)] * 4, fixed(1, UNITS)],
         [rows_of(UNITS), rows_of(UNITS), fixed(1, UNITS)],
         [shape(n, UNITS), shape(n, UNITS), shape(1, UNITS, dtype=F32)],
         [pltpu.VMEM((BLK, UNITS), F32)],
         flops=4 * n * D * UNITS,
         traffic=n * D * 4 + n * UNITS * 4 + D * UNITS * 4,
         special=2 * n * UNITS,
-    )(base, v, near, far, *pieces, *back_pieces, shift)
+    )(base, v, near, far, pieces, *back_pieces, shift)
 
 
 def out_kernel(skip, base, mixed, active, w, b0, b1, b2, b3, out):
@@ -228,7 +264,7 @@
 
 
 def pull_kernel(
-    base, dq, dk, dv, du, tokens, mean, scale, gains, q0, q1, q2, q3, w0, w1, w2, w3, out, sums, wide
+    base, dq, dk, dv, du, tokens, mean, scale, gains, q0, q1, q2, q3, w, out, sums, wide, held
 ):
     @pl.when(pl.program_id(0) == 0)
     def _():
@@ -238,7 +274,7 @@
     add = lambda v: jnp.sum(v, axis=0, keepdims=True)
     for t, v in enumerate((dq, dk, dv)):
         wide[:, 2 * HD * t : 2 * HD * (t + 1)] += add(v[...].astype(F32))
-    for r, (q, w) in enumerate(((q0, w0), (q1, w1), (q2, w2), (q3, w3))):
+    for r, q in enumerate((q0, q1, q2, q3)):
         for p in range(2):
             at = columns(place(base[0], r, p))
             one = (
@@ -246,13 +282,18 @@
                 + dot(dk[...], q[p, :, 2 * HD : 4 * HD], 1, 1)
                 + dot(dv[...], q[p, :, 4 * HD :], 1, 1)
             )
-            two = dot(du[...], w[p], 1, 1)
             normal = (tokens[:, at].astype(F32) - mean[...]) * scale[...]
             sums[0:1, at] += add(one * normal)
             sums[1:2, at] += add(one)
+            held[:, at] = one * gains[0:1, at]
+    for r in range(4):
+        for p in range(2):
+            at = columns(place(base[1], r, p))
+            two = dot(du[...], w[r, p], 1, 1)
+            normal = (tokens[:, at].astype(F32) - mean[...]) * scale[...]
             sums[2:3, at] += add(two * normal)
             sums[3:4, at] += add(two)
-            out[:, at] = (one * gains[0:1, at] + two * gains[2:3, at]).astype(BF)
+            out[:, at] = (held[:, at] + two * gains[2:3, at]).astype(BF)
 
 
 def pull_product(base, half, grads, du, tokens, mean, scale, gains, joined_pieces, pieces):
@@ -270,13 +311,14 @@
             half_rows(1),
             fixed(4, D),
             *[fixed(2, BLK, WIDE)] * 4,
-            *[fixed(2, BLK, UNITS)] * 4,
+            fixed(4, 2, BLK, UNITS),
         ],
         [rows_of(D), fixed(4, D), fixed(1, WIDE)],
         [shape(n, D), shape(4, D, dtype=F32), shape(1, WIDE, dtype=F32)],
+        [pltpu.VMEM((BLK, D), F32)],
         flops=2 * n * D * (UNITS + WIDE),
         traffic=n * D * 4 + n * UNITS * 4 + D * (UNITS + WIDE) * 2,
-    )(base, *grads, du, tokens, mean, scale, gains, *joined_pieces, *pieces)
+    )(base, *grads, du, tokens, mean, scale, gains, *joined_pieces, pieces)
 
 
 def rows_grad_kernel(count, base, v, *refs):
@@ -317,32 +359,23 @@
     )(base, v, *rights)
 
 
-def units_grad_kernel(base, v, near, far, *outs):
-    step, n = pl.program_id(0), near.shape[0]
-    part = dot(v[:n], near[...], 0, 0) + dot(v[n:], far[...], 0, 0)
-    part = part.astype(BF)
-    for j, out in enumerate(outs):
-
-        @pl.when(step == j)
-        def _(out=out):
-            out[...] = part
-
-
-def units_grad(base, v, near, far, order):
+def units_grad_kernel(v, near, far, out):
+    n = near.shape[0]
+    out[...] = (dot(v[:n], near[...], 0, 0) + dot(v[n:], far[...], 0, 0)).astype(BF)
+
+
+def units_grad(v, near, far):
     n = v.shape[0]
-
-    def chosen(i, b):
-        return (0, sum(jnp.where(i == j, r, 0) for j, r in enumerate(order)) ^ b[0])
-
     return call(
         units_grad_kernel,
-        (len(order),),
-        [pl.BlockSpec((n, BLK), chosen), fixed(n // 2, D), fixed(n // 2, D)],
-        [fixed(BLK, D)] * len(order),
-        [shape(BLK, D)] * len(order),
-        flops=2 * n * BLK * D * len(order),
-        traffic=n * D * 2 + (n + D) * BLK * 2 * len(order),
-    )(base, v, near, far)
+        (UNITS // BLK,),
+        [pl.BlockSpec((n, BLK), lambda i: (0, i)), fixed(n // 2, D), fixed(n // 2, D)],
+        rows_of(D),
+        shape(UNITS, D),
+        flops=2 * n * UNITS * D,
+        traffic=n * D * 2 + (n + D) * UNITS * 2,
+        scalars=0,
+    )(v, near, far)
 
 
 def turn(v, cos, sin):
@@ -493,7 +526,7 @@
 
 
 def swap(v, axes=("zl", "x", "core")):
-    return queue("swap", v, lambda w: lax.all_to_all(w, axes, 0, 0, tiled=True))
+    return lax.all_to_all(v, axes, 0, 0, tiled=True)
 
 
 def gather_plain(v, split):
@@ -523,33 +556,30 @@
     return join
 
 
-def reduce_tokens(near, far, span):
-    block = lambda v, f: v[f * span : (f + 1) * span]
-    got = {f: flip(block(far, f), "core") for f in (3, 1, 2, 0)}
-    total = lambda f: block(near, f).astype(F32) + got[f].astype(F32)
-    away_x = flip(total(3).astype(BF), "x")
-    mine_x = flip(total(1).astype(BF), "x")
-    from_far = flip((total(2) + away_x.astype(F32)).astype(BF), "zl")
-    return total(0) + mine_x.astype(F32) + from_far.astype(F32)
-
-
-def flip_parts(v, axis, parts=2, cut=0):
-    size = v.shape[cut] // parts
-    pieces = [lax.slice_in_dim(v, j * size, (j + 1) * size, axis=cut) for j in range(parts)]
-    return [flip(p, axis) for p in pieces]
-
-
-def dense_rows(pieces):
-    core = lax.axis_index("core")
-    zh, y = lax.axis_index("zh"), lax.axis_index("y")
-    first = core == 0
+def dense_parts(pieces):
+    zh, y, core = (lax.axis_index(a) for a in ("zh", "y", "core"))
     w = jnp.stack(pieces).reshape(2, 2, HD // 2, D)
     w = jnp.where(y == 0, w, w[:, ::-1])
     same = zh == core
-    keep, send = jnp.where(same, w[0], w[1]), jnp.where(same, w[1], w[0])
-    other = flip(send, "core")
+    return jnp.where(same, w[0], w[1]), jnp.where(same, w[1], w[0])
+
+
+def dense_join(keep, other):
+    first = lax.axis_index("core") == 0
     low, high = jnp.where(first, keep, other), jnp.where(first, other, keep)
     return jnp.stack([low, high], axis=1).reshape(2 * HD, D)
+
+
+def dense_split(g):
+    first = lax.axis_index("core") == 0
+    g = g.reshape(2, 2, HD // 2, D)
+    return jnp.where(first, g[:, 0], g[:, 1]), jnp.where(first, g[:, 1], g[:, 0])
+
+
+def dense_sort(keep, other):
+    same = lax.axis_index("zh") == lax.axis_index("core")
+    w = jnp.stack([jnp.where(same, keep, other), jnp.where(same, other, keep)])
+    return jnp.where(lax.axis_index("y") == 0, w, w[:, ::-1])
 
 
 def gather_dense_plain(w):
@@ -559,22 +589,12 @@
     return w.reshape(2 * HD, D)
 
 
-def reduce_dense(g, copies):
+def reduce_dense_plain(g):
     core, x = lax.axis_index("core"), lax.axis_index("x")
-    if copies != 2:
-        w = jnp.zeros((2, 2, 2, HD, D), F32)
-        g = g.astype(F32).reshape(1, 2, 1, HD, D)
-        w = lax.dynamic_update_slice(w, g, (core, 0, x, 0, 0)).reshape(-1, D)
-        return lax.psum_scatter(w, ("zh", "y", "x", "core"), scatter_dimension=0, tiled=True)
-    zh, y = lax.axis_index("zh"), lax.axis_index("y")
-    g = g.reshape(2, 2, HD // 2, D)
-    first, same = core == 0, zh == core
-    keep = jnp.where(first, g[:, 0], g[:, 1])
-    other = flip(jnp.where(first, g[:, 1], g[:, 0]), "core")
-    w = jnp.stack([jnp.where(same, keep, other), jnp.where(same, other, keep)])
-    w = jnp.where(y == 0, w, w[:, ::-1])
-    w = w[:, 0].astype(F32) + flip(w[:, 1], "y").astype(F32)
-    return w[0] + flip(w[1].astype(BF), "zh").astype(F32)
+    w = jnp.zeros((2, 2, 2, HD, D), F32)
+    g = g.astype(F32).reshape(1, 2, 1, HD, D)
+    w = lax.dynamic_update_slice(w, g, (core, 0, x, 0, 0)).reshape(-1, D)
+    return lax.psum_scatter(w, ("zh", "y", "x", "core"), scatter_dimension=0, tiled=True)
 
 
 def shards(
@@ -596,7 +616,6 @@
     from_hidden_weight,
     from_hidden_bias,
 ):
-    LINE.clear()
     span = block_input.shape[1]
     count = 16 * copies
     rows = D // count
@@ -604,158 +623,285 @@
     length = 4 * span
     zl, x, core = (lax.axis_index(a) for a in ("zl", "x", "core"))
     own_in, own_grad = block_input[0], output_grad[0]
-    kernel = lambda v, step, *first: queue("kernel", after(v, *first) if first else v, step)
-    base = jnp.zeros((1,), jnp.int32)
+    base = jnp.zeros((2,), jnp.int32)
     if copies == 2:
-        base = base + lax.axis_index("zh") * 2 + lax.axis_index("y")
-
-    vectors = (
-        attention_norm_gain,
-        attention_norm_bias,
-        mlp_norm_gain,
-        mlp_norm_bias,
-        dense_bias,
-        from_hidden_bias,
-        query_key_value_bias,
-        to_hidden_bias,
-    )
-    if copies == 2:
-        small = pack_rows(vectors)
-    else:
-        small = jnp.stack([jnp.pad(v, (0, BLK - v.shape[0])) for v in vectors])
-    facts = jnp.concatenate([documents[0], jnp.pad(span_order[0], (0, length - 4))])
-    small = jnp.concatenate([small, facts.astype(BF).reshape(8, BLK)], axis=0)
-    small = jnp.broadcast_to(small[None], (count, 16, BLK)).reshape(count * 16, BLK)
-
-    wide, tall = deal_columns(query_key_value_weight, to_hidden_weight, copies)
-    wide = swap(wide).reshape(2, 4 * rows, WIDE)
-    tall = swap(tall).reshape(2, 4 * rows, UNITS)
-    small = swap(small, AXES).reshape(count, 16, BLK)
-    in_zl, in_x = flip(own_in, "zl"), flip(own_in, "x")
-    if copies == 2:
-        chunk = jnp.concatenate([dense_weight, from_hidden_weight], axis=0)
-        join = lambda v: jnp.concatenate(v, axis=0)
-        back_near = flip(chunk, "y")
-        back_far = flip_parts(chunk, "zh")
-        wide_near = flip(wide, "y")
-        wide_far = flip(wide, "zh")
-        tall_near = flip(tall, "y")
-        tall_far = flip_parts(tall, "zh")
-        back_both = flip(join(back_far), "y")
-        wide_pieces = [wide, wide_near, wide_far, flip(wide_far, "y")]
-        tall_both = [flip(v, "y") for v in tall_far]
-        tall_pieces = [tall, tall_near, join(tall_far), join(tall_both)]
-        back_pieces = [chunk, back_near, join(back_far), back_both]
-    in_both = flip(in_zl, "x")
-    other_core = lambda blocks: jnp.concatenate([flip(v, "core") for v in blocks], axis=0)
-    near = [own_in, in_x, in_zl, in_both]
-    far = other_core(near)
-    near = jnp.concatenate(near, axis=0)
-    up_zl, up_x = flip(own_grad, "zl"), own_grad
-    if copies == 2:
-        up_x = after(up_x, back_far[1])
-    up_x = flip(up_x, "x")
-    if copies == 2:
-        up_zl = after(up_zl, wide_far, tall_near)
-    up_both = flip(up_zl, "x")
-    near_up = [own_grad, up_x, up_zl, up_both]
-    far_up = other_core(near_up)
-    near_up = jnp.concatenate(near_up, axis=0)
-    if copies == 2:
-        dense_w = dense_rows([p[:rows] for p in back_pieces])
-    else:
-        wide_pieces = gather_plain(wide, split_rows(copies))
-        tall_pieces = gather_plain(tall, split_rows(copies))
-        back_pieces = gather_plain(from_hidden_weight, lambda w: list(w.reshape(4, BLK, D)))
-        dense_w = gather_dense_plain(dense_weight)
-
-    row = (lax.axis_index("zh") * 2 * copies + lax.axis_index("y")) * 4
-    facts = [lax.dynamic_slice(small, (row + s * copies * 4, 8, 0), (1, 8, BLK)) for s in (zl, 1 - zl)]
-    facts = [v.astype(jnp.int32).reshape(2 * length) for v in facts]
-    small = small[:, :8].astype(F32)
-    take = lambda j, n: small[:, j, :n].reshape(-1)
-    gains = jnp.stack([take(j, rows) for j in range(4)])
-    out_shift = take(4, rows) + take(5, rows)
-    joined_shift = take(6, 3 * rows).reshape(3, 2, 2, 2, 2, HD)
-    joined_shift = lax.dynamic_slice(joined_shift, (0, core, zl, 0, x, 0), (3, 1, 1, 2, 1, HD))
-    joined_shift = joined_shift.reshape(1, WIDE)
-    hidden_shift = take(7, units).reshape(2, 2, copies, 2, 2, units)
-    hidden_shift = lax.dynamic_slice(
-        hidden_shift, (0, zl, 0, x, core, 0), (2, 1, copies, 1, 1, units)
-    ).reshape(1, UNITS)
-
-    offsets = jnp.arange(span, dtype=jnp.int32)
-    pos, doc = [], []
-    for known in facts:
-        for c in (0, 1):
-            for b in (0, 1):
-                block = (x ^ b) * 2 + (core ^ c)
-                doc.append(lax.dynamic_slice(known, (block * span,), (span,)))
-                pos.append(lax.dynamic_slice(known, (length + block,), (1,)) * span + offsets)
-    pos = jnp.concatenate(pos).reshape(2, length)
-    doc = jnp.concatenate(doc).reshape(2, length)
-    inverse = jnp.power(THETA, -jnp.arange(ROT // 2, dtype=F32) * (2.0 / ROT))
-    angles = pos.astype(F32)[:, :, None] * inverse
-    cosine, sine = jnp.cos(angles), jnp.sin(angles)
-    rest = jnp.zeros((2, length, HD - ROT), F32)
-    cos_table = jnp.concatenate([cosine, cosine, rest + 1.0], axis=-1)
-    sin_table = jnp.concatenate([-sine, sine, rest], axis=-1)
+        base = base.at[0].set(lax.axis_index("zh") * 2 + lax.axis_index("y"))
+
+    def spread_small(first):
+        vectors = (
+            first,
+            attention_norm_bias,
+            mlp_norm_gain,
+            mlp_norm_bias,
+            dense_bias,
+            from_hidden_bias,
+            query_key_value_bias,
+            to_hidden_bias,
+        )
+        if copies == 2:
+            small = pack_rows(vectors)
+        else:
+            small = jnp.stack([jnp.pad(v, (0, BLK - v.shape[0])) for v in vectors])
+        facts = jnp.concatenate([documents[0], jnp.pad(span_order[0], (0, length - 4))])
+        small = jnp.concatenate([small, facts.astype(BF).reshape(8, BLK)], axis=0)
+        small = jnp.broadcast_to(small[None], (count, 16, BLK)).reshape(count * 16, BLK)
+        return swap(small, AXES)
+
+    def unpack(small):
+        small = small.reshape(count, 16, BLK)
+        row = (lax.axis_index("zh") * 2 * copies + lax.axis_index("y")) * 4
+        facts = [lax.dynamic_slice(small, (row + s * copies * 4, 8, 0), (1, 8, BLK)) for s in (zl, 1 - zl)]
+        facts = [v.astype(jnp.int32).reshape(2 * length) for v in facts]
+        small = small[:, :8].astype(F32)
+        take = lambda j, n: small[:, j, :n].reshape(-1)
+        gains = jnp.stack([take(j, rows) for j in range(4)])
+        out_shift = take(4, rows) + take(5, rows)
+        joined_shift = take(6, 3 * rows).reshape(3, 2, 2, 2, 2, HD)
+        joined_shift = lax.dynamic_slice(joined_shift, (0, core, zl, 0, x, 0), (3, 1, 1, 2, 1, HD))
+        joined_shift = joined_shift.reshape(1, WIDE)
+        hidden_shift = take(7, units).reshape(2, 2, copies, 2, 2, units)
+        hidden_shift = lax.dynamic_slice(
+            hidden_shift, (0, zl, 0, x, core, 0), (2, 1, copies, 1, 1, units)
+        ).reshape(1, UNITS)
+
+        offsets = jnp.arange(span, dtype=jnp.int32)
+        pos, doc = [], []
+        for known in facts:
+            for c in (0, 1):
+                for b in (0, 1):
+                    block = (x ^ b) * 2 + (core ^ c)
+                    doc.append(lax.dynamic_slice(known, (block * span,), (span,)))
+                    pos.append(lax.dynamic_slice(known, (length + block,), (1,)) * span + offsets)
+        pos = jnp.concatenate(pos).reshape(2, length)
+        doc = jnp.concatenate(doc).reshape(2, length)
+        inverse = jnp.power(THETA, -jnp.arange(ROT // 2, dtype=F32) * (2.0 / ROT))
+        angles = pos.astype(F32)[:, :, None] * inverse
+        cosine, sine = jnp.cos(angles), jnp.sin(angles)
+        rest = jnp.zeros((2, length, HD - ROT), F32)
+        cos_table = jnp.concatenate([cosine, cosine, rest + 1.0], axis=-1)
+        sin_table = jnp.concatenate([-sine, sine, rest], axis=-1)
+
+
+        return gains, out_shift, joined_shift, hidden_shift, pos, doc, cos_table, sin_table
 
     order = (3, 1, 2, 0)
     ordered = lambda v: [v[order.index(r)] for r in range(4)]
-    normed_one, normed_two, mean, scale = kernel(gains, lambda v: norms(near, far, v))
-    grad_mixed = kernel(dense_w, lambda v: mixed_grad(near_up, far_up, v))
-    joined = kernel(normed_one, lambda v: joined_product(base, v, wide_pieces, joined_shift))
-    mixed, *grads = kernel(
-        joined, lambda v: attention(v, grad_mixed, cos_table, sin_table, pos, doc)
-    )
+    halves = lambda v: (v[: v.shape[0] // 2], v[v.shape[0] // 2 :])
+    join = lambda *v: jnp.concatenate(v, axis=0)
+    block = lambda v, f: v[f * span : (f + 1) * span]
+    low_sum = lambda v, w: (v.astype(F32) + w.astype(F32)).astype(BF)
     pair = copies == 2
-    ties = lambda *v: v if pair else ()
-    far_half = lambda v: half_sum(v[2], flip(v[3], "y")) if pair else v[2]
-    grad_wide = ordered(kernel(normed_one, lambda v: rows_grad(base, v, grads, order)))
-    wide_far = far_half(grad_wide)
-    half = mixed.shape[0] // 2
-    grad_dense = dot(mixed[:half], near_up, 0, 0) + dot(mixed[half:], far_up, 0, 0)
-    grad_dense = grad_dense.astype(BF)
-    active, grad_hidden, hidden_sum = kernel(
-        normed_two,
-        lambda v: hidden_products(
-            base, v, near_up, far_up, tall_pieces, back_pieces, hidden_shift
-        ),
-        grad_dense,
-    )
-    grad_tall = ordered(
-        kernel(grad_hidden, lambda v: rows_grad(base, normed_two, [v], order), *ties(wide_far))
-    )
-    wide_sum = flip(wide_far, "zh") if pair else None
-    tall_far = far_half(grad_tall)
-    grad_back = ordered(kernel(active, lambda v: units_grad(base, v, near_up, far_up, order)))
-    pull_half = lambda h, *first: kernel(
-        grad_hidden,
-        lambda v: pull_product(
-            base, h, grads, v, far if h else near, mean, scale, gains, wide_pieces, tall_pieces
-        ),
-        *first,
-    )
-    out_half = lambda h, *first: kernel(
-        mixed, lambda v: out_product(base, h, v, active, dense_w, back_pieces), *first
-    )
-    pull_far, pull_far_sums, pull_far_wide = pull_half(1, *ties(tall_far, wide_sum))
-    back_far = far_half(grad_back)
-    pull_near, pull_near_sums, pull_near_wide = pull_half(0)
-    tall_sum = flip_parts(tall_far, "zh") if pair else ()
-    out_far = out_half(1, *ties(back_far), *tall_sum[:1])
-    out_near = out_half(0, *tall_sum[1:])
-    tall_sum = jnp.concatenate(tall_sum) if pair else None
-    pull = reduce_tokens(pull_near, pull_far, span)
-    back_sum = jnp.concatenate(flip_parts(back_far, "zh")) if pair else None
-    out = reduce_tokens(out_near, out_far, span)
-
-    def near_half(v, far, join):
-        if pair:
-            return v[0].astype(F32) + flip(v[1], "y").astype(F32) + far.astype(F32)
-        w = join(jnp.stack(v).astype(F32))
-        return lax.psum_scatter(w, ("zh", "y"), scatter_dimension=0, tiled=False)
+
+    def near(d, own, names):
+        return join(own, *[d[n] for n in names.split()])
+
+    tasks, parts = {}, {}
+
+    def once(name, make):
+        if name not in parts:
+            parts[name] = make()
+        return parts[name]
+
+    facts_of = lambda d: once("facts", lambda: unpack(d["ss"]))
+
+    def move(name, axis, source):
+        tasks[name] = (source, lambda v, d: flip(v, axis))
+
+    def kernel(name, source, step):
+        tasks[name] = (source, step)
+
+    kernel(
+        "deal",
+        lambda d: query_key_value_weight,
+        lambda v, d: deal_columns(v, to_hidden_weight, copies),
+    )
+    tasks["sw"] = (lambda d: d["deal"][0], lambda v, d: swap(v).reshape(2, 4 * rows, WIDE))
+    tasks["st"] = (lambda d: d["deal"][1], lambda v, d: swap(v).reshape(2, 4 * rows, UNITS))
+    tasks["ss"] = (lambda d: attention_norm_gain, lambda v, d: spread_small(v))
+    chunk = jnp.concatenate([dense_weight, from_hidden_weight], axis=0)
+    move("An", "y", lambda d: chunk)
+    move("A0z", "zh", lambda d: halves(chunk)[0])
+    move("A1z", "zh", lambda d: halves(chunk)[1])
+    move("Af0", "y", lambda d: d["A0z"])
+    move("Af1", "y", lambda d: d["A1z"])
+    move("Wn", "y", lambda d: d["sw"])
+    move("Wz", "zh", lambda d: d["sw"])
+    move("Wf", "y", lambda d: d["Wz"])
+    late = lambda v, d: after(v, d["A"][0])
+    back_of = lambda d: [
+        chunk,
+        d["An"],
+        join(late(d["A0z"], d), late(d["A1z"], d)),
+        join(late(d["Af0"], d), late(d["Af1"], d)),
+    ]
+    back = lambda d: once("back", lambda: back_of(d))
+    wide = lambda d: [d["sw"], d["Wn"], d["Wz"], d["Wf"]]
+    tasks["Tg"] = (
+        lambda d: d["st"],
+        lambda v, d: lax.all_gather(v, ("zh", "y"), axis=0, tiled=False),
+    )
+    tasks["Br"] = (
+        lambda d: d["B"],
+        lambda v, d: lax.psum_scatter(v, ("zh", "y"), scatter_dimension=0, tiled=True),
+    )
+    tall_of = lambda d: d["Tg"] if pair else jnp.stack(split_rows(copies)(d["Tg"]))
+    tall = lambda d: once("tall", lambda: tall_of(d))
+    if not pair:
+        back_of = lambda d: gather_plain(from_hidden_weight, lambda w: list(w.reshape(4, BLK, D)))
+        wide = lambda d: once("wide", lambda: gather_plain(d["sw"], split_rows(copies)))
+    dense_two_of = lambda d: dense_parts([p[:rows] for p in (chunk, d["An"], d["A0z"], d["Af0"])])
+    dense_two = lambda d: once("dense_two", lambda: dense_two_of(d))
+    move("dc", "core", lambda d: dense_two(d)[1])
+    dense_of = lambda d: dense_join(dense_two(d)[0], d["dc"])
+    dense = lambda d: once("dense", lambda: dense_of(d))
+    if not pair:
+        dense_of = lambda d: gather_dense_plain(dense_weight)
+
+    for n, own in (("i", own_in), ("u", own_grad)):
+        move(n + "x", "x", lambda d, own=own: own)
+        move(n + "z", "zl", lambda d, own=own: own)
+        move(n + "b", "x", lambda d, n=n: d[n + "z"])
+        move(n + "0", "core", lambda d, own=own: own)
+        move(n + "1", "core", lambda d, n=n: d[n + "x"])
+        move(n + "2", "core", lambda d, n=n: d[n + "z"])
+        move(n + "3", "core", lambda d, n=n: d[n + "b"])
+    tokens_of = lambda d: (near(d, own_in, "ix iz ib"), join(*[d[n] for n in ("i0", "i1", "i2", "i3")]))
+    tokens = lambda d: once("tokens", lambda: tokens_of(d))
+    upstream_of = lambda d: (near(d, own_grad, "ux uz ub"), join(*[d[n] for n in ("u0", "u1", "u2", "u3")]))
+    upstream = lambda d: once("upstream", lambda: upstream_of(d))
+
+    kernel("norms", lambda d: facts_of(d)[0], lambda v, d: norms(*tokens(d), v))
+    kernel("dO", lambda d: dense(d), lambda v, d: mixed_grad(*upstream(d), v))
+    kernel(
+        "joined",
+        lambda d: d["norms"][0],
+        lambda v, d: joined_product(base, v, wide(d), facts_of(d)[2]),
+    )
+    kernel(
+        "A",
+        lambda d: (d["joined"], d["dO"])[0],
+        lambda v, d: attention(v, d["dO"], *[facts_of(d)[j] for j in (6, 7, 4, 5)]),
+    )
+    heads = lambda d: d["A"]
+    kernel(
+        "W",
+        lambda d: d["norms"][0],
+        lambda v, d: ordered(rows_grad(base, v, heads(d)[1:], order)),
+    )
+    kernel(
+        "H",
+        lambda d: d["norms"][1],
+        lambda v, d: hidden_products(base, v, *upstream(d), tall(d), back(d), facts_of(d)[3]),
+    )
+    kernel(
+        "T",
+        lambda d: d["H"][1],
+        lambda v, d: ordered(rows_grad(base, d["norms"][1], [v], order)),
+    )
+    kernel(
+        "B", lambda d: d["H"][0], lambda v, d: units_grad(v, *upstream(d))
+    )
+    for h, n in ((1, "f"), (0, "n")):
+        kernel(
+            "P" + n,
+            lambda d: d["H"][1],
+            lambda v, d, h=h: pull_product(
+                base, h, heads(d)[1:], v, tokens(d)[h], *d["norms"][2:], facts_of(d)[0], wide(d), tall(d)
+            ),
+        )
+        kernel(
+            "O" + n,
+            lambda d: d["H"][0],
+            lambda v, d, h=h: out_product(base, h, heads(d)[0], v, dense(d), back(d)),
+        )
+
+    def grad_dense(d):
+        mixed, (near_up, far_up) = heads(d)[0], upstream(d)
+        low, high = halves(mixed)
+        return (dot(low, near_up, 0, 0) + dot(high, far_up, 0, 0)).astype(BF)
+
+    g_dense = lambda d: once("g_dense", lambda: grad_dense(d))
+    g_sort = lambda d: once("sort", lambda: dense_sort(dense_split(g_dense(d))[0], d["gd"]))
+    for n in "WT":
+        move(n + "3", "y", lambda d, n=n: d[n][3])
+        move(n + "1", "y", lambda d, n=n: d[n][1])
+    far_sum = lambda d, n: once(n + "far", lambda: low_sum(d[n][2], d[n + "3"]))
+    move("zW", "zh", lambda d: far_sum(d, "W"))
+    move("zT0", "zh", lambda d: halves(far_sum(d, "T"))[0])
+    move("zT1", "zh", lambda d: halves(far_sum(d, "T"))[1])
+    move("gd", "core", lambda d: dense_split(g_dense(d))[1])
+    move("D1", "y", lambda d: g_sort(d)[:, 1])
+    dense_y = lambda d: once("dense_y", lambda: g_sort(d)[:, 0].astype(F32) + d["D1"].astype(F32))
+    move("zD", "zh", lambda d: dense_y(d)[1].astype(BF))
+    add = lambda d, n, far: d[n][0].astype(F32) + d[n + "1"].astype(F32) + far.astype(F32)
+
+    for n, k in (("p", "P"), ("o", "O")):
+        part = lambda d, which, k=k: d[k + which][0] if k == "P" else d[k + which]
+        total = lambda d, f, n=n, part=part: block(part(d, "n"), f).astype(F32) + d[f"{n}c{f}"].astype(F32)
+        for f in range(4):
+            move(f"{n}c{f}", "core", lambda d, f=f, part=part: block(part(d, "f"), f))
+        move(n + "3", "x", lambda d, total=total: total(d, 3).astype(BF))
+        move(n + "1", "x", lambda d, total=total: total(d, 1).astype(BF))
+        move(
+            n + "z",
+            "zl",
+            lambda d, n=n, total=total: (total(d, 2) + d[n + "3"].astype(F32)).astype(BF),
+        )
+        tasks[n] = lambda d, n=n, total=total: (
+            total(d, 0) + d[n + "1"].astype(F32) + d[n + "z"].astype(F32)
+        )
+
+    grad_own = own_grad.astype(F32)
+
+    def all_sums(v, w, hidden_sum):
+        joined_sum = lax.dynamic_update_slice(
+            jnp.zeros((3, 2, 2, 2, 2, HD), F32),
+            (v[2] + w[2]).reshape(3, 1, 1, 2, 1, HD),
+            (0, core, zl, 0, x, 0),
+        )
+        hidden_sum = lax.dynamic_update_slice(
+            jnp.zeros((2, 2, copies, 2, 2, units), F32),
+            hidden_sum.reshape(2, 1, copies, 1, 1, units),
+            (0, zl, 0, x, core, 0),
+        )
+        sums = [*(v[1] + w[1]), jnp.sum(grad_own, axis=0), joined_sum, hidden_sum]
+        return jnp.concatenate([s.reshape(count, -1) for s in sums], axis=1)
+
+    tasks["gs"] = (
+        lambda d: all_sums(d["Pn"], d["Pf"], d["H"][2]),
+        lambda v, d: jnp.sum(swap(v, AXES), axis=0),
+    )
+    tasks["gw"] = (
+        lambda d: add(d, "W", d["zW"]).astype(BF).reshape(8, rows, WIDE),
+        lambda v, d: swap(v),
+    )
+    tasks["gt"] = (
+        lambda d: add(d, "T", join(d["zT0"], d["zT1"])).astype(BF).reshape(8, rows, UNITS),
+        lambda v, d: swap(v),
+    )
+
+    if pair:
+        d = run(tasks)
+        pull, out = tasks["p"](d), tasks["o"](d)
+        sums, grad_wide, grad_tall = d["gs"], d["gw"], d["gt"]
+        grad_dense = dense_y(d)[0] + d["zD"].astype(F32)
+    else:
+        names = [*CFG["y"], *CFG["zh"], "dc", "gd", "gw", "gt"]
+        d = run(tasks, names)
+        pull, out, sums = tasks["p"](d), tasks["o"](d), d["gs"]
+
+        def scatter(pieces, plan):
+            w = plan(jnp.stack(pieces).astype(F32))
+            return lax.psum_scatter(w, ("zh", "y"), scatter_dimension=0, tiled=False)
+
+        grad_wide = swap(scatter(d["W"], join_rows(copies)).astype(BF).reshape(8, rows, WIDE))
+        grad_tall = swap(scatter(d["T"], join_rows(copies)).astype(BF).reshape(8, rows, UNITS))
+        grad_dense = reduce_dense_plain(g_dense(d))
+
+    grad_back = d["Br"].astype(F32)
+    out_shift = facts_of(d)[1]
+    grad_wide = collect_columns(grad_wide, 0, copies)
+    grad_tall = collect_columns(grad_tall, 1, copies)
 
     own_wide = own_in.astype(F32)
     block_output = (own_wide + (out + out_shift)).astype(BF)[None]
@@ -767,31 +913,10 @@
         - jnp.mean(pull, axis=-1, keepdims=True)
         - own_normal * jnp.mean(pull * own_normal, axis=-1, keepdims=True)
     )
-    grad_own = own_grad.astype(F32)
     input_grad = (grad_own + pull).astype(BF)[None]
 
-    vectors = pull_near_sums + pull_far_sums
-    joined_sum = (pull_near_wide + pull_far_wide).reshape(3, 1, 1, 2, 1, HD)
-    joined_sum = lax.dynamic_update_slice(
-        jnp.zeros((3, 2, 2, 2, 2, HD), F32), joined_sum, (0, core, zl, 0, x, 0)
-    )
-    hidden_sum = lax.dynamic_update_slice(
-        jnp.zeros((2, 2, copies, 2, 2, units), F32),
-        hidden_sum.reshape(2, 1, copies, 1, 1, units),
-        (0, zl, 0, x, core, 0),
-    )
-    sums = [*vectors, jnp.sum(grad_own, axis=0), joined_sum, hidden_sum]
-    sums = jnp.concatenate([v.reshape(count, -1) for v in sums], axis=1)
-    sums = jnp.sum(swap(sums, AXES), axis=0)
     cut = lambda a, n: sums[a : a + n]
     bias_sum = cut(4 * rows, rows)
-
-    grad_wide = near_half(grad_wide, wide_sum, join_rows(copies)).astype(BF)
-    grad_wide = collect_columns(swap(grad_wide.reshape(8, rows, WIDE)), 0, copies)
-    grad_tall = near_half(grad_tall, tall_sum, join_rows(copies)).astype(BF)
-    grad_tall = collect_columns(swap(grad_tall.reshape(8, rows, UNITS)), 1, copies)
-    grad_dense = reduce_dense(grad_dense, copies)
-    grad_back = near_half(grad_back, back_sum, lambda w: w.reshape(2 * copies, units, D))
 
 
     return (

time: 601 us -> 608 us (1.012)
  waiting for transfers between devices: 200 us -> 184 us
  between operations: 7.31 us -> 20.7 us
  starting transfers between devices: 71.3 us -> 63 us
  Pallas kernels: 195 us -> 203 us
    ppermute x55 -> x47, waiting for transfers between devices: 181 us -> 169 us  [flip(): return lax.ppermute(v, axis, [(0, 1), (1, 0)])]
    ppermute x55 -> x47, starting transfers between devices: 49.2 us -> 40.1 us  [flip(): return lax.ppermute(v, axis, [(0, 1), (1, 0)])]
    unnamed x156 -> x123, local copies, waits for them, and re-layouts: 24.9 us -> 30.7 us
    slice x10 -> x8, local copies, waits for them, and re-layouts: 15.8 us -> 12.6 us  [the longest x2 8.55 us: shards(): block = lambda v, f: v[f * span:(f + 1) * span]]
  transfers between devices with their start and end apart: 61 -> 55, of which waited for: 20 -> 14; matrix products, arithmetic and copies ran while one was open for 18% -> 18% of each run, Pallas kernels for 22% -> 31%
where the time goes in v3:
time: 608 us; the launch traced here: 600 us
  Pallas kernels  203 us (33%)
  waiting for transfers between devices  184 us (30%)
  local copies, waits for them, and re-layouts  65.9 us (11%)
  starting transfers between devices  63 us (10%)
  other arithmetic  58.5 us (10%)
  between operations  20.7 us (3%)
    ppermute x47, waiting for transfers between devices, flip(): return lax.ppermute(v, axis, [(0, 1), (1, 0)])  169 us
    ppermute x47, starting transfers between devices, flip(): return lax.ppermute(v, axis, [(0, 1), (1, 0)])  40.1 us
    pallas_call x2, Pallas kernels, pull_product(): call(pull_kernel, (steps,), [*[half_rows(2 * HD)] * 3, half_rows(UNITS),...  35.3 us
    pallas_call x1, Pallas kernels, attention(): call(attention_kernel, (2, 2, length // BLK), [part(0), whole(2), whole(4...  34.8 us
    unnamed x123, local copies, waits for them, and re-layouts  30.7 us
    pallas_call x1, Pallas kernels, hidden_products(): call(functools.partial(hidden_kernel, tall - BLK), (n // BLK,), [rows_of(...  29.2 us
    pallas_call x2, Pallas kernels, rows_grad(): call(functools.partial(rows_grad_kernel, len(rights)), (2 * len(order),),...  28.8 us
    all_to_all x6, starting transfers between devices, swap(): return lax.all_to_all(v, axes, 0, 0, tiled=True)  22.7 us
  transfers between devices with their start and end apart: 55, of which 14 were waited for; matrix products, arithmetic and copies ran while one was open for 18% of the time, Pallas kernels for 31%

profile of v3, /device:TPU:0, one launch (start us, length us, event | category | flops | bytes accessed | tf_op | source)
XLA Modules:
  0.0 599.7 jit_solution(8337887564912119481)
XLA Ops:
  7.2 3.1 collective-permute-start.1
  19.2 4.0 all-to-all-start
  25.7 1.8 collective-permute-start.7
  28.4 2.4 collective-permute-start.9
  30.8 2.0 slice.179
  34.4 11.6 %all-to-all-done = bf16[32,16,256]{2,1,0:T(8,128)(2,1)S(1)} async-done(((bf16[32,16,256]{2,1,0:T(8,128)(2,1)}), bf16[32,16,256]{2,1,0:T(8,128)(2,1)S(1)}, u32[]{:S(2)}, u32[]{:S(2)}) %all-to-all-start) | async-done | bytes 262176 | tf_op jit(solution)/shard_map/all_to_all | solution.py:529
  46.0 3.5 all-to-all-start.1
  57.0 5.5 fusion.18
  62.6 1.9 reshape.228.pq
  64.6 1.9 broadcast_in_dim_reshape.13.eq
  69.7 1.9 collective-permute-start.2
  74.9 2.4 constant_dynamic-update-slice_fusion.3
  78.2 4.3 all-to-all-start.2
  82.5 13.4 %collective-permute-done.2 = bf16[256,2048]{1,0:T(8,128)(2,1)} collective-permute-done((bf16[256,2048]{1,0:T(8,128)(2,1)}, bf16[256,2048]{1,0:T(8,128)(2,1)}, u32[]{:S(2)}, u32[]{:S(2)}) %collective-permute-start.2) | collective-permute-done | bytes 1048608 | tf_op jit(solution)/shard_map/ppermute | solution.py:54
  96.0 2.0 collective-permute-start.13
  98.5 2.3 constant_dynamic-update-slice_fusion.2
  100.8 2.4 constant_dynamic-update-slice_fusion.1
  103.1 3.7 pad_maximum_fusion.near.tokens
  106.8 25.6 %collective-permute-done.10.w2.q2 = bf16[2,256,768]{2,1,0:T(8,128)(2,1)} collective-permute-done((bf16[2,256,768]{2,1,0:T(8,128)(2,1)S(1)}, bf16[2,256,768]{2,1,0:T(8,128)(2,1)}, u32[]{:S(2)}, u32[]{:S(2)}) %collective-permute-start.10) | collective-permute-done | bytes 786464 | tf_op jit(solution)/shard_map/ppermute | solution.py:54
  137.6 14.4 %shard_map.265 = (bf16[2048,2048]{1,0:T(8,128)(2,1)}, bf16[2048,2048]{1,0:T(8,128)(2,1)}, f32[2048,1]{1,0:T(8,128)S(1)}, f32[2048,1]{1,0:T(8,128)S(1)}) custom-call(bf16[1024,2048]{1,0:T(8,128)(2,1)} %pad_maximum_fusion.near.tokens, bf16[1024,2048]{1,0:T(8,128)(2,1)} %constant_dynamic-update-slice_fusion.far.tokens, f32[4,2048]{1,0:T(4,128)S(1)} %pad_maximum_fusion.5.gains), custom_call_target="tpu_custom_call" | custom-call | flops 41943040 | bytes 25165824 | tf_op jit(solution)/shard_map/pallas_call | solution.py:155
  154.4 8.9 %collective-permute-done.21 = bf16[160,2048]{1,0:T(8,128)(2,1)} collective-permute-done((bf16[160,2048]{1,0:T(8,128)(2,1)}, bf16[160,2048]{1,0:T(8,128)(2,1)}, u32[]{:S(2)}, u32[]{:S(2)}) %collective-permute-start.21) | collective-permute-done | bytes 655392 | tf_op jit(solution)/shard_map/ppermute | solution.py:54
  163.6 12.9 %shard_map.266 = f32[2048,768]{1,0:T(8,128)} custom-call(s32[2]{0:T(128)S(1)} %scatter.4.base, bf16[2048,2048]{1,0:T(8,128)(2,1)} %get-tuple-element.135.v, bf16[2,256,768]{2,1,0:T(8,128)(2,1)S(1)} %bitcast.160, bf16[2,256,768]{2,1,0:T(8,128)(2,1)S(1)} %collective-permute-done.8.w1.q1, bf16[2,256,768]{2,1,0:T(8,128)(2,1)} %collective-permute-done.10.w2.q2, ...), custom_call_target="tpu_custom_call" | custom-call | flops 6442450944 | bytes 17825792 | tf_op jit(solution)/shard_map/pallas_call | solution.py:177
  177.1 4.0 pad_maximum_fusion.1.near
  184.4 2.0 copy-done.33
  186.3 8.5 %shard_map.267 = bf16[2048,256]{1,0:T(8,128)(2,1)S(1)} custom-call(bf16[1024,2048]{1,0:T(8,128)(2,1)} %pad_maximum_fusion.1.near, bf16[1024,2048]{1,0:T(8,128)(2,1)} %copy-done.33, bf16[256,2048]{1,0:T(8,128)(2,1)S(1)} %bitcast.152), custom_call_target="tpu_custom_call" | custom-call | flops 2147483648 | bytes 8388608 | tf_op jit(solution)/shard_map/pallas_call | solution.py:194
  195.8 34.8 %shard_map.268 = (bf16[2,2,512,256]{3,2,1,0:T(8,128)(2,1)S(1)}, bf16[2,2,512,256]{3,2,1,0:T(8,128)(2,1)S(1)}, bf16[2,2,512,256]{3,2,1,0:T(8,128)(2,1)S(1)}, bf16[2,2,512,256]{3,2,1,0:T(8,128)(2,1)}) custom-call(f32[2,2,512,768]{3,2,1,0:T(8,128)} %bitcast.204, f32[2,2,512,768]{3,2,1,0:T(8,128)} %bitcast.205, f32[2,2,512,768]{3,2,1,0:T(8,128)} %bitcast.206, ...), custom_call_target="tpu_custom_call" | custom-call | flops 7516192768 | bytes 12582912 | tf_op jit(solution)/shard_map/pallas_call | solution.py:435
  232.6 13.5 %shard_map.269 = (bf16[512,768]{1,0:T(8,128)(2,1)}, bf16[512,768]{1,0:T(8,128)(2,1)}, bf16[512,768]{1,0:T(8,128)(2,1)S(1)}, bf16[512,768]{1,0:T(8,128)(2,1)S(1)}) custom-call(s32[2]{0:T(128)S(1)} %scatter.4.base, bf16[2048,2048]{1,0:T(8,128)(2,1)} %get-tuple-element.135.v, bf16[2048,256]{1,0:T(8,128)(2,1)} %bitcast.174, bf16[2048,256]{1,0:T(8,128)(2,1)} %bitcast.177, ...), custom_call_target="tpu_custom_call" | custom-call | flops 6442450944 | bytes 11534336 | tf_op jit(solution)/shard_map/pallas_call | solution.py:351
  246.1 1.9 collective-permute-start.23
  249.3 3.5 fusion
  261.1 29.2 %shard_map.270 = (bf16[2048,1024]{1,0:T(8,128)(2,1)}, bf16[2048,1024]{1,0:T(8,128)(2,1)}, f32[1,1024]{1,0:T(1,128)S(1)}) custom-call(s32[2]{0:T(128)S(1)} %scatter.4.base, bf16[2048,2048]{1,0:T(8,128)(2,1)} %get-tuple-element.140.v, bf16[1024,2048]{1,0:T(8,128)(2,1)} %pad_maximum_fusion.1.near, bf16[1024,2048]{1,0:T(8,128)(2,1)} %copy-done.33, ...), custom_call_target="tpu_custom_call" | custom-call | flops 17179869184 | bytes 33554432 | tf_op jit(solution)/shard_map/pallas_call | solution.py:231
  290.3 15.3 %shard_map.271 = (bf16[512,1024]{1,0:T(8,128)(2,1)S(1)}, bf16[512,1024]{1,0:T(8,128)(2,1)S(1)}, bf16[512,1024]{1,0:T(8,128)(2,1)S(1)}, bf16[512,1024]{1,0:T(8,128)(2,1)}) custom-call(s32[2]{0:T(128)S(1)} %scatter.4.base, bf16[2048,2048]{1,0:T(8,128)(2,1)} %get-tuple-element.140.v, bf16[2048,1024]{1,0:T(8,128)(2,1)} %get-tuple-element.165.refs_0_.du), custom_call_target="tpu_custom_call" | custom-call | flops 8589934592 | bytes 12582912 | tf_op jit(solution)/shard_map/pallas_call | solution.py:351
  306.8 17.7 %shard_map.272 = (bf16[1024,2048]{1,0:T(8,128)(2,1)}, f32[4,2048]{1,0:T(4,128)S(1)}, f32[1,768]{1,0:T(1,128)S(1)}) custom-call(s32[2]{0:T(128)S(1)} %scatter.4.base, bf16[2048,256]{1,0:T(8,128)(2,1)} %bitcast.175, bf16[2048,256]{1,0:T(8,128)(2,1)} %bitcast.178, bf16[2048,256]{1,0:T(8,128)(2,1)} %bitcast.208, ...), custom_call_target="tpu_custom_call" | custom-call | flops 7516192768 | bytes 19922944 | tf_op jit(solution)/shard_map/pallas_call | solution.py:303
  324.4 4.1 fusion.23
  334.9 32.6 %collective-permute-done.25 = bf16[512,768]{1,0:T(8,128)(2,1)S(1)} collective-permute-done((bf16[512,768]{1,0:T(8,128)(2,1)S(1)}, bf16[512,768]{1,0:T(8,128)(2,1)S(1)}, u32[]{:S(2)}, u32[]{:S(2)}) %collective-permute-start.25) | collective-permute-done | bytes 786464 | tf_op jit(solution)/shard_map/ppermute | solution.py:54
  367.6 17.6 %shard_map.273 = (bf16[1024,2048]{1,0:T(8,128)(2,1)}, f32[4,2048]{1,0:T(4,128)S(1)}, f32[1,768]{1,0:T(1,128)S(1)}) custom-call(s32[2]{0:T(128)S(1)} %scatter.4.base, bf16[2048,256]{1,0:T(8,128)(2,1)} %bitcast.176, bf16[2048,256]{1,0:T(8,128)(2,1)} %bitcast.179, bf16[2048,256]{1,0:T(8,128)(2,1)} %bitcast.209, ...), custom_call_target="tpu_custom_call" | custom-call | flops 7516192768 | bytes 19922944 | tf_op jit(solution)/shard_map/pallas_call | solution.py:303
  385.2 7.0 %collective-permute-done.26 = bf16[256,1024]{1,0:T(8,128)(2,1)S(1)} collective-permute-done((bf16[256,1024]{1,0:T(8,128)(2,1)S(1)}, bf16[256,1024]{1,0:T(8,128)(2,1)S(1)}, u32[]{:S(2)}, u32[]{:S(2)}) %collective-permute-start.26) | collective-permute-done | bytes 524320 | tf_op jit(solution)/shard_map/ppermute | solution.py:54
  393.1 14.4 %shard_map.274 = bf16[1024,2048]{1,0:T(8,128)(2,1)} custom-call(bf16[2048,1024]{1,0:T(8,128)(2,1)} %get-tuple-element.169.v.active, bf16[1024,2048]{1,0:T(8,128)(2,1)} %pad_maximum_fusion.1.near, bf16[1024,2048]{1,0:T(8,128)(2,1)} %copy-done.33), custom_call_target="tpu_custom_call" | custom-call | flops 8589934592 | bytes 16777216 | tf_op jit(solution)/shard_map/pallas_call | solution.py:369
  407.5 3.0 add_convert_fusion.3
  411.9 10.3 %shard_map.275 = bf16[1024,2048]{1,0:T(8,128)(2,1)} custom-call(s32[2]{0:T(128)S(1)} %scatter.4.base, bf16[2048,256]{1,0:T(8,128)(2,1)S(1)} %bitcast.156, bf16[2048,1024]{1,0:T(8,128)(2,1)} %get-tuple-element.169.v.active, bf16[256,2048]{1,0:T(8,128)(2,1)S(1)} %bitcast.153, bf16[320,2048]{1,0:T(8,128)(2,1)S(1)} %copy-done.9, ...), custom_call_target="tpu_custom_call" | custom-call | flops 5368709120 | bytes 10485760 | tf_op jit(solution)/shard_map/pallas_call | solution.py:255
  422.2 4.5 fusion.22
  426.7 2.2 collective-permute-start.35
  428.9 2.3 add_convert_fusion.8
  431.2 3.6 all-to-all-start.3
  435.9 4.7 add_convert_fusion
  440.6 1.9 collective-permute-start.39
  442.4 6.3 %collective-permute-done.35 = bf16[2,64,2048]{2,1,0:T(8,128)(2,1)} collective-permute-done((bf16[2,64,2048]{2,1,0:T(8,128)(2,1)}, bf16[2,64,2048]{2,1,0:T(8,128)(2,1)}, u32[]{:S(2)}, u32[]{:S(2)}) %collective-permute-start.35) | collective-permute-done | bytes 524320 | tf_op jit(solution)/shard_map/ppermute | solution.py:54
  448.8 2.5 collective-permute-start.36
  451.5 2.3 collective-permute-start.33
  453.8 10.1 %shard_map.276 = bf16[1024,2048]{1,0:T(8,128)(2,1)} custom-call(s32[2]{0:T(128)S(1)} %scatter.4.base, bf16[2048,256]{1,0:T(8,128)(2,1)S(1)} %bitcast.157, bf16[2048,1024]{1,0:T(8,128)(2,1)} %get-tuple-element.169.v.active, bf16[256,2048]{1,0:T(8,128)(2,1)S(1)} %bitcast.154, bf16[320,2048]{1,0:T(8,128)(2,1)S(1)} %copy-done.10, ...), custom_call_target="tpu_custom_call" | custom-call | flops 5368709120 | bytes 10485760 | tf_op jit(solution)/shard_map/pallas_call | solution.py:255
  464.5 2.9 add_convert_fusion.5
  469.7 15.5 %collective-permute-done.33 = bf16[256,1024]{1,0:T(8,128)(2,1)S(1)} collective-permute-done((bf16[256,1024]{1,0:T(8,128)(2,1)S(1)}, bf16[256,1024]{1,0:T(8,128)(2,1)S(1)}, u32[]{:S(2)}, u32[]{:S(2)}) %collective-permute-start.33) | collective-permute-done | bytes 524320 | tf_op jit(solution)/shard_map/ppermute | solution.py:54
  486.8 3.7 all-to-all-start.4
  494.7 1.9 collective-permute-start.44
  496.7 2.3 convert_add_fusion.3
  499.0 5.0 add_convert_fusion.6
  505.4 32.3 %collective-permute-done.44 = bf16[256,2048]{1,0:T(8,128)(2,1)} collective-permute-done((bf16[256,2048]{1,0:T(8,128)(2,1)}, bf16[256,2048]{1,0:T(8,128)(2,1)}, u32[]{:S(2)}, u32[]{:S(2)}) %collective-permute-start.44) | collective-permute-done | bytes 1048608 | tf_op jit(solution)/shard_map/ppermute | solution.py:54
  538.8 2.0 collective-permute-start.46
  540.8 3.2 fusion.21
  543.9 24.4 %collective-permute-done.45 = bf16[256,2048]{1,0:T(8,128)(2,1)S(1)} collective-permute-done((bf16[256,2048]{1,0:T(8,128)(2,1)}, bf16[256,2048]{1,0:T(8,128)(2,1)S(1)}, u32[]{:S(2)}, u32[]{:S(2)}) %collective-permute-start.45) | collective-permute-done | bytes 1048608 | tf_op jit(solution)/shard_map/ppermute | solution.py:54
  568.3 5.8 convert_reduce_fusion.1
  575.8 3.6 all-to-all-start.5
  579.5 1.9 fusion.14
  584.1 3.2 all-to-all-done.5
  589.1 2.8 convert_element_type.232
  (306 shorter events, 77.1 us)
Async XLA Ops:
  7.2 62.5 %collective-permute-start.1 = (bf16[256,2048]{1,0:T(8,128)(2,1)}, bf16[256,2048]{1,0:T(8,128)(2,1)}, u32[]{:S(2)}, u32[]{:S(2)}) collective-permute-start(bf16[256,2048]{1,0:T(8,128)(2,1)} %bitcast.180), channel_id=1, source_target_pairs={{0,8},{8,0},{1,9},{9,1},{2,10},{10,2},{3,11},{11,3},{4,12},{12,4},... | collective-permute-start | bytes 3145736 | tf_op jit(solution)/shard_map/ppermute | solution.py:54
  10.3 59.4 %collective-permute-start = (bf16[256,2048]{1,0:T(8,128)(2,1)}, bf16[256,2048]{1,0:T(8,128)(2,1)}, u32[]{:S(2)}, u32[]{:S(2)}) collective-permute-start(bf16[256,2048]{1,0:T(8,128)(2,1)} %bitcast.181), channel_id=1, source_target_pairs={{0,2},{2,0},{1,3},{3,1},{4,6},{6,4},{5,7},{7,5},{8,10},{10,8},{9,1... | collective-permute-start | bytes 3145736 | tf_op jit(solution)/shard_map/ppermute | solution.py:54
  11.8 61.5 %collective-permute-start.3 = (bf16[256,2048]{1,0:T(8,128)(2,1)}, bf16[256,2048]{1,0:T(8,128)(2,1)}, u32[]{:S(2)}, u32[]{:S(2)}) collective-permute-start(bf16[256,2048]{1,0:T(8,128)(2,1)} %bitcast.182), channel_id=1, source_target_pairs={{0,1},{1,0},{2,3},{3,2},{4,5},{5,4},{6,7},{7,6},{8,9},{9,8},{10,11... | collective-permute-start | bytes 3145736 | tf_op jit(solution)/shard_map/ppermute | solution.py:54
  19.2 26.8 %all-to-all-start = ((bf16[32,16,256]{2,1,0:T(8,128)(2,1)}), bf16[32,16,256]{2,1,0:T(8,128)(2,1)S(1)}, u32[]{:S(2)}, u32[]{:S(2)}) async-start(bf16[32,16,256]{2,1,0:T(8,128)(2,1)} %broadcast_in_dim.60), calls=%async_computation | async-start | bytes 524288 | tf_op jit(solution)/shard_map/all_to_all | solution.py:529
  25.7 45.9 %collective-permute-start.7 = (bf16[320,2048]{1,0:T(8,128)(2,1)S(1)}, bf16[320,2048]{1,0:T(8,128)(2,1)}, u32[]{:S(2)}, u32[]{:S(2)}) collective-permute-start(bf16[320,2048]{1,0:T(8,128)(2,1)S(1)} %constant_dynamic-update-slice_fusion.4.b0), channel_id=1, source_target_pairs={{0,4},{4,0},{1,5},{5,1},{2,6},{6,2},{3,7},{7,3},{8,12},{12,8},{9,1... | collective-permute-start | bytes 3932168 | tf_op jit(solution)/shard_map/ppermute | solution.py:54
  28.4 43.7 %collective-permute-start.9 = (bf16[160,2048]{1,0:T(8,128)(2,1)}, bf16[160,2048]{1,0:T(8,128)(2,1)}, u32[]{:S(2)}, u32[]{:S(2)}) collective-permute-start(bf16[160,2048]{1,0:T(8,128)(2,1)} %slice.223), channel_id=1, source_target_pairs={{0,16},{16,0},{1,17},{17,1},{2,18},{18,2},{3,19},{19,3},{4,20},{20... | collective-permute-start | bytes 1966088 | tf_op jit(solution)/shard_map/ppermute | solution.py:54
  46.0 26.1 %all-to-all-start.1 = ((bf16[8,64,768]{2,1,0:T(8,128)(2,1)}), bf16[8,64,768]{2,1,0:T(8,128)(2,1)S(1)}, u32[]{:S(2)}, u32[]{:S(2)}) async-start(bf16[8,64,768]{2,1,0:T(8,128)(2,1)} %get-tuple-element.115), calls=%async_computation.1 | async-start | bytes 1572864 | tf_op jit(solution)/shard_map/all_to_all | solution.py:529
  69.7 26.3 %collective-permute-start.2 = (bf16[256,2048]{1,0:T(8,128)(2,1)}, bf16[256,2048]{1,0:T(8,128)(2,1)}, u32[]{:S(2)}, u32[]{:S(2)}) collective-permute-start(bf16[256,2048]{1,0:T(8,128)(2,1)} %collective-permute-done.1), channel_id=1, source_target_pairs={{0,2},{2,0},{1,3},{3,1},{4,6},{6,4},{5,7},{7,5},{8,10},{10,8},{9,1... | collective-permute-start | bytes 3145736 | tf_op jit(solution)/shard_map/ppermute | solution.py:54
  71.6 29.2 %collective-permute-start.5 = (bf16[256,2048]{1,0:T(8,128)(2,1)}, bf16[256,2048]{1,0:T(8,128)(2,1)}, u32[]{:S(2)}, u32[]{:S(2)}) collective-permute-start(bf16[256,2048]{1,0:T(8,128)(2,1)} %collective-permute-done.1), channel_id=1, source_target_pairs={{0,1},{1,0},{2,3},{3,2},{4,5},{5,4},{6,7},{7,6},{8,9},{9,8},{10,11... | collective-permute-start | bytes 3145736 | tf_op jit(solution)/shard_map/ppermute | solution.py:54
  71.6 26.4 %collective-permute-start.4 = (bf16[256,2048]{1,0:T(8,128)(2,1)}, bf16[256,2048]{1,0:T(8,128)(2,1)}, u32[]{:S(2)}, u32[]{:S(2)}) collective-permute-start(bf16[256,2048]{1,0:T(8,128)(2,1)} %collective-permute-done), channel_id=1, source_target_pairs={{0,1},{1,0},{2,3},{3,2},{4,5},{5,4},{6,7},{7,6},{8,9},{9,8},{10,11... | collective-permute-start | bytes 3145736 | tf_op jit(solution)/shard_map/ppermute | solution.py:54
  72.1 23.8 %collective-permute-start.8 = (bf16[2,256,768]{2,1,0:T(8,128)(2,1)S(1)}, bf16[2,256,768]{2,1,0:T(8,128)(2,1)S(1)}, u32[]{:S(2)}, u32[]{:S(2)}) collective-permute-start(bf16[2,256,768]{2,1,0:T(8,128)(2,1)S(1)} %bitcast.158), channel_id=1, source_target_pairs={{0,4},{4,0},{1,5},{5,1},{2,6},{6,2},{3,7},{7,3},{8,12},{12,8},{9,1... | collective-permute-start | bytes 2359304 | tf_op jit(solution)/shard_map/ppermute | solution.py:54
  73.3 61.4 %collective-permute-start.14 = (bf16[256,2048]{1,0:T(8,128)(2,1)}, bf16[256,2048]{1,0:T(8,128)(2,1)}, u32[]{:S(2)}, u32[]{:S(2)}) collective-permute-start(bf16[256,2048]{1,0:T(8,128)(2,1)} %bitcast.11), channel_id=1, source_target_pairs={{0,8},{8,0},{1,9},{9,1},{2,10},{10,2},{3,11},{11,3},{4,12},{12,4},... | collective-permute-start | bytes 3145736 | tf_op jit(solution)/shard_map/ppermute | solution.py:54
  78.2 76.0 %all-to-all-start.2 = ((bf16[8,64,1024]{2,1,0:T(8,128)(2,1)}), bf16[8,64,1024]{2,1,0:T(8,128)(2,1)}, u32[]{:S(2)}, u32[]{:S(2)}) async-start(bf16[8,64,1024]{2,1,0:T(8,128)(2,1)} %get-tuple-element.142), calls=%async_computation.2 | async-start | bytes 2097152 | tf_op jit(solution)/shard_map/all_to_all | solution.py:529
  82.5 20.7 %copy-start.27 = (bf16[1,256,2048]{2,1,0:T(8,128)(2,1)S(1)}, bf16[1,256,2048]{2,1,0:T(8,128)(2,1)}, u32[]{:S(2)}) copy-start(bf16[1,256,2048]{2,1,0:T(8,128)(2,1)} %param.18) | copy-start | bytes 3145732
  82.5 175.9 %all-gather.2.cloned.1.call-start = ((), (), s32[]{:S(2)}) async-start(), calls=%async_computation.7 | async-start | bytes 5242880 | tf_op jit(solution)/shard_map/all_gather | solution.py:741
  96.0 36.5 %collective-permute-start.10 = (bf16[2,256,768]{2,1,0:T(8,128)(2,1)S(1)}, bf16[2,256,768]{2,1,0:T(8,128)(2,1)}, u32[]{:S(2)}, u32[]{:S(2)}) collective-permute-start(bf16[2,256,768]{2,1,0:T(8,128)(2,1)S(1)} %bitcast.159), channel_id=1, source_target_pairs={{0,16},{16,0},{1,17},{17,1},{2,18},{18,2},{3,19},{19,3},{4,20},{20... | collective-permute-start | bytes 2359304 | tf_op jit(solution)/shard_map/ppermute | solution.py:54
  96.0 67.6 %copy-start.23 = (bf16[2,256,768]{2,1,0:T(8,128)(2,1)}, bf16[2,256,768]{2,1,0:T(8,128)(2,1)S(1)}, u32[]{:S(2)}) copy-start(bf16[2,256,768]{2,1,0:T(8,128)(2,1)S(1)} %collective-permute-done.8.w1.q1) | copy-start | bytes 2359300
  96.0 37.6 %collective-permute-start.13 = (bf16[256,2048]{1,0:T(8,128)(2,1)}, bf16[256,2048]{1,0:T(8,128)(2,1)}, u32[]{:S(2)}, u32[]{:S(2)}) collective-permute-start(bf16[256,2048]{1,0:T(8,128)(2,1)} %bitcast.11), channel_id=1, source_target_pairs={{0,2},{2,0},{1,3},{3,1},{4,6},{6,4},{5,7},{7,5},{8,10},{10,8},{9,1... | collective-permute-start | bytes 3145736 | tf_op jit(solution)/shard_map/ppermute | solution.py:54
  98.0 34.5 %collective-permute-start.11 = (bf16[160,2048]{1,0:T(8,128)(2,1)}, bf16[160,2048]{1,0:T(8,128)(2,1)S(1)}, u32[]{:S(2)}, u32[]{:S(2)}) collective-permute-start(bf16[160,2048]{1,0:T(8,128)(2,1)} %collective-permute-done.9), channel_id=1, source_target_pairs={{0,4},{4,0},{1,5},{5,1},{2,6},{6,2},{3,7},{7,3},{8,12},{12,8},{9,1... | collective-permute-start | bytes 1966088 | tf_op jit(solution)/shard_map/ppermute | solution.py:54
  100.8 34.4 %collective-permute-start.6 = (bf16[256,2048]{1,0:T(8,128)(2,1)}, bf16[256,2048]{1,0:T(8,128)(2,1)S(1)}, u32[]{:S(2)}, u32[]{:S(2)}) collective-permute-start(bf16[256,2048]{1,0:T(8,128)(2,1)} %collective-permute-done.2), channel_id=1, source_target_pairs={{0,1},{1,0},{2,3},{3,2},{4,5},{5,4},{6,7},{7,6},{8,9},{9,8},{10,11... | collective-permute-start | bytes 3145736 | tf_op jit(solution)/shard_map/ppermute | solution.py:54
  103.1 29.5 %copy-start.44 = (bf16[64,2048]{1,0:T(8,128)(2,1)S(1)}, bf16[64,2048]{1,0:T(8,128)(2,1)}, u32[]{:S(2)}) copy-start(bf16[64,2048]{1,0:T(8,128)(2,1)} %param.26) | copy-start | bytes 786436
  132.5 20.5 %collective-permute-start.16 = (bf16[256,2048]{1,0:T(8,128)(2,1)}, bf16[256,2048]{1,0:T(8,128)(2,1)S(1)}, u32[]{:S(2)}, u32[]{:S(2)}) collective-permute-start(bf16[256,2048]{1,0:T(8,128)(2,1)} %bitcast.11), channel_id=1, source_target_pairs={{0,1},{1,0},{2,3},{3,2},{4,5},{5,4},{6,7},{7,6},{8,9},{9,8},{10,11... | collective-permute-start | bytes 3145736 | tf_op jit(solution)/shard_map/ppermute | solution.py:54
  132.5 30.8 %collective-permute-start.21 = (bf16[160,2048]{1,0:T(8,128)(2,1)}, bf16[160,2048]{1,0:T(8,128)(2,1)}, u32[]{:S(2)}, u32[]{:S(2)}) collective-permute-start(bf16[160,2048]{1,0:T(8,128)(2,1)} %slice.179), channel_id=1, source_target_pairs={{0,16},{16,0},{1,17},{17,1},{2,18},{18,2},{3,19},{19,3},{4,20},{20... | collective-permute-start | bytes 1966088 | tf_op jit(solution)/shard_map/ppermute | solution.py:54
  133.6 29.7 %collective-permute-start.12 = (bf16[2,256,768]{2,1,0:T(8,128)(2,1)}, bf16[2,256,768]{2,1,0:T(8,128)(2,1)}, u32[]{:S(2)}, u32[]{:S(2)}) collective-permute-start(bf16[2,256,768]{2,1,0:T(8,128)(2,1)} %collective-permute-done.10.w2.q2), channel_id=1, source_target_pairs={{0,4},{4,0},{1,5},{5,1},{2,6},{6,2},{3,7},{7,3},{8,12},{12,8},{9,1... | collective-permute-start | bytes 2359304 | tf_op jit(solution)/shard_map/ppermute | solution.py:54
  134.7 41.8 %collective-permute-start.17 = (bf16[256,2048]{1,0:T(8,128)(2,1)}, bf16[256,2048]{1,0:T(8,128)(2,1)}, u32[]{:S(2)}, u32[]{:S(2)}) collective-permute-start(bf16[256,2048]{1,0:T(8,128)(2,1)} %collective-permute-done.13), channel_id=1, source_target_pairs={{0,1},{1,0},{2,3},{3,2},{4,5},{5,4},{6,7},{7,6},{8,9},{9,8},{10,11... | collective-permute-start | bytes 3145736 | tf_op jit(solution)/shard_map/ppermute | solution.py:54
  135.2 41.4 %collective-permute-start.15 = (bf16[256,2048]{1,0:T(8,128)(2,1)}, bf16[256,2048]{1,0:T(8,128)(2,1)}, u32[]{:S(2)}, u32[]{:S(2)}) collective-permute-start(bf16[256,2048]{1,0:T(8,128)(2,1)} %collective-permute-done.14), channel_id=1, source_target_pairs={{0,2},{2,0},{1,3},{3,1},{4,6},{6,4},{5,7},{7,5},{8,10},{10,8},{9,1... | collective-permute-start | bytes 3145736 | tf_op jit(solution)/shard_map/ppermute | solution.py:54
  153.0 23.6 %copy-start.20 = (f32[2048,1]{1,0:T(8,128)}, f32[2048,1]{1,0:T(8,128)S(1)}, u32[]{:S(2)}) copy-start(f32[2048,1]{1,0:T(8,128)S(1)} %get-tuple-element.163.scale) | copy-start | bytes 24580
  153.0 29.6 %collective-permute-start.18 = (bf16[256,2048]{1,0:T(8,128)(2,1)}, bf16[256,2048]{1,0:T(8,128)(2,1)}, u32[]{:S(2)}, u32[]{:S(2)}) collective-permute-start(bf16[256,2048]{1,0:T(8,128)(2,1)} %collective-permute-done.14), channel_id=1, source_target_pairs={{0,1},{1,0},{2,3},{3,2},{4,5},{5,4},{6,7},{7,6},{8,9},{9,8},{10,11... | collective-permute-start | bytes 3145736 | tf_op jit(solution)/shard_map/ppermute | solution.py:54
  154.2 434.9 %reduce-scatter.2.cloned.1.call-start = ((), (), s32[]{:S(2)}) async-start(), calls=%async_computation.8 | async-start | bytes 5242880 | tf_op jit(solution)/shard_map/reduce_scatter | solution.py:745
  163.3 82.7 %collective-permute-start.22 = (bf16[160,2048]{1,0:T(8,128)(2,1)}, bf16[160,2048]{1,0:T(8,128)(2,1)S(1)}, u32[]{:S(2)}, u32[]{:S(2)}) collective-permute-start(bf16[160,2048]{1,0:T(8,128)(2,1)} %collective-permute-done.21), channel_id=1, source_target_pairs={{0,4},{4,0},{1,5},{5,1},{2,6},{6,2},{3,7},{7,3},{8,12},{12,8},{9,1... | collective-permute-start | bytes 1966088 | tf_op jit(solution)/shard_map/ppermute | solution.py:54
  176.5 7.4 %collective-permute-start.20 = (bf16[2,64,2048]{2,1,0:T(8,128)(2,1)}, bf16[2,64,2048]{2,1,0:T(8,128)(2,1)S(1)}, u32[]{:S(2)}, u32[]{:S(2)}) collective-permute-start(bf16[2,64,2048]{2,1,0:T(8,128)(2,1)} %fusion.13), channel_id=1, source_target_pairs={{0,1},{1,0},{2,3},{3,2},{4,5},{5,4},{6,7},{7,6},{8,9},{9,8},{10,11... | collective-permute-start | bytes 1572872 | tf_op jit(solution)/shard_map/ppermute | solution.py:54
  176.6 7.6 %collective-permute-start.19 = (bf16[256,2048]{1,0:T(8,128)(2,1)}, bf16[256,2048]{1,0:T(8,128)(2,1)S(1)}, u32[]{:S(2)}, u32[]{:S(2)}) collective-permute-start(bf16[256,2048]{1,0:T(8,128)(2,1)} %collective-permute-done.15), channel_id=1, source_target_pairs={{0,1},{1,0},{2,3},{3,2},{4,5},{5,4},{6,7},{7,6},{8,9},{9,8},{10,11... | collective-permute-start | bytes 3145736 | tf_op jit(solution)/shard_map/ppermute | solution.py:54
  246.1 44.2 %collective-permute-start.23 = (bf16[512,768]{1,0:T(8,128)(2,1)}, bf16[512,768]{1,0:T(8,128)(2,1)}, u32[]{:S(2)}, u32[]{:S(2)}) collective-permute-start(bf16[512,768]{1,0:T(8,128)(2,1)} %get-tuple-element.152), channel_id=1, source_target_pairs={{0,4},{4,0},{1,5},{5,1},{2,6},{6,2},{3,7},{7,3},{8,12},{12,8},{9,1... | collective-permute-start | bytes 2359304 | tf_op jit(solution)/shard_map/ppermute | solution.py:54
  252.9 4.0 collective-permute-start.30
  306.6 25.5 %collective-permute-start.24 = (bf16[512,1024]{1,0:T(8,128)(2,1)S(1)}, bf16[512,1024]{1,0:T(8,128)(2,1)S(1)}, u32[]{:S(2)}, u32[]{:S(2)}) collective-permute-start(bf16[512,1024]{1,0:T(8,128)(2,1)S(1)} %get-tuple-element.156), channel_id=1, source_target_pairs={{0,4},{4,0},{1,5},{5,1},{2,6},{6,2},{3,7},{7,3},{8,12},{12,8},{9,1... | collective-permute-start | bytes 3145736 | tf_op jit(solution)/shard_map/ppermute | solution.py:54
  328.5 38.9 %collective-permute-start.37 = (bf16[256,2048]{1,0:T(8,128)(2,1)S(1)}, bf16[256,2048]{1,0:T(8,128)(2,1)S(1)}, u32[]{:S(2)}, u32[]{:S(2)}) collective-permute-start(bf16[256,2048]{1,0:T(8,128)(2,1)S(1)} %get-tuple-element.182), channel_id=1, source_target_pairs={{0,1},{1,0},{2,3},{3,2},{4,5},{5,4},{6,7},{7,6},{8,9},{9,8},{10,11... | collective-permute-start | bytes 3145736 | tf_op jit(solution)/shard_map/ppermute | solution.py:54
  330.2 37.3 %collective-permute-start.25 = (bf16[512,768]{1,0:T(8,128)(2,1)S(1)}, bf16[512,768]{1,0:T(8,128)(2,1)S(1)}, u32[]{:S(2)}, u32[]{:S(2)}) collective-permute-start(bf16[512,768]{1,0:T(8,128)(2,1)S(1)} %add_convert_fusion.9), channel_id=1, source_target_pairs={{0,16},{16,0},{1,17},{17,1},{2,18},{18,2},{3,19},{19,3},{4,20},{20... | collective-permute-start | bytes 2359304 | tf_op jit(solution)/shard_map/ppermute | solution.py:54
  331.1 95.6 %collective-permute-start.27 = (bf16[256,2048]{1,0:T(8,128)(2,1)}, bf16[256,2048]{1,0:T(8,128)(2,1)}, u32[]{:S(2)}, u32[]{:S(2)}) collective-permute-start(bf16[256,2048]{1,0:T(8,128)(2,1)} %get-tuple-element.170), channel_id=1, source_target_pairs={{0,1},{1,0},{2,3},{3,2},{4,5},{5,4},{6,7},{7,6},{8,9},{9,8},{10,11... | collective-permute-start | bytes 3145736 | tf_op jit(solution)/shard_map/ppermute | solution.py:54
  331.4 103.5 %collective-permute-start.31 = (bf16[256,2048]{1,0:T(8,128)(2,1)}, bf16[256,2048]{1,0:T(8,128)(2,1)}, u32[]{:S(2)}, u32[]{:S(2)}) collective-permute-start(bf16[256,2048]{1,0:T(8,128)(2,1)} %get-tuple-element.174), channel_id=1, source_target_pairs={{0,1},{1,0},{2,3},{3,2},{4,5},{5,4},{6,7},{7,6},{8,9},{9,8},{10,11... | collective-permute-start | bytes 3145736 | tf_op jit(solution)/shard_map/ppermute | solution.py:54
  332.2 94.6 %collective-permute-start.34 = (bf16[512,768]{1,0:T(8,128)(2,1)}, bf16[512,768]{1,0:T(8,128)(2,1)}, u32[]{:S(2)}, u32[]{:S(2)}) collective-permute-start(bf16[512,768]{1,0:T(8,128)(2,1)} %get-tuple-element.179), channel_id=1, source_target_pairs={{0,4},{4,0},{1,5},{5,1},{2,6},{6,2},{3,7},{7,3},{8,12},{12,8},{9,1... | collective-permute-start | bytes 2359304 | tf_op jit(solution)/shard_map/ppermute | solution.py:54
  367.4 17.8 %copy-start.45 = (bf16[512,768]{1,0:T(8,128)(2,1)}, bf16[512,768]{1,0:T(8,128)(2,1)S(1)}, u32[]{:S(2)}) copy-start(bf16[512,768]{1,0:T(8,128)(2,1)S(1)} %collective-permute-done.25) | copy-start | bytes 2359300
  367.5 24.8 %collective-permute-start.26 = (bf16[256,1024]{1,0:T(8,128)(2,1)S(1)}, bf16[256,1024]{1,0:T(8,128)(2,1)S(1)}, u32[]{:S(2)}, u32[]{:S(2)}) collective-permute-start(bf16[256,1024]{1,0:T(8,128)(2,1)S(1)} %get-tuple-element.159), channel_id=1, source_target_pairs={{0,16},{16,0},{1,17},{17,1},{2,18},{18,2},{3,19},{19,3},{4,20},{20... | collective-permute-start | bytes 1572872 | tf_op jit(solution)/shard_map/ppermute | solution.py:54
  367.5 96.5 %collective-permute-start.42 = (bf16[256,2048]{1,0:T(8,128)(2,1)}, bf16[256,2048]{1,0:T(8,128)(2,1)}, u32[]{:S(2)}, u32[]{:S(2)}) collective-permute-start(bf16[256,2048]{1,0:T(8,128)(2,1)} %get-tuple-element.187), channel_id=1, source_target_pairs={{0,1},{1,0},{2,3},{3,2},{4,5},{5,4},{6,7},{7,6},{8,9},{9,8},{10,11... | collective-permute-start | bytes 3145736 | tf_op jit(solution)/shard_map/ppermute | solution.py:54
  410.5 25.4 %collective-permute-start.38 = (bf16[256,2048]{1,0:T(8,128)(2,1)}, bf16[256,2048]{1,0:T(8,128)(2,1)}, u32[]{:S(2)}, u32[]{:S(2)}) collective-permute-start(bf16[256,2048]{1,0:T(8,128)(2,1)} %add_convert_fusion.3), channel_id=1, source_target_pairs={{0,2},{2,0},{1,3},{3,1},{4,6},{6,4},{5,7},{7,5},{8,10},{10,8},{9,1... | collective-permute-start | bytes 3145736 | tf_op jit(solution)/shard_map/ppermute | solution.py:54
  426.7 37.3 %collective-permute-start.28 = (bf16[256,2048]{1,0:T(8,128)(2,1)}, bf16[256,2048]{1,0:T(8,128)(2,1)}, u32[]{:S(2)}, u32[]{:S(2)}) collective-permute-start(bf16[256,2048]{1,0:T(8,128)(2,1)} %get-tuple-element.171), channel_id=1, source_target_pairs={{0,1},{1,0},{2,3},{3,2},{4,5},{5,4},{6,7},{7,6},{8,9},{9,8},{10,11... | collective-permute-start | bytes 3145736 | tf_op jit(solution)/shard_map/ppermute | solution.py:54
  426.7 22.1 %collective-permute-start.35 = (bf16[2,64,2048]{2,1,0:T(8,128)(2,1)}, bf16[2,64,2048]{2,1,0:T(8,128)(2,1)}, u32[]{:S(2)}, u32[]{:S(2)}) collective-permute-start(bf16[2,64,2048]{2,1,0:T(8,128)(2,1)} %slice_bitcast_fusion.2), channel_id=1, source_target_pairs={{0,4},{4,0},{1,5},{5,1},{2,6},{6,2},{3,7},{7,3},{8,12},{12,8},{9,1... | collective-permute-start | bytes 1572872 | tf_op jit(solution)/shard_map/ppermute | solution.py:54
  431.2 55.6 %all-to-all-start.3 = ((bf16[8,64,768]{2,1,0:T(8,128)(2,1)}), bf16[8,64,768]{2,1,0:T(8,128)(2,1)S(1)}, u32[]{:S(2)}, u32[]{:S(2)}) async-start(bf16[8,64,768]{2,1,0:T(8,128)(2,1)} %bitcast.188), calls=%async_computation.3 | async-start | bytes 1572864 | tf_op jit(solution)/shard_map/all_to_all | solution.py:529
  434.8 19.0 %copy-start.10 = (bf16[320,2048]{1,0:T(8,128)(2,1)S(1)}, bf16[320,2048]{1,0:T(8,128)(2,1)}, u32[]{:S(2)}) copy-start(bf16[320,2048]{1,0:T(8,128)(2,1)} %copy-done.7) | copy-start | bytes 3932164
  440.6 28.3 %collective-permute-start.39 = (bf16[256,2048]{1,0:T(8,128)(2,1)S(1)}, bf16[256,2048]{1,0:T(8,128)(2,1)S(1)}, u32[]{:S(2)}, u32[]{:S(2)}) collective-permute-start(bf16[256,2048]{1,0:T(8,128)(2,1)S(1)} %get-tuple-element.184), channel_id=1, source_target_pairs={{0,2},{2,0},{1,3},{3,1},{4,6},{6,4},{5,7},{7,5},{8,10},{10,8},{9,1... | collective-permute-start | bytes 3145736 | tf_op jit(solution)/shard_map/ppermute | solution.py:54
  448.8 36.4 %collective-permute-start.36 = (bf16[512,1024]{1,0:T(8,128)(2,1)S(1)}, bf16[512,1024]{1,0:T(8,128)(2,1)S(1)}, u32[]{:S(2)}, u32[]{:S(2)}) collective-permute-start(bf16[512,1024]{1,0:T(8,128)(2,1)S(1)} %copy-done.22), channel_id=1, source_target_pairs={{0,4},{4,0},{1,5},{5,1},{2,6},{6,2},{3,7},{7,3},{8,12},{12,8},{9,1... | collective-permute-start | bytes 3145736 | tf_op jit(solution)/shard_map/ppermute | solution.py:54
  451.5 33.7 %collective-permute-start.33 = (bf16[256,1024]{1,0:T(8,128)(2,1)S(1)}, bf16[256,1024]{1,0:T(8,128)(2,1)S(1)}, u32[]{:S(2)}, u32[]{:S(2)}) collective-permute-start(bf16[256,1024]{1,0:T(8,128)(2,1)S(1)} %copy-done.47), channel_id=1, source_target_pairs={{0,16},{16,0},{1,17},{17,1},{2,18},{18,2},{3,19},{19,3},{4,20},{20... | collective-permute-start | bytes 1572872 | tf_op jit(solution)/shard_map/ppermute | solution.py:54
  463.9 21.2 %copy-start.43 = (bf16[512,1024]{1,0:T(8,128)(2,1)S(1)}, bf16[512,1024]{1,0:T(8,128)(2,1)}, u32[]{:S(2)}) copy-start(bf16[512,1024]{1,0:T(8,128)(2,1)} %get-tuple-element.160) | copy-start | bytes 3145732
  463.9 21.2 %copy-start.49 = (bf16[256,1024]{1,0:T(8,128)(2,1)S(1)}, bf16[256,1024]{1,0:T(8,128)(2,1)}, u32[]{:S(2)}) copy-start(bf16[256,1024]{1,0:T(8,128)(2,1)} %copy-done.48) | copy-start | bytes 1572868
  464.0 35.0 %collective-permute-start.32 = (bf16[256,2048]{1,0:T(8,128)(2,1)}, bf16[256,2048]{1,0:T(8,128)(2,1)}, u32[]{:S(2)}, u32[]{:S(2)}) collective-permute-start(bf16[256,2048]{1,0:T(8,128)(2,1)} %get-tuple-element.175), channel_id=1, source_target_pairs={{0,1},{1,0},{2,3},{3,2},{4,5},{5,4},{6,7},{7,6},{8,9},{9,8},{10,11... | collective-permute-start | bytes 3145736 | tf_op jit(solution)/shard_map/ppermute | solution.py:54
  464.0 34.9 %collective-permute-start.43 = (bf16[256,2048]{1,0:T(8,128)(2,1)}, bf16[256,2048]{1,0:T(8,128)(2,1)}, u32[]{:S(2)}, u32[]{:S(2)}) collective-permute-start(bf16[256,2048]{1,0:T(8,128)(2,1)} %get-tuple-element.188), channel_id=1, source_target_pairs={{0,1},{1,0},{2,3},{3,2},{4,5},{5,4},{6,7},{7,6},{8,9},{9,8},{10,11... | collective-permute-start | bytes 3145736 | tf_op jit(solution)/shard_map/ppermute | solution.py:54
  468.8 30.1 %collective-permute-start.40 = (bf16[256,2048]{1,0:T(8,128)(2,1)}, bf16[256,2048]{1,0:T(8,128)(2,1)}, u32[]{:S(2)}, u32[]{:S(2)}) collective-permute-start(bf16[256,2048]{1,0:T(8,128)(2,1)} %add_convert_fusion.5), channel_id=1, source_target_pairs={{0,2},{2,0},{1,3},{3,1},{4,6},{6,4},{5,7},{7,5},{8,10},{10,8},{9,1... | collective-permute-start | bytes 3145736 | tf_op jit(solution)/shard_map/ppermute | solution.py:54
  486.8 50.9 %all-to-all-start.4 = ((bf16[8,64,1024]{2,1,0:T(8,128)(2,1)}), bf16[8,64,1024]{2,1,0:T(8,128)(2,1)S(1)}, u32[]{:S(2)}, u32[]{:S(2)}) async-start(bf16[8,64,1024]{2,1,0:T(8,128)(2,1)} %bitcast.187), calls=%async_computation.4 | async-start | bytes 2097152 | tf_op jit(solution)/shard_map/all_to_all | solution.py:529
  494.7 43.0 %collective-permute-start.44 = (bf16[256,2048]{1,0:T(8,128)(2,1)}, bf16[256,2048]{1,0:T(8,128)(2,1)}, u32[]{:S(2)}, u32[]{:S(2)}) collective-permute-start(bf16[256,2048]{1,0:T(8,128)(2,1)} %get-tuple-element.190), channel_id=1, source_target_pairs={{0,8},{8,0},{1,9},{9,1},{2,10},{10,2},{3,11},{11,3},{4,12},{12,4},... | collective-permute-start | bytes 3145736 | tf_op jit(solution)/shard_map/ppermute | solution.py:54
  499.0 45.0 %collective-permute-start.29 = (bf16[256,2048]{1,0:T(8,128)(2,1)}, bf16[256,2048]{1,0:T(8,128)(2,1)}, u32[]{:S(2)}, u32[]{:S(2)}) collective-permute-start(bf16[256,2048]{1,0:T(8,128)(2,1)} %get-tuple-element.172), channel_id=1, source_target_pairs={{0,1},{1,0},{2,3},{3,2},{4,5},{5,4},{6,7},{7,6},{8,9},{9,8},{10,11... | collective-permute-start | bytes 3145736 | tf_op jit(solution)/shard_map/ppermute | solution.py:54
  503.9 40.0 %collective-permute-start.41 = (bf16[256,2048]{1,0:T(8,128)(2,1)}, bf16[256,2048]{1,0:T(8,128)(2,1)}, u32[]{:S(2)}, u32[]{:S(2)}) collective-permute-start(bf16[256,2048]{1,0:T(8,128)(2,1)} %get-tuple-element.186), channel_id=1, source_target_pairs={{0,2},{2,0},{1,3},{3,1},{4,6},{6,4},{5,7},{7,5},{8,10},{10,8},{9,1... | collective-permute-start | bytes 3145736 | tf_op jit(solution)/shard_map/ppermute | solution.py:54
  537.7 30.6 %collective-permute-start.45 = (bf16[256,2048]{1,0:T(8,128)(2,1)}, bf16[256,2048]{1,0:T(8,128)(2,1)S(1)}, u32[]{:S(2)}, u32[]{:S(2)}) collective-permute-start(bf16[256,2048]{1,0:T(8,128)(2,1)} %get-tuple-element.191), channel_id=1, source_target_pairs={{0,8},{8,0},{1,9},{9,1},{2,10},{10,2},{3,11},{11,3},{4,12},{12,4},... | collective-permute-start | bytes 3145736 | tf_op jit(solution)/shard_map/ppermute | solution.py:54
  538.8 29.6 %copy-start.37 = (bf16[256,2048]{1,0:T(8,128)(2,1)S(1)}, bf16[256,2048]{1,0:T(8,128)(2,1)}, u32[]{:S(2)}) copy-start(bf16[256,2048]{1,0:T(8,128)(2,1)} %copy-done.36) | copy-start | bytes 3145732
  538.8 40.7 %collective-permute-start.46 = (bf16[64,2048]{1,0:T(8,128)(2,1)S(1)}, bf16[64,2048]{1,0:T(8,128)(2,1)S(1)}, u32[]{:S(2)}, u32[]{:S(2)}) collective-permute-start(bf16[64,2048]{1,0:T(8,128)(2,1)S(1)} %fusion.19), channel_id=1, source_target_pairs={{0,16},{16,0},{1,17},{17,1},{2,18},{18,2},{3,19},{19,3},{4,20},{20... | collective-permute-start | bytes 786440 | tf_op jit(solution)/shard_map/ppermute | solution.py:54
  575.8 11.4 %all-to-all-start.5 = ((f32[32,1,768]{2,1,0:T(1,128)}), f32[32,1,768]{2,1,0:T(1,128)S(1)}, u32[]{:S(2)}, u32[]{:S(2)}) async-start(f32[32,1,768]{2,1,0:T(1,128)} %copy.92), calls=%async_computation.5 | async-start | bytes 196608 | tf_op jit(solution)/shard_map/all_to_all | solution.py:529
  (43 other events, 213.0 us)
Sparse Core Ops, SparseCore 0:
  154.3 86.5 all-gather.1
  407.6 106.6 reduce-scatter.1

commit v4 on v3

--- a/solution.py
+++ b/solution.py
@@ -27,21 +27,22 @@
 
 
 CFG = {
-    "swap": ["sw", "st", "ss", "gw", "gt", "gs"],
-    "kernel": ["deal", "norms", "joined", "dO", "A", "W", "H", "T", "Pf", "Pn", "B", "Of", "On"],
+    "swap": ["sw", "st", "ss", "gs", "gw", "gt"],
+    "kernel": ["deal", "norms", "joined", "dO", "A", "W", "H", "T", "B", "Pf", "Pn", "Of", "On"],
     "x": ["ix", "ib", "ux", "ub", "p3", "p1", "o3", "o1"],
     "zl": ["iz", "uz", "pz", "oz"],
     "core": ["i0", "i1", "i2", "i3", "u0", "u1", "u2", "u3", "dc", "gd", "pc3", "pc1", "pc2", "pc0", "oc3", "oc1", "oc2", "oc0"],
-    "y": ["An", "Wn", "Af0", "Wf", "Af1", "W3", "T3", "W1", "D1", "T1"],
-    "zh": ["A0z", "Wz", "A1z", "zW", "zT0", "zT1", "zD"],
+    "y": ["An", "Wn", "Af0", "Wf", "Af1", "W3", "T3", "D1", "W1", "T1"],
+    "zh": ["A0z", "Wz", "A1z", "zW", "zT0", "zD", "zT1"],
     "sc": ["Tg", "Br"],
     "depth": {"core": 3},
     "ties": {
         "T": ["W3"],
-        "Pn": ["zW", "T3"],
-        "B": ["zT0"],
+        "Pf": ["zW", "T3"],
+        "Of": ["zT0"],
+        "o3": ["W1", "gs"],
         "o1": ["zT1", "T1"],
-        "oz": ["gt"],
+        "oz": ["gw"],
     },
 }
 

time: 608 us -> 586 us (0.964)
  waiting for transfers between devices: 184 us -> 166 us
    ppermute x47, waiting for transfers between devices: 169 us -> 152 us  [flip(): return lax.ppermute(v, axis, [(0, 1), (1, 0)])]
    unnamed x123 -> x131, local copies, waits for them, and re-layouts: 30.7 us -> 33.2 us
  transfers between devices with their start and end apart: 55 -> 55, of which waited for: 14 -> 13; matrix products, arithmetic and copies ran while one was open for 18% -> 17% of each run, Pallas kernels for 31% -> 29%
where the time goes in v4:
time: 586 us; the launch traced here: 579 us
  Pallas kernels  203 us (35%)
  waiting for transfers between devices  166 us (28%)
  starting transfers between devices  64.2 us (11%)
  local copies, waits for them, and re-layouts  61.3 us (10%)
  other arithmetic  58.4 us (10%)
  between operations  20.7 us (4%)
    ppermute x47, waiting for transfers between devices, flip(): return lax.ppermute(v, axis, [(0, 1), (1, 0)])  152 us
    ppermute x47, starting transfers between devices, flip(): return lax.ppermute(v, axis, [(0, 1), (1, 0)])  38.5 us
    pallas_call x2, Pallas kernels, pull_product(): call(pull_kernel, (steps,), [*[half_rows(2 * HD)] * 3, half_rows(UNITS),...  35.4 us
    pallas_call x1, Pallas kernels, attention(): call(attention_kernel, (2, 2, length // BLK), [part(0), whole(2), whole(4...  35 us
    unnamed x131, local copies, waits for them, and re-layouts  33.2 us
    pallas_call x1, Pallas kernels, hidden_products(): call(functools.partial(hidden_kernel, tall - BLK), (n // BLK,), [rows_of(...  29.4 us
    pallas_call x2, Pallas kernels, rows_grad(): call(functools.partial(rows_grad_kernel, len(rights)), (2 * len(order),),...  28.3 us
    all_to_all x6, starting transfers between devices, swap(): return lax.all_to_all(v, axes, 0, 0, tiled=True)  25.4 us
  transfers between devices with their start and end apart: 55, of which 13 were waited for; matrix products, arithmetic and copies ran while one was open for 17% of the time, Pallas kernels for 29%

profile of v4, /device:TPU:0, one launch (start us, length us, event | category | flops | bytes accessed | tf_op | source)
XLA Modules:
  0.0 578.9 jit_solution(10124193221600195376)
XLA Ops:
  7.2 3.1 collective-permute-start.1
  19.2 4.0 all-to-all-start
  25.5 1.8 collective-permute-start.7
  28.3 2.4 collective-permute-start.9
  30.7 2.0 slice.179
  35.8 10.3 %all-to-all-done = bf16[32,16,256]{2,1,0:T(8,128)(2,1)S(1)} async-done(((bf16[32,16,256]{2,1,0:T(8,128)(2,1)}), bf16[32,16,256]{2,1,0:T(8,128)(2,1)S(1)}, u32[]{:S(2)}, u32[]{:S(2)}) %all-to-all-start) | async-done | bytes 262176 | tf_op jit(solution)/shard_map/all_to_all | solution.py:530
  46.1 3.5 all-to-all-start.1
  57.1 5.5 fusion.18
  62.7 1.8 reshape.228.pq
  64.7 1.9 broadcast_in_dim_reshape.13.eq
  69.8 1.9 collective-permute-start.2
  75.0 2.4 constant_dynamic-update-slice_fusion.3
  78.4 4.3 all-to-all-start.2
  82.9 13.2 %collective-permute-done.2 = bf16[256,2048]{1,0:T(8,128)(2,1)} collective-permute-done((bf16[256,2048]{1,0:T(8,128)(2,1)}, bf16[256,2048]{1,0:T(8,128)(2,1)}, u32[]{:S(2)}, u32[]{:S(2)}) %collective-permute-start.2) | collective-permute-done | bytes 1048608 | tf_op jit(solution)/shard_map/ppermute | solution.py:55
  96.6 2.3 constant_dynamic-update-slice_fusion.2
  98.9 2.1 collective-permute-start.13
  101.0 2.3 constant_dynamic-update-slice_fusion.1
  103.3 3.7 pad_maximum_fusion.near.tokens
  107.0 25.6 %collective-permute-done.10.w2.q2 = bf16[2,256,768]{2,1,0:T(8,128)(2,1)} collective-permute-done((bf16[2,256,768]{2,1,0:T(8,128)(2,1)S(1)}, bf16[2,256,768]{2,1,0:T(8,128)(2,1)}, u32[]{:S(2)}, u32[]{:S(2)}) %collective-permute-start.10) | collective-permute-done | bytes 786464 | tf_op jit(solution)/shard_map/ppermute | solution.py:55
  137.4 14.4 %shard_map.265 = (bf16[2048,2048]{1,0:T(8,128)(2,1)}, bf16[2048,2048]{1,0:T(8,128)(2,1)}, f32[2048,1]{1,0:T(8,128)S(1)}, f32[2048,1]{1,0:T(8,128)S(1)}) custom-call(bf16[1024,2048]{1,0:T(8,128)(2,1)} %pad_maximum_fusion.near.tokens, bf16[1024,2048]{1,0:T(8,128)(2,1)} %constant_dynamic-update-slice_fusion.far.tokens, f32[4,2048]{1,0:T(4,128)S(1)} %pad_maximum_fusion.5.gains), custom_call_target="tpu_custom_call" | custom-call | flops 41943040 | bytes 25165824 | tf_op jit(solution)/shard_map/pallas_call | solution.py:156
  154.3 9.1 %collective-permute-done.21 = bf16[160,2048]{1,0:T(8,128)(2,1)} collective-permute-done((bf16[160,2048]{1,0:T(8,128)(2,1)}, bf16[160,2048]{1,0:T(8,128)(2,1)}, u32[]{:S(2)}, u32[]{:S(2)}) %collective-permute-start.21) | collective-permute-done | bytes 655392 | tf_op jit(solution)/shard_map/ppermute | solution.py:55
  163.7 13.0 %shard_map.266 = f32[2048,768]{1,0:T(8,128)} custom-call(s32[2]{0:T(128)S(1)} %scatter.4.base, bf16[2048,2048]{1,0:T(8,128)(2,1)} %get-tuple-element.135.v, bf16[2,256,768]{2,1,0:T(8,128)(2,1)S(1)} %bitcast.160, bf16[2,256,768]{2,1,0:T(8,128)(2,1)S(1)} %collective-permute-done.8.w1.q1, bf16[2,256,768]{2,1,0:T(8,128)(2,1)} %collective-permute-done.10.w2.q2, ...), custom_call_target="tpu_custom_call" | custom-call | flops 6442450944 | bytes 17825792 | tf_op jit(solution)/shard_map/pallas_call | solution.py:178
  177.3 4.0 pad_maximum_fusion.1.near
  184.5 2.0 copy-done.37
  186.5 8.5 %shard_map.267 = bf16[2048,256]{1,0:T(8,128)(2,1)S(1)} custom-call(bf16[1024,2048]{1,0:T(8,128)(2,1)} %pad_maximum_fusion.1.near, bf16[1024,2048]{1,0:T(8,128)(2,1)} %copy-done.37, bf16[256,2048]{1,0:T(8,128)(2,1)S(1)} %bitcast.152), custom_call_target="tpu_custom_call" | custom-call | flops 2147483648 | bytes 8388608 | tf_op jit(solution)/shard_map/pallas_call | solution.py:195
  195.9 35.0 %shard_map.268 = (bf16[2,2,512,256]{3,2,1,0:T(8,128)(2,1)S(1)}, bf16[2,2,512,256]{3,2,1,0:T(8,128)(2,1)S(1)}, bf16[2,2,512,256]{3,2,1,0:T(8,128)(2,1)S(1)}, bf16[2,2,512,256]{3,2,1,0:T(8,128)(2,1)}) custom-call(f32[2,2,512,768]{3,2,1,0:T(8,128)} %bitcast.204, f32[2,2,512,768]{3,2,1,0:T(8,128)} %bitcast.205, f32[2,2,512,768]{3,2,1,0:T(8,128)} %bitcast.206, ...), custom_call_target="tpu_custom_call" | custom-call | flops 7516192768 | bytes 12582912 | tf_op jit(solution)/shard_map/pallas_call | solution.py:436
  232.3 12.9 %shard_map.269 = (bf16[512,768]{1,0:T(8,128)(2,1)}, bf16[512,768]{1,0:T(8,128)(2,1)S(1)}, bf16[512,768]{1,0:T(8,128)(2,1)S(1)}, bf16[512,768]{1,0:T(8,128)(2,1)S(1)}) custom-call(s32[2]{0:T(128)S(1)} %scatter.4.base, bf16[2048,2048]{1,0:T(8,128)(2,1)} %get-tuple-element.135.v, bf16[2048,256]{1,0:T(8,128)(2,1)} %bitcast.174, bf16[2048,256]{1,0:T(8,128)(2,1)} %bitcast.177, ...), custom_call_target="tpu_custom_call" | custom-call | flops 6442450944 | bytes 11534336 | tf_op jit(solution)/shard_map/pallas_call | solution.py:352
  245.2 4.3 fusion
  251.1 1.8 collective-permute-start.23
  260.9 29.4 %shard_map.270 = (bf16[2048,1024]{1,0:T(8,128)(2,1)}, bf16[2048,1024]{1,0:T(8,128)(2,1)}, f32[1,1024]{1,0:T(1,128)S(1)}) custom-call(s32[2]{0:T(128)S(1)} %scatter.4.base, bf16[2048,2048]{1,0:T(8,128)(2,1)} %get-tuple-element.140.v, bf16[1024,2048]{1,0:T(8,128)(2,1)} %pad_maximum_fusion.1.near, bf16[1024,2048]{1,0:T(8,128)(2,1)} %copy-done.37, ...), custom_call_target="tpu_custom_call" | custom-call | flops 17179869184 | bytes 33554432 | tf_op jit(solution)/shard_map/pallas_call | solution.py:232
  291.2 15.4 %shard_map.271 = (bf16[512,1024]{1,0:T(8,128)(2,1)}, bf16[512,1024]{1,0:T(8,128)(2,1)S(1)}, bf16[512,1024]{1,0:T(8,128)(2,1)S(1)}, bf16[512,1024]{1,0:T(8,128)(2,1)}) custom-call(s32[2]{0:T(128)S(1)} %scatter.4.base, bf16[2048,2048]{1,0:T(8,128)(2,1)} %get-tuple-element.140.v, bf16[2048,1024]{1,0:T(8,128)(2,1)} %get-tuple-element.166.refs_0_.du), custom_call_target="tpu_custom_call" | custom-call | flops 8589934592 | bytes 12582912 | tf_op jit(solution)/shard_map/pallas_call | solution.py:352
  308.0 14.3 %shard_map.272 = bf16[1024,2048]{1,0:T(8,128)(2,1)} custom-call(bf16[2048,1024]{1,0:T(8,128)(2,1)} %get-tuple-element.169.v.active, bf16[1024,2048]{1,0:T(8,128)(2,1)} %pad_maximum_fusion.1.near, bf16[1024,2048]{1,0:T(8,128)(2,1)} %copy-done.37), custom_call_target="tpu_custom_call" | custom-call | flops 8589934592 | bytes 16777216 | tf_op jit(solution)/shard_map/pallas_call | solution.py:370
  322.3 22.8 %collective-permute-done.25 = bf16[512,768]{1,0:T(8,128)(2,1)} collective-permute-done((bf16[512,768]{1,0:T(8,128)(2,1)}, bf16[512,768]{1,0:T(8,128)(2,1)}, u32[]{:S(2)}, u32[]{:S(2)}) %collective-permute-start.25) | collective-permute-done | bytes 786464 | tf_op jit(solution)/shard_map/ppermute | solution.py:55
  347.3 17.7 %shard_map.273 = (bf16[1024,2048]{1,0:T(8,128)(2,1)}, f32[4,2048]{1,0:T(4,128)S(1)}, f32[1,768]{1,0:T(1,128)S(1)}) custom-call(s32[2]{0:T(128)S(1)} %scatter.4.base, bf16[2048,256]{1,0:T(8,128)(2,1)} %bitcast.175, bf16[2048,256]{1,0:T(8,128)(2,1)} %bitcast.178, bf16[2048,256]{1,0:T(8,128)(2,1)} %bitcast.208, ...), custom_call_target="tpu_custom_call" | custom-call | flops 7516192768 | bytes 19922944 | tf_op jit(solution)/shard_map/pallas_call | solution.py:304
  367.6 17.7 %shard_map.274 = (bf16[1024,2048]{1,0:T(8,128)(2,1)}, f32[4,2048]{1,0:T(4,128)S(1)}, f32[1,768]{1,0:T(1,128)S(1)}) custom-call(s32[2]{0:T(128)S(1)} %scatter.4.base, bf16[2048,256]{1,0:T(8,128)(2,1)} %bitcast.176, bf16[2048,256]{1,0:T(8,128)(2,1)} %bitcast.179, bf16[2048,256]{1,0:T(8,128)(2,1)} %bitcast.209, ...), custom_call_target="tpu_custom_call" | custom-call | flops 7516192768 | bytes 19922944 | tf_op jit(solution)/shard_map/pallas_call | solution.py:304
  386.7 5.5 all-to-all-start.3
  392.2 4.5 fusion.23
  397.0 1.7 collective-permute-start.33
  401.4 10.3 %shard_map.275 = bf16[1024,2048]{1,0:T(8,128)(2,1)} custom-call(s32[2]{0:T(128)S(1)} %scatter.4.base, bf16[2048,256]{1,0:T(8,128)(2,1)S(1)} %bitcast.156, bf16[2048,1024]{1,0:T(8,128)(2,1)} %get-tuple-element.169.v.active, bf16[256,2048]{1,0:T(8,128)(2,1)S(1)} %bitcast.153, bf16[320,2048]{1,0:T(8,128)(2,1)S(1)} %copy-done.11, ...), custom_call_target="tpu_custom_call" | custom-call | flops 5368709120 | bytes 10485760 | tf_op jit(solution)/shard_map/pallas_call | solution.py:256
  411.7 4.6 collective-permute-done.33
  416.2 2.5 collective-permute-start.36
  420.1 2.0 add_convert_fusion.3
  423.5 2.5 collective-permute-start.34
  426.0 2.2 fusion.22
  428.7 16.7 %collective-permute-done.39 = bf16[256,2048]{1,0:T(8,128)(2,1)S(1)} collective-permute-done((bf16[256,2048]{1,0:T(8,128)(2,1)S(1)}, bf16[256,2048]{1,0:T(8,128)(2,1)S(1)}, u32[]{:S(2)}, u32[]{:S(2)}) %collective-permute-start.39) | collective-permute-done | bytes 1048608 | tf_op jit(solution)/shard_map/ppermute | solution.py:55
  445.4 4.0 add_convert_fusion.1
  450.6 10.0 %shard_map.276 = bf16[1024,2048]{1,0:T(8,128)(2,1)} custom-call(s32[2]{0:T(128)S(1)} %scatter.4.base, bf16[2048,256]{1,0:T(8,128)(2,1)S(1)} %bitcast.157, bf16[2048,1024]{1,0:T(8,128)(2,1)} %get-tuple-element.169.v.active, bf16[256,2048]{1,0:T(8,128)(2,1)S(1)} %bitcast.154, bf16[320,2048]{1,0:T(8,128)(2,1)S(1)} %copy-done.11, ...), custom_call_target="tpu_custom_call" | custom-call | flops 5368709120 | bytes 10485760 | tf_op jit(solution)/shard_map/pallas_call | solution.py:256
  460.7 2.6 collective-permute-start.35
  463.3 2.6 add_convert_fusion.8
  465.9 3.7 all-to-all-start.4
  470.2 2.9 add_convert_fusion.5
  473.1 1.7 collective-permute-start.41
  476.5 11.0 %collective-permute-done.35 = bf16[256,1024]{1,0:T(8,128)(2,1)} collective-permute-done((bf16[256,1024]{1,0:T(8,128)(2,1)S(1)}, bf16[256,1024]{1,0:T(8,128)(2,1)}, u32[]{:S(2)}, u32[]{:S(2)}) %collective-permute-start.35) | collective-permute-done | bytes 524320 | tf_op jit(solution)/shard_map/ppermute | solution.py:55
  488.1 14.6 %collective-permute-done.37 = bf16[512,1024]{1,0:T(8,128)(2,1)} collective-permute-done((bf16[512,1024]{1,0:T(8,128)(2,1)S(1)}, bf16[512,1024]{1,0:T(8,128)(2,1)}, u32[]{:S(2)}, u32[]{:S(2)}) %collective-permute-start.37) | collective-permute-done | bytes 1048608 | tf_op jit(solution)/shard_map/ppermute | solution.py:55
  502.7 3.5 add_convert_fusion
  506.1 4.4 all-to-all-start.5
  510.6 5.1 add_convert_fusion.6
  515.8 13.1 %collective-permute-done.45 = bf16[256,2048]{1,0:T(8,128)(2,1)} collective-permute-done((bf16[256,2048]{1,0:T(8,128)(2,1)}, bf16[256,2048]{1,0:T(8,128)(2,1)}, u32[]{:S(2)}, u32[]{:S(2)}) %collective-permute-start.45) | collective-permute-done | bytes 1048608 | tf_op jit(solution)/shard_map/ppermute | solution.py:55
  528.8 2.3 collective-permute-start.42
  533.2 3.2 fusion.21
  536.4 3.6 all-to-all-done.5.source
  541.4 20.9 %collective-permute-done.46 = bf16[256,2048]{1,0:T(8,128)(2,1)} collective-permute-done((bf16[256,2048]{1,0:T(8,128)(2,1)}, bf16[256,2048]{1,0:T(8,128)(2,1)}, u32[]{:S(2)}, u32[]{:S(2)}) %collective-permute-start.46) | collective-permute-done | bytes 1048608 | tf_op jit(solution)/shard_map/ppermute | solution.py:55
  562.3 6.0 %fusion.12 = (bf16[1,256,2048]{2,1,0:T(8,128)(2,1)}, bf16[1,256,2048]{2,1,0:T(8,128)(2,1)}) fusion(f32[256]{0:T(256)S(1)} %broadcast_multiply_fusion, f32[256]{0:T(256)S(1)} %broadcast_multiply_fusion.1, f32[256]{0:T(256)S(1)} %add_rsqrt_fusion, f32[256]{0:T(256)S(1)} %broadcast_multiply_fusion.2, bf16[1,256,2048]{2,1,0:T(8,128)(2,1)} %param.19, ...), kind=kLoop, calls=%fused_computation.35 | loop fusion | flops 14155776 | bytes 12595200 | tf_op jit(solution)/shard_map/broadcast_in_dim | solution.py:917
  568.3 2.8 convert_element_type.232
  (315 shorter events, 71.6 us)
Async XLA Ops:
  7.2 62.6 %collective-permute-start.1 = (bf16[256,2048]{1,0:T(8,128)(2,1)}, bf16[256,2048]{1,0:T(8,128)(2,1)}, u32[]{:S(2)}, u32[]{:S(2)}) collective-permute-start(bf16[256,2048]{1,0:T(8,128)(2,1)} %bitcast.180), channel_id=1, source_target_pairs={{0,8},{8,0},{1,9},{9,1},{2,10},{10,2},{3,11},{11,3},{4,12},{12,4},... | collective-permute-start | bytes 3145736 | tf_op jit(solution)/shard_map/ppermute | solution.py:55
  10.3 59.5 %collective-permute-start = (bf16[256,2048]{1,0:T(8,128)(2,1)}, bf16[256,2048]{1,0:T(8,128)(2,1)}, u32[]{:S(2)}, u32[]{:S(2)}) collective-permute-start(bf16[256,2048]{1,0:T(8,128)(2,1)} %bitcast.181), channel_id=1, source_target_pairs={{0,2},{2,0},{1,3},{3,1},{4,6},{6,4},{5,7},{7,5},{8,10},{10,8},{9,1... | collective-permute-start | bytes 3145736 | tf_op jit(solution)/shard_map/ppermute | solution.py:55
  11.8 61.7 %collective-permute-start.3 = (bf16[256,2048]{1,0:T(8,128)(2,1)}, bf16[256,2048]{1,0:T(8,128)(2,1)}, u32[]{:S(2)}, u32[]{:S(2)}) collective-permute-start(bf16[256,2048]{1,0:T(8,128)(2,1)} %bitcast.182), channel_id=1, source_target_pairs={{0,1},{1,0},{2,3},{3,2},{4,5},{5,4},{6,7},{7,6},{8,9},{9,8},{10,11... | collective-permute-start | bytes 3145736 | tf_op jit(solution)/shard_map/ppermute | solution.py:55
  19.2 27.0 %all-to-all-start = ((bf16[32,16,256]{2,1,0:T(8,128)(2,1)}), bf16[32,16,256]{2,1,0:T(8,128)(2,1)S(1)}, u32[]{:S(2)}, u32[]{:S(2)}) async-start(bf16[32,16,256]{2,1,0:T(8,128)(2,1)} %broadcast_in_dim.60), calls=%async_computation | async-start | bytes 524288 | tf_op jit(solution)/shard_map/all_to_all | solution.py:530
  25.5 46.2 %collective-permute-start.7 = (bf16[320,2048]{1,0:T(8,128)(2,1)S(1)}, bf16[320,2048]{1,0:T(8,128)(2,1)}, u32[]{:S(2)}, u32[]{:S(2)}) collective-permute-start(bf16[320,2048]{1,0:T(8,128)(2,1)S(1)} %constant_dynamic-update-slice_fusion.4.b0), channel_id=1, source_target_pairs={{0,4},{4,0},{1,5},{5,1},{2,6},{6,2},{3,7},{7,3},{8,12},{12,8},{9,1... | collective-permute-start | bytes 3932168 | tf_op jit(solution)/shard_map/ppermute | solution.py:55
  28.3 43.9 %collective-permute-start.9 = (bf16[160,2048]{1,0:T(8,128)(2,1)}, bf16[160,2048]{1,0:T(8,128)(2,1)}, u32[]{:S(2)}, u32[]{:S(2)}) collective-permute-start(bf16[160,2048]{1,0:T(8,128)(2,1)} %slice.223), channel_id=1, source_target_pairs={{0,16},{16,0},{1,17},{17,1},{2,18},{18,2},{3,19},{19,3},{4,20},{20... | collective-permute-start | bytes 1966088 | tf_op jit(solution)/shard_map/ppermute | solution.py:55
  46.1 26.1 %all-to-all-start.1 = ((bf16[8,64,768]{2,1,0:T(8,128)(2,1)}), bf16[8,64,768]{2,1,0:T(8,128)(2,1)S(1)}, u32[]{:S(2)}, u32[]{:S(2)}) async-start(bf16[8,64,768]{2,1,0:T(8,128)(2,1)} %get-tuple-element.115), calls=%async_computation.1 | async-start | bytes 1572864 | tf_op jit(solution)/shard_map/all_to_all | solution.py:530
  69.8 26.3 %collective-permute-start.2 = (bf16[256,2048]{1,0:T(8,128)(2,1)}, bf16[256,2048]{1,0:T(8,128)(2,1)}, u32[]{:S(2)}, u32[]{:S(2)}) collective-permute-start(bf16[256,2048]{1,0:T(8,128)(2,1)} %collective-permute-done.1), channel_id=1, source_target_pairs={{0,2},{2,0},{1,3},{3,1},{4,6},{6,4},{5,7},{7,5},{8,10},{10,8},{9,1... | collective-permute-start | bytes 3145736 | tf_op jit(solution)/shard_map/ppermute | solution.py:55
  71.7 24.5 %collective-permute-start.4 = (bf16[256,2048]{1,0:T(8,128)(2,1)}, bf16[256,2048]{1,0:T(8,128)(2,1)}, u32[]{:S(2)}, u32[]{:S(2)}) collective-permute-start(bf16[256,2048]{1,0:T(8,128)(2,1)} %collective-permute-done), channel_id=1, source_target_pairs={{0,1},{1,0},{2,3},{3,2},{4,5},{5,4},{6,7},{7,6},{8,9},{9,8},{10,11... | collective-permute-start | bytes 3145736 | tf_op jit(solution)/shard_map/ppermute | solution.py:55
  71.7 27.2 %collective-permute-start.5 = (bf16[256,2048]{1,0:T(8,128)(2,1)}, bf16[256,2048]{1,0:T(8,128)(2,1)}, u32[]{:S(2)}, u32[]{:S(2)}) collective-permute-start(bf16[256,2048]{1,0:T(8,128)(2,1)} %collective-permute-done.1), channel_id=1, source_target_pairs={{0,1},{1,0},{2,3},{3,2},{4,5},{5,4},{6,7},{7,6},{8,9},{9,8},{10,11... | collective-permute-start | bytes 3145736 | tf_op jit(solution)/shard_map/ppermute | solution.py:55
  72.2 91.5 %copy-start.3 = (bf16[8,64,768]{2,1,0:T(8,128)(2,1)}, bf16[8,64,768]{2,1,0:T(8,128)(2,1)S(1)}, u32[]{:S(2)}) copy-start(bf16[8,64,768]{2,1,0:T(8,128)(2,1)S(1)} %all-to-all-done.1) | copy-start | bytes 2359300
  72.2 23.8 %collective-permute-start.8 = (bf16[2,256,768]{2,1,0:T(8,128)(2,1)S(1)}, bf16[2,256,768]{2,1,0:T(8,128)(2,1)S(1)}, u32[]{:S(2)}, u32[]{:S(2)}) collective-permute-start(bf16[2,256,768]{2,1,0:T(8,128)(2,1)S(1)} %bitcast.158), channel_id=1, source_target_pairs={{0,4},{4,0},{1,5},{5,1},{2,6},{6,2},{3,7},{7,3},{8,12},{12,8},{9,1... | collective-permute-start | bytes 2359304 | tf_op jit(solution)/shard_map/ppermute | solution.py:55
  73.5 60.2 %collective-permute-start.14 = (bf16[256,2048]{1,0:T(8,128)(2,1)}, bf16[256,2048]{1,0:T(8,128)(2,1)}, u32[]{:S(2)}, u32[]{:S(2)}) collective-permute-start(bf16[256,2048]{1,0:T(8,128)(2,1)} %bitcast.11), channel_id=1, source_target_pairs={{0,8},{8,0},{1,9},{9,1},{2,10},{10,2},{3,11},{11,3},{4,12},{12,4},... | collective-permute-start | bytes 3145736 | tf_op jit(solution)/shard_map/ppermute | solution.py:55
  78.4 75.9 %all-to-all-start.2 = ((bf16[8,64,1024]{2,1,0:T(8,128)(2,1)}), bf16[8,64,1024]{2,1,0:T(8,128)(2,1)}, u32[]{:S(2)}, u32[]{:S(2)}) async-start(bf16[8,64,1024]{2,1,0:T(8,128)(2,1)} %get-tuple-element.142), calls=%async_computation.2 | async-start | bytes 2097152 | tf_op jit(solution)/shard_map/all_to_all | solution.py:530
  82.7 20.7 %copy-start.30 = (bf16[1,256,2048]{2,1,0:T(8,128)(2,1)S(1)}, bf16[1,256,2048]{2,1,0:T(8,128)(2,1)}, u32[]{:S(2)}) copy-start(bf16[1,256,2048]{2,1,0:T(8,128)(2,1)} %param.18) | copy-start | bytes 3145732
  82.7 175.6 %all-gather.2.cloned.1.call-start = ((), (), s32[]{:S(2)}) async-start(), calls=%async_computation.7 | async-start | bytes 5242880 | tf_op jit(solution)/shard_map/all_gather | solution.py:742
  96.1 36.5 %collective-permute-start.10 = (bf16[2,256,768]{2,1,0:T(8,128)(2,1)S(1)}, bf16[2,256,768]{2,1,0:T(8,128)(2,1)}, u32[]{:S(2)}, u32[]{:S(2)}) collective-permute-start(bf16[2,256,768]{2,1,0:T(8,128)(2,1)S(1)} %bitcast.159), channel_id=1, source_target_pairs={{0,16},{16,0},{1,17},{17,1},{2,18},{18,2},{3,19},{19,3},{4,20},{20... | collective-permute-start | bytes 2359304 | tf_op jit(solution)/shard_map/ppermute | solution.py:55
  96.1 67.6 %copy-start.24 = (bf16[2,256,768]{2,1,0:T(8,128)(2,1)}, bf16[2,256,768]{2,1,0:T(8,128)(2,1)S(1)}, u32[]{:S(2)}) copy-start(bf16[2,256,768]{2,1,0:T(8,128)(2,1)S(1)} %collective-permute-done.8.w1.q1) | copy-start | bytes 2359300
  96.1 40.1 %collective-permute-start.6 = (bf16[256,2048]{1,0:T(8,128)(2,1)}, bf16[256,2048]{1,0:T(8,128)(2,1)S(1)}, u32[]{:S(2)}, u32[]{:S(2)}) collective-permute-start(bf16[256,2048]{1,0:T(8,128)(2,1)} %collective-permute-done.2), channel_id=1, source_target_pairs={{0,1},{1,0},{2,3},{3,2},{4,5},{5,4},{6,7},{7,6},{8,9},{9,8},{10,11... | collective-permute-start | bytes 3145736 | tf_op jit(solution)/shard_map/ppermute | solution.py:55
  96.2 36.4 %collective-permute-start.11 = (bf16[160,2048]{1,0:T(8,128)(2,1)}, bf16[160,2048]{1,0:T(8,128)(2,1)S(1)}, u32[]{:S(2)}, u32[]{:S(2)}) collective-permute-start(bf16[160,2048]{1,0:T(8,128)(2,1)} %collective-permute-done.9), channel_id=1, source_target_pairs={{0,4},{4,0},{1,5},{5,1},{2,6},{6,2},{3,7},{7,3},{8,12},{12,8},{9,1... | collective-permute-start | bytes 1966088 | tf_op jit(solution)/shard_map/ppermute | solution.py:55
  98.9 35.9 %collective-permute-start.13 = (bf16[256,2048]{1,0:T(8,128)(2,1)}, bf16[256,2048]{1,0:T(8,128)(2,1)}, u32[]{:S(2)}, u32[]{:S(2)}) collective-permute-start(bf16[256,2048]{1,0:T(8,128)(2,1)} %bitcast.11), channel_id=1, source_target_pairs={{0,2},{2,0},{1,3},{3,1},{4,6},{6,4},{5,7},{7,5},{8,10},{10,8},{9,1... | collective-permute-start | bytes 3145736 | tf_op jit(solution)/shard_map/ppermute | solution.py:55
  103.3 29.4 %copy-start.48 = (bf16[64,2048]{1,0:T(8,128)(2,1)S(1)}, bf16[64,2048]{1,0:T(8,128)(2,1)}, u32[]{:S(2)}) copy-start(bf16[64,2048]{1,0:T(8,128)(2,1)} %param.26) | copy-start | bytes 786436
  132.6 20.2 %collective-permute-start.16 = (bf16[256,2048]{1,0:T(8,128)(2,1)}, bf16[256,2048]{1,0:T(8,128)(2,1)S(1)}, u32[]{:S(2)}, u32[]{:S(2)}) collective-permute-start(bf16[256,2048]{1,0:T(8,128)(2,1)} %bitcast.11), channel_id=1, source_target_pairs={{0,1},{1,0},{2,3},{3,2},{4,5},{5,4},{6,7},{7,6},{8,9},{9,8},{10,11... | collective-permute-start | bytes 3145736 | tf_op jit(solution)/shard_map/ppermute | solution.py:55
  132.6 30.8 %collective-permute-start.21 = (bf16[160,2048]{1,0:T(8,128)(2,1)}, bf16[160,2048]{1,0:T(8,128)(2,1)}, u32[]{:S(2)}, u32[]{:S(2)}) collective-permute-start(bf16[160,2048]{1,0:T(8,128)(2,1)} %slice.179), channel_id=1, source_target_pairs={{0,16},{16,0},{1,17},{17,1},{2,18},{18,2},{3,19},{19,3},{4,20},{20... | collective-permute-start | bytes 1966088 | tf_op jit(solution)/shard_map/ppermute | solution.py:55
  133.7 29.7 %collective-permute-start.12 = (bf16[2,256,768]{2,1,0:T(8,128)(2,1)}, bf16[2,256,768]{2,1,0:T(8,128)(2,1)}, u32[]{:S(2)}, u32[]{:S(2)}) collective-permute-start(bf16[2,256,768]{2,1,0:T(8,128)(2,1)} %collective-permute-done.10.w2.q2), channel_id=1, source_target_pairs={{0,4},{4,0},{1,5},{5,1},{2,6},{6,2},{3,7},{7,3},{8,12},{12,8},{9,1... | collective-permute-start | bytes 2359304 | tf_op jit(solution)/shard_map/ppermute | solution.py:55
  134.8 41.9 %collective-permute-start.15 = (bf16[256,2048]{1,0:T(8,128)(2,1)}, bf16[256,2048]{1,0:T(8,128)(2,1)}, u32[]{:S(2)}, u32[]{:S(2)}) collective-permute-start(bf16[256,2048]{1,0:T(8,128)(2,1)} %collective-permute-done.14), channel_id=1, source_target_pairs={{0,2},{2,0},{1,3},{3,1},{4,6},{6,4},{5,7},{7,5},{8,10},{10,8},{9,1... | collective-permute-start | bytes 3145736 | tf_op jit(solution)/shard_map/ppermute | solution.py:55
  136.1 40.7 %collective-permute-start.17 = (bf16[256,2048]{1,0:T(8,128)(2,1)}, bf16[256,2048]{1,0:T(8,128)(2,1)}, u32[]{:S(2)}, u32[]{:S(2)}) collective-permute-start(bf16[256,2048]{1,0:T(8,128)(2,1)} %collective-permute-done.13), channel_id=1, source_target_pairs={{0,1},{1,0},{2,3},{3,2},{4,5},{5,4},{6,7},{7,6},{8,9},{9,8},{10,11... | collective-permute-start | bytes 3145736 | tf_op jit(solution)/shard_map/ppermute | solution.py:55
  152.8 23.9 %copy-start.23 = (f32[2048,1]{1,0:T(8,128)}, f32[2048,1]{1,0:T(8,128)S(1)}, u32[]{:S(2)}) copy-start(f32[2048,1]{1,0:T(8,128)S(1)} %get-tuple-element.164.scale) | copy-start | bytes 24580
  152.8 29.9 %collective-permute-start.18 = (bf16[256,2048]{1,0:T(8,128)(2,1)}, bf16[256,2048]{1,0:T(8,128)(2,1)}, u32[]{:S(2)}, u32[]{:S(2)}) collective-permute-start(bf16[256,2048]{1,0:T(8,128)(2,1)} %collective-permute-done.14), channel_id=1, source_target_pairs={{0,1},{1,0},{2,3},{3,2},{4,5},{5,4},{6,7},{7,6},{8,9},{9,8},{10,11... | collective-permute-start | bytes 3145736 | tf_op jit(solution)/shard_map/ppermute | solution.py:55
  163.4 87.7 %collective-permute-start.22 = (bf16[160,2048]{1,0:T(8,128)(2,1)}, bf16[160,2048]{1,0:T(8,128)(2,1)S(1)}, u32[]{:S(2)}, u32[]{:S(2)}) collective-permute-start(bf16[160,2048]{1,0:T(8,128)(2,1)} %collective-permute-done.21), channel_id=1, source_target_pairs={{0,4},{4,0},{1,5},{5,1},{2,6},{6,2},{3,7},{7,3},{8,12},{12,8},{9,1... | collective-permute-start | bytes 1966088 | tf_op jit(solution)/shard_map/ppermute | solution.py:55
  176.7 7.7 %collective-permute-start.19 = (bf16[256,2048]{1,0:T(8,128)(2,1)}, bf16[256,2048]{1,0:T(8,128)(2,1)S(1)}, u32[]{:S(2)}, u32[]{:S(2)}) collective-permute-start(bf16[256,2048]{1,0:T(8,128)(2,1)} %collective-permute-done.15), channel_id=1, source_target_pairs={{0,1},{1,0},{2,3},{3,2},{4,5},{5,4},{6,7},{7,6},{8,9},{9,8},{10,11... | collective-permute-start | bytes 3145736 | tf_op jit(solution)/shard_map/ppermute | solution.py:55
  176.8 7.2 %collective-permute-start.20 = (bf16[2,64,2048]{2,1,0:T(8,128)(2,1)}, bf16[2,64,2048]{2,1,0:T(8,128)(2,1)S(1)}, u32[]{:S(2)}, u32[]{:S(2)}) collective-permute-start(bf16[2,64,2048]{2,1,0:T(8,128)(2,1)} %fusion.13), channel_id=1, source_target_pairs={{0,1},{1,0},{2,3},{3,2},{4,5},{5,4},{6,7},{7,6},{8,9},{9,8},{10,11... | collective-permute-start | bytes 1572872 | tf_op jit(solution)/shard_map/ppermute | solution.py:55
  195.9 35.1 %copy-start.38 = (bf16[1024,2048]{1,0:T(8,128)(2,1)S(1)}, bf16[1024,2048]{1,0:T(8,128)(2,1)}, u32[]{:S(2)}) copy-start(bf16[1024,2048]{1,0:T(8,128)(2,1)} %copy-done.37) | copy-start | bytes 12582916
  249.7 5.5 collective-permute-start.30
  251.1 39.2 %collective-permute-start.23 = (bf16[512,768]{1,0:T(8,128)(2,1)}, bf16[512,768]{1,0:T(8,128)(2,1)S(1)}, u32[]{:S(2)}, u32[]{:S(2)}) collective-permute-start(bf16[512,768]{1,0:T(8,128)(2,1)} %get-tuple-element.152), channel_id=1, source_target_pairs={{0,4},{4,0},{1,5},{5,1},{2,6},{6,2},{3,7},{7,3},{8,12},{12,8},{9,1... | collective-permute-start | bytes 2359304 | tf_op jit(solution)/shard_map/ppermute | solution.py:55
  306.6 38.5 %collective-permute-start.24 = (bf16[512,1024]{1,0:T(8,128)(2,1)}, bf16[512,1024]{1,0:T(8,128)(2,1)}, u32[]{:S(2)}, u32[]{:S(2)}) collective-permute-start(bf16[512,1024]{1,0:T(8,128)(2,1)} %get-tuple-element.156), channel_id=1, source_target_pairs={{0,4},{4,0},{1,5},{5,1},{2,6},{6,2},{3,7},{7,3},{8,12},{12,8},{9,1... | collective-permute-start | bytes 3145736 | tf_op jit(solution)/shard_map/ppermute | solution.py:55
  307.9 37.2 %collective-permute-start.25 = (bf16[512,768]{1,0:T(8,128)(2,1)}, bf16[512,768]{1,0:T(8,128)(2,1)}, u32[]{:S(2)}, u32[]{:S(2)}) collective-permute-start(bf16[512,768]{1,0:T(8,128)(2,1)} %add_convert_fusion.9), channel_id=1, source_target_pairs={{0,16},{16,0},{1,17},{17,1},{2,18},{18,2},{3,19},{19,3},{4,20},{20... | collective-permute-start | bytes 2359304 | tf_op jit(solution)/shard_map/ppermute | solution.py:55
  367.6 32.4 %collective-permute-start.26 = (bf16[256,1024]{1,0:T(8,128)(2,1)}, bf16[256,1024]{1,0:T(8,128)(2,1)}, u32[]{:S(2)}, u32[]{:S(2)}) collective-permute-start(bf16[256,1024]{1,0:T(8,128)(2,1)} %get-tuple-element.159), channel_id=1, source_target_pairs={{0,16},{16,0},{1,17},{17,1},{2,18},{18,2},{3,19},{19,3},{4,20},{20... | collective-permute-start | bytes 1572872 | tf_op jit(solution)/shard_map/ppermute | solution.py:55
  386.7 13.3 %all-to-all-start.3 = ((f32[32,1,768]{2,1,0:T(1,128)}), f32[32,1,768]{2,1,0:T(1,128)S(1)}, u32[]{:S(2)}, u32[]{:S(2)}) async-start(f32[32,1,768]{2,1,0:T(1,128)} %copy.92), calls=%async_computation.3 | async-start | bytes 196608 | tf_op jit(solution)/shard_map/all_to_all | solution.py:530
  392.2 176.1 %reduce-scatter.2.cloned.1.call-start = ((), (), s32[]{:S(2)}) async-start(), calls=%async_computation.8 | async-start | bytes 5242880 | tf_op jit(solution)/shard_map/reduce_scatter | solution.py:746
  396.8 23.3 %collective-permute-start.38 = (bf16[256,2048]{1,0:T(8,128)(2,1)}, bf16[256,2048]{1,0:T(8,128)(2,1)}, u32[]{:S(2)}, u32[]{:S(2)}) collective-permute-start(bf16[256,2048]{1,0:T(8,128)(2,1)} %get-tuple-element.188), channel_id=1, source_target_pairs={{0,1},{1,0},{2,3},{3,2},{4,5},{5,4},{6,7},{7,6},{8,9},{9,8},{10,11... | collective-permute-start | bytes 3145736 | tf_op jit(solution)/shard_map/ppermute | solution.py:55
  397.0 19.2 %collective-permute-start.33 = (bf16[2,64,2048]{2,1,0:T(8,128)(2,1)}, bf16[2,64,2048]{2,1,0:T(8,128)(2,1)}, u32[]{:S(2)}, u32[]{:S(2)}) collective-permute-start(bf16[2,64,2048]{2,1,0:T(8,128)(2,1)} %slice_bitcast_fusion.1), channel_id=1, source_target_pairs={{0,4},{4,0},{1,5},{5,1},{2,6},{6,2},{3,7},{7,3},{8,12},{12,8},{9,1... | collective-permute-start | bytes 1572872 | tf_op jit(solution)/shard_map/ppermute | solution.py:55
  398.9 29.2 %collective-permute-start.31 = (bf16[256,2048]{1,0:T(8,128)(2,1)}, bf16[256,2048]{1,0:T(8,128)(2,1)}, u32[]{:S(2)}, u32[]{:S(2)}) collective-permute-start(bf16[256,2048]{1,0:T(8,128)(2,1)} %get-tuple-element.174), channel_id=1, source_target_pairs={{0,1},{1,0},{2,3},{3,2},{4,5},{5,4},{6,7},{7,6},{8,9},{9,8},{10,11... | collective-permute-start | bytes 3145736 | tf_op jit(solution)/shard_map/ppermute | solution.py:55
  399.1 29.1 %collective-permute-start.27 = (bf16[256,2048]{1,0:T(8,128)(2,1)}, bf16[256,2048]{1,0:T(8,128)(2,1)}, u32[]{:S(2)}, u32[]{:S(2)}) collective-permute-start(bf16[256,2048]{1,0:T(8,128)(2,1)} %get-tuple-element.170), channel_id=1, source_target_pairs={{0,1},{1,0},{2,3},{3,2},{4,5},{5,4},{6,7},{7,6},{8,9},{9,8},{10,11... | collective-permute-start | bytes 3145736 | tf_op jit(solution)/shard_map/ppermute | solution.py:55
  416.2 47.0 %collective-permute-start.36 = (bf16[512,768]{1,0:T(8,128)(2,1)S(1)}, bf16[512,768]{1,0:T(8,128)(2,1)}, u32[]{:S(2)}, u32[]{:S(2)}) collective-permute-start(bf16[512,768]{1,0:T(8,128)(2,1)S(1)} %copy-done.27), channel_id=1, source_target_pairs={{0,4},{4,0},{1,5},{5,1},{2,6},{6,2},{3,7},{7,3},{8,12},{12,8},{9,1... | collective-permute-start | bytes 2359304 | tf_op jit(solution)/shard_map/ppermute | solution.py:55
  422.1 23.3 %collective-permute-start.39 = (bf16[256,2048]{1,0:T(8,128)(2,1)S(1)}, bf16[256,2048]{1,0:T(8,128)(2,1)S(1)}, u32[]{:S(2)}, u32[]{:S(2)}) collective-permute-start(bf16[256,2048]{1,0:T(8,128)(2,1)S(1)} %add_convert_fusion.3), channel_id=1, source_target_pairs={{0,2},{2,0},{1,3},{3,1},{4,6},{6,4},{5,7},{7,5},{8,10},{10,8},{9,1... | collective-permute-start | bytes 3145736 | tf_op jit(solution)/shard_map/ppermute | solution.py:55
  423.5 37.2 %collective-permute-start.34 = (bf16[64,2048]{1,0:T(8,128)(2,1)S(1)}, bf16[64,2048]{1,0:T(8,128)(2,1)S(1)}, u32[]{:S(2)}, u32[]{:S(2)}) collective-permute-start(bf16[64,2048]{1,0:T(8,128)(2,1)S(1)} %fusion.19), channel_id=1, source_target_pairs={{0,16},{16,0},{1,17},{17,1},{2,18},{18,2},{3,19},{19,3},{4,20},{20... | collective-permute-start | bytes 786440 | tf_op jit(solution)/shard_map/ppermute | solution.py:55
  428.1 41.5 %collective-permute-start.43 = (bf16[256,2048]{1,0:T(8,128)(2,1)}, bf16[256,2048]{1,0:T(8,128)(2,1)}, u32[]{:S(2)}, u32[]{:S(2)}) collective-permute-start(bf16[256,2048]{1,0:T(8,128)(2,1)} %get-tuple-element.193), channel_id=1, source_target_pairs={{0,1},{1,0},{2,3},{3,2},{4,5},{5,4},{6,7},{7,6},{8,9},{9,8},{10,11... | collective-permute-start | bytes 3145736 | tf_op jit(solution)/shard_map/ppermute | solution.py:55
  428.2 41.7 %collective-permute-start.28 = (bf16[256,2048]{1,0:T(8,128)(2,1)}, bf16[256,2048]{1,0:T(8,128)(2,1)}, u32[]{:S(2)}, u32[]{:S(2)}) collective-permute-start(bf16[256,2048]{1,0:T(8,128)(2,1)} %get-tuple-element.171), channel_id=1, source_target_pairs={{0,1},{1,0},{2,3},{3,2},{4,5},{5,4},{6,7},{7,6},{8,9},{9,8},{10,11... | collective-permute-start | bytes 3145736 | tf_op jit(solution)/shard_map/ppermute | solution.py:55
  449.4 23.7 %collective-permute-start.40 = (bf16[256,2048]{1,0:T(8,128)(2,1)}, bf16[256,2048]{1,0:T(8,128)(2,1)}, u32[]{:S(2)}, u32[]{:S(2)}) collective-permute-start(bf16[256,2048]{1,0:T(8,128)(2,1)} %get-tuple-element.190), channel_id=1, source_target_pairs={{0,2},{2,0},{1,3},{3,1},{4,6},{6,4},{5,7},{7,5},{8,10},{10,8},{9,1... | collective-permute-start | bytes 3145736 | tf_op jit(solution)/shard_map/ppermute | solution.py:55
  460.7 26.8 %collective-permute-start.35 = (bf16[256,1024]{1,0:T(8,128)(2,1)S(1)}, bf16[256,1024]{1,0:T(8,128)(2,1)}, u32[]{:S(2)}, u32[]{:S(2)}) collective-permute-start(bf16[256,1024]{1,0:T(8,128)(2,1)S(1)} %copy-done.51), channel_id=1, source_target_pairs={{0,16},{16,0},{1,17},{17,1},{2,18},{18,2},{3,19},{19,3},{4,20},{20... | collective-permute-start | bytes 1572872 | tf_op jit(solution)/shard_map/ppermute | solution.py:55
  463.3 47.3 %collective-permute-start.32 = (bf16[256,2048]{1,0:T(8,128)(2,1)}, bf16[256,2048]{1,0:T(8,128)(2,1)}, u32[]{:S(2)}, u32[]{:S(2)}) collective-permute-start(bf16[256,2048]{1,0:T(8,128)(2,1)} %get-tuple-element.175), channel_id=1, source_target_pairs={{0,1},{1,0},{2,3},{3,2},{4,5},{5,4},{6,7},{7,6},{8,9},{9,8},{10,11... | collective-permute-start | bytes 3145736 | tf_op jit(solution)/shard_map/ppermute | solution.py:55
  465.9 40.2 %all-to-all-start.4 = ((bf16[8,64,768]{2,1,0:T(8,128)(2,1)}), bf16[8,64,768]{2,1,0:T(8,128)(2,1)S(1)}, u32[]{:S(2)}, u32[]{:S(2)}) async-start(bf16[8,64,768]{2,1,0:T(8,128)(2,1)} %bitcast.188), calls=%async_computation.4 | async-start | bytes 1572864 | tf_op jit(solution)/shard_map/all_to_all | solution.py:530
  469.6 33.0 %collective-permute-start.37 = (bf16[512,1024]{1,0:T(8,128)(2,1)S(1)}, bf16[512,1024]{1,0:T(8,128)(2,1)}, u32[]{:S(2)}, u32[]{:S(2)}) collective-permute-start(bf16[512,1024]{1,0:T(8,128)(2,1)S(1)} %copy-done.21), channel_id=1, source_target_pairs={{0,4},{4,0},{1,5},{5,1},{2,6},{6,2},{3,7},{7,3},{8,12},{12,8},{9,1... | collective-permute-start | bytes 3145736 | tf_op jit(solution)/shard_map/ppermute | solution.py:55
  469.8 40.8 %collective-permute-start.44 = (bf16[256,2048]{1,0:T(8,128)(2,1)}, bf16[256,2048]{1,0:T(8,128)(2,1)}, u32[]{:S(2)}, u32[]{:S(2)}) collective-permute-start(bf16[256,2048]{1,0:T(8,128)(2,1)} %get-tuple-element.194), channel_id=1, source_target_pairs={{0,1},{1,0},{2,3},{3,2},{4,5},{5,4},{6,7},{7,6},{8,9},{9,8},{10,11... | collective-permute-start | bytes 3145736 | tf_op jit(solution)/shard_map/ppermute | solution.py:55
  473.1 37.5 %collective-permute-start.41 = (bf16[256,2048]{1,0:T(8,128)(2,1)}, bf16[256,2048]{1,0:T(8,128)(2,1)}, u32[]{:S(2)}, u32[]{:S(2)}) collective-permute-start(bf16[256,2048]{1,0:T(8,128)(2,1)} %add_convert_fusion.5), channel_id=1, source_target_pairs={{0,2},{2,0},{1,3},{3,1},{4,6},{6,4},{5,7},{7,5},{8,10},{10,8},{9,1... | collective-permute-start | bytes 3145736 | tf_op jit(solution)/shard_map/ppermute | solution.py:55
  487.5 41.3 %collective-permute-start.45 = (bf16[256,2048]{1,0:T(8,128)(2,1)}, bf16[256,2048]{1,0:T(8,128)(2,1)}, u32[]{:S(2)}, u32[]{:S(2)}) collective-permute-start(bf16[256,2048]{1,0:T(8,128)(2,1)} %get-tuple-element.196), channel_id=1, source_target_pairs={{0,8},{8,0},{1,9},{9,1},{2,10},{10,2},{3,11},{11,3},{4,12},{12,4},... | collective-permute-start | bytes 3145736 | tf_op jit(solution)/shard_map/ppermute | solution.py:55
  488.1 83.0 %copy-start.55 = (f32[64]{0:T(128)}, f32[64]{0:T(128)S(1)}, u32[]{:S(2)}) copy-start(f32[64]{0:T(128)S(1)} %get-tuple-element.282) | copy-start | bytes 772
  502.7 38.8 %collective-permute-start.29 = (bf16[256,2048]{1,0:T(8,128)(2,1)}, bf16[256,2048]{1,0:T(8,128)(2,1)}, u32[]{:S(2)}, u32[]{:S(2)}) collective-permute-start(bf16[256,2048]{1,0:T(8,128)(2,1)} %get-tuple-element.172), channel_id=1, source_target_pairs={{0,1},{1,0},{2,3},{3,2},{4,5},{5,4},{6,7},{7,6},{8,9},{9,8},{10,11... | collective-permute-start | bytes 3145736 | tf_op jit(solution)/shard_map/ppermute | solution.py:55
  506.1 33.9 %all-to-all-start.5 = ((bf16[8,64,1024]{2,1,0:T(8,128)(2,1)}), bf16[8,64,1024]{2,1,0:T(8,128)(2,1)S(1)}, u32[]{:S(2)}, u32[]{:S(2)}) async-start(bf16[8,64,1024]{2,1,0:T(8,128)(2,1)} %bitcast.187), calls=%async_computation.5 | async-start | bytes 2097152 | tf_op jit(solution)/shard_map/all_to_all | solution.py:530
  510.6 20.5 %copy-start.45 = (f32[2,64,2048]{2,1,0:T(8,128)S(1)}, f32[2,64,2048]{2,1,0:T(8,128)}, u32[]{:S(2)}) copy-start(f32[2,64,2048]{2,1,0:T(8,128)} %copy-done.44) | copy-start | bytes 3145732
  510.6 20.5 %copy-start.54 = (bf16[64,2048]{1,0:T(8,128)(2,1)S(1)}, bf16[64,2048]{1,0:T(8,128)(2,1)}, u32[]{:S(2)}) copy-start(bf16[64,2048]{1,0:T(8,128)(2,1)} %copy-done.53) | copy-start | bytes 786436
  528.8 33.5 %collective-permute-start.46 = (bf16[256,2048]{1,0:T(8,128)(2,1)}, bf16[256,2048]{1,0:T(8,128)(2,1)}, u32[]{:S(2)}, u32[]{:S(2)}) collective-permute-start(bf16[256,2048]{1,0:T(8,128)(2,1)} %get-tuple-element.197), channel_id=1, source_target_pairs={{0,8},{8,0},{1,9},{9,1},{2,10},{10,2},{3,11},{11,3},{4,12},{12,4},... | collective-permute-start | bytes 3145736 | tf_op jit(solution)/shard_map/ppermute | solution.py:55
  528.8 33.5 %collective-permute-start.42 = (bf16[256,2048]{1,0:T(8,128)(2,1)}, bf16[256,2048]{1,0:T(8,128)(2,1)}, u32[]{:S(2)}, u32[]{:S(2)}) collective-permute-start(bf16[256,2048]{1,0:T(8,128)(2,1)} %get-tuple-element.192), channel_id=1, source_target_pairs={{0,2},{2,0},{1,3},{3,1},{4,6},{6,4},{5,7},{7,5},{8,10},{10,8},{9,1... | collective-permute-start | bytes 3145736 | tf_op jit(solution)/shard_map/ppermute | solution.py:55
  (47 other events, 223.4 us)
Sparse Core Ops, SparseCore 0:
  154.4 86.8 all-gather.1
  399.1 112.9 reduce-scatter.1

commit v5 on v4

--- a/solution.py
+++ b/solution.py
@@ -33,7 +33,7 @@
     "zl": ["iz", "uz", "pz", "oz"],
     "core": ["i0", "i1", "i2", "i3", "u0", "u1", "u2", "u3", "dc", "gd", "pc3", "pc1", "pc2", "pc0", "oc3", "oc1", "oc2", "oc0"],
     "y": ["An", "Wn", "Af0", "Wf", "Af1", "W3", "T3", "D1", "W1", "T1"],
-    "zh": ["A0z", "Wz", "A1z", "zW", "zT0", "zD", "zT1"],
+    "zh": ["A0z", "Wz", "A1z", "zW", "zT0", "zT1", "zD"],
     "sc": ["Tg", "Br"],
     "depth": {"core": 3},
     "ties": {

time: 586 us -> 599 us (1.022)
  waiting for transfers between devices: 166 us -> 181 us
  starting transfers between devices: 64.2 us -> 56.8 us
    all_to_all x6, waiting for transfers between devices: 14.4 us -> 26.9 us  [swap(): return lax.all_to_all(v, axes, 0, 0, tiled=True)]
    ppermute x47, starting transfers between devices: 38.5 us -> 31.3 us  [flip(): return lax.ppermute(v, axis, [(0, 1), (1, 0)])]
    unnamed x131 -> x121, local copies, waits for them, and re-layouts: 33.2 us -> 32.2 us
  transfers between devices with their start and end apart: 55 -> 55, of which waited for: 13 -> 13; matrix products, arithmetic and copies ran while one was open for 17% -> 18% of each run, Pallas kernels for 29% -> 32%
where the time goes in v5:
time: 599 us; the launch traced here: 590 us
  Pallas kernels  203 us (34%)
  waiting for transfers between devices  181 us (30%)
  local copies, waits for them, and re-layouts  62.5 us (10%)
  other arithmetic  60.5 us (10%)
  starting transfers between devices  56.8 us (9%)
  between operations  20.6 us (3%)
    ppermute x47, waiting for transfers between devices, flip(): return lax.ppermute(v, axis, [(0, 1), (1, 0)])  154 us
    pallas_call x2, Pallas kernels, pull_product(): call(pull_kernel, (steps,), [*[half_rows(2 * HD)] * 3, half_rows(UNITS),...  35.5 us
    pallas_call x1, Pallas kernels, attention(): call(attention_kernel, (2, 2, length // BLK), [part(0), whole(2), whole(4...  35 us
    unnamed x121, local copies, waits for them, and re-layouts  32.2 us
    ppermute x47, starting transfers between devices, flip(): return lax.ppermute(v, axis, [(0, 1), (1, 0)])  31.3 us
    pallas_call x1, Pallas kernels, hidden_products(): call(functools.partial(hidden_kernel, tall - BLK), (n // BLK,), [rows_of(...  29.2 us
    pallas_call x2, Pallas kernels, rows_grad(): call(functools.partial(rows_grad_kernel, len(rights)), (2 * len(order),),...  28.6 us
    all_to_all x6, waiting for transfers between devices, swap(): return lax.all_to_all(v, axes, 0, 0, tiled=True)  26.9 us
  transfers between devices with their start and end apart: 55, of which 13 were waited for; matrix products, arithmetic and copies ran while one was open for 18% of the time, Pallas kernels for 32%

profile of v5, /device:TPU:0, one launch (start us, length us, event | category | flops | bytes accessed | tf_op | source)
XLA Modules:
  0.0 590.0 jit_solution(15766885992979333660)
XLA Ops:
  7.2 3.1 collective-permute-start.1
  10.3 1.5 collective-permute-start
  19.2 4.0 all-to-all-start
  25.5 1.8 collective-permute-start.7
  28.3 2.4 collective-permute-start.9
  30.6 2.0 slice.179
  37.2 1.6 fusion.8
  38.9 7.3 %all-to-all-done = bf16[32,16,256]{2,1,0:T(8,128)(2,1)S(1)} async-done(((bf16[32,16,256]{2,1,0:T(8,128)(2,1)}), bf16[32,16,256]{2,1,0:T(8,128)(2,1)S(1)}, u32[]{:S(2)}, u32[]{:S(2)}) %all-to-all-start) | async-done | bytes 262176 | tf_op jit(solution)/shard_map/all_to_all | solution.py:530
  46.2 3.5 all-to-all-start.1
  57.2 5.5 fusion.18
  62.8 1.9 reshape.228.pq
  64.7 1.9 broadcast_in_dim_reshape.13.eq
  69.9 1.9 collective-permute-start.2
  73.6 1.6 collective-permute-start.14
  75.1 2.4 constant_dynamic-update-slice_fusion.3
  78.5 4.3 all-to-all-start.2
  82.8 13.3 %collective-permute-done.2 = bf16[256,2048]{1,0:T(8,128)(2,1)} collective-permute-done((bf16[256,2048]{1,0:T(8,128)(2,1)}, bf16[256,2048]{1,0:T(8,128)(2,1)}, u32[]{:S(2)}, u32[]{:S(2)}) %collective-permute-start.2) | collective-permute-done | bytes 1048608 | tf_op jit(solution)/shard_map/ppermute | solution.py:55
  96.7 2.3 constant_dynamic-update-slice_fusion.2
  99.0 2.1 collective-permute-start.13
  101.0 2.4 constant_dynamic-update-slice_fusion.1
  103.4 3.7 pad_maximum_fusion.near.tokens
  107.1 25.6 %collective-permute-done.10.w2.q2 = bf16[2,256,768]{2,1,0:T(8,128)(2,1)} collective-permute-done((bf16[2,256,768]{2,1,0:T(8,128)(2,1)S(1)}, bf16[2,256,768]{2,1,0:T(8,128)(2,1)}, u32[]{:S(2)}, u32[]{:S(2)}) %collective-permute-start.10) | collective-permute-done | bytes 786464 | tf_op jit(solution)/shard_map/ppermute | solution.py:55
  137.5 14.4 %shard_map.265 = (bf16[2048,2048]{1,0:T(8,128)(2,1)}, bf16[2048,2048]{1,0:T(8,128)(2,1)}, f32[2048,1]{1,0:T(8,128)S(1)}, f32[2048,1]{1,0:T(8,128)S(1)}) custom-call(bf16[1024,2048]{1,0:T(8,128)(2,1)} %pad_maximum_fusion.near.tokens, bf16[1024,2048]{1,0:T(8,128)(2,1)} %constant_dynamic-update-slice_fusion.far.tokens, f32[4,2048]{1,0:T(4,128)S(1)} %pad_maximum_fusion.5.gains), custom_call_target="tpu_custom_call" | custom-call | flops 41943040 | bytes 25165824 | tf_op jit(solution)/shard_map/pallas_call | solution.py:156
  154.6 8.9 %collective-permute-done.21 = bf16[160,2048]{1,0:T(8,128)(2,1)} collective-permute-done((bf16[160,2048]{1,0:T(8,128)(2,1)}, bf16[160,2048]{1,0:T(8,128)(2,1)}, u32[]{:S(2)}, u32[]{:S(2)}) %collective-permute-start.21) | collective-permute-done | bytes 655392 | tf_op jit(solution)/shard_map/ppermute | solution.py:55
  163.8 13.0 %shard_map.266 = f32[2048,768]{1,0:T(8,128)} custom-call(s32[2]{0:T(128)S(1)} %scatter.4.base, bf16[2048,2048]{1,0:T(8,128)(2,1)} %get-tuple-element.135.v, bf16[2,256,768]{2,1,0:T(8,128)(2,1)S(1)} %bitcast.160, bf16[2,256,768]{2,1,0:T(8,128)(2,1)S(1)} %collective-permute-done.8.w1.q1, bf16[2,256,768]{2,1,0:T(8,128)(2,1)} %collective-permute-done.10.w2.q2, ...), custom_call_target="tpu_custom_call" | custom-call | flops 6442450944 | bytes 17825792 | tf_op jit(solution)/shard_map/pallas_call | solution.py:178
  177.3 4.0 pad_maximum_fusion.1.near
  184.6 2.0 copy-done.36
  186.5 8.5 %shard_map.267 = bf16[2048,256]{1,0:T(8,128)(2,1)S(1)} custom-call(bf16[1024,2048]{1,0:T(8,128)(2,1)} %pad_maximum_fusion.1.near, bf16[1024,2048]{1,0:T(8,128)(2,1)} %copy-done.36, bf16[256,2048]{1,0:T(8,128)(2,1)S(1)} %bitcast.152), custom_call_target="tpu_custom_call" | custom-call | flops 2147483648 | bytes 8388608 | tf_op jit(solution)/shard_map/pallas_call | solution.py:195
  196.0 35.0 %shard_map.268 = (bf16[2,2,512,256]{3,2,1,0:T(8,128)(2,1)S(1)}, bf16[2,2,512,256]{3,2,1,0:T(8,128)(2,1)S(1)}, bf16[2,2,512,256]{3,2,1,0:T(8,128)(2,1)S(1)}, bf16[2,2,512,256]{3,2,1,0:T(8,128)(2,1)}) custom-call(f32[2,2,512,768]{3,2,1,0:T(8,128)} %bitcast.203, f32[2,2,512,768]{3,2,1,0:T(8,128)} %bitcast.204, f32[2,2,512,768]{3,2,1,0:T(8,128)} %bitcast.205, ...), custom_call_target="tpu_custom_call" | custom-call | flops 7516192768 | bytes 12582912 | tf_op jit(solution)/shard_map/pallas_call | solution.py:436
  232.3 12.9 %shard_map.269 = (bf16[512,768]{1,0:T(8,128)(2,1)}, bf16[512,768]{1,0:T(8,128)(2,1)S(1)}, bf16[512,768]{1,0:T(8,128)(2,1)S(1)}, bf16[512,768]{1,0:T(8,128)(2,1)S(1)}) custom-call(s32[2]{0:T(128)S(1)} %scatter.4.base, bf16[2048,2048]{1,0:T(8,128)(2,1)} %get-tuple-element.135.v, bf16[2048,256]{1,0:T(8,128)(2,1)} %bitcast.174, bf16[2048,256]{1,0:T(8,128)(2,1)} %bitcast.177, ...), custom_call_target="tpu_custom_call" | custom-call | flops 6442450944 | bytes 11534336 | tf_op jit(solution)/shard_map/pallas_call | solution.py:352
  245.3 4.3 fusion
  251.2 1.8 collective-permute-start.23
  260.2 29.2 %shard_map.270 = (bf16[2048,1024]{1,0:T(8,128)(2,1)}, bf16[2048,1024]{1,0:T(8,128)(2,1)}, f32[1,1024]{1,0:T(1,128)S(1)}) custom-call(s32[2]{0:T(128)S(1)} %scatter.4.base, bf16[2048,2048]{1,0:T(8,128)(2,1)} %get-tuple-element.140.v, bf16[1024,2048]{1,0:T(8,128)(2,1)} %pad_maximum_fusion.1.near, bf16[1024,2048]{1,0:T(8,128)(2,1)} %copy-done.36, ...), custom_call_target="tpu_custom_call" | custom-call | flops 17179869184 | bytes 33554432 | tf_op jit(solution)/shard_map/pallas_call | solution.py:232
  290.3 15.6 %shard_map.271 = (bf16[512,1024]{1,0:T(8,128)(2,1)}, bf16[512,1024]{1,0:T(8,128)(2,1)S(1)}, bf16[512,1024]{1,0:T(8,128)(2,1)S(1)}, bf16[512,1024]{1,0:T(8,128)(2,1)}) custom-call(s32[2]{0:T(128)S(1)} %scatter.4.base, bf16[2048,2048]{1,0:T(8,128)(2,1)} %get-tuple-element.140.v, bf16[2048,1024]{1,0:T(8,128)(2,1)} %get-tuple-element.166.refs_0_.du), custom_call_target="tpu_custom_call" | custom-call | flops 8589934592 | bytes 12582912 | tf_op jit(solution)/shard_map/pallas_call | solution.py:352
  307.3 14.3 %shard_map.272 = bf16[1024,2048]{1,0:T(8,128)(2,1)} custom-call(bf16[2048,1024]{1,0:T(8,128)(2,1)} %get-tuple-element.169.v.active, bf16[1024,2048]{1,0:T(8,128)(2,1)} %pad_maximum_fusion.1.near, bf16[1024,2048]{1,0:T(8,128)(2,1)} %copy-done.36), custom_call_target="tpu_custom_call" | custom-call | flops 8589934592 | bytes 16777216 | tf_op jit(solution)/shard_map/pallas_call | solution.py:370
  321.6 54.5 %collective-permute-done.25 = bf16[512,768]{1,0:T(8,128)(2,1)} collective-permute-done((bf16[512,768]{1,0:T(8,128)(2,1)}, bf16[512,768]{1,0:T(8,128)(2,1)}, u32[]{:S(2)}, u32[]{:S(2)}) %collective-permute-start.25) | collective-permute-done | bytes 786464 | tf_op jit(solution)/shard_map/ppermute | solution.py:55
  378.4 17.8 %shard_map.273 = (bf16[1024,2048]{1,0:T(8,128)(2,1)}, f32[4,2048]{1,0:T(4,128)S(1)}, f32[1,768]{1,0:T(1,128)S(1)}) custom-call(s32[2]{0:T(128)S(1)} %scatter.4.base, bf16[2048,256]{1,0:T(8,128)(2,1)} %bitcast.175, bf16[2048,256]{1,0:T(8,128)(2,1)} %bitcast.178, bf16[2048,256]{1,0:T(8,128)(2,1)} %bitcast.207, ...), custom_call_target="tpu_custom_call" | custom-call | flops 7516192768 | bytes 19922944 | tf_op jit(solution)/shard_map/pallas_call | solution.py:304
  396.2 4.3 fusion.23
  400.5 1.5 add_convert_fusion.7
  403.2 17.7 %shard_map.274 = (bf16[1024,2048]{1,0:T(8,128)(2,1)}, f32[4,2048]{1,0:T(4,128)S(1)}, f32[1,768]{1,0:T(1,128)S(1)}) custom-call(s32[2]{0:T(128)S(1)} %scatter.4.base, bf16[2048,256]{1,0:T(8,128)(2,1)} %bitcast.176, bf16[2048,256]{1,0:T(8,128)(2,1)} %bitcast.179, bf16[2048,256]{1,0:T(8,128)(2,1)} %bitcast.208, ...), custom_call_target="tpu_custom_call" | custom-call | flops 7516192768 | bytes 19922944 | tf_op jit(solution)/shard_map/pallas_call | solution.py:304
  422.3 6.0 %all-to-all-start.3 = ((f32[32,1,768]{2,1,0:T(1,128)}), f32[32,1,768]{2,1,0:T(1,128)S(1)}, u32[]{:S(2)}, u32[]{:S(2)}) async-start(f32[32,1,768]{2,1,0:T(1,128)} %copy.92), calls=%async_computation.3 | async-start | bytes 196608 | tf_op jit(solution)/shard_map/all_to_all | solution.py:530
  429.7 1.9 collective-permute-start.34
  431.5 15.2 %all-to-all-done.3 = f32[32,1,768]{2,1,0:T(1,128)S(1)} async-done(((f32[32,1,768]{2,1,0:T(1,128)}), f32[32,1,768]{2,1,0:T(1,128)S(1)}, u32[]{:S(2)}, u32[]{:S(2)}) %all-to-all-start.3) | async-done | bytes 98336 | tf_op jit(solution)/shard_map/all_to_all | solution.py:530
  448.6 1.9 add_convert_fusion.3
  452.6 10.0 %shard_map.275 = bf16[1024,2048]{1,0:T(8,128)(2,1)} custom-call(s32[2]{0:T(128)S(1)} %scatter.4.base, bf16[2048,256]{1,0:T(8,128)(2,1)S(1)} %bitcast.156, bf16[2048,1024]{1,0:T(8,128)(2,1)} %get-tuple-element.169.v.active, bf16[256,2048]{1,0:T(8,128)(2,1)S(1)} %bitcast.153, bf16[320,2048]{1,0:T(8,128)(2,1)S(1)} %copy-done.11, ...), custom_call_target="tpu_custom_call" | custom-call | flops 5368709120 | bytes 10485760 | tf_op jit(solution)/shard_map/pallas_call | solution.py:256
  463.8 4.5 fusion.22
  468.9 6.9 %collective-permute-done.38 = bf16[256,2048]{1,0:T(8,128)(2,1)S(1)} collective-permute-done((bf16[256,2048]{1,0:T(8,128)(2,1)S(1)}, bf16[256,2048]{1,0:T(8,128)(2,1)S(1)}, u32[]{:S(2)}, u32[]{:S(2)}) %collective-permute-start.38) | collective-permute-done | bytes 1048608 | tf_op jit(solution)/shard_map/ppermute | solution.py:55
  475.8 4.0 add_convert_fusion.1
  480.5 10.0 %shard_map.276 = bf16[1024,2048]{1,0:T(8,128)(2,1)} custom-call(s32[2]{0:T(128)S(1)} %scatter.4.base, bf16[2048,256]{1,0:T(8,128)(2,1)S(1)} %bitcast.157, bf16[2048,1024]{1,0:T(8,128)(2,1)} %get-tuple-element.169.v.active, bf16[256,2048]{1,0:T(8,128)(2,1)S(1)} %bitcast.154, bf16[320,2048]{1,0:T(8,128)(2,1)S(1)} %copy-done.11, ...), custom_call_target="tpu_custom_call" | custom-call | flops 5368709120 | bytes 10485760 | tf_op jit(solution)/shard_map/pallas_call | solution.py:256
  490.6 2.4 add_convert_fusion.8
  493.0 3.5 all-to-all-start.4
  497.6 2.9 add_convert_fusion.5
  500.5 10.0 %collective-permute-done.39 = bf16[256,2048]{1,0:T(8,128)(2,1)} collective-permute-done((bf16[256,2048]{1,0:T(8,128)(2,1)}, bf16[256,2048]{1,0:T(8,128)(2,1)}, u32[]{:S(2)}, u32[]{:S(2)}) %collective-permute-start.39) | collective-permute-done | bytes 1048608 | tf_op jit(solution)/shard_map/ppermute | solution.py:55
  513.1 9.0 %collective-permute-done.36 = bf16[512,1024]{1,0:T(8,128)(2,1)S(1)} collective-permute-done((bf16[512,1024]{1,0:T(8,128)(2,1)S(1)}, bf16[512,1024]{1,0:T(8,128)(2,1)S(1)}, u32[]{:S(2)}, u32[]{:S(2)}) %collective-permute-start.36) | collective-permute-done | bytes 1048608 | tf_op jit(solution)/shard_map/ppermute | solution.py:55
  522.7 2.7 add_convert_fusion
  525.4 3.8 all-to-all-start.5
  529.8 7.3 %collective-permute-done.40 = bf16[256,2048]{1,0:T(8,128)(2,1)} collective-permute-done((bf16[256,2048]{1,0:T(8,128)(2,1)}, bf16[256,2048]{1,0:T(8,128)(2,1)}, u32[]{:S(2)}, u32[]{:S(2)}) %collective-permute-start.40) | collective-permute-done | bytes 1048608 | tf_op jit(solution)/shard_map/ppermute | solution.py:55
  537.1 4.9 add_convert_fusion.6
  542.1 2.4 collective-permute-done.44
  547.9 3.2 fusion.21
  551.1 4.5 all-to-all-done.5.source
  557.0 16.4 %collective-permute-done.45 = bf16[256,2048]{1,0:T(8,128)(2,1)} collective-permute-done((bf16[256,2048]{1,0:T(8,128)(2,1)}, bf16[256,2048]{1,0:T(8,128)(2,1)}, u32[]{:S(2)}, u32[]{:S(2)}) %collective-permute-start.45) | collective-permute-done | bytes 1048608 | tf_op jit(solution)/shard_map/ppermute | solution.py:55
  573.4 6.0 %fusion.12 = (bf16[1,256,2048]{2,1,0:T(8,128)(2,1)}, bf16[1,256,2048]{2,1,0:T(8,128)(2,1)}) fusion(f32[256]{0:T(256)S(1)} %broadcast_multiply_fusion, f32[256]{0:T(256)S(1)} %broadcast_multiply_fusion.1, f32[256]{0:T(256)S(1)} %add_rsqrt_fusion, f32[256]{0:T(256)S(1)} %broadcast_multiply_fusion.2, bf16[1,256,2048]{2,1,0:T(8,128)(2,1)} %param.19, ...), kind=kLoop, calls=%fused_computation.35 | loop fusion | flops 14155776 | bytes 12595200 | tf_op jit(solution)/shard_map/broadcast_in_dim | solution.py:917
  579.4 2.8 convert_element_type.232
  (305 shorter events, 71.4 us)
Async XLA Ops:
  7.2 62.7 %collective-permute-start.1 = (bf16[256,2048]{1,0:T(8,128)(2,1)}, bf16[256,2048]{1,0:T(8,128)(2,1)}, u32[]{:S(2)}, u32[]{:S(2)}) collective-permute-start(bf16[256,2048]{1,0:T(8,128)(2,1)} %bitcast.180), channel_id=1, source_target_pairs={{0,8},{8,0},{1,9},{9,1},{2,10},{10,2},{3,11},{11,3},{4,12},{12,4},... | collective-permute-start | bytes 3145736 | tf_op jit(solution)/shard_map/ppermute | solution.py:55
  10.3 59.6 %collective-permute-start = (bf16[256,2048]{1,0:T(8,128)(2,1)}, bf16[256,2048]{1,0:T(8,128)(2,1)}, u32[]{:S(2)}, u32[]{:S(2)}) collective-permute-start(bf16[256,2048]{1,0:T(8,128)(2,1)} %bitcast.181), channel_id=1, source_target_pairs={{0,2},{2,0},{1,3},{3,1},{4,6},{6,4},{5,7},{7,5},{8,10},{10,8},{9,1... | collective-permute-start | bytes 3145736 | tf_op jit(solution)/shard_map/ppermute | solution.py:55
  11.8 61.8 %collective-permute-start.3 = (bf16[256,2048]{1,0:T(8,128)(2,1)}, bf16[256,2048]{1,0:T(8,128)(2,1)}, u32[]{:S(2)}, u32[]{:S(2)}) collective-permute-start(bf16[256,2048]{1,0:T(8,128)(2,1)} %bitcast.182), channel_id=1, source_target_pairs={{0,1},{1,0},{2,3},{3,2},{4,5},{5,4},{6,7},{7,6},{8,9},{9,8},{10,11... | collective-permute-start | bytes 3145736 | tf_op jit(solution)/shard_map/ppermute | solution.py:55
  19.2 27.0 %all-to-all-start = ((bf16[32,16,256]{2,1,0:T(8,128)(2,1)}), bf16[32,16,256]{2,1,0:T(8,128)(2,1)S(1)}, u32[]{:S(2)}, u32[]{:S(2)}) async-start(bf16[32,16,256]{2,1,0:T(8,128)(2,1)} %broadcast_in_dim.60), calls=%async_computation | async-start | bytes 524288 | tf_op jit(solution)/shard_map/all_to_all | solution.py:530
  25.5 46.3 %collective-permute-start.7 = (bf16[320,2048]{1,0:T(8,128)(2,1)S(1)}, bf16[320,2048]{1,0:T(8,128)(2,1)}, u32[]{:S(2)}, u32[]{:S(2)}) collective-permute-start(bf16[320,2048]{1,0:T(8,128)(2,1)S(1)} %constant_dynamic-update-slice_fusion.4.b0), channel_id=1, source_target_pairs={{0,4},{4,0},{1,5},{5,1},{2,6},{6,2},{3,7},{7,3},{8,12},{12,8},{9,1... | collective-permute-start | bytes 3932168 | tf_op jit(solution)/shard_map/ppermute | solution.py:55
  28.3 44.1 %collective-permute-start.9 = (bf16[160,2048]{1,0:T(8,128)(2,1)}, bf16[160,2048]{1,0:T(8,128)(2,1)}, u32[]{:S(2)}, u32[]{:S(2)}) collective-permute-start(bf16[160,2048]{1,0:T(8,128)(2,1)} %slice.223), channel_id=1, source_target_pairs={{0,16},{16,0},{1,17},{17,1},{2,18},{18,2},{3,19},{19,3},{4,20},{20... | collective-permute-start | bytes 1966088 | tf_op jit(solution)/shard_map/ppermute | solution.py:55
  46.2 26.2 %all-to-all-start.1 = ((bf16[8,64,768]{2,1,0:T(8,128)(2,1)}), bf16[8,64,768]{2,1,0:T(8,128)(2,1)S(1)}, u32[]{:S(2)}, u32[]{:S(2)}) async-start(bf16[8,64,768]{2,1,0:T(8,128)(2,1)} %get-tuple-element.115), calls=%async_computation.1 | async-start | bytes 1572864 | tf_op jit(solution)/shard_map/all_to_all | solution.py:530
  69.9 26.3 %collective-permute-start.2 = (bf16[256,2048]{1,0:T(8,128)(2,1)}, bf16[256,2048]{1,0:T(8,128)(2,1)}, u32[]{:S(2)}, u32[]{:S(2)}) collective-permute-start(bf16[256,2048]{1,0:T(8,128)(2,1)} %collective-permute-done.1), channel_id=1, source_target_pairs={{0,2},{2,0},{1,3},{3,1},{4,6},{6,4},{5,7},{7,5},{8,10},{10,8},{9,1... | collective-permute-start | bytes 3145736 | tf_op jit(solution)/shard_map/ppermute | solution.py:55
  71.8 24.5 %collective-permute-start.4 = (bf16[256,2048]{1,0:T(8,128)(2,1)}, bf16[256,2048]{1,0:T(8,128)(2,1)}, u32[]{:S(2)}, u32[]{:S(2)}) collective-permute-start(bf16[256,2048]{1,0:T(8,128)(2,1)} %collective-permute-done), channel_id=1, source_target_pairs={{0,1},{1,0},{2,3},{3,2},{4,5},{5,4},{6,7},{7,6},{8,9},{9,8},{10,11... | collective-permute-start | bytes 3145736 | tf_op jit(solution)/shard_map/ppermute | solution.py:55
  71.8 27.2 %collective-permute-start.5 = (bf16[256,2048]{1,0:T(8,128)(2,1)}, bf16[256,2048]{1,0:T(8,128)(2,1)}, u32[]{:S(2)}, u32[]{:S(2)}) collective-permute-start(bf16[256,2048]{1,0:T(8,128)(2,1)} %collective-permute-done.1), channel_id=1, source_target_pairs={{0,1},{1,0},{2,3},{3,2},{4,5},{5,4},{6,7},{7,6},{8,9},{9,8},{10,11... | collective-permute-start | bytes 3145736 | tf_op jit(solution)/shard_map/ppermute | solution.py:55
  72.3 91.5 %copy-start.3 = (bf16[8,64,768]{2,1,0:T(8,128)(2,1)}, bf16[8,64,768]{2,1,0:T(8,128)(2,1)S(1)}, u32[]{:S(2)}) copy-start(bf16[8,64,768]{2,1,0:T(8,128)(2,1)S(1)} %all-to-all-done.1) | copy-start | bytes 2359300
  72.3 23.8 %collective-permute-start.8 = (bf16[2,256,768]{2,1,0:T(8,128)(2,1)S(1)}, bf16[2,256,768]{2,1,0:T(8,128)(2,1)S(1)}, u32[]{:S(2)}, u32[]{:S(2)}) collective-permute-start(bf16[2,256,768]{2,1,0:T(8,128)(2,1)S(1)} %bitcast.158), channel_id=1, source_target_pairs={{0,4},{4,0},{1,5},{5,1},{2,6},{6,2},{3,7},{7,3},{8,12},{12,8},{9,1... | collective-permute-start | bytes 2359304 | tf_op jit(solution)/shard_map/ppermute | solution.py:55
  73.6 60.2 %collective-permute-start.14 = (bf16[256,2048]{1,0:T(8,128)(2,1)}, bf16[256,2048]{1,0:T(8,128)(2,1)}, u32[]{:S(2)}, u32[]{:S(2)}) collective-permute-start(bf16[256,2048]{1,0:T(8,128)(2,1)} %bitcast.11), channel_id=1, source_target_pairs={{0,8},{8,0},{1,9},{9,1},{2,10},{10,2},{3,11},{11,3},{4,12},{12,4},... | collective-permute-start | bytes 3145736 | tf_op jit(solution)/shard_map/ppermute | solution.py:55
  78.5 75.9 %all-to-all-start.2 = ((bf16[8,64,1024]{2,1,0:T(8,128)(2,1)}), bf16[8,64,1024]{2,1,0:T(8,128)(2,1)}, u32[]{:S(2)}, u32[]{:S(2)}) async-start(bf16[8,64,1024]{2,1,0:T(8,128)(2,1)} %get-tuple-element.142), calls=%async_computation.2 | async-start | bytes 2097152 | tf_op jit(solution)/shard_map/all_to_all | solution.py:530
  82.8 20.7 %copy-start.30 = (bf16[1,256,2048]{2,1,0:T(8,128)(2,1)S(1)}, bf16[1,256,2048]{2,1,0:T(8,128)(2,1)}, u32[]{:S(2)}) copy-start(bf16[1,256,2048]{2,1,0:T(8,128)(2,1)} %param.18) | copy-start | bytes 3145732
  82.8 174.8 %all-gather.2.cloned.1.call-start = ((), (), s32[]{:S(2)}) async-start(), calls=%async_computation.7 | async-start | bytes 5242880 | tf_op jit(solution)/shard_map/all_gather | solution.py:742
  96.2 36.5 %collective-permute-start.10 = (bf16[2,256,768]{2,1,0:T(8,128)(2,1)S(1)}, bf16[2,256,768]{2,1,0:T(8,128)(2,1)}, u32[]{:S(2)}, u32[]{:S(2)}) collective-permute-start(bf16[2,256,768]{2,1,0:T(8,128)(2,1)S(1)} %bitcast.159), channel_id=1, source_target_pairs={{0,16},{16,0},{1,17},{17,1},{2,18},{18,2},{3,19},{19,3},{4,20},{20... | collective-permute-start | bytes 2359304 | tf_op jit(solution)/shard_map/ppermute | solution.py:55
  96.2 67.6 %copy-start.24 = (bf16[2,256,768]{2,1,0:T(8,128)(2,1)}, bf16[2,256,768]{2,1,0:T(8,128)(2,1)S(1)}, u32[]{:S(2)}) copy-start(bf16[2,256,768]{2,1,0:T(8,128)(2,1)S(1)} %collective-permute-done.8.w1.q1) | copy-start | bytes 2359300
  96.2 40.1 %collective-permute-start.6 = (bf16[256,2048]{1,0:T(8,128)(2,1)}, bf16[256,2048]{1,0:T(8,128)(2,1)S(1)}, u32[]{:S(2)}, u32[]{:S(2)}) collective-permute-start(bf16[256,2048]{1,0:T(8,128)(2,1)} %collective-permute-done.2), channel_id=1, source_target_pairs={{0,1},{1,0},{2,3},{3,2},{4,5},{5,4},{6,7},{7,6},{8,9},{9,8},{10,11... | collective-permute-start | bytes 3145736 | tf_op jit(solution)/shard_map/ppermute | solution.py:55
  96.3 36.4 %collective-permute-start.11 = (bf16[160,2048]{1,0:T(8,128)(2,1)}, bf16[160,2048]{1,0:T(8,128)(2,1)S(1)}, u32[]{:S(2)}, u32[]{:S(2)}) collective-permute-start(bf16[160,2048]{1,0:T(8,128)(2,1)} %collective-permute-done.9), channel_id=1, source_target_pairs={{0,4},{4,0},{1,5},{5,1},{2,6},{6,2},{3,7},{7,3},{8,12},{12,8},{9,1... | collective-permute-start | bytes 1966088 | tf_op jit(solution)/shard_map/ppermute | solution.py:55
  99.0 36.0 %collective-permute-start.13 = (bf16[256,2048]{1,0:T(8,128)(2,1)}, bf16[256,2048]{1,0:T(8,128)(2,1)}, u32[]{:S(2)}, u32[]{:S(2)}) collective-permute-start(bf16[256,2048]{1,0:T(8,128)(2,1)} %bitcast.11), channel_id=1, source_target_pairs={{0,2},{2,0},{1,3},{3,1},{4,6},{6,4},{5,7},{7,5},{8,10},{10,8},{9,1... | collective-permute-start | bytes 3145736 | tf_op jit(solution)/shard_map/ppermute | solution.py:55
  103.4 29.4 %copy-start.46 = (bf16[64,2048]{1,0:T(8,128)(2,1)S(1)}, bf16[64,2048]{1,0:T(8,128)(2,1)}, u32[]{:S(2)}) copy-start(bf16[64,2048]{1,0:T(8,128)(2,1)} %param.26) | copy-start | bytes 786436
  132.7 20.2 %collective-permute-start.16 = (bf16[256,2048]{1,0:T(8,128)(2,1)}, bf16[256,2048]{1,0:T(8,128)(2,1)S(1)}, u32[]{:S(2)}, u32[]{:S(2)}) collective-permute-start(bf16[256,2048]{1,0:T(8,128)(2,1)} %bitcast.11), channel_id=1, source_target_pairs={{0,1},{1,0},{2,3},{3,2},{4,5},{5,4},{6,7},{7,6},{8,9},{9,8},{10,11... | collective-permute-start | bytes 3145736 | tf_op jit(solution)/shard_map/ppermute | solution.py:55
  132.7 30.8 %collective-permute-start.21 = (bf16[160,2048]{1,0:T(8,128)(2,1)}, bf16[160,2048]{1,0:T(8,128)(2,1)}, u32[]{:S(2)}, u32[]{:S(2)}) collective-permute-start(bf16[160,2048]{1,0:T(8,128)(2,1)} %slice.179), channel_id=1, source_target_pairs={{0,16},{16,0},{1,17},{17,1},{2,18},{18,2},{3,19},{19,3},{4,20},{20... | collective-permute-start | bytes 1966088 | tf_op jit(solution)/shard_map/ppermute | solution.py:55
  133.8 29.7 %collective-permute-start.12 = (bf16[2,256,768]{2,1,0:T(8,128)(2,1)}, bf16[2,256,768]{2,1,0:T(8,128)(2,1)}, u32[]{:S(2)}, u32[]{:S(2)}) collective-permute-start(bf16[2,256,768]{2,1,0:T(8,128)(2,1)} %collective-permute-done.10.w2.q2), channel_id=1, source_target_pairs={{0,4},{4,0},{1,5},{5,1},{2,6},{6,2},{3,7},{7,3},{8,12},{12,8},{9,1... | collective-permute-start | bytes 2359304 | tf_op jit(solution)/shard_map/ppermute | solution.py:55
  134.9 41.8 %collective-permute-start.15 = (bf16[256,2048]{1,0:T(8,128)(2,1)}, bf16[256,2048]{1,0:T(8,128)(2,1)}, u32[]{:S(2)}, u32[]{:S(2)}) collective-permute-start(bf16[256,2048]{1,0:T(8,128)(2,1)} %collective-permute-done.14), channel_id=1, source_target_pairs={{0,2},{2,0},{1,3},{3,1},{4,6},{6,4},{5,7},{7,5},{8,10},{10,8},{9,1... | collective-permute-start | bytes 3145736 | tf_op jit(solution)/shard_map/ppermute | solution.py:55
  136.3 40.6 %collective-permute-start.17 = (bf16[256,2048]{1,0:T(8,128)(2,1)}, bf16[256,2048]{1,0:T(8,128)(2,1)}, u32[]{:S(2)}, u32[]{:S(2)}) collective-permute-start(bf16[256,2048]{1,0:T(8,128)(2,1)} %collective-permute-done.13), channel_id=1, source_target_pairs={{0,1},{1,0},{2,3},{3,2},{4,5},{5,4},{6,7},{7,6},{8,9},{9,8},{10,11... | collective-permute-start | bytes 3145736 | tf_op jit(solution)/shard_map/ppermute | solution.py:55
  152.9 23.9 %copy-start.23 = (f32[2048,1]{1,0:T(8,128)}, f32[2048,1]{1,0:T(8,128)S(1)}, u32[]{:S(2)}) copy-start(f32[2048,1]{1,0:T(8,128)S(1)} %get-tuple-element.164.scale) | copy-start | bytes 24580
  152.9 29.9 %collective-permute-start.18 = (bf16[256,2048]{1,0:T(8,128)(2,1)}, bf16[256,2048]{1,0:T(8,128)(2,1)}, u32[]{:S(2)}, u32[]{:S(2)}) collective-permute-start(bf16[256,2048]{1,0:T(8,128)(2,1)} %collective-permute-done.14), channel_id=1, source_target_pairs={{0,1},{1,0},{2,3},{3,2},{4,5},{5,4},{6,7},{7,6},{8,9},{9,8},{10,11... | collective-permute-start | bytes 3145736 | tf_op jit(solution)/shard_map/ppermute | solution.py:55
  154.4 425.0 %reduce-scatter.2.cloned.1.call-start = ((), (), s32[]{:S(2)}) async-start(), calls=%async_computation.8 | async-start | bytes 5242880 | tf_op jit(solution)/shard_map/reduce_scatter | solution.py:746
  163.5 87.7 %collective-permute-start.22 = (bf16[160,2048]{1,0:T(8,128)(2,1)}, bf16[160,2048]{1,0:T(8,128)(2,1)S(1)}, u32[]{:S(2)}, u32[]{:S(2)}) collective-permute-start(bf16[160,2048]{1,0:T(8,128)(2,1)} %collective-permute-done.21), channel_id=1, source_target_pairs={{0,4},{4,0},{1,5},{5,1},{2,6},{6,2},{3,7},{7,3},{8,12},{12,8},{9,1... | collective-permute-start | bytes 1966088 | tf_op jit(solution)/shard_map/ppermute | solution.py:55
  176.8 7.7 %collective-permute-start.19 = (bf16[256,2048]{1,0:T(8,128)(2,1)}, bf16[256,2048]{1,0:T(8,128)(2,1)S(1)}, u32[]{:S(2)}, u32[]{:S(2)}) collective-permute-start(bf16[256,2048]{1,0:T(8,128)(2,1)} %collective-permute-done.15), channel_id=1, source_target_pairs={{0,1},{1,0},{2,3},{3,2},{4,5},{5,4},{6,7},{7,6},{8,9},{9,8},{10,11... | collective-permute-start | bytes 3145736 | tf_op jit(solution)/shard_map/ppermute | solution.py:55
  176.9 7.3 %collective-permute-start.20 = (bf16[2,64,2048]{2,1,0:T(8,128)(2,1)}, bf16[2,64,2048]{2,1,0:T(8,128)(2,1)S(1)}, u32[]{:S(2)}, u32[]{:S(2)}) collective-permute-start(bf16[2,64,2048]{2,1,0:T(8,128)(2,1)} %fusion.13), channel_id=1, source_target_pairs={{0,1},{1,0},{2,3},{3,2},{4,5},{5,4},{6,7},{7,6},{8,9},{9,8},{10,11... | collective-permute-start | bytes 1572872 | tf_op jit(solution)/shard_map/ppermute | solution.py:55
  196.0 35.1 %copy-start.37 = (bf16[1024,2048]{1,0:T(8,128)(2,1)S(1)}, bf16[1024,2048]{1,0:T(8,128)(2,1)}, u32[]{:S(2)}) copy-start(bf16[1024,2048]{1,0:T(8,128)(2,1)} %copy-done.36) | copy-start | bytes 12582916
  249.7 5.6 collective-permute-start.30
  251.2 38.2 %collective-permute-start.23 = (bf16[512,768]{1,0:T(8,128)(2,1)}, bf16[512,768]{1,0:T(8,128)(2,1)S(1)}, u32[]{:S(2)}, u32[]{:S(2)}) collective-permute-start(bf16[512,768]{1,0:T(8,128)(2,1)} %get-tuple-element.152), channel_id=1, source_target_pairs={{0,4},{4,0},{1,5},{5,1},{2,6},{6,2},{3,7},{7,3},{8,12},{12,8},{9,1... | collective-permute-start | bytes 2359304 | tf_op jit(solution)/shard_map/ppermute | solution.py:55
  306.0 70.2 %collective-permute-start.24 = (bf16[512,1024]{1,0:T(8,128)(2,1)}, bf16[512,1024]{1,0:T(8,128)(2,1)}, u32[]{:S(2)}, u32[]{:S(2)}) collective-permute-start(bf16[512,1024]{1,0:T(8,128)(2,1)} %get-tuple-element.156), channel_id=1, source_target_pairs={{0,4},{4,0},{1,5},{5,1},{2,6},{6,2},{3,7},{7,3},{8,12},{12,8},{9,1... | collective-permute-start | bytes 3145736 | tf_op jit(solution)/shard_map/ppermute | solution.py:55
  307.2 68.9 %collective-permute-start.25 = (bf16[512,768]{1,0:T(8,128)(2,1)}, bf16[512,768]{1,0:T(8,128)(2,1)}, u32[]{:S(2)}, u32[]{:S(2)}) collective-permute-start(bf16[512,768]{1,0:T(8,128)(2,1)} %add_convert_fusion.9), channel_id=1, source_target_pairs={{0,16},{16,0},{1,17},{17,1},{2,18},{18,2},{3,19},{19,3},{4,20},{20... | collective-permute-start | bytes 2359304 | tf_op jit(solution)/shard_map/ppermute | solution.py:55
  400.5 48.1 %collective-permute-start.37 = (bf16[256,2048]{1,0:T(8,128)(2,1)}, bf16[256,2048]{1,0:T(8,128)(2,1)}, u32[]{:S(2)}, u32[]{:S(2)}) collective-permute-start(bf16[256,2048]{1,0:T(8,128)(2,1)} %get-tuple-element.187), channel_id=1, source_target_pairs={{0,1},{1,0},{2,3},{3,2},{4,5},{5,4},{6,7},{7,6},{8,9},{9,8},{10,11... | collective-permute-start | bytes 3145736 | tf_op jit(solution)/shard_map/ppermute | solution.py:55
  403.2 25.1 %copy-start.38 = (bf16[2,2,64,2048]{3,2,0,1:T(8,128)(2,1)S(1)}, bf16[2,2,64,2048]{3,2,0,1:T(8,128)(2,1)}, u32[]{:S(2)}) copy-start(bf16[2,2,64,2048]{3,2,0,1:T(8,128)(2,1)} %reverse_select_fusion) | copy-start | bytes 3145732
  403.2 45.4 %collective-permute-start.26 = (bf16[256,1024]{1,0:T(8,128)(2,1)}, bf16[256,1024]{1,0:T(8,128)(2,1)}, u32[]{:S(2)}, u32[]{:S(2)}) collective-permute-start(bf16[256,1024]{1,0:T(8,128)(2,1)} %get-tuple-element.159), channel_id=1, source_target_pairs={{0,16},{16,0},{1,17},{17,1},{2,18},{18,2},{3,19},{19,3},{4,20},{20... | collective-permute-start | bytes 1572872 | tf_op jit(solution)/shard_map/ppermute | solution.py:55
  422.3 24.5 %all-to-all-start.3 = ((f32[32,1,768]{2,1,0:T(1,128)}), f32[32,1,768]{2,1,0:T(1,128)S(1)}, u32[]{:S(2)}, u32[]{:S(2)}) async-start(f32[32,1,768]{2,1,0:T(1,128)} %copy.92), calls=%async_computation.3 | async-start | bytes 196608 | tf_op jit(solution)/shard_map/all_to_all | solution.py:530
  429.2 39.2 %collective-permute-start.31 = (bf16[256,2048]{1,0:T(8,128)(2,1)}, bf16[256,2048]{1,0:T(8,128)(2,1)}, u32[]{:S(2)}, u32[]{:S(2)}) collective-permute-start(bf16[256,2048]{1,0:T(8,128)(2,1)} %get-tuple-element.174), channel_id=1, source_target_pairs={{0,1},{1,0},{2,3},{3,2},{4,5},{5,4},{6,7},{7,6},{8,9},{9,8},{10,11... | collective-permute-start | bytes 3145736 | tf_op jit(solution)/shard_map/ppermute | solution.py:55
  429.5 38.8 %collective-permute-start.27 = (bf16[256,2048]{1,0:T(8,128)(2,1)}, bf16[256,2048]{1,0:T(8,128)(2,1)}, u32[]{:S(2)}, u32[]{:S(2)}) collective-permute-start(bf16[256,2048]{1,0:T(8,128)(2,1)} %get-tuple-element.170), channel_id=1, source_target_pairs={{0,1},{1,0},{2,3},{3,2},{4,5},{5,4},{6,7},{7,6},{8,9},{9,8},{10,11... | collective-permute-start | bytes 3145736 | tf_op jit(solution)/shard_map/ppermute | solution.py:55
  429.7 33.0 %collective-permute-start.34 = (bf16[2,64,2048]{2,1,0:T(8,128)(2,1)}, bf16[2,64,2048]{2,1,0:T(8,128)(2,1)}, u32[]{:S(2)}, u32[]{:S(2)}) collective-permute-start(bf16[2,64,2048]{2,1,0:T(8,128)(2,1)} %slice_bitcast_fusion.2), channel_id=1, source_target_pairs={{0,4},{4,0},{1,5},{5,1},{2,6},{6,2},{3,7},{7,3},{8,12},{12,8},{9,1... | collective-permute-start | bytes 1572872 | tf_op jit(solution)/shard_map/ppermute | solution.py:55
  448.6 133.6 %copy-start.50 = (f32[64]{0:T(128)}, f32[64]{0:T(128)S(1)}, u32[]{:S(2)}) copy-start(f32[64]{0:T(128)S(1)} %get-tuple-element.282) | copy-start | bytes 772
  450.6 25.2 %collective-permute-start.38 = (bf16[256,2048]{1,0:T(8,128)(2,1)S(1)}, bf16[256,2048]{1,0:T(8,128)(2,1)S(1)}, u32[]{:S(2)}, u32[]{:S(2)}) collective-permute-start(bf16[256,2048]{1,0:T(8,128)(2,1)S(1)} %add_convert_fusion.3), channel_id=1, source_target_pairs={{0,2},{2,0},{1,3},{3,1},{4,6},{6,4},{5,7},{7,5},{8,10},{10,8},{9,1... | collective-permute-start | bytes 3145736 | tf_op jit(solution)/shard_map/ppermute | solution.py:55
  462.7 27.9 %collective-permute-start.35 = (bf16[512,768]{1,0:T(8,128)(2,1)S(1)}, bf16[512,768]{1,0:T(8,128)(2,1)S(1)}, u32[]{:S(2)}, u32[]{:S(2)}) collective-permute-start(bf16[512,768]{1,0:T(8,128)(2,1)S(1)} %copy-done.27), channel_id=1, source_target_pairs={{0,4},{4,0},{1,5},{5,1},{2,6},{6,2},{3,7},{7,3},{8,12},{12,8},{9,1... | collective-permute-start | bytes 2359304 | tf_op jit(solution)/shard_map/ppermute | solution.py:55
  463.5 48.8 %collective-permute-start.33 = (bf16[256,1024]{1,0:T(8,128)(2,1)}, bf16[256,1024]{1,0:T(8,128)(2,1)}, u32[]{:S(2)}, u32[]{:S(2)}) collective-permute-start(bf16[256,1024]{1,0:T(8,128)(2,1)} %get-tuple-element.176), channel_id=1, source_target_pairs={{0,16},{16,0},{1,17},{17,1},{2,18},{18,2},{3,19},{19,3},{4,20},{20... | collective-permute-start | bytes 1572872 | tf_op jit(solution)/shard_map/ppermute | solution.py:55
  468.4 28.2 %collective-permute-start.42 = (bf16[256,2048]{1,0:T(8,128)(2,1)}, bf16[256,2048]{1,0:T(8,128)(2,1)}, u32[]{:S(2)}, u32[]{:S(2)}) collective-permute-start(bf16[256,2048]{1,0:T(8,128)(2,1)} %get-tuple-element.192), channel_id=1, source_target_pairs={{0,1},{1,0},{2,3},{3,2},{4,5},{5,4},{6,7},{7,6},{8,9},{9,8},{10,11... | collective-permute-start | bytes 3145736 | tf_op jit(solution)/shard_map/ppermute | solution.py:55
  468.4 29.1 %collective-permute-start.28 = (bf16[256,2048]{1,0:T(8,128)(2,1)}, bf16[256,2048]{1,0:T(8,128)(2,1)}, u32[]{:S(2)}, u32[]{:S(2)}) collective-permute-start(bf16[256,2048]{1,0:T(8,128)(2,1)} %get-tuple-element.171), channel_id=1, source_target_pairs={{0,1},{1,0},{2,3},{3,2},{4,5},{5,4},{6,7},{7,6},{8,9},{9,8},{10,11... | collective-permute-start | bytes 3145736 | tf_op jit(solution)/shard_map/ppermute | solution.py:55
  479.8 30.6 %collective-permute-start.39 = (bf16[256,2048]{1,0:T(8,128)(2,1)}, bf16[256,2048]{1,0:T(8,128)(2,1)}, u32[]{:S(2)}, u32[]{:S(2)}) collective-permute-start(bf16[256,2048]{1,0:T(8,128)(2,1)} %get-tuple-element.189), channel_id=1, source_target_pairs={{0,2},{2,0},{1,3},{3,1},{4,6},{6,4},{5,7},{7,5},{8,10},{10,8},{9,1... | collective-permute-start | bytes 3145736 | tf_op jit(solution)/shard_map/ppermute | solution.py:55
  490.5 38.7 %collective-permute-start.32 = (bf16[256,2048]{1,0:T(8,128)(2,1)}, bf16[256,2048]{1,0:T(8,128)(2,1)}, u32[]{:S(2)}, u32[]{:S(2)}) collective-permute-start(bf16[256,2048]{1,0:T(8,128)(2,1)} %get-tuple-element.175), channel_id=1, source_target_pairs={{0,1},{1,0},{2,3},{3,2},{4,5},{5,4},{6,7},{7,6},{8,9},{9,8},{10,11... | collective-permute-start | bytes 3145736 | tf_op jit(solution)/shard_map/ppermute | solution.py:55
  493.0 32.4 %all-to-all-start.4 = ((bf16[8,64,768]{2,1,0:T(8,128)(2,1)}), bf16[8,64,768]{2,1,0:T(8,128)(2,1)S(1)}, u32[]{:S(2)}, u32[]{:S(2)}) async-start(bf16[8,64,768]{2,1,0:T(8,128)(2,1)} %bitcast.187), calls=%async_computation.4 | async-start | bytes 1572864 | tf_op jit(solution)/shard_map/all_to_all | solution.py:530
  496.6 25.5 %collective-permute-start.36 = (bf16[512,1024]{1,0:T(8,128)(2,1)S(1)}, bf16[512,1024]{1,0:T(8,128)(2,1)S(1)}, u32[]{:S(2)}, u32[]{:S(2)}) collective-permute-start(bf16[512,1024]{1,0:T(8,128)(2,1)S(1)} %copy-done.21), channel_id=1, source_target_pairs={{0,4},{4,0},{1,5},{5,1},{2,6},{6,2},{3,7},{7,3},{8,12},{12,8},{9,1... | collective-permute-start | bytes 3145736 | tf_op jit(solution)/shard_map/ppermute | solution.py:55
  497.5 32.3 %collective-permute-start.43 = (bf16[256,2048]{1,0:T(8,128)(2,1)}, bf16[256,2048]{1,0:T(8,128)(2,1)}, u32[]{:S(2)}, u32[]{:S(2)}) collective-permute-start(bf16[256,2048]{1,0:T(8,128)(2,1)} %get-tuple-element.193), channel_id=1, source_target_pairs={{0,1},{1,0},{2,3},{3,2},{4,5},{5,4},{6,7},{7,6},{8,9},{9,8},{10,11... | collective-permute-start | bytes 3145736 | tf_op jit(solution)/shard_map/ppermute | solution.py:55
  500.5 22.2 %copy-start.45 = (bf16[512,1024]{1,0:T(8,128)(2,1)S(1)}, bf16[512,1024]{1,0:T(8,128)(2,1)}, u32[]{:S(2)}) copy-start(bf16[512,1024]{1,0:T(8,128)(2,1)} %get-tuple-element.160) | copy-start | bytes 3145732
  510.4 26.7 %collective-permute-start.40 = (bf16[256,2048]{1,0:T(8,128)(2,1)}, bf16[256,2048]{1,0:T(8,128)(2,1)}, u32[]{:S(2)}, u32[]{:S(2)}) collective-permute-start(bf16[256,2048]{1,0:T(8,128)(2,1)} %add_convert_fusion.5), channel_id=1, source_target_pairs={{0,2},{2,0},{1,3},{3,1},{4,6},{6,4},{5,7},{7,5},{8,10},{10,8},{9,1... | collective-permute-start | bytes 3145736 | tf_op jit(solution)/shard_map/ppermute | solution.py:55
  512.3 32.1 %collective-permute-start.44 = (bf16[256,2048]{1,0:T(8,128)(2,1)}, bf16[256,2048]{1,0:T(8,128)(2,1)}, u32[]{:S(2)}, u32[]{:S(2)}) collective-permute-start(bf16[256,2048]{1,0:T(8,128)(2,1)} %get-tuple-element.195), channel_id=1, source_target_pairs={{0,8},{8,0},{1,9},{9,1},{2,10},{10,2},{3,11},{11,3},{4,12},{12,4},... | collective-permute-start | bytes 3145736 | tf_op jit(solution)/shard_map/ppermute | solution.py:55
  522.1 23.6 %collective-permute-start.46 = (bf16[64,2048]{1,0:T(8,128)(2,1)S(1)}, bf16[64,2048]{1,0:T(8,128)(2,1)S(1)}, u32[]{:S(2)}, u32[]{:S(2)}) collective-permute-start(bf16[64,2048]{1,0:T(8,128)(2,1)S(1)} %fusion.19), channel_id=1, source_target_pairs={{0,16},{16,0},{1,17},{17,1},{2,18},{18,2},{3,19},{19,3},{4,20},{20... | collective-permute-start | bytes 786440 | tf_op jit(solution)/shard_map/ppermute | solution.py:55
  525.4 30.2 %all-to-all-start.5 = ((bf16[8,64,1024]{2,1,0:T(8,128)(2,1)}), bf16[8,64,1024]{2,1,0:T(8,128)(2,1)S(1)}, u32[]{:S(2)}, u32[]{:S(2)}) async-start(bf16[8,64,1024]{2,1,0:T(8,128)(2,1)} %bitcast.61), calls=%async_computation.5 | async-start | bytes 2097152 | tf_op jit(solution)/shard_map/all_to_all | solution.py:530
  529.3 27.8 %collective-permute-start.29 = (bf16[256,2048]{1,0:T(8,128)(2,1)}, bf16[256,2048]{1,0:T(8,128)(2,1)}, u32[]{:S(2)}, u32[]{:S(2)}) collective-permute-start(bf16[256,2048]{1,0:T(8,128)(2,1)} %get-tuple-element.172), channel_id=1, source_target_pairs={{0,1},{1,0},{2,3},{3,2},{4,5},{5,4},{6,7},{7,6},{8,9},{9,8},{10,11... | collective-permute-start | bytes 3145736 | tf_op jit(solution)/shard_map/ppermute | solution.py:55
  544.4 29.0 %collective-permute-start.45 = (bf16[256,2048]{1,0:T(8,128)(2,1)}, bf16[256,2048]{1,0:T(8,128)(2,1)}, u32[]{:S(2)}, u32[]{:S(2)}) collective-permute-start(bf16[256,2048]{1,0:T(8,128)(2,1)} %get-tuple-element.196), channel_id=1, source_target_pairs={{0,8},{8,0},{1,9},{9,1},{2,10},{10,2},{3,11},{11,3},{4,12},{12,4},... | collective-permute-start | bytes 3145736 | tf_op jit(solution)/shard_map/ppermute | solution.py:55
  544.4 29.0 %collective-permute-start.41 = (bf16[256,2048]{1,0:T(8,128)(2,1)}, bf16[256,2048]{1,0:T(8,128)(2,1)}, u32[]{:S(2)}, u32[]{:S(2)}) collective-permute-start(bf16[256,2048]{1,0:T(8,128)(2,1)} %get-tuple-element.191), channel_id=1, source_target_pairs={{0,2},{2,0},{1,3},{3,1},{4,6},{6,4},{5,7},{7,5},{8,10},{10,8},{9,1... | collective-permute-start | bytes 3145736 | tf_op jit(solution)/shard_map/ppermute | solution.py:55
  (42 other events, 177.9 us)
Sparse Core Ops, SparseCore 0:
  154.5 86.8 all-gather.1
  321.7 123.1 reduce-scatter.1
